TPU v7x, 32 devices: a whole 2x2x4 slice. The times are simulated.
32 devices in a mesh: crop: 2 (over y), row: 4 (over z), col: 4 (over x, core).
Axes of the slice: x: 2, y: 2, z: 4, core: 2. Of those that a mesh axis runs over, the one named last changes fastest.
Arguments:
- pair_tiles: bfloat16 [512, 256, 128], P(('crop', 'row'), 'col'), parts along dimension 0, may hold values from -6 to 6
- grad_out: bfloat16 [512, 256, 128], P(('crop', 'row'), 'col'), parts along dimension 0, may hold values from -6 to 6
- exponents: int32 [512, 256], P(('crop', 'row'), 'col'), parts along dimension 0, may hold values from -10 to -8
- token_mask: int32 [512], P('crop'), parts along dimension 0, may hold values from 0 to 1, as said below
- gain_in: float32 [128], replicated, may hold values from 0.1 to 1.9
- w_proj: bfloat16 [128, 512], replicated, may hold values from -0.5 to 0.5
- w_gate: bfloat16 [128, 128], replicated, may hold values from -0.5 to 0.5
- gain_out: float32 [128], replicated, may hold values from 0.1 to 1.9
- w_out: bfloat16 [128, 128], replicated, may hold values from -0.5 to 0.5
Outputs:
- d_pair: bfloat16 [512, 256, 128], P(('crop', 'row'), 'col'), parts along dimension 0
- d_wproj: float32 [256, 512], P('crop'), parts along dimension 0
- d_wgate: float32 [256, 128], P('crop'), parts along dimension 0
- d_wout: float32 [256, 128], P('crop'), parts along dimension 0
There are 2 independent parts, one for each index of `crop`. A program takes and returns all parts, laid end to end along the dimension named above; an argument that names none is the same for every part. Nothing has to cross between parts.
Inputs may be any that keep to these rules, and one draw needn't show every extreme that they name: `token_mask`: 1 on a leading run of tokens and 0 after it; the run covers at least half of the 256 tokens.
All inputs are finite; a program needn't handle non-finite values.
Results may differ from a plain program's by a relative error of at most 0.015.
The roundings to bfloat16 on the way count: a program that leaves them out, or rounds other values in their place, can miss the bound.
Values may be sent and summed in bfloat16 or wider, within the bound.
No kernel may reach another device: no remote copies, remote signals or barrier semaphores. Data moves between devices by JAX's collectives and lax.ppermute only.
A program may use at most 128 MiB of HBM per device.

v0:
```python
import jax
import jax.numpy as jnp
from jax import lax
from jax.sharding import PartitionSpec as P

EPS = 1e-05


def layer_norm(values, gain):
    center = jnp.mean(values, axis=-1, keepdims=True)
    spread = jnp.mean((values - center) ** 2, axis=-1, keepdims=True)
    inverse = lax.rsqrt(spread + EPS)
    centred = (values - center) * inverse
    return (centred * gain, centred, inverse)


def norm_back(upstream, centred, inverse, gain):
    scaled = upstream * gain
    first = jnp.mean(scaled, axis=-1, keepdims=True)
    second = jnp.mean(scaled * centred, axis=-1, keepdims=True)
    return inverse * (scaled - first - centred * second)


def local(pair_tiles, grad_out, exponents, token_mask, gain_in, w_proj, w_gate, gain_out, w_out):
    f32 = jnp.float32
    bf16 = jnp.bfloat16
    rows, cols, width = pair_tiles.shape
    crop_len = token_mask.shape[0]
    row_at = lax.axis_index("row")
    col_at = lax.axis_index("col")
    maskf = token_mask.astype(f32)
    mask_rows = lax.dynamic_slice_in_dim(maskf, row_at * rows, rows)
    mask_cols = lax.dynamic_slice_in_dim(maskf, col_at * cols, cols)
    pair_mask = (mask_rows[:, None] * mask_cols[None, :])[..., None]
    normed_f, centred, inverse = layer_norm(pair_tiles.astype(f32), gain_in)
    normed = normed_f.astype(bf16)
    flat = normed.reshape(-1, width)
    projected = jnp.dot(flat, w_proj, preferred_element_type=f32).reshape(rows, cols, 4 * width)
    gate_a = projected[..., :width]
    value_a = projected[..., width : 2 * width]
    gate_b = projected[..., 2 * width : 3 * width]
    value_b = projected[..., 3 * width :]
    sig_a = jax.nn.sigmoid(gate_a)
    sig_b = jax.nn.sigmoid(gate_b)
    left = (pair_mask * sig_a * value_a).astype(bf16)
    right_raw = pair_mask * sig_b * value_b
    bound = (448.0 * jnp.exp2(exponents.astype(f32)))[..., None]
    right = jnp.clip(right_raw, -bound, bound).astype(bf16)
    inside = (jnp.abs(right_raw) <= bound).astype(f32)
    panel = lax.all_gather(right, "row", axis=0, tiled=True)
    tri_cols = lax.psum_scatter(
        jnp.einsum("jkc,ikc->jic", panel, left, preferred_element_type=f32).astype(jnp.bfloat16),
        "col",
        scatter_dimension=0,
        tiled=True,
    ).astype(jnp.float32)
    tri = jnp.transpose(tri_cols, (1, 0, 2))
    tnorm_f, tcentred, tinverse = layer_norm(tri, gain_out)
    tnorm = tnorm_f.astype(bf16)
    tflat = tnorm.reshape(-1, width)
    opened = jax.nn.sigmoid(jnp.dot(flat, w_gate, preferred_element_type=f32)).reshape(
        rows, cols, width
    )
    outproj = jnp.dot(tflat, w_out, preferred_element_type=f32).reshape(rows, cols, width)
    upstream = grad_out.astype(f32)
    d_open = upstream * outproj
    d_outproj = (upstream * opened).astype(bf16).reshape(-1, width)
    g_out = jnp.dot(tflat.T, d_outproj, preferred_element_type=f32)
    d_tnorm = jnp.dot(d_outproj, w_out.T, preferred_element_type=f32).reshape(rows, cols, width)
    d_tri = norm_back(d_tnorm, tcentred, tinverse, gain_out).astype(bf16)
    d_gatepre = (d_open * opened * (1.0 - opened)).astype(bf16).reshape(-1, width)
    g_gate = jnp.dot(flat.T, d_gatepre, preferred_element_type=f32)
    grad_full = lax.all_gather(d_tri, "col", axis=1, tiled=True)
    d_left = jnp.einsum("ijc,jkc->ikc", grad_full, panel, preferred_element_type=f32)
    d_right = (
        lax.psum_scatter(
            jnp.einsum("ijc,ikc->jkc", grad_full, left, preferred_element_type=f32).astype(
                jnp.bfloat16
            ),
            "row",
            scatter_dimension=0,
            tiled=True,
        ).astype(jnp.float32)
        * inside
    )
    d_gate_a = d_left * pair_mask * value_a * sig_a * (1.0 - sig_a)
    d_value_a = d_left * pair_mask * sig_a
    d_gate_b = d_right * pair_mask * value_b * sig_b * (1.0 - sig_b)
    d_value_b = d_right * pair_mask * sig_b
    d_proj = (
        jnp.concatenate([d_gate_a, d_value_a, d_gate_b, d_value_b], axis=-1)
        .astype(bf16)
        .reshape(-1, 4 * width)
    )
    g_proj = jnp.dot(flat.T, d_proj, preferred_element_type=f32)
    d_normed = jnp.dot(d_proj, w_proj.T, preferred_element_type=f32) + jnp.dot(
        d_gatepre, w_gate.T, preferred_element_type=f32
    )
    d_pair = norm_back(d_normed.reshape(rows, cols, width), centred, inverse, gain_in).astype(bf16)
    sum_proj, sum_gate, sum_out = lax.psum((g_proj, g_gate, g_out), ("row", "col"))
    return (d_pair, sum_proj / crop_len, sum_gate / crop_len, sum_out / crop_len)


def solution(mesh):
    return jax.shard_map(
        local,
        mesh=mesh,
        in_specs=(
            P(("crop", "row"), "col", None),
            P(("crop", "row"), "col", None),
            P(("crop", "row"), "col"),
            P("crop"),
            P(),
            P(),
            P(),
            P(),
            P(),
        ),
        out_specs=(
            P(("crop", "row"), "col", None),
            P("crop", None),
            P("crop", None),
            P("crop", None),
        ),
        check_vma=False,
    )
```

profile of v0, /device:TPU:0, one launch (start us, length us, event | category | flops | bytes accessed | tf_op | source)
XLA Modules:
  0.0 432.6 jit_solution(13707802590525659649)
XLA Ops:
  8.8 1.8 convert_reduce_fusion
  10.7 2.3 fusion.29
  15.7 3.2 copy-done.1
  18.9 2.8 minimum_convert_fusion
  21.9 3.4 multiply_convert_fusion.4
  25.3 4.7 %copy.30 = bf16[64,64,128]{0,1,2:T(8,128)(2,1)S(1)} copy(bf16[64,64,128]{2,1,0:T(8,128)(2,1)} %multiply_convert_fusion.4) | data formatting | bytes 2097152 | tf_op jit(solution)/shard_map/convert_element_type | solution.py:45
  30.0 75.4 %all-gather.3.cloned.1.call-done = bf16[256,64,128]{2,1,0:T(8,128)(2,1)} async-done(((bf16[64,64,128]{2,1,0:T(8,128)(2,1)}), bf16[256,64,128]{2,1,0:T(8,128)(2,1)}) %all-gather.3.cloned.1.call-update) | async-done | bytes 4194320 | tf_op jit(solution)/shard_map/all_gather | solution.py:50
  105.4 7.4 %copy.27 = bf16[256,64,128]{0,1,2:T(8,128)(2,1)} copy(bf16[256,64,128]{2,1,0:T(8,128)(2,1)} %all-gather.3.cloned.1.call-done) | data formatting | bytes 8388608 | tf_op jit(solution)/shard_map/all_gather | solution.py:50
  112.8 5.4 %convert_bitcast_fusion.1 = bf16[256,64,128]{0,1,2:T(8,128)(2,1)} fusion(bf16[64,64,128]{0,1,2:T(8,128)(2,1)S(1)} %copy.30, bf16[256,64,128]{0,1,2:T(8,128)(2,1)} %copy.27), kind=kOutput, calls=%fused_computation.22 | convolution fusion | flops 270532608 | bytes 9437184 | tf_op jit(solution)/shard_map/jkc,ikc->jic/dot_general | solution.py:52
  118.2 7.3 %copy.24 = bf16[256,64,128]{2,1,0:T(8,128)(2,1)} copy(bf16[256,64,128]{0,1,2:T(8,128)(2,1)} %convert_bitcast_fusion.1) | data formatting | bytes 8388608 | tf_op jit(solution)/shard_map/convert_element_type | solution.py:52
  126.3 3.3 fusion.2
  129.6 39.1 %reduce-scatter.3.cloned.1.call-done = bf16[64,64,128]{2,1,0:T(8,128)(2,1)} async-done(((bf16[256,64,128]{2,1,0:T(8,128)(2,1)}), bf16[64,64,128]{2,1,0:T(8,128)(2,1)}) %reduce-scatter.3.cloned.1.call-update) | async-done | bytes 1048592 | tf_op jit(solution)/shard_map/reduce_scatter | solution.py:51
  168.8 2.3 bitcast_reduce_fusion
  171.1 2.4 fusion.50
  173.5 5.0 %multiply_reduce_fusion.1 = (f32[64,64]{1,0:T(8,128)S(1)}, f32[64,64]{1,0:T(8,128)S(1)}, f32[64,64,128]{2,1,0:T(8,128)S(1)}) fusion(f32[128]{0:T(128)S(1)} %copy-done.22, f32[64,64]{1,0:T(8,128)S(1)} %add_rsqrt_fusion, f32[64,64]{1,0:T(8,128)S(1)} %broadcast_multiply_fusion.7, bf16[64,64,128]{2,1,0:T(8,128)(2,1)S(1)} %copy-done.5, ...), kind=kOutput, calls=%fused_computation.74 | convolution fusion | flops 139452416 | bytes 6390272 | tf_op jit(solution)/shard_map/dot_general | solution.py:69
  178.5 3.3 fusion.48
  181.8 1.6 copy.26
  183.5 34.6 %all-gather.5.cloned.1.call-done = bf16[64,256,128]{2,0,1:T(8,128)(2,1)} async-done(((bf16[64,64,128]{2,0,1:T(8,128)(2,1)}), bf16[64,256,128]{2,0,1:T(8,128)(2,1)}) %all-gather.5.cloned.1.call-update) | async-done | bytes 4194320 | tf_op jit(solution)/shard_map/all_gather | solution.py:73
  218.1 7.3 %copy.28 = bf16[64,256,128]{1,0,2:T(8,128)(2,1)} copy(bf16[64,256,128]{2,0,1:T(8,128)(2,1)} %all-gather.5.cloned.1.call-done) | data formatting | bytes 8388608 | tf_op jit(solution)/shard_map/all_gather | solution.py:73
  225.5 5.4 %fusion.70 = bf16[128,64,256]{2,1,0:T(8,128)(2,1)} fusion(bf16[64,64,128]{0,1,2:T(8,128)(2,1)S(1)} %copy.30, bf16[64,256,128]{1,0,2:T(8,128)(2,1)} %copy.28), kind=kOutput, calls=%fused_computation.103 | convolution fusion | flops 268435456 | bytes 9437184 | tf_op jit(solution)/shard_map/ijc,ikc->jkc/dot_general | solution.py:77
  230.8 7.3 %copy.32 = bf16[128,64,256]{0,1,2:T(8,128)(2,1)} copy(bf16[128,64,256]{2,1,0:T(8,128)(2,1)} %fusion.70) | data formatting | bytes 8388608 | tf_op jit(solution)/shard_map/ijc,ikc->jkc/dot_general | solution.py:77
  239.4 4.5 %fusion.33 = bf16[64,64,128]{2,1,0:T(8,128)(2,1)S(1)} fusion(f32[64,64,128]{2,1,0:T(8,128)} %bitcast.82, bf16[64,64,128]{2,1,0:T(8,128)(2,1)} %param.10, f32[128]{0:T(128)S(1)} %copy-done.22, f32[64,64]{1,0:T(8,128)S(1)} %add_rsqrt_fusion, f32[64,64]{1,0:T(8,128)S(1)} %broadcast_multiply_fusion.7, bf16[64,64,128]{2,1,0:T(8,128)(2,1)S(1)} %copy-done.6, ...), kind=kOutput, calls=%fused_computation.41 | convolution fusion | flops 139984896 | bytes 5308928 | tf_op jit(solution)/shard_map/dot_general | solution.py:64
  246.5 4.2 convolution_bitcast_fusion
  250.7 3.2 fusion.69
  253.9 4.5 %copy.29 = f32[128,64,64]{0,1,2:T(8,128)S(1)} copy(f32[128,64,64]{2,1,0:T(8,128)} %fusion.69) | data formatting | bytes 4194304 | tf_op jit(solution)/shard_map/ijc,jkc->ikc/dot_general | solution.py:74
  258.4 56.7 %reduce-scatter.5.cloned.1.call-done = bf16[64,64,128]{2,1,0:T(8,128)(2,1)} async-done(((bf16[256,64,128]{2,1,0:T(8,128)(2,1)}), bf16[64,64,128]{2,1,0:T(8,128)(2,1)}) %reduce-scatter.5.cloned.1.call-update) | async-done | bytes 1048592 | tf_op jit(solution)/shard_map/reduce_scatter | solution.py:76
  315.1 5.4 %multiply_convert_fusion.3 = (bf16[64,64,128]{2,1,0:T(8,128)(2,1)S(1)}, bf16[64,64,128]{2,1,0:T(8,128)(2,1)S(1)}, bf16[64,64,128]{2,1,0:T(8,128)(2,1)S(1)}, bf16[64,64,128]{2,1,0:T(8,128)(2,1)S(1)}) fusion(f32[128,64,64]{0,1,2:T(8,128)S(1)} %copy.29, f32[64,64,512]{2,1,0:T(8,128)} %copy-done.1, f32[64,64]{1,0:T(8,128)S(1)} %get-tuple-element.21, ...), kind=kLoop, calls=%fused_computation.70 | loop fusion | flops 14680064 | bytes 15761408 | tf_op jit(solution)/shard_map/convert.12
  324.1 3.1 fusion.3
  328.0 1.8 fusion.25
  329.9 3.3 fusion.28
  333.2 88.3 %all-reduce.3.cloned.1.call-done = (f32[128,512]{1,0:T(8,128)}, f32[128,128]{1,0:T(8,128)}, f32[128,128]{1,0:T(8,128)}) async-done(((f32[128,512]{1,0:T(8,128)}, f32[128,128]{1,0:T(8,128)}, f32[128,128]{1,0:T(8,128)}), (f32[128,512]{1,0:T(8,128)}, f32[128,128]{1,0:T(8,128)}, f32[128,128]{1,0:T(8,128)})) %all-reduce.3.cloned.1.call-update) | async-done | bytes 393232 | tf_op jit(solution)/shard_map/psum | solution.py:100
  421.5 1.7 broadcast_multiply_fusion
  (75 shorter events, 16.3 us)
Async XLA Ops:
  7.2 7.3 %copy-start = (bf16[128,512]{1,0:T(8,128)(2,1)S(1)}, bf16[128,512]{1,0:T(8,128)(2,1)}, u32[]{:S(2)}) copy-start(bf16[128,512]{1,0:T(8,128)(2,1)} %param.14) | copy-start | bytes 393220
  7.2 5.9 %copy-start.18 = (s32[64,64]{1,0:T(8,128)S(1)}, s32[64,64]{1,0:T(8,128)}, u32[]{:S(2)}) copy-start(s32[64,64]{1,0:T(8,128)} %param.11) | copy-start | bytes 49156
  7.2 6.0 %copy-start.4 = (bf16[64,64,128]{2,1,0:T(8,128)(2,1)S(1)}, bf16[64,64,128]{2,1,0:T(8,128)(2,1)}, u32[]{:S(2)}) copy-start(bf16[64,64,128]{2,1,0:T(8,128)(2,1)} %param.9) | copy-start | bytes 3145732
  7.2 6.0 %copy-start.21 = (f32[128]{0:T(128)S(1)}, f32[128]{0:T(128)}, u32[]{:S(2)}) copy-start(f32[128]{0:T(128)} %param.13) | copy-start | bytes 1540
  7.2 98.2 %all-gather.3.cloned.1.call-start = ((), (), s32[]{:S(2)}) async-start(), calls=%async_computation.2 | async-start | bytes 5242880 | tf_op jit(solution)/shard_map/all_gather | solution.py:50
  14.5 1.2 copy-start.7
  15.7 3.2 copy-start.1
  21.8 147.0 %reduce-scatter.3.cloned.1.call-start = ((), (), s32[]{:S(2)}) async-start(), calls=%async_computation.3 | async-start | bytes 5242880 | tf_op jit(solution)/shard_map/reduce_scatter | solution.py:51
  125.6 0.8 copy-start.20
  125.6 92.5 %all-gather.5.cloned.1.call-start = ((), (), s32[]{:S(2)}) async-start(), calls=%async_computation.4 | async-start | bytes 5242880 | tf_op jit(solution)/shard_map/all_gather | solution.py:73
  129.6 43.9 %copy-start.19 = (bf16[128,128]{1,0:T(8,128)(2,1)S(1)}, bf16[128,128]{1,0:T(8,128)(2,1)}, u32[]{:S(2)}) copy-start(bf16[128,128]{1,0:T(8,128)(2,1)} %param.17) | copy-start | bytes 98308
  129.6 43.9 %copy-start.22 = (f32[128]{0:T(128)S(1)}, f32[128]{0:T(128)}, u32[]{:S(2)}) copy-start(f32[128]{0:T(128)} %param.16) | copy-start | bytes 1540
  168.8 4.7 %copy-start.5 = (bf16[64,64,128]{2,1,0:T(8,128)(2,1)S(1)}, bf16[64,64,128]{2,1,0:T(8,128)(2,1)}, u32[]{:S(2)}) copy-start(bf16[64,64,128]{2,1,0:T(8,128)(2,1)} %reduce-scatter.3.cloned.1.call-done) | copy-start | bytes 3145732
  168.8 4.7 %copy-start.11 = (bf16[64,64,128]{2,1,0:T(8,128)(2,1)S(1)}, bf16[64,64,128]{2,1,0:T(8,128)(2,1)}, u32[]{:S(2)}) copy-start(bf16[64,64,128]{2,1,0:T(8,128)(2,1)} %param.10) | copy-start | bytes 3145732
  183.5 131.7 %reduce-scatter.5.cloned.1.call-start = ((), (), s32[]{:S(2)}) async-start(), calls=%async_computation.5 | async-start | bytes 5242880 | tf_op jit(solution)/shard_map/reduce_scatter | solution.py:76
  238.2 1.2 copy-start.6
  238.2 6.6 %copy-start.8 = (bf16[64,64,128]{2,1,0:T(8,128)(2,1)S(1)}, bf16[64,64,128]{2,1,0:T(8,128)(2,1)}, u32[]{:S(2)}) copy-start(bf16[64,64,128]{2,1,0:T(8,128)(2,1)} %copy-done.7) | copy-start | bytes 3145732
  238.2 183.3 %all-reduce.3.cloned.1.call-start = ((), (), s32[]{:S(2)}) async-start(), calls=%async_computation.6 | async-start | bytes 786432 | tf_op jit(solution)/shard_map/psum | solution.py:100
  239.4 11.3 %copy-start.3 = (bf16[64,256,128]{1,0,2:T(8,128)(2,1)S(1)}, bf16[64,256,128]{1,0,2:T(8,128)(2,1)}, u32[]{:S(2)}) copy-start(bf16[64,256,128]{1,0,2:T(8,128)(2,1)} %copy.28) | copy-start | bytes 12582916
  243.9 1.0 copy-start.12
  244.8 1.7 copy-start.10
  246.5 4.2 copy-start.2
  315.1 7.5 %copy-start.9 = (bf16[64,64,128]{2,1,0:T(8,128)(2,1)S(1)}, bf16[64,64,128]{2,1,0:T(8,128)(2,1)}, u32[]{:S(2)}) copy-start(bf16[64,64,128]{2,1,0:T(8,128)(2,1)} %copy-done.7) | copy-start | bytes 3145732
  320.6 1.0 copy-start.14
  320.6 1.3 copy-start.15
  320.6 1.6 copy-start.16
  320.6 2.0 copy-start.17
  324.1 3.1 copy-start.13
Sparse Core Ops, SparseCore 0:
  21.9 83.4 all-gather.2
  125.7 43.0 reduce-scatter.2
  183.6 34.4 all-gather.4
  238.3 76.7 reduce-scatter.4
  330.0 91.4 all-reduce.2
where the time goes:
time: 434 us; the launch traced here: 433 us
  waiting for transfers between devices  294 us (68%)
  local copies, waits for them, and re-layouts  48.6 us (11%)
  matrix products  38.6 us (9%)
  other arithmetic  36.4 us (8%)
  between operations  14.1 us (3%)
    psum x1, waiting for transfers between devices, local(): lax.psum((g_proj, g_gate, g_out), ('row', 'col'))  88.3 us
    all_gather x1, waiting for transfers between devices, local(): panel = lax.all_gather(right, 'row', axis=0, tiled=True)  75.4 us
    reduce_scatter x1, waiting for transfers between devices, local(): lax.psum_scatter(jnp.einsum('ijc,ikc->jkc', grad_full, left, preferred_el...  56.7 us
    reduce_scatter x1, waiting for transfers between devices, local(): lax.psum_scatter(jnp.einsum('jkc,ikc->jic', panel, left, preferred_elemen...  39.1 us
    all_gather x1, waiting for transfers between devices, local(): grad_full = lax.all_gather(d_tri, 'col', axis=1, tiled=True)  34.6 us
  transfers between devices with their start and end apart: 5, of which 5 were waited for; matrix products, arithmetic and copies ran while one was open for 7% of the time, Pallas kernels for 0%

commit v1 on v0

--- a/solution.py
+++ b/solution.py
@@ -1,6 +1,10 @@
+import functools
+
 import jax
 import jax.numpy as jnp
 from jax import lax
+from jax.experimental import pallas as pl
+from jax.experimental.pallas import tpu as pltpu
 from jax.sharding import PartitionSpec as P
 
 EPS = 1e-05
@@ -21,7 +25,7 @@
     return inverse * (scaled - first - centred * second)
 
 
-def local(pair_tiles, grad_out, exponents, token_mask, gain_in, w_proj, w_gate, gain_out, w_out):
+def plain(pair_tiles, grad_out, exponents, token_mask, gain_in, w_proj, w_gate, gain_out, w_out):
     f32 = jnp.float32
     bf16 = jnp.bfloat16
     rows, cols, width = pair_tiles.shape
@@ -101,9 +105,477 @@
     return (d_pair, sum_proj / crop_len, sum_gate / crop_len, sum_out / crop_len)
 
 
+SUB = 16
+HALF = 64
+WIDTH = 128
+LANES = SUB * HALF
+GROUP = 16
+NT = (((1,), (1,)), ((), ()))
+NN = (((1,), (0,)), ((), ()))
+TN = (((0,), (0,)), ((), ()))
+F32 = jnp.float32
+BF16 = jnp.bfloat16
+
+
+def mm(a, b, dims):
+    return lax.dot_general(a, b, dims, preferred_element_type=F32)
+
+
+def params():
+    return pltpu.CompilerParams(vmem_limit_bytes=40 * 1024 * 1024)
+
+
+def cost(flops, size, exps=0):
+    return pl.CostEstimate(flops=flops, bytes_accessed=size, transcendentals=exps)
+
+
+def first_half(rows):
+    return lax.broadcasted_iota(jnp.int32, (rows, WIDTH), 1) < HALF
+
+
+def swap_halves(a, b):
+    first = first_half(HALF)
+    return (
+        jnp.where(first, a, pltpu.roll(b, HALF, 1)),
+        jnp.where(first, pltpu.roll(a, HALF, 1), b),
+    )
+
+
+def eye():
+    row = lax.broadcasted_iota(jnp.int32, (WIDTH, WIDTH), 0)
+    lane = lax.broadcasted_iota(jnp.int32, (WIDTH, WIDTH), 1)
+    return (row == lane).astype(F32).astype(BF16)
+
+
+def to_channels(cells):
+    return mm(eye(), cells, NT)
+
+
+def to_cells(channels):
+    return mm(channels, eye(), TN)
+
+
+def stage_rows(channels, buf):
+    for t in range(SUB // 2):
+        part = channels[:, t * WIDTH : (t + 1) * WIDTH]
+        one, two = swap_halves(part[:HALF], part[HALF:])
+        buf[(2 * t) * HALF : (2 * t + 1) * HALF, :] = one
+        buf[(2 * t + 1) * HALF : (2 * t + 2) * HALF, :] = two
+
+
+def panel_row(buf, p):
+    return buf[pl.ds(p, SUB, stride=HALF), :]
+
+
+def channels_of(panels, buf, out):
+    buf[...] = panels.reshape(LANES, WIDTH)
+    for t in range(SUB // 2):
+        one = buf[pl.ds(2 * t, HALF, stride=SUB), :]
+        two = buf[pl.ds(2 * t + 1, HALF, stride=SUB), :]
+        low, high = swap_halves(one, two)
+        out[:HALF, t * WIDTH : (t + 1) * WIDTH] = low
+        out[HALF:, t * WIDTH : (t + 1) * WIDTH] = high
+    return out[...]
+
+
+def norm_channels(values, gain):
+    center = jnp.mean(values, axis=0, keepdims=True)
+    spread = jnp.mean((values - center) ** 2, axis=0, keepdims=True)
+    inverse = lax.rsqrt(spread + EPS)
+    centred = (values - center) * inverse
+    return centred * gain, centred, inverse
+
+
+def norm_back_channels(upstream, centred, inverse, gain):
+    scaled = upstream * gain
+    first = jnp.mean(scaled, axis=0, keepdims=True)
+    second = jnp.mean(scaled * centred, axis=0, keepdims=True)
+    return inverse * (scaled - first - centred * second)
+
+
+def right_kernel(x_ref, gain_ref, w_ref, mask_ref, bound_ref, out_ref, buf):
+    values = to_channels(x_ref[...].reshape(LANES, WIDTH))
+    normed = norm_channels(values, gain_ref[...])[0].astype(BF16)
+    proj = mm(w_ref[...], normed, NN)
+    raw = mask_ref[...] * jax.nn.sigmoid(proj[:WIDTH]) * proj[WIDTH:]
+    bound = bound_ref[...]
+    stage_rows(jnp.clip(raw, -bound, bound), buf)
+    for p in range(HALF):
+        out_ref[p] = panel_row(buf, p).astype(BF16)
+
+
+def left_kernel(x_ref, gain_ref, w_ref, mask_ref, out_ref, buf):
+    values = to_channels(x_ref[...].reshape(LANES, WIDTH))
+    normed = norm_channels(values, gain_ref[...])[0].astype(BF16)
+    proj = mm(w_ref[...], normed, NN)
+    stage_rows(mask_ref[...] * jax.nn.sigmoid(proj[:WIDTH]) * proj[WIDTH:], buf)
+    first = first_half(SUB)
+    for p in range(HALF):
+        row = panel_row(buf, p)
+        out_ref[p, 0] = jnp.where(first, row, 0.0).astype(BF16)
+        out_ref[p, 1] = jnp.where(first, 0.0, row).astype(BF16)
+
+
+def tri_kernel(place_ref, r0, r1, r2, r3, left_ref, out_ref, panel_ref):
+    slots = (r0, r1, r2, r3)
+    place = [place_ref[m] for m in range(4)]
+    for p in range(GROUP):
+        right = jnp.concatenate([r[p] for r in slots], axis=0)
+        left = left_ref[p].reshape(WIDTH, WIDTH)
+        tri = mm(right, left, NT).astype(BF16)
+        for m in range(4):
+            out_ref[place[m], p] = tri[m * SUB : (m + 1) * SUB]
+            panel_ref[place[m], p] = slots[m][p]
+
+
+def mid_kernel(
+    a_ref, b_ref, c_ref, x_ref, grad_ref, gain_in_ref, gain_out_ref, gate_t_ref, out_t_ref, out_w_ref,
+    dtri_ref, dgate_ref, g_out_ref, g_gate_ref, buf, wide,
+):
+    tri = channels_of(
+        a_ref[...].astype(F32) + b_ref[...].astype(F32) + c_ref[...].astype(F32), buf, wide
+    )
+    tnorm_f, tcentred, tinverse = norm_channels(tri, gain_out_ref[...])
+    tnorm = tnorm_f.astype(BF16)
+
+    def turned(ref):
+        buf[...] = ref[...].astype(F32).reshape(LANES, WIDTH)
+        rows = [buf[pl.ds(j, HALF, stride=SUB), :] for j in range(SUB)]
+        return to_channels(jnp.concatenate(rows, axis=0).astype(BF16))
+
+    normed = norm_channels(turned(x_ref), gain_in_ref[...])[0].astype(BF16)
+    upstream = turned(grad_ref)
+    opened = jax.nn.sigmoid(mm(gate_t_ref[...], normed, NN))
+    outproj = mm(out_t_ref[...], tnorm, NN)
+    d_open = upstream * outproj
+    d_outproj = (upstream * opened).astype(BF16)
+    g_out_ref[...] = mm(tnorm, d_outproj, NT)
+    d_tnorm = mm(out_w_ref[...], d_outproj, NN)
+    d_tri = norm_back_channels(d_tnorm, tcentred, tinverse, gain_out_ref[...])
+    d_gatepre = (d_open * opened * (1.0 - opened)).astype(BF16)
+    g_gate_ref[...] = mm(normed, d_gatepre, NT)
+    stage_rows(d_tri, buf)
+    for p in range(HALF):
+        dtri_ref[p] = panel_row(buf, p).astype(BF16)
+    buf[...] = to_cells(d_gatepre)
+    for i in range(HALF):
+        dgate_ref[i] = panel_row(buf, i).astype(BF16)
+
+
+def dright_kernel(place_ref, d0, d1, d2, d3, left_ref, out_ref):
+    blocks = (d0, d1, d2, d3)
+    place = [place_ref[m] for m in range(4)]
+    for p in range(GROUP):
+        grads = jnp.concatenate([d[p] for d in blocks], axis=0)
+        left = left_ref[p].reshape(WIDTH, WIDTH)
+        part = mm(grads, left, NN).astype(BF16)
+        for m in range(4):
+            out_ref[place[m], p] = part[m * SUB : (m + 1) * SUB]
+
+
+def dleft_kernel(*refs):
+    out_ref = refs[-1]
+    parts = (len(refs) - 1) // 5
+    grad_refs, panel_refs = refs[: 4 * parts], refs[4 * parts : 5 * parts]
+    first = first_half(HALF)
+    for p in range(GROUP):
+        grads = jnp.concatenate([d[p] for d in grad_refs], axis=0)
+        right = jnp.concatenate([r[q, p] for r in panel_refs for q in range(4)], axis=0)
+        both = mm(grads, right, TN)
+        out_ref[p] = jnp.where(first, both[:HALF], both[HALF:])
+
+
+def final_kernel(
+    x_ref, dleft_ref, dr_a_ref, dr_b_ref, mask_ref, bound_ref, gain_ref, w_t_ref, w_ref, gate_ref,
+    q0, q1, q2, q3, prev_ref, out_ref, g_ref, buf, wide,
+):
+    values = to_channels(x_ref[...].reshape(LANES, WIDTH))
+    normed_f, centred, inverse = norm_channels(values, gain_ref[...])
+    normed = normed_f.astype(BF16)
+    mask = mask_ref[...]
+    bound = bound_ref[...]
+
+    gates = mm(w_t_ref[: 2 * WIDTH], normed, NN)
+    sig = jax.nn.sigmoid(gates[:WIDTH])
+    d_left = channels_of(dleft_ref[...], buf, wide)
+    d_gate_a = (d_left * mask * gates[WIDTH:] * sig * (1.0 - sig)).astype(BF16)
+    d_value_a = (d_left * mask * sig).astype(BF16)
+
+    gates = mm(w_t_ref[2 * WIDTH :], normed, NN)
+    sig = jax.nn.sigmoid(gates[:WIDTH])
+    inside = jnp.abs(mask * sig * gates[WIDTH:]) <= bound
+    d_right = channels_of(dr_a_ref[...].astype(F32) + dr_b_ref[0].astype(F32), buf, wide)
+    d_right = jnp.where(inside, d_right, 0.0)
+    d_gate_b = (d_right * mask * gates[WIDTH:] * sig * (1.0 - sig)).astype(BF16)
+    d_value_b = (d_right * mask * sig).astype(BF16)
+
+    d_proj = jnp.concatenate([d_gate_a, d_value_a, d_gate_b, d_value_b], axis=0)
+    g_ref[...] = prev_ref[...] + mm(normed, d_proj, NT)
+    d_gate = jnp.concatenate([q[...] for q in (q0, q1, q2, q3)], axis=1).reshape(LANES, WIDTH)
+    d_normed = mm(w_ref[...], d_proj, NN) + mm(gate_ref[...], d_gate, NT)
+    d_pair = norm_back_channels(d_normed, centred, inverse, gain_ref[...]).astype(BF16)
+    out_ref[...] = to_cells(d_pair).astype(BF16).reshape(SUB, HALF, WIDTH)
+
+
+def whole(array):
+    return pl.BlockSpec(array.shape, lambda i: (0,) * array.ndim)
+
+
+def block(shape, at):
+    return pl.BlockSpec(shape, lambda i: at)
+
+
+SMEM = pl.BlockSpec(memory_space=pltpu.SMEM)
+BUF = pltpu.VMEM((LANES, WIDTH), F32)
+WIDE = pltpu.VMEM((WIDTH, LANES), F32)
+PANEL = jax.ShapeDtypeStruct((HALF, SUB, WIDTH), BF16)
+PANEL_SPEC = pl.BlockSpec((GROUP, SUB, WIDTH), lambda i: (i, 0, 0))
+FOUR = jax.ShapeDtypeStruct((4, HALF, SUB, WIDTH), BF16)
+FOUR_SPEC = pl.BlockSpec((4, GROUP, SUB, WIDTH), lambda i: (0, i, 0, 0))
+LEFT_SPEC = pl.BlockSpec((GROUP, 2, HALF, WIDTH), lambda i: (i, 0, 0, 0))
+
+
+def right_part(s, pair, gain, w_b, mask, bound):
+    return pl.pallas_call(
+        right_kernel,
+        grid=(1,),
+        out_shape=PANEL,
+        in_specs=[
+            block((SUB, HALF, WIDTH), (s, 0, 0)), whole(gain), whole(w_b),
+            block((1, LANES), (0, s)), block((1, LANES), (0, s)),
+        ],
+        out_specs=block((HALF, SUB, WIDTH), (0, 0, 0)),
+        scratch_shapes=[BUF],
+        compiler_params=params(),
+        cost_estimate=cost(4 * LANES * WIDTH * WIDTH, 1 << 19, LANES * WIDTH),
+        name="right_part",
+    )(pair, gain, w_b, mask, bound)
+
+
+def left_part(pair, gain, w_a, mask):
+    return pl.pallas_call(
+        left_kernel,
+        grid=(HALF // SUB,),
+        out_shape=jax.ShapeDtypeStruct((HALF, 2, HALF, WIDTH), BF16),
+        in_specs=[
+            pl.BlockSpec((SUB, HALF, WIDTH), lambda i: (i, 0, 0)), whole(gain), whole(w_a),
+            pl.BlockSpec((1, LANES), lambda i: (0, i)),
+        ],
+        out_specs=pl.BlockSpec((HALF, 2, SUB, WIDTH), lambda i: (0, 0, i, 0)),
+        scratch_shapes=[BUF],
+        compiler_params=params(),
+        cost_estimate=cost(16 * LANES * WIDTH * WIDTH, 3 << 20, 4 * LANES * WIDTH),
+        name="left_part",
+    )(pair, gain, w_a, mask)
+
+
+def tri_part(place, slots, left):
+    return pl.pallas_call(
+        tri_kernel,
+        grid=(HALF // GROUP,),
+        out_shape=(FOUR, FOUR),
+        in_specs=[SMEM] + [PANEL_SPEC] * 4 + [LEFT_SPEC],
+        out_specs=(FOUR_SPEC, FOUR_SPEC),
+        compiler_params=params(),
+        cost_estimate=cost(2 * HALF * HALF * WIDTH * WIDTH, 5 << 20),
+        name="tri_part",
+    )(place, *slots, left)
+
+
+def mid_part(s, parts, pair, grad, gain_in, gain_out, gate_t, out_t, w_out):
+    square = jax.ShapeDtypeStruct((WIDTH, WIDTH), F32)
+    columns = block((HALF, SUB, WIDTH), (0, s, 0))
+    small = [gain_in, gain_out, gate_t, out_t, w_out]
+    return pl.pallas_call(
+        mid_kernel,
+        grid=(1,),
+        out_shape=(PANEL, PANEL, square, square),
+        in_specs=[block((HALF, SUB, WIDTH), (0, 0, 0))] * 3 + [columns] * 2 + [whole(a) for a in small],
+        out_specs=(
+            block(PANEL.shape, (0, 0, 0)), block(PANEL.shape, (0, 0, 0)),
+            block(square.shape, (0, 0)), block(square.shape, (0, 0)),
+        ),
+        scratch_shapes=[BUF, WIDE],
+        compiler_params=params(),
+        cost_estimate=cost(12 * LANES * WIDTH * WIDTH, 2 << 20, LANES * WIDTH),
+        name="mid_part",
+    )(*parts, pair, grad, *small)
+
+
+def dright_part(place, blocks, left):
+    return pl.pallas_call(
+        dright_kernel,
+        grid=(HALF // GROUP,),
+        out_shape=FOUR,
+        in_specs=[SMEM] + [PANEL_SPEC] * 4 + [LEFT_SPEC],
+        out_specs=FOUR_SPEC,
+        compiler_params=params(),
+        cost_estimate=cost(2 * HALF * HALF * WIDTH * WIDTH, 4 << 20),
+        name="dright_part",
+    )(place, *blocks, left)
+
+
+def dleft_part(grads, panels):
+    return pl.pallas_call(
+        dleft_kernel,
+        grid=(HALF // GROUP,),
+        out_shape=jax.ShapeDtypeStruct((HALF, HALF, WIDTH), F32),
+        in_specs=[PANEL_SPEC] * len(grads) + [FOUR_SPEC] * len(panels),
+        out_specs=pl.BlockSpec((GROUP, HALF, WIDTH), lambda i: (i, 0, 0)),
+        compiler_params=params(),
+        cost_estimate=cost(8 * HALF * HALF * WIDTH * WIDTH, 10 << 20),
+        name="dleft_part",
+    )(*grads, *panels)
+
+
+def final_part(s, pair, dleft, dr_a, dr_b, mask, bound, gain, w_t, w_proj, w_gate, gates, so_far, into):
+    small = [gain, w_t, w_proj, w_gate]
+    in_specs = [
+        block((SUB, HALF, WIDTH), (s, 0, 0)),
+        block((HALF, SUB, WIDTH), (0, s, 0)),
+        block((HALF, SUB, WIDTH), (0, 0, 0)),
+        block((1, HALF, SUB, WIDTH), (0, 0, 0, 0)),
+        block((1, LANES), (0, s)),
+        block((1, LANES), (0, s)),
+    ]
+    in_specs += [whole(a) for a in small]
+    in_specs += [block((SUB, SUB, WIDTH), (s, 0, 0))] * 4 + [whole(so_far)]
+    operands = [pair, dleft, dr_a, dr_b, mask, bound, *small, *gates, so_far]
+    aliases = {}
+    body = final_kernel
+    if into is not None:
+        in_specs.append(pl.BlockSpec(memory_space=pl.ANY))
+        aliases = {len(operands): 0}
+        operands.append(into)
+
+        def body(*refs):
+            count = len(operands) - 1
+            final_kernel(*refs[:count], *refs[count + 1 :])
+
+    return pl.pallas_call(
+        body,
+        grid=(1,),
+        out_shape=(
+            jax.ShapeDtypeStruct((HALF, HALF, WIDTH), BF16),
+            jax.ShapeDtypeStruct(so_far.shape, F32),
+        ),
+        in_specs=in_specs,
+        out_specs=(block((SUB, HALF, WIDTH), (s, 0, 0)), block(so_far.shape, (0, 0))),
+        scratch_shapes=[BUF, WIDE],
+        input_output_aliases=aliases,
+        compiler_params=params(),
+        cost_estimate=cost(26 * LANES * WIDTH * WIDTH, 3 << 20, 2 * LANES * WIDTH),
+        name="final_part",
+    )(*operands)
+
+
+def ring_order(count):
+    return [0] + list(range(1, count, 2)) + list(reversed(range(2, count, 2)))
+
+
+def blocked(pair_tiles, grad_out, exponents, token_mask, gain_in, w_proj, w_gate, gain_out, w_out):
+    rows, cols, width = pair_tiles.shape
+    crop_len = token_mask.shape[0]
+    parts = rows // SUB
+    z = lax.axis_index("row")
+    q = lax.axis_index("col")
+    core = q % 2
+
+    order = ring_order(4)
+    hops = [(order[k], order[(k + 1) % 4]) for k in range(4)]
+    at = jnp.array([order.index(k) for k in range(4)], jnp.int32)
+    across = [(k, k ^ 2) for k in range(4)]
+    beside = [(k, k ^ 1) for k in range(4)]
+
+    def forward(a):
+        return lax.ppermute(a, "row", hops)
+
+    def over_x(a):
+        return lax.ppermute(a, "col", across)
+
+    def over_core(a):
+        return lax.ppermute(a, "col", beside)
+
+    slot_block = jnp.array(order, jnp.int32)[(at[z] - jnp.arange(4)) % 4]
+    other = slot_block ^ q
+    slot_to_rel = (other % 2) * 2 + other // 2
+    rel = jnp.arange(4)
+    rel_block = q ^ ((rel % 2) * 2 + rel // 2)
+    rel_to_slot = (at[z] - at[rel_block]) % 4
+
+    maskf = token_mask.astype(F32)
+    mask_rows = lax.dynamic_slice_in_dim(maskf, z * rows, rows)
+    mask_cols = lax.dynamic_slice_in_dim(maskf, q * cols, cols)
+    mask = (mask_rows[:, None] * mask_cols[None, :]).reshape(1, rows * cols)
+    bound = (448.0 * jnp.exp2(exponents.astype(F32))).reshape(1, rows * cols)
+    gain_in = gain_in.reshape(width, 1)
+    gain_out = gain_out.reshape(width, 1)
+    w_t = w_proj.T
+    gate_t = w_gate.T
+    out_t = w_out.T
+
+    slots = []
+    for s in range(parts):
+        held = [right_part(s, pair_tiles, gain_in, w_t[2 * width :], mask, bound)]
+        for _ in range(3):
+            held.append(forward(held[-1]))
+        slots.append(held)
+    left = left_part(pair_tiles, gain_in, w_t[: 2 * width], mask)
+
+    grads, panels, gates, drights = [], [], [], []
+    g_out = g_gate = 0.0
+    for s in range(parts):
+        tri, panel = tri_part(slot_to_rel, slots[s], left)
+        got = over_core(tri[2:])
+        mine = over_x((tri[1].astype(F32) + got[1].astype(F32)).astype(BF16))
+        d_tri, d_gate, part_out, part_gate = mid_part(
+            s, (tri[0], got[0], mine), pair_tiles, grad_out, gain_in, gain_out, gate_t, out_t, w_out
+        )
+        g_out, g_gate = g_out + part_out, g_gate + part_gate
+        far = over_x(d_tri)
+        blocks = [d_tri, far, over_core(d_tri), over_core(far)]
+        part = dright_part(rel_to_slot, blocks, left)
+        total = part[1]
+        for m in (2, 3):
+            total = (forward(total).astype(F32) + part[m].astype(F32)).astype(BF16)
+        drights.append((forward(total), part))
+        grads += blocks
+        panels.append(panel)
+        gates.append(d_gate)
+    d_left = dleft_part(grads, panels)
+
+    d_pair = None
+    g_proj = jnp.zeros((width, 4 * width), F32)
+    for s in range(parts):
+        d_pair, g_proj = final_part(
+            s, pair_tiles, d_left, *drights[s], mask, bound, gain_in, w_t, w_proj, w_gate, gates, g_proj, d_pair
+        )
+
+    def summed(a):
+        half = a.shape[0] // 2
+        mine = lax.dynamic_slice_in_dim(a, core * half, half)
+        mine = mine + over_core(lax.dynamic_slice_in_dim(a, (1 - core) * half, half))
+        mine = mine + over_x(mine)
+        for bit in (1, 2):
+            mine = mine + lax.ppermute(mine, "row", [(k, k ^ bit) for k in range(4)])
+        theirs = over_core(mine)
+        low = jnp.where(core == 0, mine, theirs)
+        high = jnp.where(core == 0, theirs, mine)
+        return jnp.concatenate([low, high], axis=0) / crop_len
+
+    early = summed(jnp.concatenate([g_out, g_gate], axis=0))
+    return d_pair, summed(g_proj), early[width:], early[:width]
+
+
+def local(pair_tiles, *rest, rows_over, cols_over):
+    if pair_tiles.shape == (HALF, HALF, WIDTH) and rows_over == cols_over == 4:
+        return blocked(pair_tiles, *rest)
+    return plain(pair_tiles, *rest)
+
+
 def solution(mesh):
     return jax.shard_map(
-        local,
+        functools.partial(local, rows_over=mesh.shape["row"], cols_over=mesh.shape["col"]),
         mesh=mesh,
         in_specs=(
             P(("crop", "row"), "col", None),

time: 434 us -> 237 us (0.55)
  waiting for transfers between devices: 294 us -> 113 us
  starting transfers between devices: 0.61 us -> 55.9 us
  Pallas kernels: 0 us -> 52.3 us
  local copies, waits for them, and re-layouts: 48.6 us -> 9.12 us
  matrix products: 38.6 us -> 0 us
  other arithmetic: 36.4 us -> 4.73 us
  between operations: 14.1 us -> 1.45 us
    ppermute x0 -> x54, waiting for transfers between devices: none -> 113 us  [the longest x24 73 us: forward(): return lax.ppermute(a, 'row', hops)]
    all_gather x2 -> x0, waiting for transfers between devices: 110 us -> none  [the longest x1 75.4 us: local(): panel = lax.all_gather(right, 'row', axis=0, tiled=True)]
    reduce_scatter x2 -> x0, waiting for transfers between devices: 95.8 us -> none  [the longest x1 56.7 us: local(): lax.psum_scatter(jnp.einsum('ijc,ikc->jkc', grad_full, left, preferred_el...]
    psum x1 -> x0, waiting for transfers between devices: 88.3 us -> none  [local(): lax.psum((g_proj, g_gate, g_out), ('row', 'col'))]
    ppermute x0 -> x54, starting transfers between devices: none -> 55.9 us  [the longest x24 32.4 us: forward(): return lax.ppermute(a, 'row', hops)]
    pallas_call x0 -> x22, Pallas kernels: none -> 52.3 us  [the longest x4 13.7 us: tri_part(): pl.pallas_call(tri_kernel, grid=(HALF // GROUP,), out_shape=(FOUR, FOUR),...]
    dot_general x12 -> x0, matrix products: 38.6 us -> none  [the longest x1 5.43 us: local(): jnp.einsum('jkc,ikc->jic', panel, left, preferred_element_type=f32)]
    all_gather x2 -> x0, local copies, waits for them, and re-layouts: 14.7 us -> none  [the longest x1 7.38 us: local(): panel = lax.all_gather(right, 'row', axis=0, tiled=True)]
  transfers between devices with their start and end apart: 5 -> 54, of which waited for: 5 -> 28; matrix products, arithmetic and copies ran while one was open for 7% -> 3% of each run, Pallas kernels for 0% -> 22%
where the time goes in v1:
time: 237 us; the launch traced here: 236 us
  waiting for transfers between devices  113 us (48%)
  starting transfers between devices  55.9 us (24%)
  Pallas kernels  52.3 us (22%)
  local copies, waits for them, and re-layouts  9.12 us (4%)
  other arithmetic  4.73 us (2%)
    ppermute x24, waiting for transfers between devices, forward(): return lax.ppermute(a, 'row', hops)  73 us
    ppermute x24, starting transfers between devices, forward(): return lax.ppermute(a, 'row', hops)  32.4 us
    ppermute x10, waiting for transfers between devices, over_x(): return lax.ppermute(a, 'col', across)  26.4 us
    pallas_call x4, Pallas kernels, tri_part(): pl.pallas_call(tri_kernel, grid=(HALF // GROUP,), out_shape=(FOUR, FOUR),...  13.7 us
    ppermute x10, starting transfers between devices, over_x(): return lax.ppermute(a, 'col', across)  12.6 us
    ppermute x4, waiting for transfers between devices, summed(): mine = mine + lax.ppermute(mine, 'row', [(k, k ^ bit) for k in range(4)])  12.5 us
    pallas_call x4, Pallas kernels, final_part(): pl.pallas_call(body, grid=(1,), out_shape=(jax.ShapeDtypeStruct((HALF, HA...  10.7 us
    pallas_call x4, Pallas kernels, mid_part(): pl.pallas_call(mid_kernel, grid=(1,), out_shape=(PANEL, PANEL, square, sq...  10.2 us
  transfers between devices with their start and end apart: 54, of which 28 were waited for; matrix products, arithmetic and copies ran while one was open for 3% of the time, Pallas kernels for 22%

profile of v1, /device:TPU:0, one launch (start us, length us, event | category | flops | bytes accessed | tf_op | source)
XLA Modules:
  0.0 236.1 jit_solution(10171682389305778360)
XLA Ops:
  6.5 3.1 %collective-permute-start = (bf16[64,16,128]{2,1,0:T(8,128)(2,1)S(1)}, bf16[64,16,128]{2,1,0:T(8,128)(2,1)S(1)}, u32[]{:S(2)}, u32[]{:S(2)}) collective-permute-start(bf16[64,16,128]{2,1,0:T(8,128)(2,1)S(1)} %right_part.4.r0), channel_id=1, source_target_pairs={{0,4},{4,12},{12,8},{8,0},{1,5},{5,13},{13,9},{9,1},{2,6},{6,14},{... | collective-permute-start | bytes 786440 | tf_op jit(solution)/shard_map/ppermute | solution.py:491
  19.6 3.7 %collective-permute-done.8.r1 = bf16[64,16,128]{2,1,0:T(8,128)(2,1)S(1)} collective-permute-done((bf16[64,16,128]{2,1,0:T(8,128)(2,1)S(1)}, bf16[64,16,128]{2,1,0:T(8,128)(2,1)S(1)}, u32[]{:S(2)}, u32[]{:S(2)}) %collective-permute-start.8) | collective-permute-done | bytes 262176 | tf_op jit(solution)/shard_map/ppermute | solution.py:491
  24.5 4.6 %collective-permute-done.16.r1 = bf16[64,16,128]{2,1,0:T(8,128)(2,1)} collective-permute-done((bf16[64,16,128]{2,1,0:T(8,128)(2,1)S(1)}, bf16[64,16,128]{2,1,0:T(8,128)(2,1)}, u32[]{:S(2)}, u32[]{:S(2)}) %collective-permute-start.16) | collective-permute-done | bytes 262176 | tf_op jit(solution)/shard_map/ppermute | solution.py:491
  30.1 4.6 %collective-permute-done.24.r1 = bf16[64,16,128]{2,1,0:T(8,128)(2,1)} collective-permute-done((bf16[64,16,128]{2,1,0:T(8,128)(2,1)S(1)}, bf16[64,16,128]{2,1,0:T(8,128)(2,1)}, u32[]{:S(2)}, u32[]{:S(2)}) %collective-permute-start.24) | collective-permute-done | bytes 262176 | tf_op jit(solution)/shard_map/ppermute | solution.py:491
  35.7 4.6 %collective-permute-done.1.r2 = bf16[64,16,128]{2,1,0:T(8,128)(2,1)} collective-permute-done((bf16[64,16,128]{2,1,0:T(8,128)(2,1)S(1)}, bf16[64,16,128]{2,1,0:T(8,128)(2,1)}, u32[]{:S(2)}, u32[]{:S(2)}) %collective-permute-start.1) | collective-permute-done | bytes 262176 | tf_op jit(solution)/shard_map/ppermute | solution.py:491
  42.6 3.3 %collective-permute-done.9.r2 = bf16[64,16,128]{2,1,0:T(8,128)(2,1)} collective-permute-done((bf16[64,16,128]{2,1,0:T(8,128)(2,1)S(1)}, bf16[64,16,128]{2,1,0:T(8,128)(2,1)}, u32[]{:S(2)}, u32[]{:S(2)}) %collective-permute-start.9) | collective-permute-done | bytes 262176 | tf_op jit(solution)/shard_map/ppermute | solution.py:491
  47.0 4.2 %left_part.1.left_ref = bf16[64,2,64,128]{3,2,1,0:T(8,128)(2,1)S(1)} custom-call(bf16[64,64,128]{2,1,0:T(8,128)(2,1)S(1)} %copy-done.1, f32[128,1]{1,0:T(8,128)S(1)} %copy.39.gain_ref.gain_in_ref.refs_6_, bf16[256,128]{1,0:T(8,128)(2,1)S(1)} %get-tuple-element.74.w_ref, f32[1,4096]{1,0:T(1,128)S(1)} %mul.66.mask_ref.refs_4_), custom_call_target="tpu_custom_call" | custom-call | flops 268435456 | bytes 3145728 | tf_op jit(solution)/shard_map/left_part/pallas_call | solution.py:356
  52.2 3.5 %collective-permute-start.18 = (bf16[64,16,128]{2,1,0:T(8,128)(2,1)}, bf16[64,16,128]{2,1,0:T(8,128)(2,1)S(1)}, u32[]{:S(2)}, u32[]{:S(2)}) collective-permute-start(bf16[64,16,128]{2,1,0:T(8,128)(2,1)} %collective-permute-done.17.r2), channel_id=1, source_target_pairs={{0,4},{4,12},{12,8},{8,0},{1,5},{5,13},{13,9},{9,1},{2,6},{6,14},{... | collective-permute-start | bytes 786440 | tf_op jit(solution)/shard_map/ppermute | solution.py:491
  58.3 4.5 %collective-permute-done.2.r3 = bf16[64,16,128]{2,1,0:T(8,128)(2,1)} collective-permute-done((bf16[64,16,128]{2,1,0:T(8,128)(2,1)}, bf16[64,16,128]{2,1,0:T(8,128)(2,1)}, u32[]{:S(2)}, u32[]{:S(2)}) %collective-permute-start.2) | collective-permute-done | bytes 262176 | tf_op jit(solution)/shard_map/ppermute | solution.py:491
  64.6 3.4 %tri_part.4 = (bf16[4,64,16,128]{3,2,1,0:T(8,128)(2,1)S(1)}, bf16[4,64,16,128]{3,2,1,0:T(8,128)(2,1)S(1)}) custom-call(s32[4]{0:T(128)S(1)} %fusion.20.place_ref, bf16[64,16,128]{2,1,0:T(8,128)(2,1)S(1)} %copy-done.11, bf16[64,16,128]{2,1,0:T(8,128)(2,1)S(1)} %copy-done.18, bf16[64,16,128]{2,1,0:T(8,128)(2,1)} %collective-permute-done.1.r2, ...), custom_call_target="tpu_custom_call" | custom-call | flops 134217728 | bytes 5242880 | tf_op jit(solution)/shard_map/tri_part/pallas_call | solution.py:373
  68.4 3.4 %tri_part.5 = (bf16[4,64,16,128]{3,2,1,0:T(8,128)(2,1)S(1)}, bf16[4,64,16,128]{3,2,1,0:T(8,128)(2,1)S(1)}) custom-call(s32[4]{0:T(128)S(1)} %fusion.20.place_ref, bf16[64,16,128]{2,1,0:T(8,128)(2,1)S(1)} %copy-done.9, bf16[64,16,128]{2,1,0:T(8,128)(2,1)S(1)} %copy-done.16, bf16[64,16,128]{2,1,0:T(8,128)(2,1)} %collective-permute-done.9.r2, ...), custom_call_target="tpu_custom_call" | custom-call | flops 134217728 | bytes 5242880 | tf_op jit(solution)/shard_map/tri_part/pallas_call | solution.py:373
  73.9 3.4 %tri_part.6 = (bf16[4,64,16,128]{3,2,1,0:T(8,128)(2,1)S(1)}, bf16[4,64,16,128]{3,2,1,0:T(8,128)(2,1)S(1)}) custom-call(s32[4]{0:T(128)S(1)} %fusion.20.place_ref, bf16[64,16,128]{2,1,0:T(8,128)(2,1)S(1)} %copy-done.7, bf16[64,16,128]{2,1,0:T(8,128)(2,1)} %collective-permute-done.16.r1, bf16[64,16,128]{2,1,0:T(8,128)(2,1)} %collective-permute-done.17.r2, ...), custom_call_target="tpu_custom_call" | custom-call | flops 134217728 | bytes 5242880 | tf_op jit(solution)/shard_map/tri_part/pallas_call | solution.py:373
  78.7 3.5 %tri_part.7 = (bf16[4,64,16,128]{3,2,1,0:T(8,128)(2,1)S(1)}, bf16[4,64,16,128]{3,2,1,0:T(8,128)(2,1)S(1)}) custom-call(s32[4]{0:T(128)S(1)} %fusion.20.place_ref, bf16[64,16,128]{2,1,0:T(8,128)(2,1)S(1)} %copy-done.5, bf16[64,16,128]{2,1,0:T(8,128)(2,1)} %collective-permute-done.24.r1, bf16[64,16,128]{2,1,0:T(8,128)(2,1)} %collective-permute-done.25.r2, ...), custom_call_target="tpu_custom_call" | custom-call | flops 134217728 | bytes 5242880 | tf_op jit(solution)/shard_map/tri_part/pallas_call | solution.py:373
  87.1 10.2 %collective-permute-done.12.c_ref = bf16[64,16,128]{2,1,0:T(8,128)(2,1)S(1)} collective-permute-done((bf16[64,16,128]{2,1,0:T(8,128)(2,1)S(1)}, bf16[64,16,128]{2,1,0:T(8,128)(2,1)S(1)}, u32[]{:S(2)}, u32[]{:S(2)}) %collective-permute-start.12) | collective-permute-done | bytes 262176 | tf_op jit(solution)/shard_map/ppermute | solution.py:494
  101.4 7.1 %collective-permute-done.28.c_ref = bf16[64,16,128]{2,1,0:T(8,128)(2,1)S(1)} collective-permute-done((bf16[64,16,128]{2,1,0:T(8,128)(2,1)S(1)}, bf16[64,16,128]{2,1,0:T(8,128)(2,1)S(1)}, u32[]{:S(2)}, u32[]{:S(2)}) %collective-permute-start.28) | collective-permute-done | bytes 262176 | tf_op jit(solution)/shard_map/ppermute | solution.py:494
  122.0 4.0 %collective-permute-done.21.refs_9_.d1 = bf16[64,16,128]{2,1,0:T(8,128)(2,1)S(1)} collective-permute-done((bf16[64,16,128]{2,1,0:T(8,128)(2,1)S(1)}, bf16[64,16,128]{2,1,0:T(8,128)(2,1)S(1)}, u32[]{:S(2)}, u32[]{:S(2)}) %collective-permute-start.21) | collective-permute-done | bytes 262176 | tf_op jit(solution)/shard_map/ppermute | solution.py:494
  133.9 3.3 %collective-permute-start.35 = (bf16[64,16,128]{2,1,0:T(8,128)(2,1)S(1)}, bf16[64,16,128]{2,1,0:T(8,128)(2,1)S(1)}, u32[]{:S(2)}, u32[]{:S(2)}) collective-permute-start(bf16[64,16,128]{2,1,0:T(8,128)(2,1)S(1)} %slice_bitcast_fusion.8), channel_id=1, source_target_pairs={{0,4},{4,12},{12,8},{8,0},{1,5},{5,13},{13,9},{9,1},{2,6},{6,14},{... | collective-permute-start | bytes 786440 | tf_op jit(solution)/shard_map/ppermute | solution.py:491
  142.8 4.0 %collective-permute-done.35 = bf16[64,16,128]{2,1,0:T(8,128)(2,1)S(1)} collective-permute-done((bf16[64,16,128]{2,1,0:T(8,128)(2,1)S(1)}, bf16[64,16,128]{2,1,0:T(8,128)(2,1)S(1)}, u32[]{:S(2)}, u32[]{:S(2)}) %collective-permute-start.35) | collective-permute-done | bytes 262176 | tf_op jit(solution)/shard_map/ppermute | solution.py:491
  147.7 4.6 %collective-permute-done.38 = bf16[64,16,128]{2,1,0:T(8,128)(2,1)S(1)} collective-permute-done((bf16[64,16,128]{2,1,0:T(8,128)(2,1)S(1)}, bf16[64,16,128]{2,1,0:T(8,128)(2,1)S(1)}, u32[]{:S(2)}, u32[]{:S(2)}) %collective-permute-start.38) | collective-permute-done | bytes 262176 | tf_op jit(solution)/shard_map/ppermute | solution.py:491
  153.3 4.6 %collective-permute-done.41 = bf16[64,16,128]{2,1,0:T(8,128)(2,1)S(1)} collective-permute-done((bf16[64,16,128]{2,1,0:T(8,128)(2,1)S(1)}, bf16[64,16,128]{2,1,0:T(8,128)(2,1)S(1)}, u32[]{:S(2)}, u32[]{:S(2)}) %collective-permute-start.41) | collective-permute-done | bytes 262176 | tf_op jit(solution)/shard_map/ppermute | solution.py:491
  159.0 10.3 %collective-permute-done.36 = bf16[64,16,128]{2,1,0:T(8,128)(2,1)S(1)} collective-permute-done((bf16[64,16,128]{2,1,0:T(8,128)(2,1)S(1)}, bf16[64,16,128]{2,1,0:T(8,128)(2,1)S(1)}, u32[]{:S(2)}, u32[]{:S(2)}) %collective-permute-start.36) | collective-permute-done | bytes 262176 | tf_op jit(solution)/shard_map/ppermute | solution.py:491
  170.2 4.6 %collective-permute-done.39 = bf16[64,16,128]{2,1,0:T(8,128)(2,1)S(1)} collective-permute-done((bf16[64,16,128]{2,1,0:T(8,128)(2,1)S(1)}, bf16[64,16,128]{2,1,0:T(8,128)(2,1)S(1)}, u32[]{:S(2)}, u32[]{:S(2)}) %collective-permute-start.39) | collective-permute-done | bytes 262176 | tf_op jit(solution)/shard_map/ppermute | solution.py:491
  175.8 4.6 %collective-permute-done.42 = bf16[64,16,128]{2,1,0:T(8,128)(2,1)S(1)} collective-permute-done((bf16[64,16,128]{2,1,0:T(8,128)(2,1)S(1)}, bf16[64,16,128]{2,1,0:T(8,128)(2,1)S(1)}, u32[]{:S(2)}, u32[]{:S(2)}) %collective-permute-start.42) | collective-permute-done | bytes 262176 | tf_op jit(solution)/shard_map/ppermute | solution.py:491
  181.5 3.4 %collective-permute-start.34 = (bf16[64,16,128]{2,1,0:T(8,128)(2,1)S(1)}, bf16[64,16,128]{2,1,0:T(8,128)(2,1)S(1)}, u32[]{:S(2)}, u32[]{:S(2)}) collective-permute-start(bf16[64,16,128]{2,1,0:T(8,128)(2,1)S(1)} %fusion.6), channel_id=1, source_target_pairs={{0,4},{4,12},{12,8},{8,0},{1,5},{5,13},{13,9},{9,1},{2,6},{6,14},{... | collective-permute-start | bytes 786440 | tf_op jit(solution)/shard_map/ppermute | solution.py:491
  187.5 9.8 %collective-permute-done.43.dr_a_ref = bf16[64,16,128]{2,1,0:T(8,128)(2,1)S(1)} collective-permute-done((bf16[64,16,128]{2,1,0:T(8,128)(2,1)S(1)}, bf16[64,16,128]{2,1,0:T(8,128)(2,1)S(1)}, u32[]{:S(2)}, u32[]{:S(2)}) %collective-permute-start.43) | collective-permute-done | bytes 262176 | tf_op jit(solution)/shard_map/ppermute | solution.py:491
  197.4 2.7 %final_part.4 = (bf16[64,64,128]{2,1,0:T(8,128)(2,1)}, f32[128,512]{1,0:T(8,128)S(1)}) custom-call(bf16[64,64,128]{2,1,0:T(8,128)(2,1)S(1)} %copy-done.1, f32[64,64,128]{2,1,0:T(8,128)S(1)} %dleft_part.1.dleft_ref.refs_1_, bf16[64,16,128]{2,1,0:T(8,128)(2,1)S(1)} %collective-permute-done.43.dr_a_ref, bf16[4,64,16,128]{3,2,1,0:T(8,128)(2,1)S(1)} %dright_part.7.dr_b_ref, ...), custom_call_target="tpu_custom_call" | custom-call | flops 436207616 | bytes 3145728 | tf_op jit(solution)/shard_map/final_part/pallas_call | solution.py:455
  200.0 2.7 %final_part.5 = (bf16[64,64,128]{2,1,0:T(8,128)(2,1)}, f32[128,512]{1,0:T(8,128)S(1)}) custom-call(bf16[64,64,128]{2,1,0:T(8,128)(2,1)S(1)} %copy-done.1, f32[64,64,128]{2,1,0:T(8,128)S(1)} %dleft_part.1.dleft_ref.refs_1_, bf16[64,16,128]{2,1,0:T(8,128)(2,1)S(1)} %collective-permute-done.40.refs_2_, ...), custom_call_target="tpu_custom_call", output_to_operand_aliasing={{0}: (15, {})} | custom-call | flops 436207616 | bytes 3145728 | tf_op jit(solution)/shard_map/final_part/pallas_call | solution.py:455
  202.7 2.7 %final_part.6 = (bf16[64,64,128]{2,1,0:T(8,128)(2,1)}, f32[128,512]{1,0:T(8,128)S(1)}) custom-call(bf16[64,64,128]{2,1,0:T(8,128)(2,1)S(1)} %copy-done.1, f32[64,64,128]{2,1,0:T(8,128)S(1)} %dleft_part.1.dleft_ref.refs_1_, bf16[64,16,128]{2,1,0:T(8,128)(2,1)S(1)} %collective-permute-done.37.refs_2_, ...), custom_call_target="tpu_custom_call", output_to_operand_aliasing={{0}: (15, {})} | custom-call | flops 436207616 | bytes 3145728 | tf_op jit(solution)/shard_map/final_part/pallas_call | solution.py:455
  213.8 3.4 %collective-permute-done.51 = f32[128,128]{1,0:T(8,128)S(1)} collective-permute-done((f32[128,128]{1,0:T(8,128)S(1)}, f32[128,128]{1,0:T(8,128)S(1)}, u32[]{:S(2)}, u32[]{:S(2)}) %collective-permute-start.51) | collective-permute-done | bytes 65568 | tf_op jit(solution)/shard_map/ppermute | solution.py:560
  218.2 3.4 %collective-permute-start.52 = (f32[128,128]{1,0:T(8,128)S(1)}, f32[128,128]{1,0:T(8,128)S(1)}, u32[]{:S(2)}, u32[]{:S(2)}) collective-permute-start(f32[128,128]{1,0:T(8,128)S(1)} %add.222), channel_id=1, source_target_pairs={{0,8},{4,12},{8,0},{12,4},{1,9},{5,13},{9,1},{13,5},{2,10},{6,14},... | collective-permute-start | bytes 196616 | tf_op jit(solution)/shard_map/ppermute | solution.py:560
  224.0 3.0 %collective-permute-start.47 = (f32[64,512]{1,0:T(8,128)S(1)}, f32[64,512]{1,0:T(8,128)S(1)}, u32[]{:S(2)}, u32[]{:S(2)}) collective-permute-start(f32[64,512]{1,0:T(8,128)S(1)} %add.210), channel_id=1, source_target_pairs={{0,8},{4,12},{8,0},{12,4},{1,9},{5,13},{9,1},{13,5},{2,10},{6,14},... | collective-permute-start | bytes 393224 | tf_op jit(solution)/shard_map/ppermute | solution.py:560
  227.0 6.9 %collective-permute-done.47 = f32[64,512]{1,0:T(8,128)S(1)} collective-permute-done((f32[64,512]{1,0:T(8,128)S(1)}, f32[64,512]{1,0:T(8,128)S(1)}, u32[]{:S(2)}, u32[]{:S(2)}) %collective-permute-start.47) | collective-permute-done | bytes 131104 | tf_op jit(solution)/shard_map/ppermute | solution.py:560
  (206 shorter events, 89.7 us)
Async XLA Ops:
  6.5 11.2 %collective-permute-start = (bf16[64,16,128]{2,1,0:T(8,128)(2,1)S(1)}, bf16[64,16,128]{2,1,0:T(8,128)(2,1)S(1)}, u32[]{:S(2)}, u32[]{:S(2)}) collective-permute-start(bf16[64,16,128]{2,1,0:T(8,128)(2,1)S(1)} %right_part.4.r0), channel_id=1, source_target_pairs={{0,4},{4,12},{12,8},{8,0},{1,5},{5,13},{13,9},{9,1},{2,6},{6,14},{... | collective-permute-start | bytes 786440 | tf_op jit(solution)/shard_map/ppermute | solution.py:491
  10.5 12.8 %collective-permute-start.8 = (bf16[64,16,128]{2,1,0:T(8,128)(2,1)S(1)}, bf16[64,16,128]{2,1,0:T(8,128)(2,1)S(1)}, u32[]{:S(2)}, u32[]{:S(2)}) collective-permute-start(bf16[64,16,128]{2,1,0:T(8,128)(2,1)S(1)} %right_part.5.r0), channel_id=1, source_target_pairs={{0,4},{4,12},{12,8},{8,0},{1,5},{5,13},{13,9},{9,1},{2,6},{6,14},{... | collective-permute-start | bytes 786440 | tf_op jit(solution)/shard_map/ppermute | solution.py:491
  14.1 14.9 %collective-permute-start.16 = (bf16[64,16,128]{2,1,0:T(8,128)(2,1)S(1)}, bf16[64,16,128]{2,1,0:T(8,128)(2,1)}, u32[]{:S(2)}, u32[]{:S(2)}) collective-permute-start(bf16[64,16,128]{2,1,0:T(8,128)(2,1)S(1)} %right_part.6.r0), channel_id=1, source_target_pairs={{0,4},{4,12},{12,8},{8,0},{1,5},{5,13},{13,9},{9,1},{2,6},{6,14},{... | collective-permute-start | bytes 786440 | tf_op jit(solution)/shard_map/ppermute | solution.py:491
  15.6 19.0 %collective-permute-start.24 = (bf16[64,16,128]{2,1,0:T(8,128)(2,1)S(1)}, bf16[64,16,128]{2,1,0:T(8,128)(2,1)}, u32[]{:S(2)}, u32[]{:S(2)}) collective-permute-start(bf16[64,16,128]{2,1,0:T(8,128)(2,1)S(1)} %right_part.7.r0), channel_id=1, source_target_pairs={{0,4},{4,12},{12,8},{8,0},{1,5},{5,13},{13,9},{9,1},{2,6},{6,14},{... | collective-permute-start | bytes 786440 | tf_op jit(solution)/shard_map/ppermute | solution.py:491
  17.7 22.6 %collective-permute-start.1 = (bf16[64,16,128]{2,1,0:T(8,128)(2,1)S(1)}, bf16[64,16,128]{2,1,0:T(8,128)(2,1)}, u32[]{:S(2)}, u32[]{:S(2)}) collective-permute-start(bf16[64,16,128]{2,1,0:T(8,128)(2,1)S(1)} %collective-permute-done.r1), channel_id=1, source_target_pairs={{0,4},{4,12},{12,8},{8,0},{1,5},{5,13},{13,9},{9,1},{2,6},{6,14},{... | collective-permute-start | bytes 786440 | tf_op jit(solution)/shard_map/ppermute | solution.py:491
  23.3 22.6 %collective-permute-start.9 = (bf16[64,16,128]{2,1,0:T(8,128)(2,1)S(1)}, bf16[64,16,128]{2,1,0:T(8,128)(2,1)}, u32[]{:S(2)}, u32[]{:S(2)}) collective-permute-start(bf16[64,16,128]{2,1,0:T(8,128)(2,1)S(1)} %collective-permute-done.8.r1), channel_id=1, source_target_pairs={{0,4},{4,12},{12,8},{8,0},{1,5},{5,13},{13,9},{9,1},{2,6},{6,14},{... | collective-permute-start | bytes 786440 | tf_op jit(solution)/shard_map/ppermute | solution.py:491
  29.0 23.2 %collective-permute-start.17 = (bf16[64,16,128]{2,1,0:T(8,128)(2,1)}, bf16[64,16,128]{2,1,0:T(8,128)(2,1)}, u32[]{:S(2)}, u32[]{:S(2)}) collective-permute-start(bf16[64,16,128]{2,1,0:T(8,128)(2,1)} %collective-permute-done.16.r1), channel_id=1, source_target_pairs={{0,4},{4,12},{12,8},{8,0},{1,5},{5,13},{13,9},{9,1},{2,6},{6,14},{... | collective-permute-start | bytes 786440 | tf_op jit(solution)/shard_map/ppermute | solution.py:491
  34.6 22.5 %collective-permute-start.25 = (bf16[64,16,128]{2,1,0:T(8,128)(2,1)}, bf16[64,16,128]{2,1,0:T(8,128)(2,1)}, u32[]{:S(2)}, u32[]{:S(2)}) collective-permute-start(bf16[64,16,128]{2,1,0:T(8,128)(2,1)} %collective-permute-done.24.r1), channel_id=1, source_target_pairs={{0,4},{4,12},{12,8},{8,0},{1,5},{5,13},{13,9},{9,1},{2,6},{6,14},{... | collective-permute-start | bytes 786440 | tf_op jit(solution)/shard_map/ppermute | solution.py:491
  40.3 22.5 %collective-permute-start.2 = (bf16[64,16,128]{2,1,0:T(8,128)(2,1)}, bf16[64,16,128]{2,1,0:T(8,128)(2,1)}, u32[]{:S(2)}, u32[]{:S(2)}) collective-permute-start(bf16[64,16,128]{2,1,0:T(8,128)(2,1)} %collective-permute-done.1.r2), channel_id=1, source_target_pairs={{0,4},{4,12},{12,8},{8,0},{1,5},{5,13},{13,9},{9,1},{2,6},{6,14},{... | collective-permute-start | bytes 786440 | tf_op jit(solution)/shard_map/ppermute | solution.py:491
  45.9 22.5 %collective-permute-start.10 = (bf16[64,16,128]{2,1,0:T(8,128)(2,1)}, bf16[64,16,128]{2,1,0:T(8,128)(2,1)}, u32[]{:S(2)}, u32[]{:S(2)}) collective-permute-start(bf16[64,16,128]{2,1,0:T(8,128)(2,1)} %collective-permute-done.9.r2), channel_id=1, source_target_pairs={{0,4},{4,12},{12,8},{8,0},{1,5},{5,13},{13,9},{9,1},{2,6},{6,14},{... | collective-permute-start | bytes 786440 | tf_op jit(solution)/shard_map/ppermute | solution.py:491
  52.2 21.7 %collective-permute-start.18 = (bf16[64,16,128]{2,1,0:T(8,128)(2,1)}, bf16[64,16,128]{2,1,0:T(8,128)(2,1)S(1)}, u32[]{:S(2)}, u32[]{:S(2)}) collective-permute-start(bf16[64,16,128]{2,1,0:T(8,128)(2,1)} %collective-permute-done.17.r2), channel_id=1, source_target_pairs={{0,4},{4,12},{12,8},{8,0},{1,5},{5,13},{13,9},{9,1},{2,6},{6,14},{... | collective-permute-start | bytes 786440 | tf_op jit(solution)/shard_map/ppermute | solution.py:491
  57.1 21.5 %collective-permute-start.26 = (bf16[64,16,128]{2,1,0:T(8,128)(2,1)}, bf16[64,16,128]{2,1,0:T(8,128)(2,1)S(1)}, u32[]{:S(2)}, u32[]{:S(2)}) collective-permute-start(bf16[64,16,128]{2,1,0:T(8,128)(2,1)} %collective-permute-done.25.r2), channel_id=1, source_target_pairs={{0,4},{4,12},{12,8},{8,0},{1,5},{5,13},{13,9},{9,1},{2,6},{6,14},{... | collective-permute-start | bytes 786440 | tf_op jit(solution)/shard_map/ppermute | solution.py:491
  68.1 14.2 %collective-permute-start.3 = (bf16[2,64,16,128]{3,2,1,0:T(8,128)(2,1)S(1)}, bf16[2,64,16,128]{3,2,1,0:T(8,128)(2,1)S(1)}, u32[]{:S(2)}, u32[]{:S(2)}) collective-permute-start(bf16[2,64,16,128]{3,2,1,0:T(8,128)(2,1)S(1)} %slice.114), channel_id=1, source_target_pairs={{0,1},{1,0},{2,3},{3,2},{4,5},{5,4},{6,7},{7,6},{8,9},{9,8},{10,11... | collective-permute-start | bytes 1572872 | tf_op jit(solution)/shard_map/ppermute | solution.py:497
  71.8 12.3 %collective-permute-start.11 = (bf16[2,64,16,128]{3,2,1,0:T(8,128)(2,1)S(1)}, bf16[2,64,16,128]{3,2,1,0:T(8,128)(2,1)S(1)}, u32[]{:S(2)}, u32[]{:S(2)}) collective-permute-start(bf16[2,64,16,128]{3,2,1,0:T(8,128)(2,1)S(1)} %slice.119), channel_id=1, source_target_pairs={{0,1},{1,0},{2,3},{3,2},{4,5},{5,4},{6,7},{7,6},{8,9},{9,8},{10,11... | collective-permute-start | bytes 1572872 | tf_op jit(solution)/shard_map/ppermute | solution.py:497
  82.5 33.4 %collective-permute-start.4 = (bf16[64,16,128]{2,1,0:T(8,128)(2,1)S(1)}, bf16[64,16,128]{2,1,0:T(8,128)(2,1)S(1)}, u32[]{:S(2)}, u32[]{:S(2)}) collective-permute-start(bf16[64,16,128]{2,1,0:T(8,128)(2,1)S(1)} %fusion.8), channel_id=1, source_target_pairs={{0,2},{1,3},{2,0},{3,1},{4,6},{5,7},{6,4},{7,5},{8,10},{9,11},{10,... | collective-permute-start | bytes 786440 | tf_op jit(solution)/shard_map/ppermute | solution.py:494
  84.2 13.1 %collective-permute-start.12 = (bf16[64,16,128]{2,1,0:T(8,128)(2,1)S(1)}, bf16[64,16,128]{2,1,0:T(8,128)(2,1)S(1)}, u32[]{:S(2)}, u32[]{:S(2)}) collective-permute-start(bf16[64,16,128]{2,1,0:T(8,128)(2,1)S(1)} %fusion.9), channel_id=1, source_target_pairs={{0,2},{1,3},{2,0},{3,1},{4,6},{5,7},{6,4},{7,5},{8,10},{9,11},{10,... | collective-permute-start | bytes 786440 | tf_op jit(solution)/shard_map/ppermute | solution.py:494
  84.8 27.9 %collective-permute-start.20 = (bf16[64,16,128]{2,1,0:T(8,128)(2,1)S(1)}, bf16[64,16,128]{2,1,0:T(8,128)(2,1)S(1)}, u32[]{:S(2)}, u32[]{:S(2)}) collective-permute-start(bf16[64,16,128]{2,1,0:T(8,128)(2,1)S(1)} %fusion.10), channel_id=1, source_target_pairs={{0,2},{1,3},{2,0},{3,1},{4,6},{5,7},{6,4},{7,5},{8,10},{9,11},{10,... | collective-permute-start | bytes 786440 | tf_op jit(solution)/shard_map/ppermute | solution.py:494
  86.5 22.0 %collective-permute-start.28 = (bf16[64,16,128]{2,1,0:T(8,128)(2,1)S(1)}, bf16[64,16,128]{2,1,0:T(8,128)(2,1)S(1)}, u32[]{:S(2)}, u32[]{:S(2)}) collective-permute-start(bf16[64,16,128]{2,1,0:T(8,128)(2,1)S(1)} %fusion.11), channel_id=1, source_target_pairs={{0,2},{1,3},{2,0},{3,1},{4,6},{5,7},{6,4},{7,5},{8,10},{9,11},{10,... | collective-permute-start | bytes 786440 | tf_op jit(solution)/shard_map/ppermute | solution.py:494
  99.8 20.6 %collective-permute-start.13 = (bf16[64,16,128]{2,1,0:T(8,128)(2,1)S(1)}, bf16[64,16,128]{2,1,0:T(8,128)(2,1)S(1)}, u32[]{:S(2)}, u32[]{:S(2)}) collective-permute-start(bf16[64,16,128]{2,1,0:T(8,128)(2,1)S(1)} %get-tuple-element.39.refs_4_.d0), channel_id=1, source_target_pairs={{0,2},{1,3},{2,0},{3,1},{4,6},{5,7},{6,4},{7,5},{8,10},{9,11},{10,... | collective-permute-start | bytes 786440 | tf_op jit(solution)/shard_map/ppermute | solution.py:494
  115.8 14.8 %collective-permute-start.22 = (bf16[64,16,128]{2,1,0:T(8,128)(2,1)S(1)}, bf16[64,16,128]{2,1,0:T(8,128)(2,1)S(1)}, u32[]{:S(2)}, u32[]{:S(2)}) collective-permute-start(bf16[64,16,128]{2,1,0:T(8,128)(2,1)S(1)} %get-tuple-element.41.refs_8_.d0), channel_id=1, source_target_pairs={{0,1},{1,0},{2,3},{3,2},{4,5},{5,4},{6,7},{7,6},{8,9},{9,8},{10,11... | collective-permute-start | bytes 786440 | tf_op jit(solution)/shard_map/ppermute | solution.py:497
  133.9 12.9 %collective-permute-start.35 = (bf16[64,16,128]{2,1,0:T(8,128)(2,1)S(1)}, bf16[64,16,128]{2,1,0:T(8,128)(2,1)S(1)}, u32[]{:S(2)}, u32[]{:S(2)}) collective-permute-start(bf16[64,16,128]{2,1,0:T(8,128)(2,1)S(1)} %slice_bitcast_fusion.8), channel_id=1, source_target_pairs={{0,4},{4,12},{12,8},{8,0},{1,5},{5,13},{13,9},{9,1},{2,6},{6,14},{... | collective-permute-start | bytes 786440 | tf_op jit(solution)/shard_map/ppermute | solution.py:491
  139.0 13.4 %collective-permute-start.38 = (bf16[64,16,128]{2,1,0:T(8,128)(2,1)S(1)}, bf16[64,16,128]{2,1,0:T(8,128)(2,1)S(1)}, u32[]{:S(2)}, u32[]{:S(2)}) collective-permute-start(bf16[64,16,128]{2,1,0:T(8,128)(2,1)S(1)} %slice_bitcast_fusion.5), channel_id=1, source_target_pairs={{0,4},{4,12},{12,8},{8,0},{1,5},{5,13},{13,9},{9,1},{2,6},{6,14},{... | collective-permute-start | bytes 786440 | tf_op jit(solution)/shard_map/ppermute | solution.py:491
  140.9 17.0 %collective-permute-start.41 = (bf16[64,16,128]{2,1,0:T(8,128)(2,1)S(1)}, bf16[64,16,128]{2,1,0:T(8,128)(2,1)S(1)}, u32[]{:S(2)}, u32[]{:S(2)}) collective-permute-start(bf16[64,16,128]{2,1,0:T(8,128)(2,1)S(1)} %slice_bitcast_fusion.2), channel_id=1, source_target_pairs={{0,4},{4,12},{12,8},{8,0},{1,5},{5,13},{13,9},{9,1},{2,6},{6,14},{... | collective-permute-start | bytes 786440 | tf_op jit(solution)/shard_map/ppermute | solution.py:491
  141.8 39.7 %collective-permute-start.33 = (bf16[64,16,128]{2,1,0:T(8,128)(2,1)S(1)}, bf16[64,16,128]{2,1,0:T(8,128)(2,1)S(1)}, u32[]{:S(2)}, u32[]{:S(2)}) collective-permute-start(bf16[64,16,128]{2,1,0:T(8,128)(2,1)S(1)} %fusion.7), channel_id=1, source_target_pairs={{0,4},{4,12},{12,8},{8,0},{1,5},{5,13},{13,9},{9,1},{2,6},{6,14},{... | collective-permute-start | bytes 786440 | tf_op jit(solution)/shard_map/ppermute | solution.py:491
  146.8 22.4 %collective-permute-start.36 = (bf16[64,16,128]{2,1,0:T(8,128)(2,1)S(1)}, bf16[64,16,128]{2,1,0:T(8,128)(2,1)S(1)}, u32[]{:S(2)}, u32[]{:S(2)}) collective-permute-start(bf16[64,16,128]{2,1,0:T(8,128)(2,1)S(1)} %fusion.5), channel_id=1, source_target_pairs={{0,4},{4,12},{12,8},{8,0},{1,5},{5,13},{13,9},{9,1},{2,6},{6,14},{... | collective-permute-start | bytes 786440 | tf_op jit(solution)/shard_map/ppermute | solution.py:491
  152.5 22.4 %collective-permute-start.39 = (bf16[64,16,128]{2,1,0:T(8,128)(2,1)S(1)}, bf16[64,16,128]{2,1,0:T(8,128)(2,1)S(1)}, u32[]{:S(2)}, u32[]{:S(2)}) collective-permute-start(bf16[64,16,128]{2,1,0:T(8,128)(2,1)S(1)} %fusion.3), channel_id=1, source_target_pairs={{0,4},{4,12},{12,8},{8,0},{1,5},{5,13},{13,9},{9,1},{2,6},{6,14},{... | collective-permute-start | bytes 786440 | tf_op jit(solution)/shard_map/ppermute | solution.py:491
  158.1 22.4 %collective-permute-start.42 = (bf16[64,16,128]{2,1,0:T(8,128)(2,1)S(1)}, bf16[64,16,128]{2,1,0:T(8,128)(2,1)S(1)}, u32[]{:S(2)}, u32[]{:S(2)}) collective-permute-start(bf16[64,16,128]{2,1,0:T(8,128)(2,1)S(1)} %fusion.1), channel_id=1, source_target_pairs={{0,4},{4,12},{12,8},{8,0},{1,5},{5,13},{13,9},{9,1},{2,6},{6,14},{... | collective-permute-start | bytes 786440 | tf_op jit(solution)/shard_map/ppermute | solution.py:491
  169.3 33.4 %collective-permute-start.37 = (bf16[64,16,128]{2,1,0:T(8,128)(2,1)S(1)}, bf16[64,16,128]{2,1,0:T(8,128)(2,1)S(1)}, u32[]{:S(2)}, u32[]{:S(2)}) collective-permute-start(bf16[64,16,128]{2,1,0:T(8,128)(2,1)S(1)} %fusion.4), channel_id=1, source_target_pairs={{0,4},{4,12},{12,8},{8,0},{1,5},{5,13},{13,9},{9,1},{2,6},{6,14},{... | collective-permute-start | bytes 786440 | tf_op jit(solution)/shard_map/ppermute | solution.py:491
  174.9 25.1 %collective-permute-start.40 = (bf16[64,16,128]{2,1,0:T(8,128)(2,1)S(1)}, bf16[64,16,128]{2,1,0:T(8,128)(2,1)S(1)}, u32[]{:S(2)}, u32[]{:S(2)}) collective-permute-start(bf16[64,16,128]{2,1,0:T(8,128)(2,1)S(1)} %fusion.2), channel_id=1, source_target_pairs={{0,4},{4,12},{12,8},{8,0},{1,5},{5,13},{13,9},{9,1},{2,6},{6,14},{... | collective-permute-start | bytes 786440 | tf_op jit(solution)/shard_map/ppermute | solution.py:491
  180.5 16.8 %collective-permute-start.43 = (bf16[64,16,128]{2,1,0:T(8,128)(2,1)S(1)}, bf16[64,16,128]{2,1,0:T(8,128)(2,1)S(1)}, u32[]{:S(2)}, u32[]{:S(2)}) collective-permute-start(bf16[64,16,128]{2,1,0:T(8,128)(2,1)S(1)} %fusion), channel_id=1, source_target_pairs={{0,4},{4,12},{12,8},{8,0},{1,5},{5,13},{13,9},{9,1},{2,6},{6,14},{... | collective-permute-start | bytes 786440 | tf_op jit(solution)/shard_map/ppermute | solution.py:491
  181.5 23.9 %collective-permute-start.34 = (bf16[64,16,128]{2,1,0:T(8,128)(2,1)S(1)}, bf16[64,16,128]{2,1,0:T(8,128)(2,1)S(1)}, u32[]{:S(2)}, u32[]{:S(2)}) collective-permute-start(bf16[64,16,128]{2,1,0:T(8,128)(2,1)S(1)} %fusion.6), channel_id=1, source_target_pairs={{0,4},{4,12},{12,8},{8,0},{1,5},{5,13},{13,9},{9,1},{2,6},{6,14},{... | collective-permute-start | bytes 786440 | tf_op jit(solution)/shard_map/ppermute | solution.py:491
  185.0 23.2 %collective-permute-start.49 = (f32[128,128]{1,0:T(8,128)S(1)}, f32[128,128]{1,0:T(8,128)S(1)}, u32[]{:S(2)}, u32[]{:S(2)}) collective-permute-start(f32[128,128]{1,0:T(8,128)S(1)} %fusion.12), channel_id=1, source_target_pairs={{0,1},{1,0},{2,3},{3,2},{4,5},{5,4},{6,7},{7,6},{8,9},{9,8},{10,11... | collective-permute-start | bytes 196616 | tf_op jit(solution)/shard_map/ppermute | solution.py:497
  (43 other events, 535.9 us)

commit v2 on v1

v2 whole, which is shorter than its diff:
```python
import functools

import jax
import jax.numpy as jnp
from jax import lax
from jax.experimental import pallas as pl
from jax.experimental.pallas import tpu as pltpu
from jax.sharding import PartitionSpec as P

EPS = 1e-05


def layer_norm(values, gain):
    center = jnp.mean(values, axis=-1, keepdims=True)
    spread = jnp.mean((values - center) ** 2, axis=-1, keepdims=True)
    inverse = lax.rsqrt(spread + EPS)
    centred = (values - center) * inverse
    return (centred * gain, centred, inverse)


def norm_back(upstream, centred, inverse, gain):
    scaled = upstream * gain
    first = jnp.mean(scaled, axis=-1, keepdims=True)
    second = jnp.mean(scaled * centred, axis=-1, keepdims=True)
    return inverse * (scaled - first - centred * second)


def plain(pair_tiles, grad_out, exponents, token_mask, gain_in, w_proj, w_gate, gain_out, w_out):
    f32 = jnp.float32
    bf16 = jnp.bfloat16
    rows, cols, width = pair_tiles.shape
    crop_len = token_mask.shape[0]
    row_at = lax.axis_index("row")
    col_at = lax.axis_index("col")
    maskf = token_mask.astype(f32)
    mask_rows = lax.dynamic_slice_in_dim(maskf, row_at * rows, rows)
    mask_cols = lax.dynamic_slice_in_dim(maskf, col_at * cols, cols)
    pair_mask = (mask_rows[:, None] * mask_cols[None, :])[..., None]
    normed_f, centred, inverse = layer_norm(pair_tiles.astype(f32), gain_in)
    normed = normed_f.astype(bf16)
    flat = normed.reshape(-1, width)
    projected = jnp.dot(flat, w_proj, preferred_element_type=f32).reshape(rows, cols, 4 * width)
    gate_a = projected[..., :width]
    value_a = projected[..., width : 2 * width]
    gate_b = projected[..., 2 * width : 3 * width]
    value_b = projected[..., 3 * width :]
    sig_a = jax.nn.sigmoid(gate_a)
    sig_b = jax.nn.sigmoid(gate_b)
    left = (pair_mask * sig_a * value_a).astype(bf16)
    right_raw = pair_mask * sig_b * value_b
    bound = (448.0 * jnp.exp2(exponents.astype(f32)))[..., None]
    right = jnp.clip(right_raw, -bound, bound).astype(bf16)
    inside = (jnp.abs(right_raw) <= bound).astype(f32)
    panel = lax.all_gather(right, "row", axis=0, tiled=True)
    tri_cols = lax.psum_scatter(
        jnp.einsum("jkc,ikc->jic", panel, left, preferred_element_type=f32).astype(jnp.bfloat16),
        "col",
        scatter_dimension=0,
        tiled=True,
    ).astype(jnp.float32)
    tri = jnp.transpose(tri_cols, (1, 0, 2))
    tnorm_f, tcentred, tinverse = layer_norm(tri, gain_out)
    tnorm = tnorm_f.astype(bf16)
    tflat = tnorm.reshape(-1, width)
    opened = jax.nn.sigmoid(jnp.dot(flat, w_gate, preferred_element_type=f32)).reshape(
        rows, cols, width
    )
    outproj = jnp.dot(tflat, w_out, preferred_element_type=f32).reshape(rows, cols, width)
    upstream = grad_out.astype(f32)
    d_open = upstream * outproj
    d_outproj = (upstream * opened).astype(bf16).reshape(-1, width)
    g_out = jnp.dot(tflat.T, d_outproj, preferred_element_type=f32)
    d_tnorm = jnp.dot(d_outproj, w_out.T, preferred_element_type=f32).reshape(rows, cols, width)
    d_tri = norm_back(d_tnorm, tcentred, tinverse, gain_out).astype(bf16)
    d_gatepre = (d_open * opened * (1.0 - opened)).astype(bf16).reshape(-1, width)
    g_gate = jnp.dot(flat.T, d_gatepre, preferred_element_type=f32)
    grad_full = lax.all_gather(d_tri, "col", axis=1, tiled=True)
    d_left = jnp.einsum("ijc,jkc->ikc", grad_full, panel, preferred_element_type=f32)
    d_right = (
        lax.psum_scatter(
            jnp.einsum("ijc,ikc->jkc", grad_full, left, preferred_element_type=f32).astype(
                jnp.bfloat16
            ),
            "row",
            scatter_dimension=0,
            tiled=True,
        ).astype(jnp.float32)
        * inside
    )
    d_gate_a = d_left * pair_mask * value_a * sig_a * (1.0 - sig_a)
    d_value_a = d_left * pair_mask * sig_a
    d_gate_b = d_right * pair_mask * value_b * sig_b * (1.0 - sig_b)
    d_value_b = d_right * pair_mask * sig_b
    d_proj = (
        jnp.concatenate([d_gate_a, d_value_a, d_gate_b, d_value_b], axis=-1)
        .astype(bf16)
        .reshape(-1, 4 * width)
    )
    g_proj = jnp.dot(flat.T, d_proj, preferred_element_type=f32)
    d_normed = jnp.dot(d_proj, w_proj.T, preferred_element_type=f32) + jnp.dot(
        d_gatepre, w_gate.T, preferred_element_type=f32
    )
    d_pair = norm_back(d_normed.reshape(rows, cols, width), centred, inverse, gain_in).astype(bf16)
    sum_proj, sum_gate, sum_out = lax.psum((g_proj, g_gate, g_out), ("row", "col"))
    return (d_pair, sum_proj / crop_len, sum_gate / crop_len, sum_out / crop_len)


SUB = 16
HALF = 64
WIDTH = 128
LANES = SUB * HALF
GROUP = 16
NT = (((1,), (1,)), ((), ()))
NN = (((1,), (0,)), ((), ()))
TN = (((0,), (0,)), ((), ()))
F32 = jnp.float32
BF16 = jnp.bfloat16


def mm(a, b, dims):
    return lax.dot_general(a, b, dims, preferred_element_type=F32)


def params():
    return pltpu.CompilerParams(vmem_limit_bytes=40 * 1024 * 1024)


def cost(flops, size, exps=0):
    return pl.CostEstimate(flops=flops, bytes_accessed=size, transcendentals=exps)


def first_half(rows):
    return lax.broadcasted_iota(jnp.int32, (rows, WIDTH), 1) < HALF


def swap_halves(a, b):
    first = first_half(HALF)
    return (
        jnp.where(first, a, pltpu.roll(b, HALF, 1)),
        jnp.where(first, pltpu.roll(a, HALF, 1), b),
    )


def eye():
    row = lax.broadcasted_iota(jnp.int32, (WIDTH, WIDTH), 0)
    lane = lax.broadcasted_iota(jnp.int32, (WIDTH, WIDTH), 1)
    return (row == lane).astype(F32).astype(BF16)


def to_channels(cells):
    return mm(eye(), cells, NT)


def to_cells(channels):
    return mm(channels, eye(), TN)


def stage_rows(channels, buf):
    for t in range(SUB // 2):
        part = channels[:, t * WIDTH : (t + 1) * WIDTH]
        one, two = swap_halves(part[:HALF], part[HALF:])
        buf[(2 * t) * HALF : (2 * t + 1) * HALF, :] = one
        buf[(2 * t + 1) * HALF : (2 * t + 2) * HALF, :] = two


def panel_row(buf, p):
    return buf[pl.ds(p, SUB, stride=HALF), :]


def channels_of(panels, buf, out):
    buf[...] = panels.reshape(LANES, WIDTH)
    for t in range(SUB // 2):
        one = buf[pl.ds(2 * t, HALF, stride=SUB), :]
        two = buf[pl.ds(2 * t + 1, HALF, stride=SUB), :]
        low, high = swap_halves(one, two)
        out[:HALF, t * WIDTH : (t + 1) * WIDTH] = low
        out[HALF:, t * WIDTH : (t + 1) * WIDTH] = high
    return out[...]


def norm_channels(values, gain):
    center = jnp.mean(values, axis=0, keepdims=True)
    spread = jnp.mean((values - center) ** 2, axis=0, keepdims=True)
    inverse = lax.rsqrt(spread + EPS)
    centred = (values - center) * inverse
    return centred * gain, centred, inverse


def norm_back_channels(upstream, centred, inverse, gain):
    scaled = upstream * gain
    first = jnp.mean(scaled, axis=0, keepdims=True)
    second = jnp.mean(scaled * centred, axis=0, keepdims=True)
    return inverse * (scaled - first - centred * second)


def column(row):
    at = lax.broadcasted_iota(jnp.int32, (WIDTH, WIDTH), 0)
    lane = lax.broadcasted_iota(jnp.int32, (WIDTH, WIDTH), 1)
    return jnp.sum(jnp.where(at == lane, row, 0.0), axis=1, keepdims=True)


def mask_lanes(token_ref, s):
    valid = jnp.sum(token_ref[...].astype(F32), axis=1, keepdims=True)
    lane = lax.broadcasted_iota(jnp.int32, (1, LANES), 1)
    row = lane // HALF + (lax.axis_index("row") * HALF + s * SUB)
    col = lane % HALF + lax.axis_index("col") * HALF
    return (jnp.maximum(row, col).astype(F32) < valid).astype(F32)


def bound_lanes(exponent_ref):
    bound = 448.0 * jnp.exp2(exponent_ref[...].astype(F32))
    return jnp.concatenate([bound[i : i + 1] for i in range(SUB)], axis=1)


def normed_cells(x_ref, gain_ref):
    gain = column(gain_ref[...])
    normed, centred, inverse = norm_channels(to_channels(x_ref[...].reshape(LANES, WIDTH)), gain)
    return normed.astype(BF16), centred, inverse, gain


def right_kernel(s, x_ref, gain_ref, w_ref, token_ref, exponent_ref, out_ref, buf):
    normed = normed_cells(x_ref, gain_ref)[0]
    proj = mm(w_ref[...], normed, TN)
    raw = mask_lanes(token_ref, s) * jax.nn.sigmoid(proj[:WIDTH]) * proj[WIDTH:]
    bound = bound_lanes(exponent_ref)
    stage_rows(jnp.clip(raw, -bound, bound), buf)
    for p in range(HALF):
        out_ref[p] = panel_row(buf, p).astype(BF16)


def left_kernel(x_ref, gain_ref, w_ref, token_ref, out_ref, buf):
    normed = normed_cells(x_ref, gain_ref)[0]
    proj = mm(w_ref[...], normed, TN)
    mask = mask_lanes(token_ref, pl.program_id(0))
    stage_rows(mask * jax.nn.sigmoid(proj[:WIDTH]) * proj[WIDTH:], buf)
    first = first_half(SUB)
    for p in range(HALF):
        row = panel_row(buf, p)
        out_ref[p, 0] = jnp.where(first, row, 0.0).astype(BF16)
        out_ref[p, 1] = jnp.where(first, 0.0, row).astype(BF16)


def tri_kernel(own, up1, up2, up3, down1, down2, down3, left_ref, keep_ref, near_ref, send_ref, panel_ref):
    z, q = lax.axis_index("row"), lax.axis_index("col")
    for d in range(4):
        other = ((z + d) & 3) ^ q
        place = (other & 1) * 2 + (other >> 1)
        if d == 0:
            panel_ref[place] = own[...]
        else:
            panel_ref[place] = (up1, up2, up3)[d - 1][...] + (down1, down2, down3)[3 - d][...]
    for p in range(GROUP):
        right = jnp.concatenate([panel_ref[r, p] for r in range(4)], axis=0)
        tri = mm(right, left_ref[p].reshape(WIDTH, WIDTH), NT).astype(BF16)
        keep_ref[p] = tri[:SUB]
        near_ref[p] = tri[SUB : 2 * SUB]
        send_ref[0, p] = tri[2 * SUB : 3 * SUB]
        send_ref[1, p] = tri[3 * SUB :]


def mid_kernel(
    a_ref, b_ref, c_ref, x_ref, grad_ref, gain_in_ref, gain_out_ref, gate_ref, out_w_ref,
    dtri_ref, dgate_ref, g_out_ref, g_gate_ref, buf, wide,
):
    gain_out = column(gain_out_ref[...])
    tri = channels_of(
        a_ref[...].astype(F32) + b_ref[0].astype(F32) + c_ref[...].astype(F32), buf, wide
    )
    tnorm_f, tcentred, tinverse = norm_channels(tri, gain_out)
    tnorm = tnorm_f.astype(BF16)

    def turned(ref):
        buf[...] = ref[...].astype(F32).reshape(LANES, WIDTH)
        rows = [buf[pl.ds(j, HALF, stride=SUB), :] for j in range(SUB)]
        return to_channels(jnp.concatenate(rows, axis=0).astype(BF16))

    normed = norm_channels(turned(x_ref), column(gain_in_ref[...]))[0].astype(BF16)
    upstream = turned(grad_ref)
    opened = jax.nn.sigmoid(mm(gate_ref[...], normed, TN))
    outproj = mm(out_w_ref[...], tnorm, TN)
    d_open = upstream * outproj
    d_outproj = (upstream * opened).astype(BF16)
    g_out_ref[...] = mm(tnorm, d_outproj, NT)
    d_tnorm = mm(out_w_ref[...], d_outproj, NN)
    d_tri = norm_back_channels(d_tnorm, tcentred, tinverse, gain_out)
    d_gatepre = (d_open * opened * (1.0 - opened)).astype(BF16)
    g_gate_ref[...] = mm(normed, d_gatepre, NT)
    stage_rows(d_tri, buf)
    for p in range(HALF):
        dtri_ref[p] = panel_row(buf, p).astype(BF16)
    buf[...] = to_cells(d_gatepre)
    for i in range(HALF):
        dgate_ref[i] = panel_row(buf, i).astype(BF16)


def dright_kernel(d0, d1, d2, d3, left_ref, p0, p1, p2, p3, held):
    z, q = lax.axis_index("row"), lax.axis_index("col")
    for r, ref in enumerate((d0, d1, d2, d3)):
        slot = ((q ^ ((r % 2) * 2 + r // 2)) - z + 4) & 3
        held[slot] = ref[...]
    for p in range(GROUP):
        grads = jnp.concatenate([held[d, p] for d in range(4)], axis=0)
        part = mm(grads, left_ref[p].reshape(WIDTH, WIDTH), NN).astype(BF16)
        for d, ref in enumerate((p0, p1, p2, p3)):
            ref[p] = part[d * SUB : (d + 1) * SUB]


def dleft_kernel(*refs):
    out_ref = refs[-1]
    parts = (len(refs) - 1) // 5
    grad_refs, panel_refs = refs[: 4 * parts], refs[4 * parts : 5 * parts]
    first = first_half(HALF)
    for p in range(GROUP):
        grads = jnp.concatenate([d[p] for d in grad_refs], axis=0)
        right = jnp.concatenate([r[q, p] for r in panel_refs for q in range(4)], axis=0)
        both = mm(grads, right, TN)
        out_ref[p] = jnp.where(first, both[:HALF], both[HALF:])


def gate_grads(upstream, mask, sig, value):
    d_gate = (upstream * mask * value * sig * (1.0 - sig)).astype(BF16)
    d_value = (upstream * mask * sig).astype(BF16)
    return jnp.concatenate([d_gate, d_value], axis=0)


def final_a_kernel(
    x_ref, dleft_ref, token_ref, gain_ref, w_ref, gate_ref, q0, q1, q2, q3, out_ref, g_ref, buf, wide
):
    s = pl.program_id(0)
    normed = normed_cells(x_ref, gain_ref)[0]
    proj = mm(w_ref[...], normed, TN)
    d_left = channels_of(dleft_ref[...], buf, wide)
    d_proj = gate_grads(d_left, mask_lanes(token_ref, s), jax.nn.sigmoid(proj[:WIDTH]), proj[WIDTH:])
    d_gate = jnp.concatenate([q[...] for q in (q0, q1, q2, q3)], axis=1).reshape(LANES, WIDTH)
    out_ref[...] = mm(w_ref[...], d_proj, NN) + mm(gate_ref[...], d_gate, NT)

    @pl.when(s == 0)
    def start():
        g_ref[...] = jnp.zeros_like(g_ref)

    g_ref[...] += mm(normed, d_proj, NT)


def final_b_kernel(
    s, x_ref, part_ref, a_ref, b_ref, c_ref, token_ref, exponent_ref, gain_ref, w_ref, into_ref,
    out_ref, g_ref, buf, wide,
):
    normed, centred, inverse, gain = normed_cells(x_ref, gain_ref)
    proj = mm(w_ref[...], normed, TN)
    mask = mask_lanes(token_ref, s)
    sig = jax.nn.sigmoid(proj[:WIDTH])
    inside = jnp.abs(mask * sig * proj[WIDTH:]) <= bound_lanes(exponent_ref)
    d_right = channels_of(
        a_ref[...].astype(F32) + b_ref[...].astype(F32) + c_ref[...].astype(F32), buf, wide
    )
    d_proj = gate_grads(jnp.where(inside, d_right, 0.0), mask, sig, proj[WIDTH:])
    g_ref[...] = mm(normed, d_proj, NT)
    d_normed = part_ref[...] + mm(w_ref[...], d_proj, NN)
    d_pair = norm_back_channels(d_normed, centred, inverse, gain).astype(BF16)
    out_ref[...] = to_cells(d_pair).astype(BF16).reshape(SUB, HALF, WIDTH)


def whole(array):
    return pl.BlockSpec(array.shape, lambda i: (0,) * array.ndim)


def block(shape, at):
    return pl.BlockSpec(shape, lambda i: at)


BUF = pltpu.VMEM((LANES, WIDTH), F32)
WIDE = pltpu.VMEM((WIDTH, LANES), F32)
PANEL = jax.ShapeDtypeStruct((HALF, SUB, WIDTH), BF16)
PANEL_SPEC = pl.BlockSpec((GROUP, SUB, WIDTH), lambda i: (i, 0, 0))
FOUR = jax.ShapeDtypeStruct((4, HALF, SUB, WIDTH), BF16)
FOUR_SPEC = pl.BlockSpec((4, GROUP, SUB, WIDTH), lambda i: (0, i, 0, 0))
TWO = jax.ShapeDtypeStruct((2, HALF, SUB, WIDTH), BF16)
TWO_SPEC = pl.BlockSpec((2, GROUP, SUB, WIDTH), lambda i: (0, i, 0, 0))
LEFT_SPEC = pl.BlockSpec((GROUP, 2, HALF, WIDTH), lambda i: (i, 0, 0, 0))
WHOLE_PANEL = pl.BlockSpec(PANEL.shape, lambda i: (0, 0, 0))


def right_part(s, pair, gain, w_proj, tokens, exponents):
    return pl.pallas_call(
        functools.partial(right_kernel, s),
        grid=(1,),
        out_shape=PANEL,
        in_specs=[
            block((SUB, HALF, WIDTH), (s, 0, 0)), whole(gain), block((WIDTH, 2 * WIDTH), (0, 1)),
            whole(tokens), block((SUB, HALF), (s, 0)),
        ],
        out_specs=WHOLE_PANEL,
        scratch_shapes=[BUF],
        compiler_params=params(),
        cost_estimate=cost(4 * LANES * WIDTH * WIDTH, 1 << 19, LANES * WIDTH),
        name="right_part",
    )(pair, gain, w_proj, tokens, exponents)


def left_part(pair, gain, w_proj, tokens):
    return pl.pallas_call(
        left_kernel,
        grid=(HALF // SUB,),
        out_shape=jax.ShapeDtypeStruct((HALF, 2, HALF, WIDTH), BF16),
        in_specs=[
            pl.BlockSpec((SUB, HALF, WIDTH), lambda i: (i, 0, 0)), whole(gain),
            block((WIDTH, 2 * WIDTH), (0, 0)), whole(tokens),
        ],
        out_specs=pl.BlockSpec((HALF, 2, SUB, WIDTH), lambda i: (0, 0, i, 0)),
        scratch_shapes=[BUF],
        compiler_params=params(),
        cost_estimate=cost(16 * LANES * WIDTH * WIDTH, 3 << 20, 4 * LANES * WIDTH),
        name="left_part",
    )(pair, gain, w_proj, tokens)


def tri_part(slots, left):
    return pl.pallas_call(
        tri_kernel,
        grid=(HALF // GROUP,),
        out_shape=(PANEL, PANEL, TWO, FOUR),
        in_specs=[PANEL_SPEC] * 7 + [LEFT_SPEC],
        out_specs=(PANEL_SPEC, PANEL_SPEC, TWO_SPEC, FOUR_SPEC),
        compiler_params=params(),
        cost_estimate=cost(2 * HALF * HALF * WIDTH * WIDTH, 5 << 20),
        name="tri_part",
    )(*slots, left)


def mid_part(s, parts, pair, grad, gain_in, gain_out, w_gate, w_out):
    square = jax.ShapeDtypeStruct((WIDTH, WIDTH), F32)
    columns = block((HALF, SUB, WIDTH), (0, s, 0))
    small = [gain_in, gain_out, w_gate, w_out]
    return pl.pallas_call(
        mid_kernel,
        grid=(1,),
        out_shape=(PANEL, PANEL, square, square),
        in_specs=[WHOLE_PANEL, block((1, HALF, SUB, WIDTH), (0, 0, 0, 0)), WHOLE_PANEL]
        + [columns] * 2
        + [whole(a) for a in small],
        out_specs=(WHOLE_PANEL, WHOLE_PANEL, block(square.shape, (0, 0)), block(square.shape, (0, 0))),
        scratch_shapes=[BUF, WIDE],
        compiler_params=params(),
        cost_estimate=cost(12 * LANES * WIDTH * WIDTH, 2 << 20, LANES * WIDTH),
        name="mid_part",
    )(*parts, pair, grad, *small)


def dright_part(blocks, left):
    return pl.pallas_call(
        dright_kernel,
        grid=(HALF // GROUP,),
        out_shape=(PANEL,) * 4,
        in_specs=[PANEL_SPEC] * 4 + [LEFT_SPEC],
        out_specs=(PANEL_SPEC,) * 4,
        scratch_shapes=[pltpu.VMEM((4, GROUP, SUB, WIDTH), BF16)],
        compiler_params=params(),
        cost_estimate=cost(2 * HALF * HALF * WIDTH * WIDTH, 4 << 20),
        name="dright_part",
    )(*blocks, left)


def dleft_part(grads, panels):
    return pl.pallas_call(
        dleft_kernel,
        grid=(HALF // GROUP,),
        out_shape=jax.ShapeDtypeStruct((HALF, HALF, WIDTH), F32),
        in_specs=[PANEL_SPEC] * len(grads) + [FOUR_SPEC] * len(panels),
        out_specs=pl.BlockSpec((GROUP, HALF, WIDTH), lambda i: (i, 0, 0)),
        compiler_params=params(),
        cost_estimate=cost(8 * HALF * HALF * WIDTH * WIDTH, 10 << 20),
        name="dleft_part",
    )(*grads, *panels)


def final_a_part(pair, dleft, tokens, gain, w_proj, w_gate, gates):
    return pl.pallas_call(
        final_a_kernel,
        grid=(HALF // SUB,),
        out_shape=(
            jax.ShapeDtypeStruct((WIDTH, HALF * HALF), F32),
            jax.ShapeDtypeStruct((WIDTH, 2 * WIDTH), F32),
        ),
        in_specs=[
            pl.BlockSpec((SUB, HALF, WIDTH), lambda i: (i, 0, 0)),
            pl.BlockSpec((HALF, SUB, WIDTH), lambda i: (0, i, 0)),
            whole(tokens), whole(gain), block((WIDTH, 2 * WIDTH), (0, 0)), whole(w_gate),
        ]
        + [pl.BlockSpec((SUB, SUB, WIDTH), lambda i: (i, 0, 0))] * 4,
        out_specs=(
            pl.BlockSpec((WIDTH, LANES), lambda i: (0, i)),
            block((WIDTH, 2 * WIDTH), (0, 0)),
        ),
        scratch_shapes=[BUF, WIDE],
        compiler_params=params(),
        cost_estimate=cost(56 * LANES * WIDTH * WIDTH, 8 << 20, 4 * LANES * WIDTH),
        name="final_a_part",
    )(pair, dleft, tokens, gain, w_proj, w_gate, *gates)


def final_b_part(s, pair, part, sums, tokens, exponents, gain, w_proj, into):
    return pl.pallas_call(
        functools.partial(final_b_kernel, s),
        grid=(1,),
        out_shape=(
            jax.ShapeDtypeStruct((HALF, HALF, WIDTH), BF16),
            jax.ShapeDtypeStruct((WIDTH, 2 * WIDTH), F32),
        ),
        in_specs=[
            block((SUB, HALF, WIDTH), (s, 0, 0)),
            block((WIDTH, LANES), (0, s)),
            WHOLE_PANEL, WHOLE_PANEL, WHOLE_PANEL,
            whole(tokens), block((SUB, HALF), (s, 0)), whole(gain),
            block((WIDTH, 2 * WIDTH), (0, 1)),
            pl.BlockSpec(memory_space=pl.ANY),
        ],
        out_specs=(block((SUB, HALF, WIDTH), (s, 0, 0)), block((WIDTH, 2 * WIDTH), (0, 0))),
        scratch_shapes=[BUF, WIDE],
        input_output_aliases={9: 0} if into.shape == pair.shape else {},
        compiler_params=params(),
        cost_estimate=cost(14 * LANES * WIDTH * WIDTH, 2 << 20, LANES * WIDTH),
        name="final_b_part",
    )(pair, part, *sums, tokens, exponents, gain, w_proj, into)


def after(array, *others):
    return lax.optimization_barrier((array, *others))[0]


def blocked(pair_tiles, grad_out, exponents, token_mask, gain_in, w_proj, w_gate, gain_out, w_out):
    rows, cols, width = pair_tiles.shape
    crop_len = token_mask.shape[0]
    parts = rows // SUB
    core = lax.axis_index("col") % 2
    x_at = lax.axis_index("col") // 2
    tokens = token_mask.reshape(1, crop_len)
    gain_in = gain_in.reshape(1, width)
    gain_out = gain_out.reshape(1, width)

    def up(a, t):
        return lax.ppermute(a, "row", [(k, k + 1) for k in range(t - 1, 3)])

    def down(a, t):
        return lax.ppermute(a, "row", [(k, k - 1) for k in range(4 - t, 0, -1)])

    def sum_up(a, t):
        return lax.ppermute(a, "row", [(k, k + 1) for k in range(t)])

    def sum_down(a, t):
        return lax.ppermute(a, "row", [(k, k - 1) for k in range(3, 3 - t, -1)])

    def over_x(a):
        return lax.ppermute(a, "col", [(k, k ^ 2) for k in range(4)])

    def over_core(a):
        return lax.ppermute(a, "col", [(k, k ^ 1) for k in range(4)])

    def plus(a, b):
        return (a.astype(F32) + b.astype(F32)).astype(BF16)

    slots = []
    ready = ()
    for s in range(parts):
        own = after(right_part(s, pair_tiles, gain_in, w_proj, tokens, exponents), *ready)
        ups, downs = [own], [own]
        for t in (1, 2, 3):
            ups.append(up(ups[-1], t))
            downs.append(down(downs[-1], t))
        ready = (ups[2], downs[2])
        slots.append((own, *downs[1:], *ups[1:]))
    left = left_part(pair_tiles, gain_in, w_proj, tokens)

    grads, panels, gates, sums = [], [], [], []
    g_out = g_gate = 0.0
    for s in range(parts):
        keep, near, send, panel = tri_part(slots[s], left)
        got = over_core(send)
        mine = over_x(plus(near, got[1]))
        d_tri, d_gate, part_out, part_gate = mid_part(
            s, (keep, got, mine), pair_tiles, grad_out, gain_in, gain_out, w_gate, w_out
        )
        g_out, g_gate = g_out + part_out, g_gate + part_gate
        far = over_x(d_tri)
        blocks = [d_tri, far, over_core(d_tri), over_core(far)]
        part = dright_part(blocks, left)
        rise, fall = part[3], part[1]
        for t in (1, 2):
            rise = plus(sum_up(rise, t), part[3 - t])
            fall = plus(sum_down(fall, t), part[1 + t])
        sums.append((part[0], sum_up(rise, 3), sum_down(fall, 3)))
        grads += blocks
        panels.append(panel)
        gates.append(d_gate)
    d_left = dleft_part(grads, panels)
    partial, g_a = final_a_part(pair_tiles, d_left, tokens, gain_in, w_proj, w_gate, gates)

    d_pair = gain_in
    g_b = []
    for s in range(parts):
        d_pair, part_b = final_b_part(
            s, pair_tiles, partial, sums[s], tokens, exponents, gain_in, w_proj, d_pair
        )
        g_b.append(part_b)

    def exchange(a, send, at):
        half = a.shape[0] // 2
        return lax.dynamic_slice_in_dim(a, at * half, half) + send(
            lax.dynamic_slice_in_dim(a, (1 - at) * half, half)
        )

    def join(a, send, at):
        theirs = send(a)
        return jnp.concatenate([jnp.where(at == 0, a, theirs), jnp.where(at == 0, theirs, a)], axis=0)

    def over_rows(a):
        for bit in (1, 2):
            a = a + lax.ppermute(a, "row", [(k, k ^ bit) for k in range(4)])
        return a

    early = jnp.concatenate([g_out, g_gate, g_a, g_b[0] + g_b[1] + g_b[2]], axis=1)
    early = over_rows(exchange(exchange(early, over_core, core), over_x, x_at))
    early = join(join(early, over_x, x_at), over_core, core)
    late = exchange(g_b[3], over_core, core)
    late = join(over_rows(late + over_x(late)), over_core, core)
    g_proj = jnp.concatenate([early[:, 2 * width : 4 * width], early[:, 4 * width :] + late], axis=1)
    return d_pair, g_proj / crop_len, early[:, width : 2 * width] / crop_len, early[:, :width] / crop_len


def local(pair_tiles, *rest, rows_over, cols_over):
    if pair_tiles.shape == (HALF, HALF, WIDTH) and rows_over == cols_over == 4:
        return blocked(pair_tiles, *rest)
    return plain(pair_tiles, *rest)


def solution(mesh):
    return jax.shard_map(
        functools.partial(local, rows_over=mesh.shape["row"], cols_over=mesh.shape["col"]),
        mesh=mesh,
        in_specs=(
            P(("crop", "row"), "col", None),
            P(("crop", "row"), "col", None),
            P(("crop", "row"), "col"),
            P("crop"),
            P(),
            P(),
            P(),
            P(),
            P(),
        ),
        out_specs=(
            P(("crop", "row"), "col", None),
            P("crop", None),
            P("crop", None),
            P("crop", None),
        ),
        check_vma=False,
    )
```

time: 237 us -> 271 us (1.14)
  starting transfers between devices: 55.9 us -> 119 us
  waiting for transfers between devices: 113 us -> 73.4 us
  local copies, waits for them, and re-layouts: 9.12 us -> 13.3 us
  Pallas kernels: 52.3 us -> 55.1 us
    ppermute x54 -> x79, starting transfers between devices: 55.9 us -> 119 us  [the longest x12 46.3 us: sum_up(): return lax.ppermute(a, 'row', [(k, k + 1) for k in range(t)])]
    ppermute x54 -> x79, waiting for transfers between devices: 113 us -> 73.4 us  [the longest x12 30.8 us: down(): return lax.ppermute(a, 'row', [(k, k - 1) for k in range(4 - t, 0, -1)])]
    unnamed x45 -> x122, local copies, waits for them, and re-layouts: 5.06 us -> 13.2 us
    convert_element_type x13 -> x16, other arithmetic: 1.55 us -> 5.03 us  [plus(): return (a.astype(F32) + b.astype(F32)).astype(BF16)]
    pallas_call x16 -> x17, Pallas kernels: 35.4 us -> 35 us  [the longest x4 9.09 us: tri_part(): pl.pallas_call(tri_kernel, grid=(HALF // GROUP,), out_shape=(PANEL, PANEL...]
  transfers between devices with their start and end apart: 54 -> 79, of which waited for: 28 -> 23; matrix products, arithmetic and copies ran while one was open for 3% -> 2% of each run, Pallas kernels for 22% -> 20%
where the time goes in v2:
time: 271 us; the launch traced here: 269 us
  starting transfers between devices  119 us (44%)
  waiting for transfers between devices  73.4 us (27%)
  Pallas kernels  55.1 us (20%)
  local copies, waits for them, and re-layouts  13.3 us (5%)
  other arithmetic  6.73 us (2%)
    ppermute x12, starting transfers between devices, sum_up(): return lax.ppermute(a, 'row', [(k, k + 1) for k in range(t)])  46.3 us
    ppermute x12, waiting for transfers between devices, down(): return lax.ppermute(a, 'row', [(k, k - 1) for k in range(4 - t, 0, -1)])  30.8 us
    ppermute x12, starting transfers between devices, up(): return lax.ppermute(a, 'row', [(k, k + 1) for k in range(t - 1, 3)])  23.3 us
    ppermute x12, starting transfers between devices, down(): return lax.ppermute(a, 'row', [(k, k - 1) for k in range(4 - t, 0, -1)])  15.6 us
    ppermute x4, waiting for transfers between devices, over_rows(): a = a + lax.ppermute(a, 'row', [(k, k ^ bit) for k in range(4)])  15.3 us
    ppermute x11, starting transfers between devices, over_x(): return lax.ppermute(a, 'col', [(k, k ^ 2) for k in range(4)])  14.6 us
    unnamed x122, local copies, waits for them, and re-layouts  13.2 us
    ppermute x11, waiting for transfers between devices, over_x(): return lax.ppermute(a, 'col', [(k, k ^ 2) for k in range(4)])  12.2 us
  transfers between devices with their start and end apart: 79, of which 23 were waited for; matrix products, arithmetic and copies ran while one was open for 2% of the time, Pallas kernels for 20%

profile of v2, /device:TPU:0, one launch (start us, length us, event | category | flops | bytes accessed | tf_op | source)
XLA Modules:
  0.0 269.4 jit_solution(1127851062214758822)
XLA Ops:
  5.8 4.9 %collective-permute-start.3 = (bf16[64,16,128]{2,1,0:T(8,128)(2,1)S(1)}, bf16[64,16,128]{2,1,0:T(8,128)(2,1)S(1)}, u32[]{:S(2)}, u32[]{:S(2)}) collective-permute-start(bf16[64,16,128]{2,1,0:T(8,128)(2,1)S(1)} %right_part.4.own), channel_id=1, source_target_pairs={{0,4},{4,8},{8,12},{1,5},{5,9},{9,13},{2,6},{6,10},{10,14},{3,7},{... | collective-permute-start | bytes 786440 | tf_op jit(solution)/shard_map/ppermute | solution.py:541
  12.1 4.2 %collective-permute-done.3.down1 = bf16[64,16,128]{2,1,0:T(8,128)(2,1)S(1)} collective-permute-done((bf16[64,16,128]{2,1,0:T(8,128)(2,1)S(1)}, bf16[64,16,128]{2,1,0:T(8,128)(2,1)S(1)}, u32[]{:S(2)}, u32[]{:S(2)}) %collective-permute-start.3) | collective-permute-done | bytes 262176 | tf_op jit(solution)/shard_map/ppermute | solution.py:541
  17.0 3.5 %collective-permute-done.up1 = bf16[64,16,128]{2,1,0:T(8,128)(2,1)S(1)} collective-permute-done((bf16[64,16,128]{2,1,0:T(8,128)(2,1)S(1)}, bf16[64,16,128]{2,1,0:T(8,128)(2,1)S(1)}, u32[]{:S(2)}, u32[]{:S(2)}) %collective-permute-start) | collective-permute-done | bytes 262176 | tf_op jit(solution)/shard_map/ppermute | solution.py:544
  22.7 6.6 %collective-permute-done.1.up2 = bf16[64,16,128]{2,1,0:T(8,128)(2,1)S(1)} collective-permute-done((bf16[64,16,128]{2,1,0:T(8,128)(2,1)S(1)}, bf16[64,16,128]{2,1,0:T(8,128)(2,1)S(1)}, u32[]{:S(2)}, u32[]{:S(2)}) %collective-permute-start.1) | collective-permute-done | bytes 262176 | tf_op jit(solution)/shard_map/ppermute | solution.py:544
  29.3 3.6 %collective-permute-start.14 = (bf16[64,16,128]{2,1,0:T(8,128)(2,1)S(1)}, bf16[64,16,128]{2,1,0:T(8,128)(2,1)S(1)}, u32[]{:S(2)}, u32[]{:S(2)}) collective-permute-start(bf16[64,16,128]{2,1,0:T(8,128)(2,1)S(1)} %right_part.5.own), channel_id=1, source_target_pairs={{0,4},{4,8},{8,12},{1,5},{5,9},{9,13},{2,6},{6,10},{10,14},{3,7},{... | collective-permute-start | bytes 786440 | tf_op jit(solution)/shard_map/ppermute | solution.py:541
  37.5 6.6 %collective-permute-done.11.up1 = bf16[64,16,128]{2,1,0:T(8,128)(2,1)S(1)} collective-permute-done((bf16[64,16,128]{2,1,0:T(8,128)(2,1)S(1)}, bf16[64,16,128]{2,1,0:T(8,128)(2,1)S(1)}, u32[]{:S(2)}, u32[]{:S(2)}) %collective-permute-start.11) | collective-permute-done | bytes 262176 | tf_op jit(solution)/shard_map/ppermute | solution.py:544
  45.4 4.2 %left_part.1.left_ref = bf16[64,2,64,128]{3,2,1,0:T(8,128)(2,1)S(1)} custom-call(bf16[64,64,128]{2,1,0:T(8,128)(2,1)S(1)} %copy-done, f32[1,128]{1,0:T(1,128)S(1)} %bitcast.25, bf16[128,512]{1,0:T(8,128)(2,1)S(1)} %copy-done.4, s32[1,256]{1,0:T(1,128)S(1)} %bitcast.40), custom_call_target="tpu_custom_call" | custom-call | flops 268435456 | bytes 3145728 | tf_op jit(solution)/shard_map/left_part/pallas_call | solution.py:401
  55.8 4.6 %collective-permute-start.25 = (bf16[64,16,128]{2,1,0:T(8,128)(2,1)S(1)}, bf16[64,16,128]{2,1,0:T(8,128)(2,1)S(1)}, u32[]{:S(2)}, u32[]{:S(2)}) collective-permute-start(bf16[64,16,128]{2,1,0:T(8,128)(2,1)S(1)} %right_part.6.own), channel_id=1, source_target_pairs={{0,4},{4,8},{8,12},{1,5},{5,9},{9,13},{2,6},{6,10},{10,14},{3,7},{... | collective-permute-start | bytes 786440 | tf_op jit(solution)/shard_map/ppermute | solution.py:541
  61.7 2.7 %collective-permute-done.13.up3 = bf16[64,16,128]{2,1,0:T(8,128)(2,1)S(1)} collective-permute-done((bf16[64,16,128]{2,1,0:T(8,128)(2,1)S(1)}, bf16[64,16,128]{2,1,0:T(8,128)(2,1)S(1)}, u32[]{:S(2)}, u32[]{:S(2)}) %collective-permute-start.13) | collective-permute-done | bytes 262176 | tf_op jit(solution)/shard_map/ppermute | solution.py:544
  74.3 5.9 %collective-permute-done.23.up2 = bf16[64,16,128]{2,1,0:T(8,128)(2,1)S(1)} collective-permute-done((bf16[64,16,128]{2,1,0:T(8,128)(2,1)S(1)}, bf16[64,16,128]{2,1,0:T(8,128)(2,1)S(1)}, u32[]{:S(2)}, u32[]{:S(2)}) %collective-permute-start.23) | collective-permute-done | bytes 262176 | tf_op jit(solution)/shard_map/ppermute | solution.py:544
  82.4 4.6 %collective-permute-start.36 = (bf16[64,16,128]{2,1,0:T(8,128)(2,1)S(1)}, bf16[64,16,128]{2,1,0:T(8,128)(2,1)S(1)}, u32[]{:S(2)}, u32[]{:S(2)}) collective-permute-start(bf16[64,16,128]{2,1,0:T(8,128)(2,1)S(1)} %right_part.7.own), channel_id=1, source_target_pairs={{0,4},{4,8},{8,12},{1,5},{5,9},{9,13},{2,6},{6,10},{10,14},{3,7},{... | collective-permute-start | bytes 786440 | tf_op jit(solution)/shard_map/ppermute | solution.py:541
  88.4 2.7 mid_part.4
  99.5 6.4 %collective-permute-done.18.c_ref = bf16[64,16,128]{2,1,0:T(8,128)(2,1)S(1)} collective-permute-done((bf16[64,16,128]{2,1,0:T(8,128)(2,1)S(1)}, bf16[64,16,128]{2,1,0:T(8,128)(2,1)S(1)}, u32[]{:S(2)}, u32[]{:S(2)}) %collective-permute-start.18) | collective-permute-done | bytes 262176 | tf_op jit(solution)/shard_map/ppermute | solution.py:553
  111.8 5.2 %collective-permute-start.62 = (bf16[64,16,128]{2,1,0:T(8,128)(2,1)S(1)}, bf16[64,16,128]{2,1,0:T(8,128)(2,1)S(1)}, u32[]{:S(2)}, u32[]{:S(2)}) collective-permute-start(bf16[64,16,128]{2,1,0:T(8,128)(2,1)S(1)} %get-tuple-element.106), channel_id=1, source_target_pairs={{0,4},{1,5},{2,6},{3,7},{16,20},{17,21},{18,22},{19,23}} | collective-permute-start | bytes 786440 | tf_op jit(solution)/shard_map/ppermute | solution.py:547
  126.0 3.2 %collective-permute-done.35.up3 = bf16[64,16,128]{2,1,0:T(8,128)(2,1)S(1)} collective-permute-done((bf16[64,16,128]{2,1,0:T(8,128)(2,1)S(1)}, bf16[64,16,128]{2,1,0:T(8,128)(2,1)S(1)}, u32[]{:S(2)}, u32[]{:S(2)}) %collective-permute-start.35) | collective-permute-done | bytes 262176 | tf_op jit(solution)/shard_map/ppermute | solution.py:544
  129.2 2.8 %tri_part.7 = (bf16[64,16,128]{2,1,0:T(8,128)(2,1)S(1)}, bf16[64,16,128]{2,1,0:T(8,128)(2,1)S(1)}, bf16[2,64,16,128]{3,2,1,0:T(8,128)(2,1)}, bf16[4,64,16,128]{3,2,1,0:T(8,128)(2,1)S(1)}) custom-call(bf16[64,16,128]{2,1,0:T(8,128)(2,1)S(1)} %right_part.7.own, bf16[64,16,128]{2,1,0:T(8,128)(2,1)S(1)} %collective-permute-done.33.up1, ...), custom_call_target="tpu_custom_call" | custom-call | flops 134217728 | bytes 5242880 | tf_op jit(solution)/shard_map/tri_part/pallas_call | solution.py:418
  132.1 3.9 %collective-permute-start.63 = (bf16[64,16,128]{2,1,0:T(8,128)(2,1)}, bf16[64,16,128]{2,1,0:T(8,128)(2,1)}, u32[]{:S(2)}, u32[]{:S(2)}) collective-permute-start(bf16[64,16,128]{2,1,0:T(8,128)(2,1)} %get-tuple-element.133), channel_id=1, source_target_pairs={{0,4},{4,8},{1,5},{5,9},{2,6},{6,10},{3,7},{7,11},{16,20},{20,24},... | collective-permute-start | bytes 786440 | tf_op jit(solution)/shard_map/ppermute | solution.py:547
  136.0 3.2 %mid_part.6 = (bf16[64,16,128]{2,1,0:T(8,128)(2,1)}, bf16[64,16,128]{2,1,0:T(8,128)(2,1)S(1)}, f32[128,128]{1,0:T(8,128)S(1)}, f32[128,128]{1,0:T(8,128)S(1)}) custom-call(bf16[64,16,128]{2,1,0:T(8,128)(2,1)S(1)} %get-tuple-element.75.a_ref, bf16[2,64,16,128]{3,2,1,0:T(8,128)(2,1)S(1)} %collective-permute-done.28.b_ref, ...), custom_call_target="tpu_custom_call" | custom-call | flops 201326592 | bytes 2097152 | tf_op jit(solution)/shard_map/mid_part/pallas_call | solution.py:434
  145.3 2.7 %dright_part.6 = (bf16[64,16,128]{2,1,0:T(8,128)(2,1)S(1)}, bf16[64,16,128]{2,1,0:T(8,128)(2,1)S(1)}, bf16[64,16,128]{2,1,0:T(8,128)(2,1)S(1)}, bf16[64,16,128]{2,1,0:T(8,128)(2,1)S(1)}) custom-call(bf16[64,16,128]{2,1,0:T(8,128)(2,1)S(1)} %copy-done.23, bf16[64,16,128]{2,1,0:T(8,128)(2,1)} %collective-permute-done.19.refs_5_.d1, ...), custom_call_target="tpu_custom_call" | custom-call | flops 134217728 | bytes 4194304 | tf_op jit(solution)/shard_map/dright_part/pallas_call | solution.py:450
  155.2 4.7 %collective-permute-start.64 = (bf16[64,16,128]{2,1,0:T(8,128)(2,1)S(1)}, bf16[64,16,128]{2,1,0:T(8,128)(2,1)S(1)}, u32[]{:S(2)}, u32[]{:S(2)}) collective-permute-start(bf16[64,16,128]{2,1,0:T(8,128)(2,1)S(1)} %add_convert_fusion.1), channel_id=1, source_target_pairs={{0,4},{4,8},{8,12},{1,5},{5,9},{9,13},{2,6},{6,10},{10,14},{3,7},{... | collective-permute-start | bytes 786440 | tf_op jit(solution)/shard_map/ppermute | solution.py:547
  168.4 3.6 %mid_part.7 = (bf16[64,16,128]{2,1,0:T(8,128)(2,1)S(1)}, bf16[64,16,128]{2,1,0:T(8,128)(2,1)S(1)}, f32[128,128]{1,0:T(8,128)S(1)}, f32[128,128]{1,0:T(8,128)S(1)}) custom-call(bf16[64,16,128]{2,1,0:T(8,128)(2,1)S(1)} %copy-done.41, bf16[2,64,16,128]{3,2,1,0:T(8,128)(2,1)} %collective-permute-done.39.b_ref, ...), custom_call_target="tpu_custom_call" | custom-call | flops 201326592 | bytes 2097152 | tf_op jit(solution)/shard_map/mid_part/pallas_call | solution.py:434
  172.0 3.8 %collective-permute-start.57 = (bf16[64,16,128]{2,1,0:T(8,128)(2,1)S(1)}, bf16[64,16,128]{2,1,0:T(8,128)(2,1)S(1)}, u32[]{:S(2)}, u32[]{:S(2)}) collective-permute-start(bf16[64,16,128]{2,1,0:T(8,128)(2,1)S(1)} %get-tuple-element.135), channel_id=1, source_target_pairs={{0,4},{4,8},{1,5},{5,9},{2,6},{6,10},{3,7},{7,11},{16,20},{20,24},... | collective-permute-start | bytes 786440 | tf_op jit(solution)/shard_map/ppermute | solution.py:547
  180.0 4.4 %collective-permute-start.51 = (bf16[64,16,128]{2,1,0:T(8,128)(2,1)S(1)}, bf16[64,16,128]{2,1,0:T(8,128)(2,1)S(1)}, u32[]{:S(2)}, u32[]{:S(2)}) collective-permute-start(bf16[64,16,128]{2,1,0:T(8,128)(2,1)S(1)} %get-tuple-element.137), channel_id=1, source_target_pairs={{0,4},{4,8},{1,5},{5,9},{2,6},{6,10},{3,7},{7,11},{16,20},{20,24},... | collective-permute-start | bytes 786440 | tf_op jit(solution)/shard_map/ppermute | solution.py:547
  185.1 3.1 %collective-permute-done.51 = bf16[64,16,128]{2,1,0:T(8,128)(2,1)S(1)} collective-permute-done((bf16[64,16,128]{2,1,0:T(8,128)(2,1)S(1)}, bf16[64,16,128]{2,1,0:T(8,128)(2,1)S(1)}, u32[]{:S(2)}, u32[]{:S(2)}) %collective-permute-start.51) | collective-permute-done | bytes 262176 | tf_op jit(solution)/shard_map/ppermute | solution.py:547
  189.6 5.3 %collective-permute-start.58 = (bf16[64,16,128]{2,1,0:T(8,128)(2,1)S(1)}, bf16[64,16,128]{2,1,0:T(8,128)(2,1)S(1)}, u32[]{:S(2)}, u32[]{:S(2)}) collective-permute-start(bf16[64,16,128]{2,1,0:T(8,128)(2,1)S(1)} %add_convert_fusion.3), channel_id=1, source_target_pairs={{0,4},{4,8},{8,12},{1,5},{5,9},{9,13},{2,6},{6,10},{10,14},{3,7},{... | collective-permute-start | bytes 786440 | tf_op jit(solution)/shard_map/ppermute | solution.py:547
  196.3 4.6 %collective-permute-start.52 = (bf16[64,16,128]{2,1,0:T(8,128)(2,1)S(1)}, bf16[64,16,128]{2,1,0:T(8,128)(2,1)S(1)}, u32[]{:S(2)}, u32[]{:S(2)}) collective-permute-start(bf16[64,16,128]{2,1,0:T(8,128)(2,1)S(1)} %add_convert_fusion.5), channel_id=1, source_target_pairs={{0,4},{4,8},{8,12},{1,5},{5,9},{9,13},{2,6},{6,10},{10,14},{3,7},{... | collective-permute-start | bytes 786440 | tf_op jit(solution)/shard_map/ppermute | solution.py:547
  202.2 3.6 %dleft_part.1.dleft_ref = f32[64,64,128]{2,1,0:T(8,128)S(1)} custom-call(bf16[64,16,128]{2,1,0:T(8,128)(2,1)S(1)} %get-tuple-element.68.refs_0_.d0, bf16[64,16,128]{2,1,0:T(8,128)(2,1)S(1)} %copy-done.17, bf16[64,16,128]{2,1,0:T(8,128)(2,1)S(1)} %copy-done.19, bf16[64,16,128]{2,1,0:T(8,128)(2,1)S(1)} %copy-done.21, bf16[64,16,128]{2,1,0:T(8,128)(2,1)S(1)} %copy-done.24, ...), custom_call_target="tpu_custom_call" | custom-call | flops 536870912 | bytes 10485760 | tf_op jit(solution)/shard_map/dleft_part/pallas_call | solution.py:464
  205.9 5.9 %final_a_part.1 = (f32[128,4096]{1,0:T(8,128)S(1)}, f32[128,256]{1,0:T(8,128)S(1)}) custom-call(bf16[64,64,128]{2,1,0:T(8,128)(2,1)S(1)} %copy-done.1, f32[64,64,128]{2,1,0:T(8,128)S(1)} %dleft_part.1.dleft_ref, s32[1,256]{1,0:T(1,128)S(1)} %bitcast.43, f32[1,128]{1,0:T(1,128)S(1)} %bitcast.32, bf16[128,512]{1,0:T(8,128)(2,1)S(1)} %copy-done.5, ...), custom_call_target="tpu_custom_call" | custom-call | flops 939524096 | bytes 8388608 | tf_op jit(solution)/shard_map/final_a_part/pallas_call | solution.py:477
  211.8 3.9 %collective-permute-start.44 = (bf16[64,16,128]{2,1,0:T(8,128)(2,1)S(1)}, bf16[64,16,128]{2,1,0:T(8,128)(2,1)S(1)}, u32[]{:S(2)}, u32[]{:S(2)}) collective-permute-start(bf16[64,16,128]{2,1,0:T(8,128)(2,1)S(1)} %get-tuple-element.94), channel_id=1, source_target_pairs={{0,4},{1,5},{2,6},{3,7},{16,20},{17,21},{18,22},{19,23}} | collective-permute-start | bytes 786440 | tf_op jit(solution)/shard_map/ppermute | solution.py:547
  232.1 5.3 %collective-permute-start.46 = (bf16[64,16,128]{2,1,0:T(8,128)(2,1)S(1)}, bf16[64,16,128]{2,1,0:T(8,128)(2,1)S(1)}, u32[]{:S(2)}, u32[]{:S(2)}) collective-permute-start(bf16[64,16,128]{2,1,0:T(8,128)(2,1)S(1)} %add_convert_fusion.7), channel_id=1, source_target_pairs={{0,4},{4,8},{8,12},{1,5},{5,9},{9,13},{2,6},{6,10},{10,14},{3,7},{... | collective-permute-start | bytes 786440 | tf_op jit(solution)/shard_map/ppermute | solution.py:547
  239.5 5.5 %collective-permute-done.70 = f32[32,768]{1,0:T(8,128)S(1)} collective-permute-done((f32[32,768]{1,0:T(8,128)S(1)}, f32[32,768]{1,0:T(8,128)S(1)}, u32[]{:S(2)}, u32[]{:S(2)}) %collective-permute-start.70) | collective-permute-done | bytes 98336 | tf_op jit(solution)/shard_map/ppermute | solution.py:617
  262.4 4.9 %collective-permute-done.77 = f32[64,256]{1,0:T(8,128)S(1)} collective-permute-done((f32[64,256]{1,0:T(8,128)S(1)}, f32[64,256]{1,0:T(8,128)S(1)}, u32[]{:S(2)}, u32[]{:S(2)}) %collective-permute-start.77) | collective-permute-done | bytes 65568 | tf_op jit(solution)/shard_map/ppermute | solution.py:617
  (308 shorter events, 127.0 us)
Async XLA Ops:
  34.3 15.4 %collective-permute-start.5 = (bf16[64,16,128]{2,1,0:T(8,128)(2,1)S(1)}, bf16[64,16,128]{2,1,0:T(8,128)(2,1)S(1)}, u32[]{:S(2)}, u32[]{:S(2)}) collective-permute-start(bf16[64,16,128]{2,1,0:T(8,128)(2,1)S(1)} %collective-permute-done.4.down2), channel_id=1, source_target_pairs={{8,12},{9,13},{10,14},{11,15},{24,28},{25,29},{26,30},{27,31}} | collective-permute-start | bytes 786440 | tf_op jit(solution)/shard_map/ppermute | solution.py:541
  35.0 14.7 %collective-permute-start.2 = (bf16[64,16,128]{2,1,0:T(8,128)(2,1)S(1)}, bf16[64,16,128]{2,1,0:T(8,128)(2,1)S(1)}, u32[]{:S(2)}, u32[]{:S(2)}) collective-permute-start(bf16[64,16,128]{2,1,0:T(8,128)(2,1)S(1)} %collective-permute-done.1.up2), channel_id=1, source_target_pairs={{4,0},{5,1},{6,2},{7,3},{20,16},{21,17},{22,18},{23,19}} | collective-permute-start | bytes 786440 | tf_op jit(solution)/shard_map/ppermute | solution.py:544
  36.8 16.0 %collective-permute-start.15 = (bf16[64,16,128]{2,1,0:T(8,128)(2,1)S(1)}, bf16[64,16,128]{2,1,0:T(8,128)(2,1)S(1)}, u32[]{:S(2)}, u32[]{:S(2)}) collective-permute-start(bf16[64,16,128]{2,1,0:T(8,128)(2,1)S(1)} %collective-permute-done.14.down1), channel_id=1, source_target_pairs={{4,8},{8,12},{5,9},{9,13},{6,10},{10,14},{7,11},{11,15},{20,24},{2... | collective-permute-start | bytes 786440 | tf_op jit(solution)/shard_map/ppermute | solution.py:541
  52.8 19.2 %collective-permute-start.6 = (bf16[2,64,16,128]{3,2,1,0:T(8,128)(2,1)S(1)}, bf16[2,64,16,128]{3,2,1,0:T(8,128)(2,1)S(1)}, u32[]{:S(2)}, u32[]{:S(2)}) collective-permute-start(bf16[2,64,16,128]{3,2,1,0:T(8,128)(2,1)S(1)} %get-tuple-element.66), channel_id=1, source_target_pairs={{0,1},{1,0},{2,3},{3,2},{4,5},{5,4},{6,7},{7,6},{8,9},{9,8},{10,11... | collective-permute-start | bytes 1572872 | tf_op jit(solution)/shard_map/ppermute | solution.py:556
  55.8 11.8 %collective-permute-start.25 = (bf16[64,16,128]{2,1,0:T(8,128)(2,1)S(1)}, bf16[64,16,128]{2,1,0:T(8,128)(2,1)S(1)}, u32[]{:S(2)}, u32[]{:S(2)}) collective-permute-start(bf16[64,16,128]{2,1,0:T(8,128)(2,1)S(1)} %right_part.6.own), channel_id=1, source_target_pairs={{0,4},{4,8},{8,12},{1,5},{5,9},{9,13},{2,6},{6,10},{10,14},{3,7},{... | collective-permute-start | bytes 786440 | tf_op jit(solution)/shard_map/ppermute | solution.py:541
  67.5 29.5 %collective-permute-start.17 = (bf16[2,64,16,128]{3,2,1,0:T(8,128)(2,1)S(1)}, bf16[2,64,16,128]{3,2,1,0:T(8,128)(2,1)S(1)}, u32[]{:S(2)}, u32[]{:S(2)}) collective-permute-start(bf16[2,64,16,128]{3,2,1,0:T(8,128)(2,1)S(1)} %get-tuple-element.71), channel_id=1, source_target_pairs={{0,1},{1,0},{2,3},{3,2},{4,5},{5,4},{6,7},{7,6},{8,9},{9,8},{10,11... | collective-permute-start | bytes 1572872 | tf_op jit(solution)/shard_map/ppermute | solution.py:556
  72.1 15.0 %collective-permute-start.7 = (bf16[64,16,128]{2,1,0:T(8,128)(2,1)S(1)}, bf16[64,16,128]{2,1,0:T(8,128)(2,1)S(1)}, u32[]{:S(2)}, u32[]{:S(2)}) collective-permute-start(bf16[64,16,128]{2,1,0:T(8,128)(2,1)S(1)} %fusion.11), channel_id=1, source_target_pairs={{0,2},{1,3},{2,0},{3,1},{4,6},{5,7},{6,4},{7,5},{8,10},{9,11},{10,... | collective-permute-start | bytes 786440 | tf_op jit(solution)/shard_map/ppermute | solution.py:553
  73.6 18.8 %collective-permute-start.27 = (bf16[64,16,128]{2,1,0:T(8,128)(2,1)S(1)}, bf16[64,16,128]{2,1,0:T(8,128)(2,1)S(1)}, u32[]{:S(2)}, u32[]{:S(2)}) collective-permute-start(bf16[64,16,128]{2,1,0:T(8,128)(2,1)S(1)} %collective-permute-done.26.down2), channel_id=1, source_target_pairs={{8,12},{9,13},{10,14},{11,15},{24,28},{25,29},{26,30},{27,31}} | collective-permute-start | bytes 786440 | tf_op jit(solution)/shard_map/ppermute | solution.py:541
  80.2 13.7 %collective-permute-start.24 = (bf16[64,16,128]{2,1,0:T(8,128)(2,1)S(1)}, bf16[64,16,128]{2,1,0:T(8,128)(2,1)S(1)}, u32[]{:S(2)}, u32[]{:S(2)}) collective-permute-start(bf16[64,16,128]{2,1,0:T(8,128)(2,1)S(1)} %collective-permute-done.23.up2), channel_id=1, source_target_pairs={{4,0},{5,1},{6,2},{7,3},{20,16},{21,17},{22,18},{23,19}} | collective-permute-start | bytes 786440 | tf_op jit(solution)/shard_map/ppermute | solution.py:544
  82.4 15.2 %collective-permute-start.36 = (bf16[64,16,128]{2,1,0:T(8,128)(2,1)S(1)}, bf16[64,16,128]{2,1,0:T(8,128)(2,1)S(1)}, u32[]{:S(2)}, u32[]{:S(2)}) collective-permute-start(bf16[64,16,128]{2,1,0:T(8,128)(2,1)S(1)} %right_part.7.own), channel_id=1, source_target_pairs={{0,4},{4,8},{8,12},{1,5},{5,9},{9,13},{2,6},{6,10},{10,14},{3,7},{... | collective-permute-start | bytes 786440 | tf_op jit(solution)/shard_map/ppermute | solution.py:541
  87.0 11.7 %collective-permute-start.33 = (bf16[64,16,128]{2,1,0:T(8,128)(2,1)S(1)}, bf16[64,16,128]{2,1,0:T(8,128)(2,1)S(1)}, u32[]{:S(2)}, u32[]{:S(2)}) collective-permute-start(bf16[64,16,128]{2,1,0:T(8,128)(2,1)S(1)} %right_part.7.own), channel_id=1, source_target_pairs={{12,8},{8,4},{4,0},{13,9},{9,5},{5,1},{14,10},{10,6},{6,2},{15,11}... | collective-permute-start | bytes 786440 | tf_op jit(solution)/shard_map/ppermute | solution.py:544
  97.0 20.7 %collective-permute-start.28 = (bf16[2,64,16,128]{3,2,1,0:T(8,128)(2,1)S(1)}, bf16[2,64,16,128]{3,2,1,0:T(8,128)(2,1)S(1)}, u32[]{:S(2)}, u32[]{:S(2)}) collective-permute-start(bf16[2,64,16,128]{3,2,1,0:T(8,128)(2,1)S(1)} %get-tuple-element.76), channel_id=1, source_target_pairs={{0,1},{1,0},{2,3},{3,2},{4,5},{5,4},{6,7},{7,6},{8,9},{9,8},{10,11... | collective-permute-start | bytes 1572872 | tf_op jit(solution)/shard_map/ppermute | solution.py:556
  97.7 12.4 %collective-permute-start.9 = (bf16[64,16,128]{2,1,0:T(8,128)(2,1)S(1)}, bf16[64,16,128]{2,1,0:T(8,128)(2,1)S(1)}, u32[]{:S(2)}, u32[]{:S(2)}) collective-permute-start(bf16[64,16,128]{2,1,0:T(8,128)(2,1)S(1)} %get-tuple-element.68.refs_0_.d0), channel_id=1, source_target_pairs={{0,1},{1,0},{2,3},{3,2},{4,5},{5,4},{6,7},{7,6},{8,9},{9,8},{10,11... | collective-permute-start | bytes 786440 | tf_op jit(solution)/shard_map/ppermute | solution.py:556
  98.8 11.9 %collective-permute-start.10 = (bf16[64,16,128]{2,1,0:T(8,128)(2,1)S(1)}, bf16[64,16,128]{2,1,0:T(8,128)(2,1)S(1)}, u32[]{:S(2)}, u32[]{:S(2)}) collective-permute-start(bf16[64,16,128]{2,1,0:T(8,128)(2,1)S(1)} %collective-permute-done.8.refs_1_.d1), channel_id=1, source_target_pairs={{0,1},{1,0},{2,3},{3,2},{4,5},{5,4},{6,7},{7,6},{8,9},{9,8},{10,11... | collective-permute-start | bytes 786440 | tf_op jit(solution)/shard_map/ppermute | solution.py:556
  98.8 18.3 %collective-permute-start.37 = (bf16[64,16,128]{2,1,0:T(8,128)(2,1)S(1)}, bf16[64,16,128]{2,1,0:T(8,128)(2,1)S(1)}, u32[]{:S(2)}, u32[]{:S(2)}) collective-permute-start(bf16[64,16,128]{2,1,0:T(8,128)(2,1)S(1)} %collective-permute-done.36.down1), channel_id=1, source_target_pairs={{4,8},{8,12},{5,9},{9,13},{6,10},{10,14},{7,11},{11,15},{20,24},{2... | collective-permute-start | bytes 786440 | tf_op jit(solution)/shard_map/ppermute | solution.py:541
  105.8 12.7 %collective-permute-start.34 = (bf16[64,16,128]{2,1,0:T(8,128)(2,1)S(1)}, bf16[64,16,128]{2,1,0:T(8,128)(2,1)S(1)}, u32[]{:S(2)}, u32[]{:S(2)}) collective-permute-start(bf16[64,16,128]{2,1,0:T(8,128)(2,1)S(1)} %collective-permute-done.33.up1), channel_id=1, source_target_pairs={{8,4},{4,0},{9,5},{5,1},{10,6},{6,2},{11,7},{7,3},{24,20},{20,16},... | collective-permute-start | bytes 786440 | tf_op jit(solution)/shard_map/ppermute | solution.py:544
  118.5 22.7 %collective-permute-start.20 = (bf16[64,16,128]{2,1,0:T(8,128)(2,1)S(1)}, bf16[64,16,128]{2,1,0:T(8,128)(2,1)S(1)}, u32[]{:S(2)}, u32[]{:S(2)}) collective-permute-start(bf16[64,16,128]{2,1,0:T(8,128)(2,1)S(1)} %get-tuple-element.73.refs_4_.d0), channel_id=1, source_target_pairs={{0,1},{1,0},{2,3},{3,2},{4,5},{5,4},{6,7},{7,6},{8,9},{9,8},{10,11... | collective-permute-start | bytes 786440 | tf_op jit(solution)/shard_map/ppermute | solution.py:556
  122.2 21.3 %collective-permute-start.21 = (bf16[64,16,128]{2,1,0:T(8,128)(2,1)}, bf16[64,16,128]{2,1,0:T(8,128)(2,1)}, u32[]{:S(2)}, u32[]{:S(2)}) collective-permute-start(bf16[64,16,128]{2,1,0:T(8,128)(2,1)} %collective-permute-done.19.refs_5_.d1), channel_id=1, source_target_pairs={{0,1},{1,0},{2,3},{3,2},{4,5},{5,4},{6,7},{7,6},{8,9},{9,8},{10,11... | collective-permute-start | bytes 786440 | tf_op jit(solution)/shard_map/ppermute | solution.py:556
  124.6 24.8 %collective-permute-start.66 = (bf16[64,16,128]{2,1,0:T(8,128)(2,1)}, bf16[64,16,128]{2,1,0:T(8,128)(2,1)}, u32[]{:S(2)}, u32[]{:S(2)}) collective-permute-start(bf16[64,16,128]{2,1,0:T(8,128)(2,1)} %get-tuple-element.132), channel_id=1, source_target_pairs={{12,8},{8,4},{13,9},{9,5},{14,10},{10,6},{15,11},{11,7},{28,24},{2... | collective-permute-start | bytes 786440 | tf_op jit(solution)/shard_map/ppermute | solution.py:550
  132.0 20.8 %collective-permute-start.39 = (bf16[2,64,16,128]{3,2,1,0:T(8,128)(2,1)}, bf16[2,64,16,128]{3,2,1,0:T(8,128)(2,1)}, u32[]{:S(2)}, u32[]{:S(2)}) collective-permute-start(bf16[2,64,16,128]{3,2,1,0:T(8,128)(2,1)} %get-tuple-element.81), channel_id=1, source_target_pairs={{0,1},{1,0},{2,3},{3,2},{4,5},{5,4},{6,7},{7,6},{8,9},{9,8},{10,11... | collective-permute-start | bytes 1572872 | tf_op jit(solution)/shard_map/ppermute | solution.py:556
  132.1 19.1 %collective-permute-start.63 = (bf16[64,16,128]{2,1,0:T(8,128)(2,1)}, bf16[64,16,128]{2,1,0:T(8,128)(2,1)}, u32[]{:S(2)}, u32[]{:S(2)}) collective-permute-start(bf16[64,16,128]{2,1,0:T(8,128)(2,1)} %get-tuple-element.133), channel_id=1, source_target_pairs={{0,4},{4,8},{1,5},{5,9},{2,6},{6,10},{3,7},{7,11},{16,20},{20,24},... | collective-permute-start | bytes 786440 | tf_op jit(solution)/shard_map/ppermute | solution.py:547
  148.0 16.1 %collective-permute-start.56 = (bf16[64,16,128]{2,1,0:T(8,128)(2,1)S(1)}, bf16[64,16,128]{2,1,0:T(8,128)(2,1)S(1)}, u32[]{:S(2)}, u32[]{:S(2)}) collective-permute-start(bf16[64,16,128]{2,1,0:T(8,128)(2,1)S(1)} %get-tuple-element.102), channel_id=1, source_target_pairs={{0,4},{1,5},{2,6},{3,7},{16,20},{17,21},{18,22},{19,23}} | collective-permute-start | bytes 786440 | tf_op jit(solution)/shard_map/ppermute | solution.py:547
  149.5 16.6 %collective-permute-start.59 = (bf16[64,16,128]{2,1,0:T(8,128)(2,1)S(1)}, bf16[64,16,128]{2,1,0:T(8,128)(2,1)S(1)}, u32[]{:S(2)}, u32[]{:S(2)}) collective-permute-start(bf16[64,16,128]{2,1,0:T(8,128)(2,1)S(1)} %get-tuple-element.104), channel_id=1, source_target_pairs={{12,8},{13,9},{14,10},{15,11},{28,24},{29,25},{30,26},{31,27}} | collective-permute-start | bytes 786440 | tf_op jit(solution)/shard_map/ppermute | solution.py:550
  152.8 36.8 %collective-permute-start.67 = (bf16[64,16,128]{2,1,0:T(8,128)(2,1)S(1)}, bf16[64,16,128]{2,1,0:T(8,128)(2,1)S(1)}, u32[]{:S(2)}, u32[]{:S(2)}) collective-permute-start(bf16[64,16,128]{2,1,0:T(8,128)(2,1)S(1)} %add_convert_fusion), channel_id=1, source_target_pairs={{12,8},{8,4},{4,0},{13,9},{9,5},{5,1},{14,10},{10,6},{6,2},{15,11}... | collective-permute-start | bytes 786440 | tf_op jit(solution)/shard_map/ppermute | solution.py:550
  155.2 56.6 %collective-permute-start.64 = (bf16[64,16,128]{2,1,0:T(8,128)(2,1)S(1)}, bf16[64,16,128]{2,1,0:T(8,128)(2,1)S(1)}, u32[]{:S(2)}, u32[]{:S(2)}) collective-permute-start(bf16[64,16,128]{2,1,0:T(8,128)(2,1)S(1)} %add_convert_fusion.1), channel_id=1, source_target_pairs={{0,4},{4,8},{8,12},{1,5},{5,9},{9,13},{2,6},{6,10},{10,14},{3,7},{... | collective-permute-start | bytes 786440 | tf_op jit(solution)/shard_map/ppermute | solution.py:547
  188.2 29.7 %collective-permute-start.61 = (bf16[64,16,128]{2,1,0:T(8,128)(2,1)S(1)}, bf16[64,16,128]{2,1,0:T(8,128)(2,1)S(1)}, u32[]{:S(2)}, u32[]{:S(2)}) collective-permute-start(bf16[64,16,128]{2,1,0:T(8,128)(2,1)S(1)} %add_convert_fusion.2), channel_id=1, source_target_pairs={{12,8},{8,4},{4,0},{13,9},{9,5},{5,1},{14,10},{10,6},{6,2},{15,11}... | collective-permute-start | bytes 786440 | tf_op jit(solution)/shard_map/ppermute | solution.py:550
  189.6 29.0 %collective-permute-start.58 = (bf16[64,16,128]{2,1,0:T(8,128)(2,1)S(1)}, bf16[64,16,128]{2,1,0:T(8,128)(2,1)S(1)}, u32[]{:S(2)}, u32[]{:S(2)}) collective-permute-start(bf16[64,16,128]{2,1,0:T(8,128)(2,1)S(1)} %add_convert_fusion.3), channel_id=1, source_target_pairs={{0,4},{4,8},{8,12},{1,5},{5,9},{9,13},{2,6},{6,10},{10,14},{3,7},{... | collective-permute-start | bytes 786440 | tf_op jit(solution)/shard_map/ppermute | solution.py:547
  195.0 25.8 %collective-permute-start.55 = (bf16[64,16,128]{2,1,0:T(8,128)(2,1)S(1)}, bf16[64,16,128]{2,1,0:T(8,128)(2,1)S(1)}, u32[]{:S(2)}, u32[]{:S(2)}) collective-permute-start(bf16[64,16,128]{2,1,0:T(8,128)(2,1)S(1)} %add_convert_fusion.4), channel_id=1, source_target_pairs={{12,8},{8,4},{4,0},{13,9},{9,5},{5,1},{14,10},{10,6},{6,2},{15,11}... | collective-permute-start | bytes 786440 | tf_op jit(solution)/shard_map/ppermute | solution.py:550
  196.3 24.5 %collective-permute-start.52 = (bf16[64,16,128]{2,1,0:T(8,128)(2,1)S(1)}, bf16[64,16,128]{2,1,0:T(8,128)(2,1)S(1)}, u32[]{:S(2)}, u32[]{:S(2)}) collective-permute-start(bf16[64,16,128]{2,1,0:T(8,128)(2,1)S(1)} %add_convert_fusion.5), channel_id=1, source_target_pairs={{0,4},{4,8},{8,12},{1,5},{5,9},{9,13},{2,6},{6,10},{10,14},{3,7},{... | collective-permute-start | bytes 786440 | tf_op jit(solution)/shard_map/ppermute | solution.py:547
  228.2 17.7 %collective-permute-start.49 = (bf16[64,16,128]{2,1,0:T(8,128)(2,1)S(1)}, bf16[64,16,128]{2,1,0:T(8,128)(2,1)S(1)}, u32[]{:S(2)}, u32[]{:S(2)}) collective-permute-start(bf16[64,16,128]{2,1,0:T(8,128)(2,1)S(1)} %add_convert_fusion.6), channel_id=1, source_target_pairs={{12,8},{8,4},{4,0},{13,9},{9,5},{5,1},{14,10},{10,6},{6,2},{15,11}... | collective-permute-start | bytes 786440 | tf_op jit(solution)/shard_map/ppermute | solution.py:550
  232.1 13.8 %collective-permute-start.46 = (bf16[64,16,128]{2,1,0:T(8,128)(2,1)S(1)}, bf16[64,16,128]{2,1,0:T(8,128)(2,1)S(1)}, u32[]{:S(2)}, u32[]{:S(2)}) collective-permute-start(bf16[64,16,128]{2,1,0:T(8,128)(2,1)S(1)} %add_convert_fusion.7), channel_id=1, source_target_pairs={{0,4},{4,8},{8,12},{1,5},{5,9},{9,13},{2,6},{6,10},{10,14},{3,7},{... | collective-permute-start | bytes 786440 | tf_op jit(solution)/shard_map/ppermute | solution.py:547
  255.5 11.9 %collective-permute-start.73 = (f32[64,768]{1,0:T(8,128)S(1)}, f32[64,768]{1,0:T(8,128)S(1)}, u32[]{:S(2)}, u32[]{:S(2)}) collective-permute-start(f32[64,768]{1,0:T(8,128)S(1)} %pad_maximum_fusion.1), channel_id=1, source_target_pairs={{0,1},{1,0},{2,3},{3,2},{4,5},{5,4},{6,7},{7,6},{8,9},{9,8},{10,11... | collective-permute-start | bytes 589832 | tf_op jit(solution)/shard_map/ppermute | solution.py:556
  (108 other events, 983.5 us)

commit v3 on v2

--- a/solution.py
+++ b/solution.py
@@ -122,7 +122,7 @@
 
 
 def params():
-    return pltpu.CompilerParams(vmem_limit_bytes=40 * 1024 * 1024)
+    return pltpu.CompilerParams(vmem_limit_bytes=56 * 1024 * 1024)
 
 
 def cost(flops, size, exps=0):
@@ -240,15 +240,11 @@
         out_ref[p, 1] = jnp.where(first, 0.0, row).astype(BF16)
 
 
-def tri_kernel(own, up1, up2, up3, down1, down2, down3, left_ref, keep_ref, near_ref, send_ref, panel_ref):
+def tri_kernel(s0, s1, s2, s3, left_ref, keep_ref, near_ref, send_ref, panel_ref):
     z, q = lax.axis_index("row"), lax.axis_index("col")
-    for d in range(4):
-        other = ((z + d) & 3) ^ q
-        place = (other & 1) * 2 + (other >> 1)
-        if d == 0:
-            panel_ref[place] = own[...]
-        else:
-            panel_ref[place] = (up1, up2, up3)[d - 1][...] + (down1, down2, down3)[3 - d][...]
+    for e, ref in enumerate((s0, s1, s2, s3)):
+        other = z ^ e ^ q
+        panel_ref[(other & 1) * 2 + (other >> 1)] = ref[...]
     for p in range(GROUP):
         right = jnp.concatenate([panel_ref[r, p] for r in range(4)], axis=0)
         tri = mm(right, left_ref[p].reshape(WIDTH, WIDTH), NT).astype(BF16)
@@ -293,16 +289,17 @@
         dgate_ref[i] = panel_row(buf, i).astype(BF16)
 
 
-def dright_kernel(d0, d1, d2, d3, left_ref, p0, p1, p2, p3, held):
+def dright_kernel(d0, d1, d2, d3, left_ref, p0, p13, p2, held):
     z, q = lax.axis_index("row"), lax.axis_index("col")
     for r, ref in enumerate((d0, d1, d2, d3)):
-        slot = ((q ^ ((r % 2) * 2 + r // 2)) - z + 4) & 3
-        held[slot] = ref[...]
+        held[q ^ z ^ ((r % 2) * 2 + r // 2)] = ref[...]
     for p in range(GROUP):
         grads = jnp.concatenate([held[d, p] for d in range(4)], axis=0)
         part = mm(grads, left_ref[p].reshape(WIDTH, WIDTH), NN).astype(BF16)
-        for d, ref in enumerate((p0, p1, p2, p3)):
-            ref[p] = part[d * SUB : (d + 1) * SUB]
+        p0[p] = part[:SUB]
+        p13[0, p] = part[SUB : 2 * SUB]
+        p2[p] = part[2 * SUB : 3 * SUB]
+        p13[1, p] = part[3 * SUB :]
 
 
 def dleft_kernel(*refs):
@@ -351,7 +348,7 @@
     sig = jax.nn.sigmoid(proj[:WIDTH])
     inside = jnp.abs(mask * sig * proj[WIDTH:]) <= bound_lanes(exponent_ref)
     d_right = channels_of(
-        a_ref[...].astype(F32) + b_ref[...].astype(F32) + c_ref[...].astype(F32), buf, wide
+        a_ref[...].astype(F32) + b_ref[0].astype(F32) + c_ref[...].astype(F32), buf, wide
     )
     d_proj = gate_grads(jnp.where(inside, d_right, 0.0), mask, sig, proj[WIDTH:])
     g_ref[...] = mm(normed, d_proj, NT)
@@ -419,7 +416,7 @@
         tri_kernel,
         grid=(HALF // GROUP,),
         out_shape=(PANEL, PANEL, TWO, FOUR),
-        in_specs=[PANEL_SPEC] * 7 + [LEFT_SPEC],
+        in_specs=[PANEL_SPEC] * 4 + [LEFT_SPEC],
         out_specs=(PANEL_SPEC, PANEL_SPEC, TWO_SPEC, FOUR_SPEC),
         compiler_params=params(),
         cost_estimate=cost(2 * HALF * HALF * WIDTH * WIDTH, 5 << 20),
@@ -450,9 +447,9 @@
     return pl.pallas_call(
         dright_kernel,
         grid=(HALF // GROUP,),
-        out_shape=(PANEL,) * 4,
+        out_shape=(PANEL, TWO, PANEL),
         in_specs=[PANEL_SPEC] * 4 + [LEFT_SPEC],
-        out_specs=(PANEL_SPEC,) * 4,
+        out_specs=(PANEL_SPEC, TWO_SPEC, PANEL_SPEC),
         scratch_shapes=[pltpu.VMEM((4, GROUP, SUB, WIDTH), BF16)],
         compiler_params=params(),
         cost_estimate=cost(2 * HALF * HALF * WIDTH * WIDTH, 4 << 20),
@@ -509,7 +506,7 @@
         in_specs=[
             block((SUB, HALF, WIDTH), (s, 0, 0)),
             block((WIDTH, LANES), (0, s)),
-            WHOLE_PANEL, WHOLE_PANEL, WHOLE_PANEL,
+            WHOLE_PANEL, block((1, HALF, SUB, WIDTH), (0, 0, 0, 0)), WHOLE_PANEL,
             whole(tokens), block((SUB, HALF), (s, 0)), whole(gain),
             block((WIDTH, 2 * WIDTH), (0, 1)),
             pl.BlockSpec(memory_space=pl.ANY),
@@ -537,17 +534,8 @@
     gain_in = gain_in.reshape(1, width)
     gain_out = gain_out.reshape(1, width)
 
-    def up(a, t):
-        return lax.ppermute(a, "row", [(k, k + 1) for k in range(t - 1, 3)])
-
-    def down(a, t):
-        return lax.ppermute(a, "row", [(k, k - 1) for k in range(4 - t, 0, -1)])
-
-    def sum_up(a, t):
-        return lax.ppermute(a, "row", [(k, k + 1) for k in range(t)])
-
-    def sum_down(a, t):
-        return lax.ppermute(a, "row", [(k, k - 1) for k in range(3, 3 - t, -1)])
+    def over_row(a, bit):
+        return lax.ppermute(a, "row", [(k, k ^ bit) for k in range(4)])
 
     def over_x(a):
         return lax.ppermute(a, "col", [(k, k ^ 2) for k in range(4)])
@@ -562,12 +550,9 @@
     ready = ()
     for s in range(parts):
         own = after(right_part(s, pair_tiles, gain_in, w_proj, tokens, exponents), *ready)
-        ups, downs = [own], [own]
-        for t in (1, 2, 3):
-            ups.append(up(ups[-1], t))
-            downs.append(down(downs[-1], t))
-        ready = (ups[2], downs[2])
-        slots.append((own, *downs[1:], *ups[1:]))
+        far = over_row(own, 2)
+        slots.append((own, over_row(own, 1), far, over_row(far, 1)))
+        ready = (far,)
     left = left_part(pair_tiles, gain_in, w_proj, tokens)
 
     grads, panels, gates, sums = [], [], [], []
@@ -582,12 +567,9 @@
         g_out, g_gate = g_out + part_out, g_gate + part_gate
         far = over_x(d_tri)
         blocks = [d_tri, far, over_core(d_tri), over_core(far)]
-        part = dright_part(blocks, left)
-        rise, fall = part[3], part[1]
-        for t in (1, 2):
-            rise = plus(sum_up(rise, t), part[3 - t])
-            fall = plus(sum_down(fall, t), part[1 + t])
-        sums.append((part[0], sum_up(rise, 3), sum_down(fall, 3)))
+        stay, pair, cross = dright_part(blocks, left)
+        got = over_row(pair, 1)
+        sums.append((stay, got, over_row(plus(cross, got[1]), 2)))
         grads += blocks
         panels.append(panel)
         gates.append(d_gate)
@@ -614,7 +596,7 @@
 
     def over_rows(a):
         for bit in (1, 2):
-            a = a + lax.ppermute(a, "row", [(k, k ^ bit) for k in range(4)])
+            a = a + over_row(a, bit)
         return a
 
     early = jnp.concatenate([g_out, g_gate, g_a, g_b[0] + g_b[1] + g_b[2]], axis=1)

time: 271 us -> 254 us (0.937)
  starting transfers between devices: 119 us -> 43.7 us
  Pallas kernels: 55.1 us -> 99.7 us
  waiting for transfers between devices: 73.4 us -> 89.2 us
    ppermute x52 -> x24, starting transfers between devices: 102 us -> 24.2 us  [over_row(): return lax.ppermute(a, 'row', [(k, k ^ bit) for k in range(4)])]
    ppermute x52 -> x24, waiting for transfers between devices: 60.6 us -> 76.3 us  [over_row(): return lax.ppermute(a, 'row', [(k, k ^ bit) for k in range(4)])]
    pallas_call x4, Pallas kernels: 9.09 us -> 19.6 us  [tri_part(): pl.pallas_call(tri_kernel, grid=(HALF // GROUP,), out_shape=(PANEL, PANEL...]
    pallas_call x4, Pallas kernels: 7.6 us -> 17.4 us  [dright_part(): pl.pallas_call(dright_kernel, grid=(HALF // GROUP,), out_shape=(PANEL, TW...]
    pallas_call x4, Pallas kernels: 3.84 us -> 10.6 us  [right_part(): pl.pallas_call(functools.partial(right_kernel, s), grid=(1,), out_shape=P...]
    pallas_call x4, Pallas kernels: 12.2 us -> 18.4 us  [mid_part(): pl.pallas_call(mid_kernel, grid=(1,), out_shape=(PANEL, PANEL, square, sq...]
    pallas_call x4, Pallas kernels: 8.59 us -> 14.1 us  [final_b_part(): pl.pallas_call(functools.partial(final_b_kernel, s), grid=(1,), out_shape...]
    ppermute x11, starting transfers between devices: 14.6 us -> 18.4 us  [over_x(): return lax.ppermute(a, 'col', [(k, k ^ 2) for k in range(4)])]
  transfers between devices with their start and end apart: 79 -> 51, of which waited for: 23 -> 23; matrix products, arithmetic and copies ran while one was open for 2% -> 2% of each run, Pallas kernels for 20% -> 38%
where the time goes in v3:
time: 254 us; the launch traced here: 253 us
  Pallas kernels  99.7 us (39%)
  waiting for transfers between devices  89.2 us (35%)
  starting transfers between devices  43.7 us (17%)
  local copies, waits for them, and re-layouts  13.8 us (5%)
  other arithmetic  5.11 us (2%)
    ppermute x24, waiting for transfers between devices, over_row(): return lax.ppermute(a, 'row', [(k, k ^ bit) for k in range(4)])  76.3 us
    ppermute x24, starting transfers between devices, over_row(): return lax.ppermute(a, 'row', [(k, k ^ bit) for k in range(4)])  24.2 us
    pallas_call x4, Pallas kernels, tri_part(): pl.pallas_call(tri_kernel, grid=(HALF // GROUP,), out_shape=(PANEL, PANEL...  19.6 us
    ppermute x11, starting transfers between devices, over_x(): return lax.ppermute(a, 'col', [(k, k ^ 2) for k in range(4)])  18.4 us
    pallas_call x4, Pallas kernels, mid_part(): pl.pallas_call(mid_kernel, grid=(1,), out_shape=(PANEL, PANEL, square, sq...  18.4 us
    pallas_call x4, Pallas kernels, dright_part(): pl.pallas_call(dright_kernel, grid=(HALF // GROUP,), out_shape=(PANEL, TW...  17.4 us
    pallas_call x4, Pallas kernels, final_b_part(): pl.pallas_call(functools.partial(final_b_kernel, s), grid=(1,), out_shape...  14.1 us
    unnamed x128, local copies, waits for them, and re-layouts  12.9 us
  transfers between devices with their start and end apart: 51, of which 23 were waited for; matrix products, arithmetic and copies ran while one was open for 2% of the time, Pallas kernels for 38%

profile of v3, /device:TPU:0, one launch (start us, length us, event | category | flops | bytes accessed | tf_op | source)
XLA Modules:
  0.0 252.9 jit_solution(2330082313940857507)
XLA Ops:
  3.3 4.0 %collective-permute-start.1 = (bf16[64,16,128]{2,1,0:T(8,128)(2,1)}, bf16[64,16,128]{2,1,0:T(8,128)(2,1)S(1)}, u32[]{:S(2)}, u32[]{:S(2)}) collective-permute-start(bf16[64,16,128]{2,1,0:T(8,128)(2,1)} %right_part.4.s0), channel_id=1, source_target_pairs={{0,8},{4,12},{8,0},{12,4},{1,9},{5,13},{9,1},{13,5},{2,10},{6,14},... | collective-permute-start | bytes 786440 | tf_op jit(solution)/shard_map/ppermute | solution.py:538
  10.0 9.5 %collective-permute-done.1.s2 = bf16[64,16,128]{2,1,0:T(8,128)(2,1)S(1)} collective-permute-done((bf16[64,16,128]{2,1,0:T(8,128)(2,1)}, bf16[64,16,128]{2,1,0:T(8,128)(2,1)S(1)}, u32[]{:S(2)}, u32[]{:S(2)}) %collective-permute-start.1) | collective-permute-done | bytes 262176 | tf_op jit(solution)/shard_map/ppermute | solution.py:538
  19.5 4.1 %collective-permute-start = (bf16[64,16,128]{2,1,0:T(8,128)(2,1)}, bf16[64,16,128]{2,1,0:T(8,128)(2,1)S(1)}, u32[]{:S(2)}, u32[]{:S(2)}) collective-permute-start(bf16[64,16,128]{2,1,0:T(8,128)(2,1)} %right_part.4.s0), channel_id=1, source_target_pairs={{0,4},{4,0},{8,12},{12,8},{1,5},{5,1},{9,13},{13,9},{2,6},{6,2},{1... | collective-permute-start | bytes 786440 | tf_op jit(solution)/shard_map/ppermute | solution.py:538
  26.3 7.5 %collective-permute-done.9.s2 = bf16[64,16,128]{2,1,0:T(8,128)(2,1)S(1)} collective-permute-done((bf16[64,16,128]{2,1,0:T(8,128)(2,1)}, bf16[64,16,128]{2,1,0:T(8,128)(2,1)S(1)}, u32[]{:S(2)}, u32[]{:S(2)}) %collective-permute-start.9) | collective-permute-done | bytes 262176 | tf_op jit(solution)/shard_map/ppermute | solution.py:538
  33.8 6.0 %left_part.1.left_ref = bf16[64,2,64,128]{3,2,1,0:T(8,128)(2,1)} custom-call(bf16[64,64,128]{2,1,0:T(8,128)(2,1)} %x_ref.27, f32[1,128]{1,0:T(1,128)} %bitcast.46, bf16[128,512]{1,0:T(8,128)(2,1)} %w_ref.19, s32[1,256]{1,0:T(1,128)} %bitcast.61), custom_call_target="tpu_custom_call" | custom-call | flops 268435456 | bytes 3145728 | tf_op jit(solution)/shard_map/left_part/pallas_call | solution.py:398
  41.9 3.7 %collective-permute-done.2.s3 = bf16[64,16,128]{2,1,0:T(8,128)(2,1)S(1)} collective-permute-done((bf16[64,16,128]{2,1,0:T(8,128)(2,1)S(1)}, bf16[64,16,128]{2,1,0:T(8,128)(2,1)S(1)}, u32[]{:S(2)}, u32[]{:S(2)}) %collective-permute-start.2) | collective-permute-done | bytes 262176 | tf_op jit(solution)/shard_map/ppermute | solution.py:538
  46.4 4.9 %tri_part.4 = (bf16[64,16,128]{2,1,0:T(8,128)(2,1)}, bf16[64,16,128]{2,1,0:T(8,128)(2,1)}, bf16[2,64,16,128]{3,2,1,0:T(8,128)(2,1)}, bf16[4,64,16,128]{3,2,1,0:T(8,128)(2,1)}) custom-call(bf16[64,16,128]{2,1,0:T(8,128)(2,1)} %right_part.4.s0, bf16[64,16,128]{2,1,0:T(8,128)(2,1)} %copy-done.49, bf16[64,16,128]{2,1,0:T(8,128)(2,1)} %copy-done.43, ...), custom_call_target="tpu_custom_call" | custom-call | flops 134217728 | bytes 5242880 | tf_op jit(solution)/shard_map/tri_part/pallas_call | solution.py:415
  57.0 4.9 %tri_part.5 = (bf16[64,16,128]{2,1,0:T(8,128)(2,1)}, bf16[64,16,128]{2,1,0:T(8,128)(2,1)}, bf16[2,64,16,128]{3,2,1,0:T(8,128)(2,1)}, bf16[4,64,16,128]{3,2,1,0:T(8,128)(2,1)}) custom-call(bf16[64,16,128]{2,1,0:T(8,128)(2,1)} %right_part.5.s0, bf16[64,16,128]{2,1,0:T(8,128)(2,1)} %copy-done.39, bf16[64,16,128]{2,1,0:T(8,128)(2,1)} %copy-done.36, ...), custom_call_target="tpu_custom_call" | custom-call | flops 134217728 | bytes 5242880 | tf_op jit(solution)/shard_map/tri_part/pallas_call | solution.py:415
  62.0 6.3 %collective-permute-done.16.s1 = bf16[64,16,128]{2,1,0:T(8,128)(2,1)S(1)} collective-permute-done((bf16[64,16,128]{2,1,0:T(8,128)(2,1)S(1)}, bf16[64,16,128]{2,1,0:T(8,128)(2,1)S(1)}, u32[]{:S(2)}, u32[]{:S(2)}) %collective-permute-start.16) | collective-permute-done | bytes 262176 | tf_op jit(solution)/shard_map/ppermute | solution.py:538
  70.4 3.9 %collective-permute-done.18.s3 = bf16[64,16,128]{2,1,0:T(8,128)(2,1)S(1)} collective-permute-done((bf16[64,16,128]{2,1,0:T(8,128)(2,1)S(1)}, bf16[64,16,128]{2,1,0:T(8,128)(2,1)S(1)}, u32[]{:S(2)}, u32[]{:S(2)}) %collective-permute-start.18) | collective-permute-done | bytes 262176 | tf_op jit(solution)/shard_map/ppermute | solution.py:538
  75.0 4.9 %tri_part.6 = (bf16[64,16,128]{2,1,0:T(8,128)(2,1)}, bf16[64,16,128]{2,1,0:T(8,128)(2,1)}, bf16[2,64,16,128]{3,2,1,0:T(8,128)(2,1)}, bf16[4,64,16,128]{3,2,1,0:T(8,128)(2,1)}) custom-call(bf16[64,16,128]{2,1,0:T(8,128)(2,1)} %right_part.6.s0, bf16[64,16,128]{2,1,0:T(8,128)(2,1)} %copy-done.38, bf16[64,16,128]{2,1,0:T(8,128)(2,1)} %copy-done.32, ...), custom_call_target="tpu_custom_call" | custom-call | flops 134217728 | bytes 5242880 | tf_op jit(solution)/shard_map/tri_part/pallas_call | solution.py:415
  85.8 4.9 %tri_part.7 = (bf16[64,16,128]{2,1,0:T(8,128)(2,1)}, bf16[64,16,128]{2,1,0:T(8,128)(2,1)}, bf16[2,64,16,128]{3,2,1,0:T(8,128)(2,1)}, bf16[4,64,16,128]{3,2,1,0:T(8,128)(2,1)}) custom-call(bf16[64,16,128]{2,1,0:T(8,128)(2,1)} %right_part.7.s0, bf16[64,16,128]{2,1,0:T(8,128)(2,1)} %copy-done.42, bf16[64,16,128]{2,1,0:T(8,128)(2,1)} %copy-done.34, ...), custom_call_target="tpu_custom_call" | custom-call | flops 134217728 | bytes 5242880 | tf_op jit(solution)/shard_map/tri_part/pallas_call | solution.py:415
  93.4 4.6 %mid_part.4 = (bf16[64,16,128]{2,1,0:T(8,128)(2,1)}, bf16[64,16,128]{2,1,0:T(8,128)(2,1)}, f32[128,128]{1,0:T(8,128)}, f32[128,128]{1,0:T(8,128)}) custom-call(bf16[64,16,128]{2,1,0:T(8,128)(2,1)} %get-tuple-element.61.a_ref, bf16[2,64,16,128]{3,2,1,0:T(8,128)(2,1)} %copy-done.4, bf16[64,16,128]{2,1,0:T(8,128)(2,1)} %copy-done.47, ...), custom_call_target="tpu_custom_call" | custom-call | flops 201326592 | bytes 2097152 | tf_op jit(solution)/shard_map/mid_part/pallas_call | solution.py:431
  100.9 4.6 %mid_part.5 = (bf16[64,16,128]{2,1,0:T(8,128)(2,1)}, bf16[64,16,128]{2,1,0:T(8,128)(2,1)}, f32[128,128]{1,0:T(8,128)}, f32[128,128]{1,0:T(8,128)}) custom-call(bf16[64,16,128]{2,1,0:T(8,128)(2,1)} %get-tuple-element.66.a_ref, bf16[2,64,16,128]{3,2,1,0:T(8,128)(2,1)} %copy-done.6, bf16[64,16,128]{2,1,0:T(8,128)(2,1)} %copy-done.48, ...), custom_call_target="tpu_custom_call" | custom-call | flops 201326592 | bytes 2097152 | tf_op jit(solution)/shard_map/mid_part/pallas_call | solution.py:431
  107.3 5.6 %collective-permute-done.20.c_ref = bf16[64,16,128]{2,1,0:T(8,128)(2,1)S(1)} collective-permute-done((bf16[64,16,128]{2,1,0:T(8,128)(2,1)S(1)}, bf16[64,16,128]{2,1,0:T(8,128)(2,1)S(1)}, u32[]{:S(2)}, u32[]{:S(2)}) %collective-permute-start.20) | collective-permute-done | bytes 262176 | tf_op jit(solution)/shard_map/ppermute | solution.py:541
  113.6 4.6 %mid_part.6 = (bf16[64,16,128]{2,1,0:T(8,128)(2,1)}, bf16[64,16,128]{2,1,0:T(8,128)(2,1)}, f32[128,128]{1,0:T(8,128)}, f32[128,128]{1,0:T(8,128)}) custom-call(bf16[64,16,128]{2,1,0:T(8,128)(2,1)} %get-tuple-element.71.a_ref, bf16[2,64,16,128]{3,2,1,0:T(8,128)(2,1)} %copy-done.5, bf16[64,16,128]{2,1,0:T(8,128)(2,1)} %copy-done.44, ...), custom_call_target="tpu_custom_call" | custom-call | flops 201326592 | bytes 2097152 | tf_op jit(solution)/shard_map/mid_part/pallas_call | solution.py:431
  121.3 4.4 %dright_part.7 = (bf16[64,16,128]{2,1,0:T(8,128)(2,1)}, bf16[2,64,16,128]{3,2,1,0:T(8,128)(2,1)}, bf16[64,16,128]{2,1,0:T(8,128)(2,1)}) custom-call(bf16[64,16,128]{2,1,0:T(8,128)(2,1)} %get-tuple-element.64.refs_0_.d0, bf16[64,16,128]{2,1,0:T(8,128)(2,1)} %copy-done.9, bf16[64,16,128]{2,1,0:T(8,128)(2,1)} %copy-done.11, bf16[64,16,128]{2,1,0:T(8,128)(2,1)} %copy-done.13, ...), custom_call_target="tpu_custom_call" | custom-call | flops 134217728 | bytes 4194304 | tf_op jit(solution)/shard_map/dright_part/pallas_call | solution.py:447
  128.5 4.4 %dright_part.6 = (bf16[64,16,128]{2,1,0:T(8,128)(2,1)}, bf16[2,64,16,128]{3,2,1,0:T(8,128)(2,1)}, bf16[64,16,128]{2,1,0:T(8,128)(2,1)}) custom-call(bf16[64,16,128]{2,1,0:T(8,128)(2,1)} %get-tuple-element.69.refs_4_.d0, bf16[64,16,128]{2,1,0:T(8,128)(2,1)} %copy-done.10, bf16[64,16,128]{2,1,0:T(8,128)(2,1)} %copy-done.12, bf16[64,16,128]{2,1,0:T(8,128)(2,1)} %copy-done.16, ...), custom_call_target="tpu_custom_call" | custom-call | flops 134217728 | bytes 4194304 | tf_op jit(solution)/shard_map/dright_part/pallas_call | solution.py:447
  134.2 4.6 %mid_part.7 = (bf16[64,16,128]{2,1,0:T(8,128)(2,1)}, bf16[64,16,128]{2,1,0:T(8,128)(2,1)}, f32[128,128]{1,0:T(8,128)}, f32[128,128]{1,0:T(8,128)}) custom-call(bf16[64,16,128]{2,1,0:T(8,128)(2,1)} %get-tuple-element.76.a_ref, bf16[2,64,16,128]{3,2,1,0:T(8,128)(2,1)} %copy-done.3, bf16[64,16,128]{2,1,0:T(8,128)(2,1)} %copy-done.41, ...), custom_call_target="tpu_custom_call" | custom-call | flops 201326592 | bytes 2097152 | tf_op jit(solution)/shard_map/mid_part/pallas_call | solution.py:431
  141.1 4.3 %dright_part.5 = (bf16[64,16,128]{2,1,0:T(8,128)(2,1)}, bf16[2,64,16,128]{3,2,1,0:T(8,128)(2,1)}, bf16[64,16,128]{2,1,0:T(8,128)(2,1)}) custom-call(bf16[64,16,128]{2,1,0:T(8,128)(2,1)} %get-tuple-element.74.refs_8_.d0, bf16[64,16,128]{2,1,0:T(8,128)(2,1)} %copy-done.15, bf16[64,16,128]{2,1,0:T(8,128)(2,1)} %copy-done.17, bf16[64,16,128]{2,1,0:T(8,128)(2,1)} %copy-done.18, ...), custom_call_target="tpu_custom_call" | custom-call | flops 134217728 | bytes 4194304 | tf_op jit(solution)/shard_map/dright_part/pallas_call | solution.py:447
  150.2 10.1 %collective-permute-done.36.b_ref = bf16[2,64,16,128]{3,2,1,0:T(8,128)(2,1)S(1)} collective-permute-done((bf16[2,64,16,128]{3,2,1,0:T(8,128)(2,1)}, bf16[2,64,16,128]{3,2,1,0:T(8,128)(2,1)S(1)}, u32[]{:S(2)}, u32[]{:S(2)}) %collective-permute-start.36) | collective-permute-done | bytes 524320 | tf_op jit(solution)/shard_map/ppermute | solution.py:538
  160.4 10.5 %collective-permute-done.34.b_ref = bf16[2,64,16,128]{3,2,1,0:T(8,128)(2,1)S(1)} collective-permute-done((bf16[2,64,16,128]{3,2,1,0:T(8,128)(2,1)}, bf16[2,64,16,128]{3,2,1,0:T(8,128)(2,1)S(1)}, u32[]{:S(2)}, u32[]{:S(2)}) %collective-permute-start.34) | collective-permute-done | bytes 524320 | tf_op jit(solution)/shard_map/ppermute | solution.py:538
  174.2 4.4 %dright_part.4 = (bf16[64,16,128]{2,1,0:T(8,128)(2,1)}, bf16[2,64,16,128]{3,2,1,0:T(8,128)(2,1)}, bf16[64,16,128]{2,1,0:T(8,128)(2,1)}) custom-call(bf16[64,16,128]{2,1,0:T(8,128)(2,1)} %get-tuple-element.79.refs_12_.d0, bf16[64,16,128]{2,1,0:T(8,128)(2,1)} %copy-done.20, bf16[64,16,128]{2,1,0:T(8,128)(2,1)} %copy-done.21, bf16[64,16,128]{2,1,0:T(8,128)(2,1)} %copy-done.22, ...), custom_call_target="tpu_custom_call" | custom-call | flops 134217728 | bytes 4194304 | tf_op jit(solution)/shard_map/dright_part/pallas_call | solution.py:447
  181.0 6.1 %dleft_part.1.dleft_ref = f32[64,64,128]{2,1,0:T(8,128)} custom-call(bf16[64,16,128]{2,1,0:T(8,128)(2,1)} %get-tuple-element.64.refs_0_.d0, bf16[64,16,128]{2,1,0:T(8,128)(2,1)} %copy-done.9, bf16[64,16,128]{2,1,0:T(8,128)(2,1)} %copy-done.11, bf16[64,16,128]{2,1,0:T(8,128)(2,1)} %copy-done.13, bf16[64,16,128]{2,1,0:T(8,128)(2,1)} %get-tuple-element.69.refs_4_.d0, ...), custom_call_target="tpu_custom_call" | custom-call | flops 536870912 | bytes 10485760 | tf_op jit(solution)/shard_map/dleft_part/pallas_call | solution.py:461
  187.1 7.5 %final_a_part.1 = (f32[128,4096]{1,0:T(8,128)}, f32[128,256]{1,0:T(8,128)}) custom-call(bf16[64,64,128]{2,1,0:T(8,128)(2,1)} %x_ref.27, f32[64,64,128]{2,1,0:T(8,128)} %dleft_part.1.dleft_ref, s32[1,256]{1,0:T(1,128)} %bitcast.63, f32[1,128]{1,0:T(1,128)} %bitcast.52, bf16[128,512]{1,0:T(8,128)(2,1)} %w_ref.19, bf16[128,128]{1,0:T(8,128)(2,1)} %gate_ref.9, ...), custom_call_target="tpu_custom_call" | custom-call | flops 939524096 | bytes 8388608 | tf_op jit(solution)/shard_map/final_a_part/pallas_call | solution.py:474
  195.3 3.5 %final_b_part.4 = (bf16[64,64,128]{2,1,0:T(8,128)(2,1)}, f32[128,256]{1,0:T(8,128)}) custom-call(bf16[64,64,128]{2,1,0:T(8,128)(2,1)} %x_ref.27, f32[128,4096]{1,0:T(8,128)} %get-tuple-element.88.part_ref, bf16[64,16,128]{2,1,0:T(8,128)(2,1)} %get-tuple-element.98.a_ref, bf16[2,64,16,128]{3,2,1,0:T(8,128)(2,1)} %copy-done.7, ...), custom_call_target="tpu_custom_call" | custom-call | flops 234881024 | bytes 2097152 | tf_op jit(solution)/shard_map/final_b_part/pallas_call | solution.py:499
  199.5 3.5 %final_b_part.5 = (bf16[64,64,128]{2,1,0:T(8,128)(2,1)}, f32[128,256]{1,0:T(8,128)}) custom-call(bf16[64,64,128]{2,1,0:T(8,128)(2,1)} %x_ref.27, f32[128,4096]{1,0:T(8,128)} %get-tuple-element.88.part_ref, bf16[64,16,128]{2,1,0:T(8,128)(2,1)} %get-tuple-element.95.a_ref, bf16[2,64,16,128]{3,2,1,0:T(8,128)(2,1)} %copy-done, ...), custom_call_target="tpu_custom_call", output_to_operand_aliasing={{0}: (9, {})} | custom-call | flops 234881024 | bytes 2097152 | tf_op jit(solution)/shard_map/final_b_part/pallas_call | solution.py:499
  203.7 3.6 %final_b_part.6 = (bf16[64,64,128]{2,1,0:T(8,128)(2,1)}, f32[128,256]{1,0:T(8,128)}) custom-call(bf16[64,64,128]{2,1,0:T(8,128)(2,1)} %x_ref.27, f32[128,4096]{1,0:T(8,128)} %get-tuple-element.88.part_ref, bf16[64,16,128]{2,1,0:T(8,128)(2,1)} %get-tuple-element.92.a_ref, bf16[2,64,16,128]{3,2,1,0:T(8,128)(2,1)} %copy-done.1, ...), custom_call_target="tpu_custom_call", output_to_operand_aliasing={{0}: (9, {})} | custom-call | flops 234881024 | bytes 2097152 | tf_op jit(solution)/shard_map/final_b_part/pallas_call | solution.py:499
  212.9 10.3 %collective-permute-done.33.c_ref = bf16[64,16,128]{2,1,0:T(8,128)(2,1)S(1)} collective-permute-done((bf16[64,16,128]{2,1,0:T(8,128)(2,1)S(1)}, bf16[64,16,128]{2,1,0:T(8,128)(2,1)S(1)}, u32[]{:S(2)}, u32[]{:S(2)}) %collective-permute-start.33) | collective-permute-done | bytes 262176 | tf_op jit(solution)/shard_map/ppermute | solution.py:538
  224.0 3.5 %final_b_part.7 = (bf16[64,64,128]{2,1,0:T(8,128)(2,1)}, f32[128,256]{1,0:T(8,128)}) custom-call(bf16[64,64,128]{2,1,0:T(8,128)(2,1)} %x_ref.27, f32[128,4096]{1,0:T(8,128)} %get-tuple-element.88.part_ref, bf16[64,16,128]{2,1,0:T(8,128)(2,1)} %get-tuple-element.89.a_ref, bf16[2,64,16,128]{3,2,1,0:T(8,128)(2,1)} %copy-done.2, ...), custom_call_target="tpu_custom_call", output_to_operand_aliasing={{0}: (9, {})} | custom-call | flops 234881024 | bytes 2097152 | tf_op jit(solution)/shard_map/final_b_part/pallas_call | solution.py:499
  236.9 4.3 %collective-permute-done.43 = f32[32,768]{1,0:T(8,128)S(1)} collective-permute-done((f32[32,768]{1,0:T(8,128)S(1)}, f32[32,768]{1,0:T(8,128)S(1)}, u32[]{:S(2)}, u32[]{:S(2)}) %collective-permute-start.43) | collective-permute-done | bytes 98336 | tf_op jit(solution)/shard_map/ppermute | solution.py:538
  244.2 5.5 %collective-permute-done.49 = f32[64,256]{1,0:T(8,128)S(1)} collective-permute-done((f32[64,256]{1,0:T(8,128)S(1)}, f32[64,256]{1,0:T(8,128)S(1)}, u32[]{:S(2)}, u32[]{:S(2)}) %collective-permute-start.49) | collective-permute-done | bytes 65568 | tf_op jit(solution)/shard_map/ppermute | solution.py:538
  (250 shorter events, 77.0 us)
Async XLA Ops:
  3.3 16.2 %collective-permute-start.1 = (bf16[64,16,128]{2,1,0:T(8,128)(2,1)}, bf16[64,16,128]{2,1,0:T(8,128)(2,1)S(1)}, u32[]{:S(2)}, u32[]{:S(2)}) collective-permute-start(bf16[64,16,128]{2,1,0:T(8,128)(2,1)} %right_part.4.s0), channel_id=1, source_target_pairs={{0,8},{4,12},{8,0},{12,4},{1,9},{5,13},{9,1},{13,5},{2,10},{6,14},... | collective-permute-start | bytes 786440 | tf_op jit(solution)/shard_map/ppermute | solution.py:538
  19.5 14.3 %collective-permute-start.9 = (bf16[64,16,128]{2,1,0:T(8,128)(2,1)}, bf16[64,16,128]{2,1,0:T(8,128)(2,1)S(1)}, u32[]{:S(2)}, u32[]{:S(2)}) collective-permute-start(bf16[64,16,128]{2,1,0:T(8,128)(2,1)} %right_part.5.s0), channel_id=1, source_target_pairs={{0,8},{4,12},{8,0},{12,4},{1,9},{5,13},{9,1},{13,5},{2,10},{6,14},... | collective-permute-start | bytes 786440 | tf_op jit(solution)/shard_map/ppermute | solution.py:538
  19.5 22.4 %collective-permute-start = (bf16[64,16,128]{2,1,0:T(8,128)(2,1)}, bf16[64,16,128]{2,1,0:T(8,128)(2,1)S(1)}, u32[]{:S(2)}, u32[]{:S(2)}) collective-permute-start(bf16[64,16,128]{2,1,0:T(8,128)(2,1)} %right_part.4.s0), channel_id=1, source_target_pairs={{0,4},{4,0},{8,12},{12,8},{1,5},{5,1},{9,13},{13,9},{2,6},{6,2},{1... | collective-permute-start | bytes 786440 | tf_op jit(solution)/shard_map/ppermute | solution.py:538
  23.6 22.1 %collective-permute-start.2 = (bf16[64,16,128]{2,1,0:T(8,128)(2,1)S(1)}, bf16[64,16,128]{2,1,0:T(8,128)(2,1)S(1)}, u32[]{:S(2)}, u32[]{:S(2)}) collective-permute-start(bf16[64,16,128]{2,1,0:T(8,128)(2,1)S(1)} %collective-permute-done.1.s2), channel_id=1, source_target_pairs={{0,4},{4,0},{8,12},{12,8},{1,5},{5,1},{9,13},{13,9},{2,6},{6,2},{1... | collective-permute-start | bytes 786440 | tf_op jit(solution)/shard_map/ppermute | solution.py:538
  33.8 20.2 %collective-permute-start.17 = (bf16[64,16,128]{2,1,0:T(8,128)(2,1)}, bf16[64,16,128]{2,1,0:T(8,128)(2,1)S(1)}, u32[]{:S(2)}, u32[]{:S(2)}) collective-permute-start(bf16[64,16,128]{2,1,0:T(8,128)(2,1)} %right_part.6.s0), channel_id=1, source_target_pairs={{0,8},{4,12},{8,0},{12,4},{1,9},{5,13},{9,1},{13,5},{2,10},{6,14},... | collective-permute-start | bytes 786440 | tf_op jit(solution)/shard_map/ppermute | solution.py:538
  39.8 14.6 %collective-permute-start.8 = (bf16[64,16,128]{2,1,0:T(8,128)(2,1)S(1)}, bf16[64,16,128]{2,1,0:T(8,128)(2,1)S(1)}, u32[]{:S(2)}, u32[]{:S(2)}) collective-permute-start(bf16[64,16,128]{2,1,0:T(8,128)(2,1)S(1)} %copy-done.25), channel_id=1, source_target_pairs={{0,4},{4,0},{8,12},{12,8},{1,5},{5,1},{9,13},{13,9},{2,6},{6,2},{1... | collective-permute-start | bytes 786440 | tf_op jit(solution)/shard_map/ppermute | solution.py:538
  41.5 14.8 %collective-permute-start.10 = (bf16[64,16,128]{2,1,0:T(8,128)(2,1)S(1)}, bf16[64,16,128]{2,1,0:T(8,128)(2,1)S(1)}, u32[]{:S(2)}, u32[]{:S(2)}) collective-permute-start(bf16[64,16,128]{2,1,0:T(8,128)(2,1)S(1)} %collective-permute-done.9.s2), channel_id=1, source_target_pairs={{0,4},{4,0},{8,12},{12,8},{1,5},{5,1},{9,13},{13,9},{2,6},{6,2},{1... | collective-permute-start | bytes 786440 | tf_op jit(solution)/shard_map/ppermute | solution.py:538
  51.2 28.7 %collective-permute-start.3 = (bf16[2,64,16,128]{3,2,1,0:T(8,128)(2,1)}, bf16[2,64,16,128]{3,2,1,0:T(8,128)(2,1)S(1)}, u32[]{:S(2)}, u32[]{:S(2)}) collective-permute-start(bf16[2,64,16,128]{3,2,1,0:T(8,128)(2,1)} %get-tuple-element.62), channel_id=1, source_target_pairs={{0,1},{1,0},{2,3},{3,2},{4,5},{5,4},{6,7},{7,6},{8,9},{9,8},{10,11... | collective-permute-start | bytes 1572872 | tf_op jit(solution)/shard_map/ppermute | solution.py:544
  54.0 14.4 %collective-permute-start.16 = (bf16[64,16,128]{2,1,0:T(8,128)(2,1)S(1)}, bf16[64,16,128]{2,1,0:T(8,128)(2,1)S(1)}, u32[]{:S(2)}, u32[]{:S(2)}) collective-permute-start(bf16[64,16,128]{2,1,0:T(8,128)(2,1)S(1)} %copy-done.23), channel_id=1, source_target_pairs={{0,4},{4,0},{8,12},{12,8},{1,5},{5,1},{9,13},{13,9},{2,6},{6,2},{1... | collective-permute-start | bytes 786440 | tf_op jit(solution)/shard_map/ppermute | solution.py:538
  54.0 15.3 %collective-permute-start.25 = (bf16[64,16,128]{2,1,0:T(8,128)(2,1)}, bf16[64,16,128]{2,1,0:T(8,128)(2,1)S(1)}, u32[]{:S(2)}, u32[]{:S(2)}) collective-permute-start(bf16[64,16,128]{2,1,0:T(8,128)(2,1)} %right_part.7.s0), channel_id=1, source_target_pairs={{0,8},{4,12},{8,0},{12,4},{1,9},{5,13},{9,1},{13,5},{2,10},{6,14},... | collective-permute-start | bytes 786440 | tf_op jit(solution)/shard_map/ppermute | solution.py:538
  54.4 19.9 %collective-permute-start.18 = (bf16[64,16,128]{2,1,0:T(8,128)(2,1)S(1)}, bf16[64,16,128]{2,1,0:T(8,128)(2,1)S(1)}, u32[]{:S(2)}, u32[]{:S(2)}) collective-permute-start(bf16[64,16,128]{2,1,0:T(8,128)(2,1)S(1)} %collective-permute-done.17.s2), channel_id=1, source_target_pairs={{0,4},{4,0},{8,12},{12,8},{1,5},{5,1},{9,13},{13,9},{2,6},{6,2},{1... | collective-permute-start | bytes 786440 | tf_op jit(solution)/shard_map/ppermute | solution.py:538
  62.0 28.9 %collective-permute-start.11 = (bf16[2,64,16,128]{3,2,1,0:T(8,128)(2,1)}, bf16[2,64,16,128]{3,2,1,0:T(8,128)(2,1)S(1)}, u32[]{:S(2)}, u32[]{:S(2)}) collective-permute-start(bf16[2,64,16,128]{3,2,1,0:T(8,128)(2,1)} %get-tuple-element.67), channel_id=1, source_target_pairs={{0,1},{1,0},{2,3},{3,2},{4,5},{5,4},{6,7},{7,6},{8,9},{9,8},{10,11... | collective-permute-start | bytes 1572872 | tf_op jit(solution)/shard_map/ppermute | solution.py:544
  68.4 13.4 %collective-permute-start.24 = (bf16[64,16,128]{2,1,0:T(8,128)(2,1)S(1)}, bf16[64,16,128]{2,1,0:T(8,128)(2,1)S(1)}, u32[]{:S(2)}, u32[]{:S(2)}) collective-permute-start(bf16[64,16,128]{2,1,0:T(8,128)(2,1)S(1)} %copy-done.24), channel_id=1, source_target_pairs={{0,4},{4,0},{8,12},{12,8},{1,5},{5,1},{9,13},{13,9},{2,6},{6,2},{1... | collective-permute-start | bytes 786440 | tf_op jit(solution)/shard_map/ppermute | solution.py:538
  69.3 15.8 %collective-permute-start.26 = (bf16[64,16,128]{2,1,0:T(8,128)(2,1)S(1)}, bf16[64,16,128]{2,1,0:T(8,128)(2,1)S(1)}, u32[]{:S(2)}, u32[]{:S(2)}) collective-permute-start(bf16[64,16,128]{2,1,0:T(8,128)(2,1)S(1)} %collective-permute-done.25.s2), channel_id=1, source_target_pairs={{0,4},{4,0},{8,12},{12,8},{1,5},{5,1},{9,13},{13,9},{2,6},{6,2},{1... | collective-permute-start | bytes 786440 | tf_op jit(solution)/shard_map/ppermute | solution.py:538
  79.9 18.5 %collective-permute-start.19 = (bf16[2,64,16,128]{3,2,1,0:T(8,128)(2,1)}, bf16[2,64,16,128]{3,2,1,0:T(8,128)(2,1)S(1)}, u32[]{:S(2)}, u32[]{:S(2)}) collective-permute-start(bf16[2,64,16,128]{3,2,1,0:T(8,128)(2,1)} %get-tuple-element.72), channel_id=1, source_target_pairs={{0,1},{1,0},{2,3},{3,2},{4,5},{5,4},{6,7},{7,6},{8,9},{9,8},{10,11... | collective-permute-start | bytes 1572872 | tf_op jit(solution)/shard_map/ppermute | solution.py:544
  90.8 27.5 %collective-permute-start.27 = (bf16[2,64,16,128]{3,2,1,0:T(8,128)(2,1)}, bf16[2,64,16,128]{3,2,1,0:T(8,128)(2,1)S(1)}, u32[]{:S(2)}, u32[]{:S(2)}) collective-permute-start(bf16[2,64,16,128]{3,2,1,0:T(8,128)(2,1)} %get-tuple-element.77), channel_id=1, source_target_pairs={{0,1},{1,0},{2,3},{3,2},{4,5},{5,4},{6,7},{7,6},{8,9},{9,8},{10,11... | collective-permute-start | bytes 1572872 | tf_op jit(solution)/shard_map/ppermute | solution.py:544
  98.5 14.5 %collective-permute-start.20 = (bf16[64,16,128]{2,1,0:T(8,128)(2,1)S(1)}, bf16[64,16,128]{2,1,0:T(8,128)(2,1)S(1)}, u32[]{:S(2)}, u32[]{:S(2)}) collective-permute-start(bf16[64,16,128]{2,1,0:T(8,128)(2,1)S(1)} %fusion.5), channel_id=1, source_target_pairs={{0,2},{1,3},{2,0},{3,1},{4,6},{5,7},{6,4},{7,5},{8,10},{9,11},{10,... | collective-permute-start | bytes 786440 | tf_op jit(solution)/shard_map/ppermute | solution.py:541
  105.4 13.3 %collective-permute-start.13 = (bf16[64,16,128]{2,1,0:T(8,128)(2,1)}, bf16[64,16,128]{2,1,0:T(8,128)(2,1)S(1)}, u32[]{:S(2)}, u32[]{:S(2)}) collective-permute-start(bf16[64,16,128]{2,1,0:T(8,128)(2,1)} %get-tuple-element.69.refs_4_.d0), channel_id=1, source_target_pairs={{0,2},{1,3},{2,0},{3,1},{4,6},{5,7},{6,4},{7,5},{8,10},{9,11},{10,... | collective-permute-start | bytes 786440 | tf_op jit(solution)/shard_map/ppermute | solution.py:541
  107.3 18.6 %collective-permute-start.14 = (bf16[64,16,128]{2,1,0:T(8,128)(2,1)}, bf16[64,16,128]{2,1,0:T(8,128)(2,1)S(1)}, u32[]{:S(2)}, u32[]{:S(2)}) collective-permute-start(bf16[64,16,128]{2,1,0:T(8,128)(2,1)} %get-tuple-element.69.refs_4_.d0), channel_id=1, source_target_pairs={{0,1},{1,0},{2,3},{3,2},{4,5},{5,4},{6,7},{7,6},{8,9},{9,8},{10,11... | collective-permute-start | bytes 786440 | tf_op jit(solution)/shard_map/ppermute | solution.py:544
  118.9 14.6 %collective-permute-start.28 = (bf16[64,16,128]{2,1,0:T(8,128)(2,1)S(1)}, bf16[64,16,128]{2,1,0:T(8,128)(2,1)S(1)}, u32[]{:S(2)}, u32[]{:S(2)}) collective-permute-start(bf16[64,16,128]{2,1,0:T(8,128)(2,1)S(1)} %fusion.4), channel_id=1, source_target_pairs={{0,2},{1,3},{2,0},{3,1},{4,6},{5,7},{6,4},{7,5},{8,10},{9,11},{10,... | collective-permute-start | bytes 786440 | tf_op jit(solution)/shard_map/ppermute | solution.py:541
  125.6 21.8 %collective-permute-start.38 = (bf16[2,64,16,128]{3,2,1,0:T(8,128)(2,1)}, bf16[2,64,16,128]{3,2,1,0:T(8,128)(2,1)S(1)}, u32[]{:S(2)}, u32[]{:S(2)}) collective-permute-start(bf16[2,64,16,128]{3,2,1,0:T(8,128)(2,1)} %get-tuple-element.99), channel_id=1, source_target_pairs={{0,4},{4,0},{8,12},{12,8},{1,5},{5,1},{9,13},{13,9},{2,6},{6,2},{1... | collective-permute-start | bytes 1572872 | tf_op jit(solution)/shard_map/ppermute | solution.py:538
  126.0 13.7 %collective-permute-start.22 = (bf16[64,16,128]{2,1,0:T(8,128)(2,1)S(1)}, bf16[64,16,128]{2,1,0:T(8,128)(2,1)S(1)}, u32[]{:S(2)}, u32[]{:S(2)}) collective-permute-start(bf16[64,16,128]{2,1,0:T(8,128)(2,1)S(1)} %copy-done.14), channel_id=1, source_target_pairs={{0,1},{1,0},{2,3},{3,2},{4,5},{5,4},{6,7},{7,6},{8,9},{9,8},{10,11... | collective-permute-start | bytes 786440 | tf_op jit(solution)/shard_map/ppermute | solution.py:544
  132.9 27.4 %collective-permute-start.36 = (bf16[2,64,16,128]{3,2,1,0:T(8,128)(2,1)}, bf16[2,64,16,128]{3,2,1,0:T(8,128)(2,1)S(1)}, u32[]{:S(2)}, u32[]{:S(2)}) collective-permute-start(bf16[2,64,16,128]{3,2,1,0:T(8,128)(2,1)} %get-tuple-element.96), channel_id=1, source_target_pairs={{0,4},{4,0},{8,12},{12,8},{1,5},{5,1},{9,13},{13,9},{2,6},{6,2},{1... | collective-permute-start | bytes 1572872 | tf_op jit(solution)/shard_map/ppermute | solution.py:538
  145.4 25.5 %collective-permute-start.34 = (bf16[2,64,16,128]{3,2,1,0:T(8,128)(2,1)}, bf16[2,64,16,128]{3,2,1,0:T(8,128)(2,1)S(1)}, u32[]{:S(2)}, u32[]{:S(2)}) collective-permute-start(bf16[2,64,16,128]{3,2,1,0:T(8,128)(2,1)} %get-tuple-element.93), channel_id=1, source_target_pairs={{0,4},{4,0},{8,12},{12,8},{1,5},{5,1},{9,13},{13,9},{2,6},{6,2},{1... | collective-permute-start | bytes 1572872 | tf_op jit(solution)/shard_map/ppermute | solution.py:538
  146.7 26.1 %collective-permute-start.30 = (bf16[64,16,128]{2,1,0:T(8,128)(2,1)S(1)}, bf16[64,16,128]{2,1,0:T(8,128)(2,1)S(1)}, u32[]{:S(2)}, u32[]{:S(2)}) collective-permute-start(bf16[64,16,128]{2,1,0:T(8,128)(2,1)S(1)} %copy-done.19), channel_id=1, source_target_pairs={{0,1},{1,0},{2,3},{3,2},{4,5},{5,4},{6,7},{7,6},{8,9},{9,8},{10,11... | collective-permute-start | bytes 786440 | tf_op jit(solution)/shard_map/ppermute | solution.py:544
  147.4 25.4 %collective-permute-start.31 = (bf16[64,16,128]{2,1,0:T(8,128)(2,1)S(1)}, bf16[64,16,128]{2,1,0:T(8,128)(2,1)S(1)}, u32[]{:S(2)}, u32[]{:S(2)}) collective-permute-start(bf16[64,16,128]{2,1,0:T(8,128)(2,1)S(1)} %collective-permute-done.29.refs_13_.d1), channel_id=1, source_target_pairs={{0,1},{1,0},{2,3},{3,2},{4,5},{5,4},{6,7},{7,6},{8,9},{9,8},{10,11... | collective-permute-start | bytes 786440 | tf_op jit(solution)/shard_map/ppermute | solution.py:544
  147.5 47.1 %collective-permute-start.39 = (bf16[64,16,128]{2,1,0:T(8,128)(2,1)S(1)}, bf16[64,16,128]{2,1,0:T(8,128)(2,1)S(1)}, u32[]{:S(2)}, u32[]{:S(2)}) collective-permute-start(bf16[64,16,128]{2,1,0:T(8,128)(2,1)S(1)} %fusion), channel_id=1, source_target_pairs={{0,8},{4,12},{8,0},{12,4},{1,9},{5,13},{9,1},{13,5},{2,10},{6,14},... | collective-permute-start | bytes 786440 | tf_op jit(solution)/shard_map/ppermute | solution.py:538
  160.3 38.5 %collective-permute-start.37 = (bf16[64,16,128]{2,1,0:T(8,128)(2,1)S(1)}, bf16[64,16,128]{2,1,0:T(8,128)(2,1)S(1)}, u32[]{:S(2)}, u32[]{:S(2)}) collective-permute-start(bf16[64,16,128]{2,1,0:T(8,128)(2,1)S(1)} %fusion.1), channel_id=1, source_target_pairs={{0,8},{4,12},{8,0},{12,4},{1,9},{5,13},{9,1},{13,5},{2,10},{6,14},... | collective-permute-start | bytes 786440 | tf_op jit(solution)/shard_map/ppermute | solution.py:538
  172.1 31.0 %collective-permute-start.35 = (bf16[64,16,128]{2,1,0:T(8,128)(2,1)S(1)}, bf16[64,16,128]{2,1,0:T(8,128)(2,1)S(1)}, u32[]{:S(2)}, u32[]{:S(2)}) collective-permute-start(bf16[64,16,128]{2,1,0:T(8,128)(2,1)S(1)} %fusion.2), channel_id=1, source_target_pairs={{0,8},{4,12},{8,0},{12,4},{1,9},{5,13},{9,1},{13,5},{2,10},{6,14},... | collective-permute-start | bytes 786440 | tf_op jit(solution)/shard_map/ppermute | solution.py:538
  178.5 29.9 %collective-permute-start.32 = (bf16[2,64,16,128]{3,2,1,0:T(8,128)(2,1)}, bf16[2,64,16,128]{3,2,1,0:T(8,128)(2,1)S(1)}, u32[]{:S(2)}, u32[]{:S(2)}) collective-permute-start(bf16[2,64,16,128]{3,2,1,0:T(8,128)(2,1)} %get-tuple-element.90), channel_id=1, source_target_pairs={{0,4},{4,0},{8,12},{12,8},{1,5},{5,1},{9,13},{13,9},{2,6},{6,2},{1... | collective-permute-start | bytes 1572872 | tf_op jit(solution)/shard_map/ppermute | solution.py:538
  208.5 14.7 %collective-permute-start.33 = (bf16[64,16,128]{2,1,0:T(8,128)(2,1)S(1)}, bf16[64,16,128]{2,1,0:T(8,128)(2,1)S(1)}, u32[]{:S(2)}, u32[]{:S(2)}) collective-permute-start(bf16[64,16,128]{2,1,0:T(8,128)(2,1)S(1)} %fusion.3), channel_id=1, source_target_pairs={{0,8},{4,12},{8,0},{12,4},{1,9},{5,13},{9,1},{13,5},{2,10},{6,14},... | collective-permute-start | bytes 786440 | tf_op jit(solution)/shard_map/ppermute | solution.py:538
  209.9 18.5 %collective-permute-start.41 = (f32[32,768]{1,0:T(8,128)S(1)}, f32[32,768]{1,0:T(8,128)S(1)}, u32[]{:S(2)}, u32[]{:S(2)}) collective-permute-start(f32[32,768]{1,0:T(8,128)S(1)} %constant_dynamic-slice_fusion.1), channel_id=1, source_target_pairs={{0,2},{1,3},{2,0},{3,1},{4,6},{5,7},{6,4},{7,5},{8,10},{9,11},{10,... | collective-permute-start | bytes 294920 | tf_op jit(solution)/shard_map/ppermute | solution.py:541
  (83 other events, 868.6 us)

commit v4 on v3

--- a/solution.py
+++ b/solution.py
@@ -106,6 +106,7 @@
 
 
 SUB = 16
+PART = 32
 HALF = 64
 WIDTH = 128
 LANES = SUB * HALF
@@ -122,7 +123,7 @@
 
 
 def params():
-    return pltpu.CompilerParams(vmem_limit_bytes=56 * 1024 * 1024)
+    return pltpu.CompilerParams(vmem_limit_bytes=16 * 1024 * 1024)
 
 
 def cost(flops, size, exps=0):
@@ -218,10 +219,10 @@
     return normed.astype(BF16), centred, inverse, gain
 
 
-def right_kernel(s, x_ref, gain_ref, w_ref, token_ref, exponent_ref, out_ref, buf):
+def right_kernel(at, x_ref, gain_ref, w_ref, token_ref, exponent_ref, out_ref, buf):
     normed = normed_cells(x_ref, gain_ref)[0]
     proj = mm(w_ref[...], normed, TN)
-    raw = mask_lanes(token_ref, s) * jax.nn.sigmoid(proj[:WIDTH]) * proj[WIDTH:]
+    raw = mask_lanes(token_ref, at + pl.program_id(0)) * jax.nn.sigmoid(proj[:WIDTH]) * proj[WIDTH:]
     bound = bound_lanes(exponent_ref)
     stage_rows(jnp.clip(raw, -bound, bound), buf)
     for p in range(HALF):
@@ -242,8 +243,9 @@
 
 def tri_kernel(s0, s1, s2, s3, left_ref, keep_ref, near_ref, send_ref, panel_ref):
     z, q = lax.axis_index("row"), lax.axis_index("col")
-    for e, ref in enumerate((s0, s1, s2, s3)):
-        other = z ^ e ^ q
+    for m, ref in enumerate((s0, s1, s2, s3)):
+        place = ((z ^ (z >> 1)) - m + 4) & 3
+        other = place ^ (place >> 1) ^ q
         panel_ref[(other & 1) * 2 + (other >> 1)] = ref[...]
     for p in range(GROUP):
         right = jnp.concatenate([panel_ref[r, p] for r in range(4)], axis=0)
@@ -289,17 +291,19 @@
         dgate_ref[i] = panel_row(buf, i).astype(BF16)
 
 
-def dright_kernel(d0, d1, d2, d3, left_ref, p0, p13, p2, held):
+def dright_kernel(*refs):
+    *grads_refs, left_ref, p0, p1, p2, p3, held = refs
     z, q = lax.axis_index("row"), lax.axis_index("col")
-    for r, ref in enumerate((d0, d1, d2, d3)):
-        held[q ^ z ^ ((r % 2) * 2 + r // 2)] = ref[...]
+    for k, ref in enumerate(grads_refs):
+        r = k % 4
+        block_at = q ^ ((r % 2) * 2 + r // 2)
+        slot = ((z ^ (z >> 1)) - (block_at ^ (block_at >> 1)) + 4) & 3
+        held[slot, :, (k // 4) * SUB : (k // 4 + 1) * SUB] = ref[...]
     for p in range(GROUP):
-        grads = jnp.concatenate([held[d, p] for d in range(4)], axis=0)
+        grads = jnp.concatenate([held[m, p] for m in range(4)], axis=0)
         part = mm(grads, left_ref[p].reshape(WIDTH, WIDTH), NN).astype(BF16)
-        p0[p] = part[:SUB]
-        p13[0, p] = part[SUB : 2 * SUB]
-        p2[p] = part[2 * SUB : 3 * SUB]
-        p13[1, p] = part[3 * SUB :]
+        for m, ref in enumerate((p0, p1, p2, p3)):
+            ref[p] = part[m * PART : (m + 1) * PART]
 
 
 def dleft_kernel(*refs):
@@ -339,19 +343,23 @@
 
 
 def final_b_kernel(
-    s, x_ref, part_ref, a_ref, b_ref, c_ref, token_ref, exponent_ref, gain_ref, w_ref, into_ref,
+    at, x_ref, part_ref, a_ref, b_ref, token_ref, exponent_ref, gain_ref, w_ref, into_ref,
     out_ref, g_ref, buf, wide,
 ):
+    step = pl.program_id(0)
     normed, centred, inverse, gain = normed_cells(x_ref, gain_ref)
     proj = mm(w_ref[...], normed, TN)
-    mask = mask_lanes(token_ref, s)
+    mask = mask_lanes(token_ref, at + step)
     sig = jax.nn.sigmoid(proj[:WIDTH])
     inside = jnp.abs(mask * sig * proj[WIDTH:]) <= bound_lanes(exponent_ref)
-    d_right = channels_of(
-        a_ref[...].astype(F32) + b_ref[0].astype(F32) + c_ref[...].astype(F32), buf, wide
-    )
+    d_right = channels_of(a_ref[...].astype(F32) + b_ref[...].astype(F32), buf, wide)
     d_proj = gate_grads(jnp.where(inside, d_right, 0.0), mask, sig, proj[WIDTH:])
-    g_ref[...] = mm(normed, d_proj, NT)
+
+    @pl.when(step == 0)
+    def start():
+        g_ref[...] = jnp.zeros_like(g_ref)
+
+    g_ref[...] += mm(normed, d_proj, NT)
     d_normed = part_ref[...] + mm(w_ref[...], d_proj, NN)
     d_pair = norm_back_channels(d_normed, centred, inverse, gain).astype(BF16)
     out_ref[...] = to_cells(d_pair).astype(BF16).reshape(SUB, HALF, WIDTH)
@@ -374,22 +382,26 @@
 TWO = jax.ShapeDtypeStruct((2, HALF, SUB, WIDTH), BF16)
 TWO_SPEC = pl.BlockSpec((2, GROUP, SUB, WIDTH), lambda i: (0, i, 0, 0))
 LEFT_SPEC = pl.BlockSpec((GROUP, 2, HALF, WIDTH), lambda i: (i, 0, 0, 0))
+LONG = jax.ShapeDtypeStruct((HALF, PART, WIDTH), BF16)
+LONG_SPEC = pl.BlockSpec((GROUP, PART, WIDTH), lambda i: (i, 0, 0))
 WHOLE_PANEL = pl.BlockSpec(PANEL.shape, lambda i: (0, 0, 0))
 
 
 def right_part(s, pair, gain, w_proj, tokens, exponents):
-    return pl.pallas_call(
-        functools.partial(right_kernel, s),
-        grid=(1,),
-        out_shape=PANEL,
+    steps = PART // SUB
+    return pl.pallas_call(
+        functools.partial(right_kernel, s * steps),
+        grid=(steps,),
+        out_shape=LONG,
         in_specs=[
-            block((SUB, HALF, WIDTH), (s, 0, 0)), whole(gain), block((WIDTH, 2 * WIDTH), (0, 1)),
-            whole(tokens), block((SUB, HALF), (s, 0)),
+            pl.BlockSpec((SUB, HALF, WIDTH), lambda i: (s * steps + i, 0, 0)),
+            whole(gain), block((WIDTH, 2 * WIDTH), (0, 1)), whole(tokens),
+            pl.BlockSpec((SUB, HALF), lambda i: (s * steps + i, 0)),
         ],
-        out_specs=WHOLE_PANEL,
+        out_specs=pl.BlockSpec((HALF, SUB, WIDTH), lambda i: (0, i, 0)),
         scratch_shapes=[BUF],
         compiler_params=params(),
-        cost_estimate=cost(4 * LANES * WIDTH * WIDTH, 1 << 19, LANES * WIDTH),
+        cost_estimate=cost(8 * LANES * WIDTH * WIDTH, 1 << 20, 2 * LANES * WIDTH),
         name="right_part",
     )(pair, gain, w_proj, tokens, exponents)
 
@@ -411,12 +423,12 @@
     )(pair, gain, w_proj, tokens)
 
 
-def tri_part(slots, left):
+def tri_part(at, slots, left):
     return pl.pallas_call(
         tri_kernel,
         grid=(HALF // GROUP,),
         out_shape=(PANEL, PANEL, TWO, FOUR),
-        in_specs=[PANEL_SPEC] * 4 + [LEFT_SPEC],
+        in_specs=[pl.BlockSpec((GROUP, SUB, WIDTH), lambda i: (i, at, 0))] * 4 + [LEFT_SPEC],
         out_specs=(PANEL_SPEC, PANEL_SPEC, TWO_SPEC, FOUR_SPEC),
         compiler_params=params(),
         cost_estimate=cost(2 * HALF * HALF * WIDTH * WIDTH, 5 << 20),
@@ -447,12 +459,12 @@
     return pl.pallas_call(
         dright_kernel,
         grid=(HALF // GROUP,),
-        out_shape=(PANEL, TWO, PANEL),
-        in_specs=[PANEL_SPEC] * 4 + [LEFT_SPEC],
-        out_specs=(PANEL_SPEC, TWO_SPEC, PANEL_SPEC),
-        scratch_shapes=[pltpu.VMEM((4, GROUP, SUB, WIDTH), BF16)],
-        compiler_params=params(),
-        cost_estimate=cost(2 * HALF * HALF * WIDTH * WIDTH, 4 << 20),
+        out_shape=(LONG,) * 4,
+        in_specs=[PANEL_SPEC] * len(blocks) + [LEFT_SPEC],
+        out_specs=(LONG_SPEC,) * 4,
+        scratch_shapes=[pltpu.VMEM((4, GROUP, PART, WIDTH), BF16)],
+        compiler_params=params(),
+        cost_estimate=cost(4 * HALF * HALF * WIDTH * WIDTH, 6 << 20),
         name="dright_part",
     )(*blocks, left)
 
@@ -496,26 +508,29 @@
 
 
 def final_b_part(s, pair, part, sums, tokens, exponents, gain, w_proj, into):
-    return pl.pallas_call(
-        functools.partial(final_b_kernel, s),
-        grid=(1,),
+    steps = PART // SUB
+    rows = pl.BlockSpec((SUB, HALF, WIDTH), lambda i: (s * steps + i, 0, 0))
+    panel = pl.BlockSpec((HALF, SUB, WIDTH), lambda i: (0, i, 0))
+    return pl.pallas_call(
+        functools.partial(final_b_kernel, s * steps),
+        grid=(steps,),
         out_shape=(
             jax.ShapeDtypeStruct((HALF, HALF, WIDTH), BF16),
             jax.ShapeDtypeStruct((WIDTH, 2 * WIDTH), F32),
         ),
         in_specs=[
-            block((SUB, HALF, WIDTH), (s, 0, 0)),
-            block((WIDTH, LANES), (0, s)),
-            WHOLE_PANEL, block((1, HALF, SUB, WIDTH), (0, 0, 0, 0)), WHOLE_PANEL,
-            whole(tokens), block((SUB, HALF), (s, 0)), whole(gain),
-            block((WIDTH, 2 * WIDTH), (0, 1)),
+            rows,
+            pl.BlockSpec((WIDTH, LANES), lambda i: (0, s * steps + i)),
+            panel, panel, whole(tokens),
+            pl.BlockSpec((SUB, HALF), lambda i: (s * steps + i, 0)),
+            whole(gain), block((WIDTH, 2 * WIDTH), (0, 1)),
             pl.BlockSpec(memory_space=pl.ANY),
         ],
-        out_specs=(block((SUB, HALF, WIDTH), (s, 0, 0)), block((WIDTH, 2 * WIDTH), (0, 0))),
+        out_specs=(rows, block((WIDTH, 2 * WIDTH), (0, 0))),
         scratch_shapes=[BUF, WIDE],
-        input_output_aliases={9: 0} if into.shape == pair.shape else {},
-        compiler_params=params(),
-        cost_estimate=cost(14 * LANES * WIDTH * WIDTH, 2 << 20, LANES * WIDTH),
+        input_output_aliases={8: 0} if into.shape == pair.shape else {},
+        compiler_params=params(),
+        cost_estimate=cost(28 * LANES * WIDTH * WIDTH, 4 << 20, 2 * LANES * WIDTH),
         name="final_b_part",
     )(pair, part, *sums, tokens, exponents, gain, w_proj, into)
 
@@ -525,15 +540,17 @@
 
 
 def blocked(pair_tiles, grad_out, exponents, token_mask, gain_in, w_proj, w_gate, gain_out, w_out):
-    rows, cols, width = pair_tiles.shape
+    width = pair_tiles.shape[-1]
     crop_len = token_mask.shape[0]
-    parts = rows // SUB
     core = lax.axis_index("col") % 2
     x_at = lax.axis_index("col") // 2
     tokens = token_mask.reshape(1, crop_len)
     gain_in = gain_in.reshape(1, width)
     gain_out = gain_out.reshape(1, width)
 
+    def forward(a):
+        return lax.ppermute(a, "row", [(0, 1), (1, 3), (3, 2), (2, 0)])
+
     def over_row(a, bit):
         return lax.ppermute(a, "row", [(k, k ^ bit) for k in range(4)])
 
@@ -546,43 +563,61 @@
     def plus(a, b):
         return (a.astype(F32) + b.astype(F32)).astype(BF16)
 
-    slots = []
-    ready = ()
-    for s in range(parts):
-        own = after(right_part(s, pair_tiles, gain_in, w_proj, tokens, exponents), *ready)
-        far = over_row(own, 2)
-        slots.append((own, over_row(own, 1), far, over_row(far, 1)))
-        ready = (far,)
+    def gather(own):
+        held = [own]
+        for _ in range(3):
+            held.append(forward(held[-1]))
+        return held
+
+    own = [right_part(s, pair_tiles, gain_in, w_proj, tokens, exponents) for s in range(2)]
     left = left_part(pair_tiles, gain_in, w_proj, tokens)
-
-    grads, panels, gates, sums = [], [], [], []
-    g_out = g_gate = 0.0
-    for s in range(parts):
-        keep, near, send, panel = tri_part(slots[s], left)
-        got = over_core(send)
-        mine = over_x(plus(near, got[1]))
-        d_tri, d_gate, part_out, part_gate = mid_part(
-            s, (keep, got, mine), pair_tiles, grad_out, gain_in, gain_out, w_gate, w_out
+    slots = [gather(own[0])]
+    slots.append(gather(after(own[1], slots[0][3])))
+
+    def triangles(s):
+        out = []
+        for at in range(PART // SUB):
+            keep, near, send, panel = tri_part(at, slots[s], left)
+            got = over_core(send)
+            out.append((keep, got, over_x(plus(near, got[1])), panel))
+        return out
+
+    def middle(s, at, parts):
+        return mid_part(
+            s * (PART // SUB) + at, parts, pair_tiles, grad_out, gain_in, gain_out, w_gate, w_out
         )
-        g_out, g_gate = g_out + part_out, g_gate + part_gate
+
+    def spread(d_tri):
         far = over_x(d_tri)
-        blocks = [d_tri, far, over_core(d_tri), over_core(far)]
-        stay, pair, cross = dright_part(blocks, left)
-        got = over_row(pair, 1)
-        sums.append((stay, got, over_row(plus(cross, got[1]), 2)))
-        grads += blocks
-        panels.append(panel)
-        gates.append(d_gate)
-    d_left = dleft_part(grads, panels)
-    partial, g_a = final_a_part(pair_tiles, d_left, tokens, gain_in, w_proj, w_gate, gates)
-
-    d_pair = gain_in
-    g_b = []
-    for s in range(parts):
-        d_pair, part_b = final_b_part(
-            s, pair_tiles, partial, sums[s], tokens, exponents, gain_in, w_proj, d_pair
-        )
-        g_b.append(part_b)
+        return [d_tri, far, over_core(d_tri), over_core(far)]
+
+    tri = triangles(0)
+    mids = []
+    for at, (keep, got, mine, _) in enumerate(tri):
+        mids.append(middle(0, at, (keep, got, after(mine, slots[1][1]))))
+    panels = [t[3] for t in tri]
+    blocks = [b for m in mids for b in spread(m[0])]
+    first = dright_part([after(blocks[0], slots[1][2])] + blocks[1:], left)
+
+    total = plus(forward(first[1]), first[2])
+    tri = triangles(1)
+    for at, (keep, got, mine, _) in enumerate(tri):
+        mids.append(middle(1, at, (keep, got, after(mine, total) if at else mine)))
+    panels += [t[3] for t in tri]
+    total = plus(forward(total), first[3])
+    more = [b for m in mids[2:] for b in spread(m[0])]
+    second = dright_part([after(more[0], total)] + more[1:], left)
+    sums_a = (first[0], forward(total))
+
+    total = plus(forward(second[1]), second[2])
+    total = plus(forward(total), second[3])
+    d_left = dleft_part([after(blocks[0], second[0])] + blocks[1:] + more, panels)
+    partial, g_a = final_a_part(pair_tiles, d_left, tokens, gain_in, w_proj, w_gate, [m[1] for m in mids])
+    d_pair, g_first = final_b_part(
+        0, pair_tiles, partial, sums_a, tokens, exponents, gain_in, w_proj, gain_in
+    )
+    g_out = sum(m[2] for m in mids)
+    g_gate = sum(m[3] for m in mids)
 
     def exchange(a, send, at):
         half = a.shape[0] // 2
@@ -599,10 +634,14 @@
             a = a + over_row(a, bit)
         return a
 
-    early = jnp.concatenate([g_out, g_gate, g_a, g_b[0] + g_b[1] + g_b[2]], axis=1)
+    early = jnp.concatenate([g_out, g_gate, g_a, g_first], axis=1)
     early = over_rows(exchange(exchange(early, over_core, core), over_x, x_at))
     early = join(join(early, over_x, x_at), over_core, core)
-    late = exchange(g_b[3], over_core, core)
+    sums_b = (second[0], after(forward(total), early))
+    d_pair, late = final_b_part(
+        1, pair_tiles, partial, sums_b, tokens, exponents, gain_in, w_proj, d_pair
+    )
+    late = exchange(late, over_core, core)
     late = join(over_rows(late + over_x(late)), over_core, core)
     g_proj = jnp.concatenate([early[:, 2 * width : 4 * width], early[:, 4 * width :] + late], axis=1)
     return d_pair, g_proj / crop_len, early[:, width : 2 * width] / crop_len, early[:, :width] / crop_len

time: 254 us -> 231 us (0.909)
  Pallas kernels: 99.7 us -> 52.8 us
  waiting for transfers between devices: 89.2 us -> 114 us
  starting transfers between devices: 43.7 us -> 36.4 us
  other arithmetic: 5.11 us -> 9.52 us
    ppermute x0 -> x12, waiting for transfers between devices: none -> 67.1 us  [forward(): return lax.ppermute(a, 'row', [(0, 1), (1, 3), (3, 2), (2, 0)])]
    ppermute x24 -> x4, waiting for transfers between devices: 76.3 us -> 24.2 us  [over_row(): return lax.ppermute(a, 'row', [(k, k ^ bit) for k in range(4)])]
    pallas_call x12 -> x6, Pallas kernels: 42.1 us -> 18.4 us  [the longest x2 9.58 us: final_b_part(): pl.pallas_call(functools.partial(final_b_kernel, s * steps), grid=(steps,...]
    ppermute x24 -> x4, starting transfers between devices: 24.2 us -> 3.47 us  [over_row(): return lax.ppermute(a, 'row', [(k, k ^ bit) for k in range(4)])]
    ppermute x0 -> x12, starting transfers between devices: none -> 14.9 us  [forward(): return lax.ppermute(a, 'row', [(0, 1), (1, 3), (3, 2), (2, 0)])]
    ppermute x11, waiting for transfers between devices: 9.49 us -> 21.4 us  [over_x(): return lax.ppermute(a, 'col', [(k, k ^ 2) for k in range(4)])]
    pallas_call x4, Pallas kernels: 19.6 us -> 8.64 us  [tri_part(): pl.pallas_call(tri_kernel, grid=(HALF // GROUP,), out_shape=(PANEL, PANEL...]
    pallas_call x4, Pallas kernels: 18.4 us -> 11.8 us  [mid_part(): pl.pallas_call(mid_kernel, grid=(1,), out_shape=(PANEL, PANEL, square, sq...]
  transfers between devices with their start and end apart: 51 -> 43, of which waited for: 23 -> 20; matrix products, arithmetic and copies ran while one was open for 2% -> 4% of each run, Pallas kernels for 38% -> 20%
where the time goes in v4:
time: 231 us; the launch traced here: 230 us
  waiting for transfers between devices  114 us (49%)
  Pallas kernels  52.8 us (23%)
  starting transfers between devices  36.4 us (16%)
  local copies, waits for them, and re-layouts  15.4 us (7%)
  other arithmetic  9.52 us (4%)
    ppermute x12, waiting for transfers between devices, forward(): return lax.ppermute(a, 'row', [(0, 1), (1, 3), (3, 2), (2, 0)])  67.1 us
    ppermute x4, waiting for transfers between devices, over_row(): return lax.ppermute(a, 'row', [(k, k ^ bit) for k in range(4)])  24.2 us
    ppermute x11, waiting for transfers between devices, over_x(): return lax.ppermute(a, 'col', [(k, k ^ 2) for k in range(4)])  21.4 us
    ppermute x11, starting transfers between devices, over_x(): return lax.ppermute(a, 'col', [(k, k ^ 2) for k in range(4)])  15.1 us
    ppermute x12, starting transfers between devices, forward(): return lax.ppermute(a, 'row', [(0, 1), (1, 3), (3, 2), (2, 0)])  14.9 us
    unnamed x116, local copies, waits for them, and re-layouts  14.7 us
    pallas_call x4, Pallas kernels, mid_part(): pl.pallas_call(mid_kernel, grid=(1,), out_shape=(PANEL, PANEL, square, sq...  11.8 us
    pallas_call x2, Pallas kernels, final_b_part(): pl.pallas_call(functools.partial(final_b_kernel, s * steps), grid=(steps,...  9.58 us
  transfers between devices with their start and end apart: 43, of which 20 were waited for; matrix products, arithmetic and copies ran while one was open for 4% of the time, Pallas kernels for 20%

profile of v4, /device:TPU:0, one launch (start us, length us, event | category | flops | bytes accessed | tf_op | source)
XLA Modules:
  0.0 229.8 jit_solution(17934657490181083922)
XLA Ops:
  6.9 3.1 %collective-permute-start = (bf16[64,32,128]{2,1,0:T(8,128)(2,1)S(1)}, bf16[64,32,128]{2,1,0:T(8,128)(2,1)S(1)}, u32[]{:S(2)}, u32[]{:S(2)}) collective-permute-start(bf16[64,32,128]{2,1,0:T(8,128)(2,1)S(1)} %right_part.2.s0), channel_id=1, source_target_pairs={{0,4},{4,12},{12,8},{8,0},{1,5},{5,13},{13,9},{9,1},{2,6},{6,14},{... | collective-permute-start | bytes 1572872 | tf_op jit(solution)/shard_map/ppermute | solution.py:552
  9.9 12.9 %collective-permute-done.s1 = bf16[64,32,128]{2,1,0:T(8,128)(2,1)S(1)} collective-permute-done((bf16[64,32,128]{2,1,0:T(8,128)(2,1)S(1)}, bf16[64,32,128]{2,1,0:T(8,128)(2,1)S(1)}, u32[]{:S(2)}, u32[]{:S(2)}) %collective-permute-start) | collective-permute-done | bytes 524320 | tf_op jit(solution)/shard_map/ppermute | solution.py:552
  23.7 13.2 %collective-permute-done.1.s2 = bf16[64,32,128]{2,1,0:T(8,128)(2,1)S(1)} collective-permute-done((bf16[64,32,128]{2,1,0:T(8,128)(2,1)S(1)}, bf16[64,32,128]{2,1,0:T(8,128)(2,1)S(1)}, u32[]{:S(2)}, u32[]{:S(2)}) %collective-permute-start.1) | collective-permute-done | bytes 524320 | tf_op jit(solution)/shard_map/ppermute | solution.py:552
  39.4 10.6 %collective-permute-done.2.s3 = bf16[64,32,128]{2,1,0:T(8,128)(2,1)S(1)} collective-permute-done((bf16[64,32,128]{2,1,0:T(8,128)(2,1)S(1)}, bf16[64,32,128]{2,1,0:T(8,128)(2,1)S(1)}, u32[]{:S(2)}, u32[]{:S(2)}) %collective-permute-start.2) | collective-permute-done | bytes 524320 | tf_op jit(solution)/shard_map/ppermute | solution.py:552
  50.2 4.2 %left_part.1.left_ref.refs_8_ = bf16[64,2,64,128]{3,2,1,0:T(8,128)(2,1)S(1)} custom-call(bf16[64,64,128]{2,1,0:T(8,128)(2,1)S(1)} %copy-done, f32[1,128]{1,0:T(1,128)S(1)} %bitcast.25, bf16[128,512]{1,0:T(8,128)(2,1)S(1)} %copy-done.3, s32[1,256]{1,0:T(1,128)S(1)} %bitcast.36), custom_call_target="tpu_custom_call" | custom-call | flops 268435456 | bytes 3145728 | tf_op jit(solution)/shard_map/left_part/pallas_call | solution.py:410
  54.4 2.2 tri_part.6
  56.7 2.2 tri_part.4
  58.9 3.2 %collective-permute-done.5.s1 = bf16[64,32,128]{2,1,0:T(8,128)(2,1)S(1)} collective-permute-done((bf16[64,32,128]{2,1,0:T(8,128)(2,1)S(1)}, bf16[64,32,128]{2,1,0:T(8,128)(2,1)S(1)}, u32[]{:S(2)}, u32[]{:S(2)}) %collective-permute-start.5) | collective-permute-done | bytes 524320 | tf_op jit(solution)/shard_map/ppermute | solution.py:552
  64.2 10.1 %collective-permute-done.6.s2 = bf16[64,32,128]{2,1,0:T(8,128)(2,1)S(1)} collective-permute-done((bf16[64,32,128]{2,1,0:T(8,128)(2,1)S(1)}, bf16[64,32,128]{2,1,0:T(8,128)(2,1)S(1)}, u32[]{:S(2)}, u32[]{:S(2)}) %collective-permute-start.6) | collective-permute-done | bytes 524320 | tf_op jit(solution)/shard_map/ppermute | solution.py:552
  74.3 2.4 %collective-permute-start.7 = (bf16[64,32,128]{2,1,0:T(8,128)(2,1)S(1)}, bf16[64,32,128]{2,1,0:T(8,128)(2,1)S(1)}, u32[]{:S(2)}, u32[]{:S(2)}) collective-permute-start(bf16[64,32,128]{2,1,0:T(8,128)(2,1)S(1)} %collective-permute-done.6.s2), channel_id=1, source_target_pairs={{0,4},{4,12},{12,8},{8,0},{1,5},{5,13},{13,9},{9,1},{2,6},{6,14},{... | collective-permute-start | bytes 1572872 | tf_op jit(solution)/shard_map/ppermute | solution.py:552
  78.4 2.7 %mid_part.6 = (bf16[64,16,128]{2,1,0:T(8,128)(2,1)S(1)}, bf16[64,16,128]{2,1,0:T(8,128)(2,1)S(1)}, f32[128,128]{1,0:T(8,128)S(1)}, f32[128,128]{1,0:T(8,128)S(1)}) custom-call(bf16[64,16,128]{2,1,0:T(8,128)(2,1)S(1)} %get-tuple-element.69.a_ref, bf16[2,64,16,128]{3,2,1,0:T(8,128)(2,1)S(1)} %collective-permute-done.13.b_ref, ...), custom_call_target="tpu_custom_call" | custom-call | flops 201326592 | bytes 2097152 | tf_op jit(solution)/shard_map/mid_part/pallas_call | solution.py:443
  81.7 4.3 %collective-permute-done.4.c_ref = bf16[64,16,128]{2,1,0:T(8,128)(2,1)S(1)} collective-permute-done((bf16[64,16,128]{2,1,0:T(8,128)(2,1)S(1)}, bf16[64,16,128]{2,1,0:T(8,128)(2,1)S(1)}, u32[]{:S(2)}, u32[]{:S(2)}) %collective-permute-start.4) | collective-permute-done | bytes 262176 | tf_op jit(solution)/shard_map/ppermute | solution.py:558
  85.9 2.7 %mid_part.4 = (bf16[64,16,128]{2,1,0:T(8,128)(2,1)S(1)}, bf16[64,16,128]{2,1,0:T(8,128)(2,1)S(1)}, f32[128,128]{1,0:T(8,128)S(1)}, f32[128,128]{1,0:T(8,128)S(1)}) custom-call(bf16[64,16,128]{2,1,0:T(8,128)(2,1)S(1)} %get-tuple-element.58.a_ref, bf16[2,64,16,128]{3,2,1,0:T(8,128)(2,1)S(1)} %collective-permute-done.3.b_ref, ...), custom_call_target="tpu_custom_call" | custom-call | flops 201326592 | bytes 2097152 | tf_op jit(solution)/shard_map/mid_part/pallas_call | solution.py:443
  95.7 2.1 tri_part.5
  104.1 11.6 %collective-permute-done.18 = bf16[64,32,128]{2,1,0:T(8,128)(2,1)S(1)} collective-permute-done((bf16[64,32,128]{2,1,0:T(8,128)(2,1)S(1)}, bf16[64,32,128]{2,1,0:T(8,128)(2,1)S(1)}, u32[]{:S(2)}, u32[]{:S(2)}) %collective-permute-start.18) | collective-permute-done | bytes 524320 | tf_op jit(solution)/shard_map/ppermute | solution.py:552
  116.0 3.2 %mid_part.7 = (bf16[64,16,128]{2,1,0:T(8,128)(2,1)}, bf16[64,16,128]{2,1,0:T(8,128)(2,1)S(1)}, f32[128,128]{1,0:T(8,128)S(1)}, f32[128,128]{1,0:T(8,128)S(1)}) custom-call(bf16[64,16,128]{2,1,0:T(8,128)(2,1)S(1)} %get-tuple-element.78.a_ref, bf16[2,64,16,128]{3,2,1,0:T(8,128)(2,1)S(1)} %collective-permute-done.23.b_ref, ...), custom_call_target="tpu_custom_call" | custom-call | flops 201326592 | bytes 2097152 | tf_op jit(solution)/shard_map/mid_part/pallas_call | solution.py:443
  123.1 3.2 %mid_part.5 = (bf16[64,16,128]{2,1,0:T(8,128)(2,1)}, bf16[64,16,128]{2,1,0:T(8,128)(2,1)S(1)}, f32[128,128]{1,0:T(8,128)S(1)}, f32[128,128]{1,0:T(8,128)S(1)}) custom-call(bf16[64,16,128]{2,1,0:T(8,128)(2,1)S(1)} %get-tuple-element.64.a_ref, bf16[2,64,16,128]{3,2,1,0:T(8,128)(2,1)S(1)} %collective-permute-done.8.b_ref, ...), custom_call_target="tpu_custom_call" | custom-call | flops 201326592 | bytes 2097152 | tf_op jit(solution)/shard_map/mid_part/pallas_call | solution.py:443
  127.0 3.2 %collective-permute-done.25.refs_5_.refs_13_ = bf16[64,16,128]{2,1,0:T(8,128)(2,1)} collective-permute-done((bf16[64,16,128]{2,1,0:T(8,128)(2,1)}, bf16[64,16,128]{2,1,0:T(8,128)(2,1)}, u32[]{:S(2)}, u32[]{:S(2)}) %collective-permute-start.25) | collective-permute-done | bytes 262176 | tf_op jit(solution)/shard_map/ppermute | solution.py:558
  130.2 4.4 %collective-permute-done.20.refs_1_.refs_9_ = bf16[64,16,128]{2,1,0:T(8,128)(2,1)} collective-permute-done((bf16[64,16,128]{2,1,0:T(8,128)(2,1)}, bf16[64,16,128]{2,1,0:T(8,128)(2,1)}, u32[]{:S(2)}, u32[]{:S(2)}) %collective-permute-start.20) | collective-permute-done | bytes 262176 | tf_op jit(solution)/shard_map/ppermute | solution.py:558
  136.9 3.5 %dright_part.3 = (bf16[64,32,128]{2,1,0:T(8,128)(2,1)S(1)}, bf16[64,32,128]{2,1,0:T(8,128)(2,1)S(1)}, bf16[64,32,128]{2,1,0:T(8,128)(2,1)S(1)}, bf16[64,32,128]{2,1,0:T(8,128)(2,1)S(1)}) custom-call(bf16[64,16,128]{2,1,0:T(8,128)(2,1)} %get-tuple-element.77.refs_0_.refs_8_, bf16[64,16,128]{2,1,0:T(8,128)(2,1)} %collective-permute-done.20.refs_1_.refs_9_, ...), custom_call_target="tpu_custom_call" | custom-call | flops 268435456 | bytes 6291456 | tf_op jit(solution)/shard_map/dright_part/pallas_call | solution.py:459
  147.2 3.8 %dleft_part.1.dleft_ref = f32[64,64,128]{2,1,0:T(8,128)S(1)} custom-call(bf16[64,16,128]{2,1,0:T(8,128)(2,1)S(1)} %copy-done.16, bf16[64,16,128]{2,1,0:T(8,128)(2,1)S(1)} %copy-done.18, bf16[64,16,128]{2,1,0:T(8,128)(2,1)S(1)} %copy-done.22, bf16[64,16,128]{2,1,0:T(8,128)(2,1)S(1)} %copy-done.26, bf16[64,16,128]{2,1,0:T(8,128)(2,1)S(1)} %get-tuple-element.73.refs_4_, ...), custom_call_target="tpu_custom_call" | custom-call | flops 536870912 | bytes 10485760 | tf_op jit(solution)/shard_map/dleft_part/pallas_call | solution.py:473
  151.2 5.9 %final_a_part.1 = (f32[128,4096]{1,0:T(8,128)S(1)}, f32[128,256]{1,0:T(8,128)S(1)}) custom-call(bf16[64,64,128]{2,1,0:T(8,128)(2,1)S(1)} %copy-done.1, f32[64,64,128]{2,1,0:T(8,128)S(1)} %dleft_part.1.dleft_ref, s32[1,256]{1,0:T(1,128)S(1)} %bitcast.37, f32[1,128]{1,0:T(1,128)S(1)} %bitcast.30, bf16[128,512]{1,0:T(8,128)(2,1)S(1)} %copy-done.4, ...), custom_call_target="tpu_custom_call" | custom-call | flops 939524096 | bytes 8388608 | tf_op jit(solution)/shard_map/final_a_part/pallas_call | solution.py:486
  157.1 4.8 %final_b_part.2 = (bf16[64,64,128]{2,1,0:T(8,128)(2,1)}, f32[128,256]{1,0:T(8,128)S(1)}) custom-call(bf16[64,64,128]{2,1,0:T(8,128)(2,1)S(1)} %copy-done.1, f32[128,4096]{1,0:T(8,128)S(1)} %get-tuple-element.93.part_ref, bf16[64,32,128]{2,1,0:T(8,128)(2,1)S(1)} %copy-done.36, bf16[64,32,128]{2,1,0:T(8,128)(2,1)} %collective-permute-done.31.b_ref, ...), custom_call_target="tpu_custom_call" | custom-call | flops 469762048 | bytes 4194304 | tf_op jit(solution)/shard_map/final_b_part/pallas_call | solution.py:514
  163.1 2.4 %collective-permute-start.29 = (bf16[64,32,128]{2,1,0:T(8,128)(2,1)}, bf16[64,32,128]{2,1,0:T(8,128)(2,1)}, u32[]{:S(2)}, u32[]{:S(2)}) collective-permute-start(bf16[64,32,128]{2,1,0:T(8,128)(2,1)} %add_convert_fusion.1), channel_id=1, source_target_pairs={{0,4},{4,12},{12,8},{8,0},{1,5},{5,13},{13,9},{9,1},{2,6},{6,14},{... | collective-permute-start | bytes 1572872 | tf_op jit(solution)/shard_map/ppermute | solution.py:552
  167.9 3.6 %collective-permute-done.33 = f32[32,768]{1,0:T(8,128)} collective-permute-done((f32[32,768]{1,0:T(8,128)}, f32[32,768]{1,0:T(8,128)}, u32[]{:S(2)}, u32[]{:S(2)}) %collective-permute-start.33) | collective-permute-done | bytes 98336 | tf_op jit(solution)/shard_map/ppermute | solution.py:558
  173.2 5.4 %collective-permute-done.29 = bf16[64,32,128]{2,1,0:T(8,128)(2,1)} collective-permute-done((bf16[64,32,128]{2,1,0:T(8,128)(2,1)}, bf16[64,32,128]{2,1,0:T(8,128)(2,1)}, u32[]{:S(2)}, u32[]{:S(2)}) %collective-permute-start.29) | collective-permute-done | bytes 524320 | tf_op jit(solution)/shard_map/ppermute | solution.py:552
  183.8 15.6 %collective-permute-done.35 = f32[32,768]{1,0:T(8,128)S(1)} collective-permute-done((f32[32,768]{1,0:T(8,128)S(1)}, f32[32,768]{1,0:T(8,128)S(1)}, u32[]{:S(2)}, u32[]{:S(2)}) %collective-permute-start.35) | collective-permute-done | bytes 98336 | tf_op jit(solution)/shard_map/ppermute | solution.py:555
  202.0 3.0 %collective-permute-done.36 = f32[32,768]{1,0:T(8,128)} collective-permute-done((f32[32,768]{1,0:T(8,128)}, f32[32,768]{1,0:T(8,128)}, u32[]{:S(2)}, u32[]{:S(2)}) %collective-permute-start.36) | collective-permute-done | bytes 98336 | tf_op jit(solution)/shard_map/ppermute | solution.py:558
  207.0 4.8 %final_b_part.3 = (bf16[64,64,128]{2,1,0:T(8,128)(2,1)}, f32[128,256]{1,0:T(8,128)S(1)}) custom-call(bf16[64,64,128]{2,1,0:T(8,128)(2,1)S(1)} %copy-done.1, f32[128,4096]{1,0:T(8,128)S(1)} %get-tuple-element.93.part_ref, bf16[64,32,128]{2,1,0:T(8,128)(2,1)S(1)} %copy-done.33, ...), custom_call_target="tpu_custom_call", output_to_operand_aliasing={{0}: (8, {})} | custom-call | flops 469762048 | bytes 4194304 | tf_op jit(solution)/shard_map/final_b_part/pallas_call | solution.py:514
  215.0 2.4 %collective-permute-done.39 = f32[64,256]{1,0:T(8,128)S(1)} collective-permute-done((f32[64,256]{1,0:T(8,128)S(1)}, f32[64,256]{1,0:T(8,128)S(1)}, u32[]{:S(2)}, u32[]{:S(2)}) %collective-permute-start.39) | collective-permute-done | bytes 65568 | tf_op jit(solution)/shard_map/ppermute | solution.py:558
  217.6 4.2 %collective-permute-done.40 = f32[64,256]{1,0:T(8,128)S(1)} collective-permute-done((f32[64,256]{1,0:T(8,128)S(1)}, f32[64,256]{1,0:T(8,128)S(1)}, u32[]{:S(2)}, u32[]{:S(2)}) %collective-permute-start.40) | collective-permute-done | bytes 65568 | tf_op jit(solution)/shard_map/ppermute | solution.py:555
  223.3 4.4 %collective-permute-done.41 = f32[64,256]{1,0:T(8,128)S(1)} collective-permute-done((f32[64,256]{1,0:T(8,128)S(1)}, f32[64,256]{1,0:T(8,128)S(1)}, u32[]{:S(2)}, u32[]{:S(2)}) %collective-permute-start.41) | collective-permute-done | bytes 65568 | tf_op jit(solution)/shard_map/ppermute | solution.py:555
  (215 shorter events, 62.9 us)
Async XLA Ops:
  6.9 16.0 %collective-permute-start = (bf16[64,32,128]{2,1,0:T(8,128)(2,1)S(1)}, bf16[64,32,128]{2,1,0:T(8,128)(2,1)S(1)}, u32[]{:S(2)}, u32[]{:S(2)}) collective-permute-start(bf16[64,32,128]{2,1,0:T(8,128)(2,1)S(1)} %right_part.2.s0), channel_id=1, source_target_pairs={{0,4},{4,12},{12,8},{8,0},{1,5},{5,13},{13,9},{9,1},{2,6},{6,14},{... | collective-permute-start | bytes 1572872 | tf_op jit(solution)/shard_map/ppermute | solution.py:552
  22.9 14.0 %collective-permute-start.1 = (bf16[64,32,128]{2,1,0:T(8,128)(2,1)S(1)}, bf16[64,32,128]{2,1,0:T(8,128)(2,1)S(1)}, u32[]{:S(2)}, u32[]{:S(2)}) collective-permute-start(bf16[64,32,128]{2,1,0:T(8,128)(2,1)S(1)} %collective-permute-done.s1), channel_id=1, source_target_pairs={{0,4},{4,12},{12,8},{8,0},{1,5},{5,13},{13,9},{9,1},{2,6},{6,14},{... | collective-permute-start | bytes 1572872 | tf_op jit(solution)/shard_map/ppermute | solution.py:552
  36.9 13.1 %collective-permute-start.2 = (bf16[64,32,128]{2,1,0:T(8,128)(2,1)S(1)}, bf16[64,32,128]{2,1,0:T(8,128)(2,1)S(1)}, u32[]{:S(2)}, u32[]{:S(2)}) collective-permute-start(bf16[64,32,128]{2,1,0:T(8,128)(2,1)S(1)} %collective-permute-done.1.s2), channel_id=1, source_target_pairs={{0,4},{4,12},{12,8},{8,0},{1,5},{5,13},{13,9},{9,1},{2,6},{6,14},{... | collective-permute-start | bytes 1572872 | tf_op jit(solution)/shard_map/ppermute | solution.py:552
  50.0 12.2 %collective-permute-start.5 = (bf16[64,32,128]{2,1,0:T(8,128)(2,1)S(1)}, bf16[64,32,128]{2,1,0:T(8,128)(2,1)S(1)}, u32[]{:S(2)}, u32[]{:S(2)}) collective-permute-start(bf16[64,32,128]{2,1,0:T(8,128)(2,1)S(1)} %right_part.3.s0), channel_id=1, source_target_pairs={{0,4},{4,12},{12,8},{8,0},{1,5},{5,13},{13,9},{9,1},{2,6},{6,14},{... | collective-permute-start | bytes 1572872 | tf_op jit(solution)/shard_map/ppermute | solution.py:552
  56.6 5.9 %collective-permute-start.13 = (bf16[2,64,16,128]{3,2,1,0:T(8,128)(2,1)S(1)}, bf16[2,64,16,128]{3,2,1,0:T(8,128)(2,1)S(1)}, u32[]{:S(2)}, u32[]{:S(2)}) collective-permute-start(bf16[2,64,16,128]{3,2,1,0:T(8,128)(2,1)S(1)} %get-tuple-element.70), channel_id=1, source_target_pairs={{0,1},{1,0},{2,3},{3,2},{4,5},{5,4},{6,7},{7,6},{8,9},{9,8},{10,11... | collective-permute-start | bytes 1572872 | tf_op jit(solution)/shard_map/ppermute | solution.py:561
  62.1 12.2 %collective-permute-start.6 = (bf16[64,32,128]{2,1,0:T(8,128)(2,1)S(1)}, bf16[64,32,128]{2,1,0:T(8,128)(2,1)S(1)}, u32[]{:S(2)}, u32[]{:S(2)}) collective-permute-start(bf16[64,32,128]{2,1,0:T(8,128)(2,1)S(1)} %collective-permute-done.5.s1), channel_id=1, source_target_pairs={{0,4},{4,12},{12,8},{8,0},{1,5},{5,13},{13,9},{9,1},{2,6},{6,14},{... | collective-permute-start | bytes 1572872 | tf_op jit(solution)/shard_map/ppermute | solution.py:552
  62.4 14.3 %collective-permute-start.3 = (bf16[2,64,16,128]{3,2,1,0:T(8,128)(2,1)S(1)}, bf16[2,64,16,128]{3,2,1,0:T(8,128)(2,1)S(1)}, u32[]{:S(2)}, u32[]{:S(2)}) collective-permute-start(bf16[2,64,16,128]{3,2,1,0:T(8,128)(2,1)S(1)} %get-tuple-element.59), channel_id=1, source_target_pairs={{0,1},{1,0},{2,3},{3,2},{4,5},{5,4},{6,7},{7,6},{8,9},{9,8},{10,11... | collective-permute-start | bytes 1572872 | tf_op jit(solution)/shard_map/ppermute | solution.py:561
  62.6 15.7 %collective-permute-start.14 = (bf16[64,16,128]{2,1,0:T(8,128)(2,1)S(1)}, bf16[64,16,128]{2,1,0:T(8,128)(2,1)S(1)}, u32[]{:S(2)}, u32[]{:S(2)}) collective-permute-start(bf16[64,16,128]{2,1,0:T(8,128)(2,1)S(1)} %fusion.1), channel_id=1, source_target_pairs={{0,2},{1,3},{2,0},{3,1},{4,6},{5,7},{6,4},{7,5},{8,10},{9,11},{10,... | collective-permute-start | bytes 786440 | tf_op jit(solution)/shard_map/ppermute | solution.py:558
  74.3 16.6 %collective-permute-start.7 = (bf16[64,32,128]{2,1,0:T(8,128)(2,1)S(1)}, bf16[64,32,128]{2,1,0:T(8,128)(2,1)S(1)}, u32[]{:S(2)}, u32[]{:S(2)}) collective-permute-start(bf16[64,32,128]{2,1,0:T(8,128)(2,1)S(1)} %collective-permute-done.6.s2), channel_id=1, source_target_pairs={{0,4},{4,12},{12,8},{8,0},{1,5},{5,13},{13,9},{9,1},{2,6},{6,14},{... | collective-permute-start | bytes 1572872 | tf_op jit(solution)/shard_map/ppermute | solution.py:552
  76.7 9.2 %collective-permute-start.4 = (bf16[64,16,128]{2,1,0:T(8,128)(2,1)S(1)}, bf16[64,16,128]{2,1,0:T(8,128)(2,1)S(1)}, u32[]{:S(2)}, u32[]{:S(2)}) collective-permute-start(bf16[64,16,128]{2,1,0:T(8,128)(2,1)S(1)} %fusion.3), channel_id=1, source_target_pairs={{0,2},{1,3},{2,0},{3,1},{4,6},{5,7},{6,4},{7,5},{8,10},{9,11},{10,... | collective-permute-start | bytes 786440 | tf_op jit(solution)/shard_map/ppermute | solution.py:558
  81.1 13.5 %collective-permute-start.15 = (bf16[64,16,128]{2,1,0:T(8,128)(2,1)S(1)}, bf16[64,16,128]{2,1,0:T(8,128)(2,1)S(1)}, u32[]{:S(2)}, u32[]{:S(2)}) collective-permute-start(bf16[64,16,128]{2,1,0:T(8,128)(2,1)S(1)} %get-tuple-element.73.refs_4_), channel_id=1, source_target_pairs={{0,2},{1,3},{2,0},{3,1},{4,6},{5,7},{6,4},{7,5},{8,10},{9,11},{10,... | collective-permute-start | bytes 786440 | tf_op jit(solution)/shard_map/ppermute | solution.py:558
  89.2 6.4 %collective-permute-start.10 = (bf16[64,16,128]{2,1,0:T(8,128)(2,1)S(1)}, bf16[64,16,128]{2,1,0:T(8,128)(2,1)S(1)}, u32[]{:S(2)}, u32[]{:S(2)}) collective-permute-start(bf16[64,16,128]{2,1,0:T(8,128)(2,1)S(1)} %get-tuple-element.84.refs_0_), channel_id=1, source_target_pairs={{0,2},{1,3},{2,0},{3,1},{4,6},{5,7},{6,4},{7,5},{8,10},{9,11},{10,... | collective-permute-start | bytes 786440 | tf_op jit(solution)/shard_map/ppermute | solution.py:558
  90.9 7.9 %collective-permute-start.16 = (bf16[64,16,128]{2,1,0:T(8,128)(2,1)S(1)}, bf16[64,16,128]{2,1,0:T(8,128)(2,1)S(1)}, u32[]{:S(2)}, u32[]{:S(2)}) collective-permute-start(bf16[64,16,128]{2,1,0:T(8,128)(2,1)S(1)} %get-tuple-element.73.refs_4_), channel_id=1, source_target_pairs={{0,1},{1,0},{2,3},{3,2},{4,5},{5,4},{6,7},{7,6},{8,9},{9,8},{10,11... | collective-permute-start | bytes 786440 | tf_op jit(solution)/shard_map/ppermute | solution.py:561
  94.1 7.7 %collective-permute-start.23 = (bf16[2,64,16,128]{3,2,1,0:T(8,128)(2,1)S(1)}, bf16[2,64,16,128]{3,2,1,0:T(8,128)(2,1)S(1)}, u32[]{:S(2)}, u32[]{:S(2)}) collective-permute-start(bf16[2,64,16,128]{3,2,1,0:T(8,128)(2,1)S(1)} %get-tuple-element.79), channel_id=1, source_target_pairs={{0,1},{1,0},{2,3},{3,2},{4,5},{5,4},{6,7},{7,6},{8,9},{9,8},{10,11... | collective-permute-start | bytes 1572872 | tf_op jit(solution)/shard_map/ppermute | solution.py:561
  100.8 15.0 %collective-permute-start.18 = (bf16[64,32,128]{2,1,0:T(8,128)(2,1)S(1)}, bf16[64,32,128]{2,1,0:T(8,128)(2,1)S(1)}, u32[]{:S(2)}, u32[]{:S(2)}) collective-permute-start(bf16[64,32,128]{2,1,0:T(8,128)(2,1)S(1)} %get-tuple-element.74), channel_id=1, source_target_pairs={{0,4},{4,12},{12,8},{8,0},{1,5},{5,13},{13,9},{9,1},{2,6},{6,14},{... | collective-permute-start | bytes 1572872 | tf_op jit(solution)/shard_map/ppermute | solution.py:552
  101.9 14.1 %collective-permute-start.24 = (bf16[64,16,128]{2,1,0:T(8,128)(2,1)S(1)}, bf16[64,16,128]{2,1,0:T(8,128)(2,1)S(1)}, u32[]{:S(2)}, u32[]{:S(2)}) collective-permute-start(bf16[64,16,128]{2,1,0:T(8,128)(2,1)S(1)} %fusion), channel_id=1, source_target_pairs={{0,2},{1,3},{2,0},{3,1},{4,6},{5,7},{6,4},{7,5},{8,10},{9,11},{10,... | collective-permute-start | bytes 786440 | tf_op jit(solution)/shard_map/ppermute | solution.py:558
  104.1 19.0 %collective-permute-start.9 = (bf16[64,16,128]{2,1,0:T(8,128)(2,1)S(1)}, bf16[64,16,128]{2,1,0:T(8,128)(2,1)S(1)}, u32[]{:S(2)}, u32[]{:S(2)}) collective-permute-start(bf16[64,16,128]{2,1,0:T(8,128)(2,1)S(1)} %fusion.2), channel_id=1, source_target_pairs={{0,2},{1,3},{2,0},{3,1},{4,6},{5,7},{6,4},{7,5},{8,10},{9,11},{10,... | collective-permute-start | bytes 786440 | tf_op jit(solution)/shard_map/ppermute | solution.py:558
  115.9 18.6 %collective-permute-start.19 = (bf16[64,32,128]{2,1,0:T(8,128)(2,1)S(1)}, bf16[64,32,128]{2,1,0:T(8,128)(2,1)S(1)}, u32[]{:S(2)}, u32[]{:S(2)}) collective-permute-start(bf16[64,32,128]{2,1,0:T(8,128)(2,1)S(1)} %add_convert_fusion.3), channel_id=1, source_target_pairs={{0,4},{4,12},{12,8},{8,0},{1,5},{5,13},{13,9},{9,1},{2,6},{6,14},{... | collective-permute-start | bytes 1572872 | tf_op jit(solution)/shard_map/ppermute | solution.py:552
  121.2 8.9 %collective-permute-start.25 = (bf16[64,16,128]{2,1,0:T(8,128)(2,1)}, bf16[64,16,128]{2,1,0:T(8,128)(2,1)}, u32[]{:S(2)}, u32[]{:S(2)}) collective-permute-start(bf16[64,16,128]{2,1,0:T(8,128)(2,1)} %get-tuple-element.82.refs_4_.refs_12_), channel_id=1, source_target_pairs={{0,2},{1,3},{2,0},{3,1},{4,6},{5,7},{6,4},{7,5},{8,10},{9,11},{10,... | collective-permute-start | bytes 786440 | tf_op jit(solution)/shard_map/ppermute | solution.py:558
  126.3 8.2 %collective-permute-start.20 = (bf16[64,16,128]{2,1,0:T(8,128)(2,1)}, bf16[64,16,128]{2,1,0:T(8,128)(2,1)}, u32[]{:S(2)}, u32[]{:S(2)}) collective-permute-start(bf16[64,16,128]{2,1,0:T(8,128)(2,1)} %get-tuple-element.77.refs_0_.refs_8_), channel_id=1, source_target_pairs={{0,2},{1,3},{2,0},{3,1},{4,6},{5,7},{6,4},{7,5},{8,10},{9,11},{10,... | collective-permute-start | bytes 786440 | tf_op jit(solution)/shard_map/ppermute | solution.py:558
  126.5 10.4 %collective-permute-start.26 = (bf16[64,16,128]{2,1,0:T(8,128)(2,1)}, bf16[64,16,128]{2,1,0:T(8,128)(2,1)}, u32[]{:S(2)}, u32[]{:S(2)}) collective-permute-start(bf16[64,16,128]{2,1,0:T(8,128)(2,1)} %get-tuple-element.82.refs_4_.refs_12_), channel_id=1, source_target_pairs={{0,1},{1,0},{2,3},{3,2},{4,5},{5,4},{6,7},{7,6},{8,9},{9,8},{10,11... | collective-permute-start | bytes 786440 | tf_op jit(solution)/shard_map/ppermute | solution.py:561
  126.5 10.4 %collective-permute-start.21 = (bf16[64,16,128]{2,1,0:T(8,128)(2,1)}, bf16[64,16,128]{2,1,0:T(8,128)(2,1)}, u32[]{:S(2)}, u32[]{:S(2)}) collective-permute-start(bf16[64,16,128]{2,1,0:T(8,128)(2,1)} %get-tuple-element.77.refs_0_.refs_8_), channel_id=1, source_target_pairs={{0,1},{1,0},{2,3},{3,2},{4,5},{5,4},{6,7},{7,6},{8,9},{9,8},{10,11... | collective-permute-start | bytes 786440 | tf_op jit(solution)/shard_map/ppermute | solution.py:561
  130.2 6.7 %collective-permute-start.27 = (bf16[64,16,128]{2,1,0:T(8,128)(2,1)}, bf16[64,16,128]{2,1,0:T(8,128)(2,1)}, u32[]{:S(2)}, u32[]{:S(2)}) collective-permute-start(bf16[64,16,128]{2,1,0:T(8,128)(2,1)} %collective-permute-done.25.refs_5_.refs_13_), channel_id=1, source_target_pairs={{0,1},{1,0},{2,3},{3,2},{4,5},{5,4},{6,7},{7,6},{8,9},{9,8},{10,11... | collective-permute-start | bytes 786440 | tf_op jit(solution)/shard_map/ppermute | solution.py:561
  135.5 21.6 %collective-permute-start.31 = (bf16[64,32,128]{2,1,0:T(8,128)(2,1)}, bf16[64,32,128]{2,1,0:T(8,128)(2,1)}, u32[]{:S(2)}, u32[]{:S(2)}) collective-permute-start(bf16[64,32,128]{2,1,0:T(8,128)(2,1)} %add_convert_fusion.2), channel_id=1, source_target_pairs={{0,4},{4,12},{12,8},{8,0},{1,5},{5,13},{13,9},{9,1},{2,6},{6,14},{... | collective-permute-start | bytes 1572872 | tf_op jit(solution)/shard_map/ppermute | solution.py:552
  140.5 21.7 %collective-permute-start.28 = (bf16[64,32,128]{2,1,0:T(8,128)(2,1)S(1)}, bf16[64,32,128]{2,1,0:T(8,128)(2,1)S(1)}, u32[]{:S(2)}, u32[]{:S(2)}) collective-permute-start(bf16[64,32,128]{2,1,0:T(8,128)(2,1)S(1)} %get-tuple-element.94), channel_id=1, source_target_pairs={{0,4},{4,12},{12,8},{8,0},{1,5},{5,13},{13,9},{9,1},{2,6},{6,14},{... | collective-permute-start | bytes 1572872 | tf_op jit(solution)/shard_map/ppermute | solution.py:552
  163.1 15.5 %collective-permute-start.29 = (bf16[64,32,128]{2,1,0:T(8,128)(2,1)}, bf16[64,32,128]{2,1,0:T(8,128)(2,1)}, u32[]{:S(2)}, u32[]{:S(2)}) collective-permute-start(bf16[64,32,128]{2,1,0:T(8,128)(2,1)} %add_convert_fusion.1), channel_id=1, source_target_pairs={{0,4},{4,12},{12,8},{8,0},{1,5},{5,13},{13,9},{9,1},{2,6},{6,14},{... | collective-permute-start | bytes 1572872 | tf_op jit(solution)/shard_map/ppermute | solution.py:552
  166.2 5.2 %collective-permute-start.33 = (f32[32,768]{1,0:T(8,128)}, f32[32,768]{1,0:T(8,128)}, u32[]{:S(2)}, u32[]{:S(2)}) collective-permute-start(f32[32,768]{1,0:T(8,128)} %constant_dynamic-slice_fusion.1), channel_id=1, source_target_pairs={{0,2},{1,3},{2,0},{3,1},{4,6},{5,7},{6,4},{7,5},{8,10},{9,11},{10,... | collective-permute-start | bytes 294920 | tf_op jit(solution)/shard_map/ppermute | solution.py:558
  172.4 10.3 %collective-permute-start.34 = (f32[32,768]{1,0:T(8,128)S(1)}, f32[32,768]{1,0:T(8,128)S(1)}, u32[]{:S(2)}, u32[]{:S(2)}) collective-permute-start(f32[32,768]{1,0:T(8,128)S(1)} %dynamic-slice_add_fusion.1), channel_id=1, source_target_pairs={{0,4},{4,0},{8,12},{12,8},{1,5},{5,1},{9,13},{13,9},{2,6},{6,2},{1... | collective-permute-start | bytes 294920 | tf_op jit(solution)/shard_map/ppermute | solution.py:555
  180.8 25.2 %collective-permute-start.30 = (bf16[64,32,128]{2,1,0:T(8,128)(2,1)}, bf16[64,32,128]{2,1,0:T(8,128)(2,1)}, u32[]{:S(2)}, u32[]{:S(2)}) collective-permute-start(bf16[64,32,128]{2,1,0:T(8,128)(2,1)} %add_convert_fusion), channel_id=1, source_target_pairs={{0,4},{4,12},{12,8},{8,0},{1,5},{5,13},{13,9},{9,1},{2,6},{6,14},{... | collective-permute-start | bytes 1572872 | tf_op jit(solution)/shard_map/ppermute | solution.py:552
  182.7 16.7 %collective-permute-start.35 = (f32[32,768]{1,0:T(8,128)S(1)}, f32[32,768]{1,0:T(8,128)S(1)}, u32[]{:S(2)}, u32[]{:S(2)}) collective-permute-start(f32[32,768]{1,0:T(8,128)S(1)} %add.109), channel_id=1, source_target_pairs={{0,8},{4,12},{8,0},{12,4},{1,9},{5,13},{9,1},{13,5},{2,10},{6,14},... | collective-permute-start | bytes 294920 | tf_op jit(solution)/shard_map/ppermute | solution.py:555
  211.8 11.4 %collective-permute-start.37 = (f32[64,768]{1,0:T(8,128)S(1)}, f32[64,768]{1,0:T(8,128)S(1)}, u32[]{:S(2)}, u32[]{:S(2)}) collective-permute-start(f32[64,768]{1,0:T(8,128)S(1)} %pad_maximum_fusion.2), channel_id=1, source_target_pairs={{0,1},{1,0},{2,3},{3,2},{4,5},{5,4},{6,7},{7,6},{8,9},{9,8},{10,11... | collective-permute-start | bytes 589832 | tf_op jit(solution)/shard_map/ppermute | solution.py:561
  221.8 5.9 %collective-permute-start.41 = (f32[64,256]{1,0:T(8,128)S(1)}, f32[64,256]{1,0:T(8,128)S(1)}, u32[]{:S(2)}, u32[]{:S(2)}) collective-permute-start(f32[64,256]{1,0:T(8,128)S(1)} %add.113), channel_id=1, source_target_pairs={{0,8},{4,12},{8,0},{12,4},{1,9},{5,13},{9,1},{13,5},{2,10},{6,14},... | collective-permute-start | bytes 196616 | tf_op jit(solution)/shard_map/ppermute | solution.py:555
  (69 other events, 397.1 us)

commit v5 on v4

--- a/solution.py
+++ b/solution.py
@@ -106,7 +106,7 @@
 
 
 SUB = 16
-PART = 32
+PART = 16
 HALF = 64
 WIDTH = 128
 LANES = SUB * HALF
@@ -258,7 +258,7 @@
 
 def mid_kernel(
     a_ref, b_ref, c_ref, x_ref, grad_ref, gain_in_ref, gain_out_ref, gate_ref, out_w_ref,
-    dtri_ref, dgate_ref, g_out_ref, g_gate_ref, buf, wide,
+    g_out_so_far, g_gate_so_far, dtri_ref, dgate_ref, g_out_ref, g_gate_ref, buf, wide,
 ):
     gain_out = column(gain_out_ref[...])
     tri = channels_of(
@@ -278,11 +278,11 @@
     outproj = mm(out_w_ref[...], tnorm, TN)
     d_open = upstream * outproj
     d_outproj = (upstream * opened).astype(BF16)
-    g_out_ref[...] = mm(tnorm, d_outproj, NT)
+    g_out_ref[...] = g_out_so_far[...] + mm(tnorm, d_outproj, NT)
     d_tnorm = mm(out_w_ref[...], d_outproj, NN)
     d_tri = norm_back_channels(d_tnorm, tcentred, tinverse, gain_out)
     d_gatepre = (d_open * opened * (1.0 - opened)).astype(BF16)
-    g_gate_ref[...] = mm(normed, d_gatepre, NT)
+    g_gate_ref[...] = g_gate_so_far[...] + mm(normed, d_gatepre, NT)
     stage_rows(d_tri, buf)
     for p in range(HALF):
         dtri_ref[p] = panel_row(buf, p).astype(BF16)
@@ -307,15 +307,15 @@
 
 
 def dleft_kernel(*refs):
-    out_ref = refs[-1]
-    parts = (len(refs) - 1) // 5
+    so_far, out_ref = refs[-2:]
+    parts = (len(refs) - 2) // 5
     grad_refs, panel_refs = refs[: 4 * parts], refs[4 * parts : 5 * parts]
     first = first_half(HALF)
     for p in range(GROUP):
         grads = jnp.concatenate([d[p] for d in grad_refs], axis=0)
         right = jnp.concatenate([r[q, p] for r in panel_refs for q in range(4)], axis=0)
         both = mm(grads, right, TN)
-        out_ref[p] = jnp.where(first, both[:HALF], both[HALF:])
+        out_ref[p] = so_far[p] + jnp.where(first, both[:HALF], both[HALF:])
 
 
 def gate_grads(upstream, mask, sig, value):
@@ -343,7 +343,7 @@
 
 
 def final_b_kernel(
-    at, x_ref, part_ref, a_ref, b_ref, token_ref, exponent_ref, gain_ref, w_ref, into_ref,
+    at, x_ref, part_ref, a_ref, b_ref, token_ref, exponent_ref, gain_ref, w_ref, so_far, into_ref,
     out_ref, g_ref, buf, wide,
 ):
     step = pl.program_id(0)
@@ -357,7 +357,7 @@
 
     @pl.when(step == 0)
     def start():
-        g_ref[...] = jnp.zeros_like(g_ref)
+        g_ref[...] = so_far[...]
 
     g_ref[...] += mm(normed, d_proj, NT)
     d_normed = part_ref[...] + mm(w_ref[...], d_proj, NN)
@@ -436,14 +436,14 @@
     )(*slots, left)
 
 
-def mid_part(s, parts, pair, grad, gain_in, gain_out, w_gate, w_out):
+def mid_part(s, parts, pair, grad, gain_in, gain_out, w_gate, w_out, g_out, g_gate):
     square = jax.ShapeDtypeStruct((WIDTH, WIDTH), F32)
     columns = block((HALF, SUB, WIDTH), (0, s, 0))
-    small = [gain_in, gain_out, w_gate, w_out]
+    small = [gain_in, gain_out, w_gate, w_out, g_out, g_gate]
     return pl.pallas_call(
         mid_kernel,
         grid=(1,),
-        out_shape=(PANEL, PANEL, square, square),
+        out_shape=(PANEL, pltpu.HBM(PANEL.shape, BF16), square, square),
         in_specs=[WHOLE_PANEL, block((1, HALF, SUB, WIDTH), (0, 0, 0, 0)), WHOLE_PANEL]
         + [columns] * 2
         + [whole(a) for a in small],
@@ -459,7 +459,7 @@
     return pl.pallas_call(
         dright_kernel,
         grid=(HALF // GROUP,),
-        out_shape=(LONG,) * 4,
+        out_shape=(pltpu.HBM(LONG.shape, BF16), LONG, LONG, LONG),
         in_specs=[PANEL_SPEC] * len(blocks) + [LEFT_SPEC],
         out_specs=(LONG_SPEC,) * 4,
         scratch_shapes=[pltpu.VMEM((4, GROUP, PART, WIDTH), BF16)],
@@ -469,17 +469,18 @@
     )(*blocks, left)
 
 
-def dleft_part(grads, panels):
+def dleft_part(grads, panels, so_far):
+    rows = pl.BlockSpec((GROUP, HALF, WIDTH), lambda i: (i, 0, 0))
     return pl.pallas_call(
         dleft_kernel,
         grid=(HALF // GROUP,),
         out_shape=jax.ShapeDtypeStruct((HALF, HALF, WIDTH), F32),
-        in_specs=[PANEL_SPEC] * len(grads) + [FOUR_SPEC] * len(panels),
-        out_specs=pl.BlockSpec((GROUP, HALF, WIDTH), lambda i: (i, 0, 0)),
+        in_specs=[PANEL_SPEC] * len(grads) + [FOUR_SPEC] * len(panels) + [rows],
+        out_specs=rows,
         compiler_params=params(),
-        cost_estimate=cost(8 * HALF * HALF * WIDTH * WIDTH, 10 << 20),
+        cost_estimate=cost(4 * HALF * HALF * WIDTH * WIDTH, 8 << 20),
         name="dleft_part",
-    )(*grads, *panels)
+    )(*grads, *panels, so_far)
 
 
 def final_a_part(pair, dleft, tokens, gain, w_proj, w_gate, gates):
@@ -507,7 +508,7 @@
     )(pair, dleft, tokens, gain, w_proj, w_gate, *gates)
 
 
-def final_b_part(s, pair, part, sums, tokens, exponents, gain, w_proj, into):
+def final_b_part(s, pair, part, sums, tokens, exponents, gain, w_proj, so_far, into):
     steps = PART // SUB
     rows = pl.BlockSpec((SUB, HALF, WIDTH), lambda i: (s * steps + i, 0, 0))
     panel = pl.BlockSpec((HALF, SUB, WIDTH), lambda i: (0, i, 0))
@@ -523,16 +524,16 @@
             pl.BlockSpec((WIDTH, LANES), lambda i: (0, s * steps + i)),
             panel, panel, whole(tokens),
             pl.BlockSpec((SUB, HALF), lambda i: (s * steps + i, 0)),
-            whole(gain), block((WIDTH, 2 * WIDTH), (0, 1)),
+            whole(gain), block((WIDTH, 2 * WIDTH), (0, 1)), whole(so_far),
             pl.BlockSpec(memory_space=pl.ANY),
         ],
         out_specs=(rows, block((WIDTH, 2 * WIDTH), (0, 0))),
         scratch_shapes=[BUF, WIDE],
-        input_output_aliases={8: 0} if into.shape == pair.shape else {},
+        input_output_aliases={9: 0} if into.shape == pair.shape else {},
         compiler_params=params(),
         cost_estimate=cost(28 * LANES * WIDTH * WIDTH, 4 << 20, 2 * LANES * WIDTH),
         name="final_b_part",
-    )(pair, part, *sums, tokens, exponents, gain, w_proj, into)
+    )(pair, part, *sums, tokens, exponents, gain, w_proj, so_far, into)
 
 
 def after(array, *others):
@@ -543,7 +544,6 @@
     width = pair_tiles.shape[-1]
     crop_len = token_mask.shape[0]
     core = lax.axis_index("col") % 2
-    x_at = lax.axis_index("col") // 2
     tokens = token_mask.reshape(1, crop_len)
     gain_in = gain_in.reshape(1, width)
     gain_out = gain_out.reshape(1, width)
@@ -563,88 +563,113 @@
     def plus(a, b):
         return (a.astype(F32) + b.astype(F32)).astype(BF16)
 
-    def gather(own):
-        held = [own]
-        for _ in range(3):
-            held.append(forward(held[-1]))
-        return held
-
-    own = [right_part(s, pair_tiles, gain_in, w_proj, tokens, exponents) for s in range(2)]
+    def right(s):
+        return right_part(s, pair_tiles, gain_in, w_proj, tokens, exponents)
+
+    a0, b0 = right(0), right(1)
     left = left_part(pair_tiles, gain_in, w_proj, tokens)
-    slots = [gather(own[0])]
-    slots.append(gather(after(own[1], slots[0][3])))
-
-    def triangles(s):
-        out = []
-        for at in range(PART // SUB):
-            keep, near, send, panel = tri_part(at, slots[s], left)
-            got = over_core(send)
-            out.append((keep, got, over_x(plus(near, got[1])), panel))
-        return out
-
-    def middle(s, at, parts):
+    a1, b1 = forward(a0), forward(b0)
+    a2, b2 = forward(a1), forward(after(b1, left))
+    c0, d0 = right(2), right(3)
+    a3, b3 = forward(after(a2, c0)), forward(after(b2, d0))
+    c1, d1 = forward(after(c0, b2)), forward(after(d0, a3))
+
+    def triangle(slots):
+        keep, near, send, panel = tri_part(0, slots, left)
+        got = over_core(send)
+        return keep, got, plus(near, got[1]), panel
+
+    g_out = g_gate = jnp.zeros((width, width), F32)
+
+    def middle(s, tri, mine):
         return mid_part(
-            s * (PART // SUB) + at, parts, pair_tiles, grad_out, gain_in, gain_out, w_gate, w_out
+            s, (tri[0], tri[1], mine), pair_tiles, grad_out, gain_in, gain_out, w_gate, w_out, g_out, g_gate
         )
 
     def spread(d_tri):
         far = over_x(d_tri)
         return [d_tri, far, over_core(d_tri), over_core(far)]
 
-    tri = triangles(0)
-    mids = []
-    for at, (keep, got, mine, _) in enumerate(tri):
-        mids.append(middle(0, at, (keep, got, after(mine, slots[1][1]))))
-    panels = [t[3] for t in tri]
-    blocks = [b for m in mids for b in spread(m[0])]
-    first = dright_part([after(blocks[0], slots[1][2])] + blocks[1:], left)
-
-    total = plus(forward(first[1]), first[2])
-    tri = triangles(1)
-    for at, (keep, got, mine, _) in enumerate(tri):
-        mids.append(middle(1, at, (keep, got, after(mine, total) if at else mine)))
-    panels += [t[3] for t in tri]
-    total = plus(forward(total), first[3])
-    more = [b for m in mids[2:] for b in spread(m[0])]
-    second = dright_part([after(more[0], total)] + more[1:], left)
-    sums_a = (first[0], forward(total))
-
-    total = plus(forward(second[1]), second[2])
-    total = plus(forward(total), second[3])
-    d_left = dleft_part([after(blocks[0], second[0])] + blocks[1:] + more, panels)
-    partial, g_a = final_a_part(pair_tiles, d_left, tokens, gain_in, w_proj, w_gate, [m[1] for m in mids])
-    d_pair, g_first = final_b_part(
-        0, pair_tiles, partial, sums_a, tokens, exponents, gain_in, w_proj, gain_in
-    )
-    g_out = sum(m[2] for m in mids)
-    g_gate = sum(m[3] for m in mids)
-
-    def exchange(a, send, at):
+    def dright(blocks, *others):
+        return dright_part([blocks[0], blocks[1], blocks[2], after(blocks[3], *others)], left)
+
+    tri_a, tri_b = triangle([a0, a1, a2, a3]), triangle([b0, b1, b2, b3])
+    x_a, x_b = over_x(tri_a[2]), over_x(tri_b[2])
+    c2, d2 = forward(after(c1, tri_a[2])), forward(after(d1, tri_b[2]))
+    dtri_a, gate_a, g_out, g_gate = middle(0, tri_a, after(x_a, d1))
+    blocks_a = spread(dtri_a)
+    dtri_b, gate_b, g_out, g_gate = middle(1, tri_b, after(x_b, c2))
+    blocks_b = spread(dtri_b)
+    c3, d3 = forward(after(c2, dtri_a)), forward(after(d2, dtri_b))
+    part_a = dright(blocks_a, d2)
+    part_b = dright(blocks_b, c3)
+    r_a, r_b = forward(part_a[1]), forward(part_b[1])
+
+    tri_c = triangle([c0, c1, c2, after(c3, part_a[1])])
+    tri_d = triangle([d0, d1, d2, after(d3, part_b[1])])
+    x_c, x_d = over_x(tri_c[2]), over_x(tri_d[2])
+    r_a = plus(r_a, part_a[2])
+    r_a2 = forward(after(r_a, tri_c[2]))
+    r_b = plus(r_b, part_b[2])
+    r_b2 = forward(after(r_b, tri_d[2]))
+    d_left = dleft_part(
+        [after(blocks_a[0], tri_d[2])] + blocks_a[1:] + blocks_b,
+        [tri_a[3], tri_b[3]],
+        jnp.zeros((HALF, HALF, WIDTH), F32),
+    )
+    dtri_c, gate_c, g_out, g_gate = middle(2, tri_c, after(x_c, r_a, d_left))
+    blocks_c = spread(dtri_c)
+    dtri_d, gate_d, g_out, g_gate = middle(3, tri_d, after(x_d, r_b))
+    blocks_d = spread(dtri_d)
+    r_a2 = plus(r_a2, part_a[3])
+    r_a3 = forward(after(r_a2, dtri_c))
+    r_b2 = plus(r_b2, part_b[3])
+    r_b3 = forward(after(r_b2, dtri_d))
+    part_c = dright(blocks_c, r_a2)
+    part_d = dright(blocks_d, r_b2)
+
+    r_c, r_d = forward(part_c[1]), forward(part_d[1])
+    d_left = dleft_part(
+        [after(blocks_c[0], part_d[1])] + blocks_c[1:] + blocks_d, [tri_c[3], tri_d[3]], d_left
+    )
+    partial, g_a = final_a_part(
+        pair_tiles, d_left, tokens, gain_in, w_proj, w_gate, [gate_a, gate_b, gate_c, gate_d]
+    )
+    r_c = forward(plus(r_c, part_c[2]))
+    r_d = forward(plus(r_d, part_d[2]))
+    zero = jnp.zeros((width, 2 * width), F32)
+
+    def final(s, sums, so_far, into):
+        return final_b_part(
+            s, pair_tiles, partial, sums, tokens, exponents, gain_in, w_proj, so_far, into
+        )
+
+    d_pair, g_first = final(0, (part_a[0], r_a3), zero, gain_in)
+    d_pair, g_first = final(1, (part_b[0], r_b3), g_first, d_pair)
+    r_c = forward(plus(r_c, part_c[3]))
+    r_d = forward(plus(r_d, part_d[3]))
+
+    def halved(a):
         half = a.shape[0] // 2
-        return lax.dynamic_slice_in_dim(a, at * half, half) + send(
-            lax.dynamic_slice_in_dim(a, (1 - at) * half, half)
+        a = lax.dynamic_slice_in_dim(a, core * half, half) + over_core(
+            lax.dynamic_slice_in_dim(a, (1 - core) * half, half)
         )
-
-    def join(a, send, at):
-        theirs = send(a)
-        return jnp.concatenate([jnp.where(at == 0, a, theirs), jnp.where(at == 0, theirs, a)], axis=0)
-
-    def over_rows(a):
-        for bit in (1, 2):
-            a = a + over_row(a, bit)
-        return a
-
-    early = jnp.concatenate([g_out, g_gate, g_a, g_first], axis=1)
-    early = over_rows(exchange(exchange(early, over_core, core), over_x, x_at))
-    early = join(join(early, over_x, x_at), over_core, core)
-    sums_b = (second[0], after(forward(total), early))
-    d_pair, late = final_b_part(
-        1, pair_tiles, partial, sums_b, tokens, exponents, gain_in, w_proj, d_pair
-    )
-    late = exchange(late, over_core, core)
-    late = join(over_rows(late + over_x(late)), over_core, core)
-    g_proj = jnp.concatenate([early[:, 2 * width : 4 * width], early[:, 4 * width :] + late], axis=1)
-    return d_pair, g_proj / crop_len, early[:, width : 2 * width] / crop_len, early[:, :width] / crop_len
+        return a + over_x(a)
+
+    early = halved(jnp.concatenate([g_out, g_gate, g_a, g_first], axis=1))
+    d_pair, g_last = final(2, (part_c[0], after(r_c, early)), zero, d_pair)
+    d_pair, g_last = final(3, (part_d[0], r_d), g_last, d_pair)
+    late = halved(g_last)
+    sums = jnp.concatenate([early[:, : 4 * width], early[:, 4 * width :] + late], axis=1)
+    for bit in (1, 2):
+        mine = sums.astype(BF16)
+        sums = mine.astype(F32) + over_row(mine, bit).astype(F32)
+    sums = sums / crop_len
+    theirs = over_core(sums)
+    sums = jnp.concatenate(
+        [jnp.where(core == 0, sums, theirs), jnp.where(core == 0, theirs, sums)], axis=0
+    )
+    return d_pair, sums[:, 2 * width :], sums[:, width : 2 * width], sums[:, :width]
 
 
 def local(pair_tiles, *rest, rows_over, cols_over):

time: 231 us -> 210 us (0.909)
  waiting for transfers between devices: 114 us -> 76.1 us
  starting transfers between devices: 36.4 us -> 56.3 us
  Pallas kernels: 52.8 us -> 61.1 us
  local copies, waits for them, and re-layouts: 15.4 us -> 8.5 us
  other arithmetic: 9.52 us -> 5.89 us
    ppermute x12 -> x24, starting transfers between devices: 14.9 us -> 40.7 us  [forward(): return lax.ppermute(a, 'row', [(0, 1), (1, 3), (3, 2), (2, 0)])]
    ppermute x12 -> x24, waiting for transfers between devices: 67.1 us -> 45.4 us  [forward(): return lax.ppermute(a, 'row', [(0, 1), (1, 3), (3, 2), (2, 0)])]
    ppermute x4 -> x2, waiting for transfers between devices: 24.2 us -> 6.66 us  [over_row(): return lax.ppermute(a, 'row', [(k, k ^ bit) for k in range(4)])]
    pallas_call x6 -> x8, Pallas kernels: 16.7 us -> 25.9 us  [the longest x4 14.3 us: mid_part(): pl.pallas_call(mid_kernel, grid=(1,), out_shape=(PANEL, pltpu.HBM(PANEL.s...]
    unnamed x116 -> x65, local copies, waits for them, and re-layouts: 14.7 us -> 8.2 us
    ppermute x11 -> x10, starting transfers between devices: 15.1 us -> 10.6 us  [over_x(): return lax.ppermute(a, 'col', [(k, k ^ 2) for k in range(4)])]
    add x9 -> x3, other arithmetic: 2.66 us -> 0.06 us  [the longest x2 0.03 us: halved(): lax.dynamic_slice_in_dim(a, core * half, half)]
    pallas_call x2 -> x4, Pallas kernels: 9.58 us -> 8.56 us  [final_b_part(): pl.pallas_call(functools.partial(final_b_kernel, s * steps), grid=(steps,...]
  transfers between devices with their start and end apart: 43 -> 51, of which waited for: 20 -> 25; matrix products, arithmetic and copies ran while one was open for 4% -> 3% of each run, Pallas kernels for 20% -> 28%
where the time goes in v5:
time: 210 us; the launch traced here: 209 us
  waiting for transfers between devices  76.1 us (36%)
  Pallas kernels  61.1 us (29%)
  starting transfers between devices  56.3 us (27%)
  local copies, waits for them, and re-layouts  8.5 us (4%)
  other arithmetic  5.89 us (3%)
    ppermute x24, waiting for transfers between devices, forward(): return lax.ppermute(a, 'row', [(0, 1), (1, 3), (3, 2), (2, 0)])  45.4 us
    ppermute x24, starting transfers between devices, forward(): return lax.ppermute(a, 'row', [(0, 1), (1, 3), (3, 2), (2, 0)])  40.7 us
    ppermute x10, waiting for transfers between devices, over_x(): return lax.ppermute(a, 'col', [(k, k ^ 2) for k in range(4)])  21.3 us
    pallas_call x4, Pallas kernels, mid_part(): pl.pallas_call(mid_kernel, grid=(1,), out_shape=(PANEL, pltpu.HBM(PANEL.s...  14.3 us
    pallas_call x4, Pallas kernels, dright_part(): pl.pallas_call(dright_kernel, grid=(HALF // GROUP,), out_shape=(pltpu.HBM...  11.6 us
    ppermute x10, starting transfers between devices, over_x(): return lax.ppermute(a, 'col', [(k, k ^ 2) for k in range(4)])  10.6 us
    pallas_call x4, Pallas kernels, final_b_part(): pl.pallas_call(functools.partial(final_b_kernel, s * steps), grid=(steps,...  8.56 us
    unnamed x65, local copies, waits for them, and re-layouts  8.2 us
  transfers between devices with their start and end apart: 51, of which 25 were waited for; matrix products, arithmetic and copies ran while one was open for 3% of the time, Pallas kernels for 28%

profile of v5, /device:TPU:0, one launch (start us, length us, event | category | flops | bytes accessed | tf_op | source)
XLA Modules:
  0.0 209.2 jit_solution(14863310854028216737)
XLA Ops:
  5.8 3.1 %collective-permute-start.3 = (bf16[64,16,128]{2,1,0:T(8,128)(2,1)S(1)}, bf16[64,16,128]{2,1,0:T(8,128)(2,1)S(1)}, u32[]{:S(2)}, u32[]{:S(2)}) collective-permute-start(bf16[64,16,128]{2,1,0:T(8,128)(2,1)S(1)} %right_part.6.s0), channel_id=1, source_target_pairs={{0,4},{4,12},{12,8},{8,0},{1,5},{5,13},{13,9},{9,1},{2,6},{6,14},{... | collective-permute-start | bytes 786440 | tf_op jit(solution)/shard_map/ppermute | solution.py:552
  9.9 2.6 %collective-permute-start = (bf16[64,16,128]{2,1,0:T(8,128)(2,1)S(1)}, bf16[64,16,128]{2,1,0:T(8,128)(2,1)S(1)}, u32[]{:S(2)}, u32[]{:S(2)}) collective-permute-start(bf16[64,16,128]{2,1,0:T(8,128)(2,1)S(1)} %right_part.5.s0), channel_id=1, source_target_pairs={{0,4},{4,12},{12,8},{8,0},{1,5},{5,13},{13,9},{9,1},{2,6},{6,14},{... | collective-permute-start | bytes 786440 | tf_op jit(solution)/shard_map/ppermute | solution.py:552
  12.5 4.5 %collective-permute-done.3.s1 = bf16[64,16,128]{2,1,0:T(8,128)(2,1)S(1)} collective-permute-done((bf16[64,16,128]{2,1,0:T(8,128)(2,1)S(1)}, bf16[64,16,128]{2,1,0:T(8,128)(2,1)S(1)}, u32[]{:S(2)}, u32[]{:S(2)}) %collective-permute-start.3) | collective-permute-done | bytes 262176 | tf_op jit(solution)/shard_map/ppermute | solution.py:552
  18.2 4.2 %left_part.1.left_ref.refs_4_ = bf16[64,2,64,128]{3,2,1,0:T(8,128)(2,1)S(1)} custom-call(bf16[64,64,128]{2,1,0:T(8,128)(2,1)S(1)} %copy-done, f32[1,128]{1,0:T(1,128)S(1)} %bitcast.25, bf16[128,512]{1,0:T(8,128)(2,1)S(1)} %copy-done.3, s32[1,256]{1,0:T(1,128)S(1)} %bitcast.40), custom_call_target="tpu_custom_call" | custom-call | flops 268435456 | bytes 3145728 | tf_op jit(solution)/shard_map/left_part/pallas_call | solution.py:410
  22.7 3.2 %collective-permute-start.1 = (bf16[64,16,128]{2,1,0:T(8,128)(2,1)S(1)}, bf16[64,16,128]{2,1,0:T(8,128)(2,1)S(1)}, u32[]{:S(2)}, u32[]{:S(2)}) collective-permute-start(bf16[64,16,128]{2,1,0:T(8,128)(2,1)S(1)} %collective-permute-done.s1), channel_id=1, source_target_pairs={{0,4},{4,12},{12,8},{8,0},{1,5},{5,13},{13,9},{9,1},{2,6},{6,14},{... | collective-permute-start | bytes 786440 | tf_op jit(solution)/shard_map/ppermute | solution.py:552
  30.4 3.5 %collective-permute-done.1.s2 = bf16[64,16,128]{2,1,0:T(8,128)(2,1)S(1)} collective-permute-done((bf16[64,16,128]{2,1,0:T(8,128)(2,1)S(1)}, bf16[64,16,128]{2,1,0:T(8,128)(2,1)S(1)}, u32[]{:S(2)}, u32[]{:S(2)}) %collective-permute-start.1) | collective-permute-done | bytes 262176 | tf_op jit(solution)/shard_map/ppermute | solution.py:552
  35.1 4.4 %collective-permute-done.5.s3 = bf16[64,16,128]{2,1,0:T(8,128)(2,1)S(1)} collective-permute-done((bf16[64,16,128]{2,1,0:T(8,128)(2,1)S(1)}, bf16[64,16,128]{2,1,0:T(8,128)(2,1)S(1)}, u32[]{:S(2)}, u32[]{:S(2)}) %collective-permute-start.5) | collective-permute-done | bytes 262176 | tf_op jit(solution)/shard_map/ppermute | solution.py:552
  41.7 2.6 %collective-permute-done.14.s3 = bf16[64,16,128]{2,1,0:T(8,128)(2,1)S(1)} collective-permute-done((bf16[64,16,128]{2,1,0:T(8,128)(2,1)S(1)}, bf16[64,16,128]{2,1,0:T(8,128)(2,1)S(1)}, u32[]{:S(2)}, u32[]{:S(2)}) %collective-permute-start.14) | collective-permute-done | bytes 262176 | tf_op jit(solution)/shard_map/ppermute | solution.py:552
  47.3 3.4 %collective-permute-start.9 = (bf16[64,16,128]{2,1,0:T(8,128)(2,1)S(1)}, bf16[64,16,128]{2,1,0:T(8,128)(2,1)S(1)}, u32[]{:S(2)}, u32[]{:S(2)}) collective-permute-start(bf16[64,16,128]{2,1,0:T(8,128)(2,1)S(1)} %right_part.7.s0), channel_id=1, source_target_pairs={{0,4},{4,12},{12,8},{8,0},{1,5},{5,13},{13,9},{9,1},{2,6},{6,14},{... | collective-permute-start | bytes 786440 | tf_op jit(solution)/shard_map/ppermute | solution.py:552
  53.0 3.5 %collective-permute-done.2.s1 = bf16[64,16,128]{2,1,0:T(8,128)(2,1)S(1)} collective-permute-done((bf16[64,16,128]{2,1,0:T(8,128)(2,1)S(1)}, bf16[64,16,128]{2,1,0:T(8,128)(2,1)S(1)}, u32[]{:S(2)}, u32[]{:S(2)}) %collective-permute-start.2) | collective-permute-done | bytes 262176 | tf_op jit(solution)/shard_map/ppermute | solution.py:552
  57.3 4.8 %collective-permute-done.9.s1 = bf16[64,16,128]{2,1,0:T(8,128)(2,1)S(1)} collective-permute-done((bf16[64,16,128]{2,1,0:T(8,128)(2,1)S(1)}, bf16[64,16,128]{2,1,0:T(8,128)(2,1)S(1)}, u32[]{:S(2)}, u32[]{:S(2)}) %collective-permute-start.9) | collective-permute-done | bytes 262176 | tf_op jit(solution)/shard_map/ppermute | solution.py:552
  62.1 3.6 %mid_part.4 = (bf16[64,16,128]{2,1,0:T(8,128)(2,1)S(1)}, bf16[64,16,128]{2,1,0:T(8,128)(2,1)}, f32[128,128]{1,0:T(8,128)S(1)}, f32[128,128]{1,0:T(8,128)S(1)}) custom-call(bf16[64,16,128]{2,1,0:T(8,128)(2,1)S(1)} %get-tuple-element.94.a_ref, bf16[2,64,16,128]{3,2,1,0:T(8,128)(2,1)S(1)} %collective-permute-done.6.b_ref, ...), custom_call_target="tpu_custom_call" | custom-call | flops 201326592 | bytes 2097152 | tf_op jit(solution)/shard_map/mid_part/pallas_call | solution.py:443
  67.2 3.5 %mid_part.5 = (bf16[64,16,128]{2,1,0:T(8,128)(2,1)S(1)}, bf16[64,16,128]{2,1,0:T(8,128)(2,1)}, f32[128,128]{1,0:T(8,128)S(1)}, f32[128,128]{1,0:T(8,128)S(1)}) custom-call(bf16[64,16,128]{2,1,0:T(8,128)(2,1)S(1)} %get-tuple-element.110.a_ref, bf16[2,64,16,128]{3,2,1,0:T(8,128)(2,1)S(1)} %collective-permute-done.15.b_ref, ...), custom_call_target="tpu_custom_call" | custom-call | flops 201326592 | bytes 2097152 | tf_op jit(solution)/shard_map/mid_part/pallas_call | solution.py:443
  73.6 3.4 %collective-permute-start.10 = (bf16[64,16,128]{2,1,0:T(8,128)(2,1)S(1)}, bf16[64,16,128]{2,1,0:T(8,128)(2,1)S(1)}, u32[]{:S(2)}, u32[]{:S(2)}) collective-permute-start(bf16[64,16,128]{2,1,0:T(8,128)(2,1)S(1)} %collective-permute-done.7.s2), channel_id=1, source_target_pairs={{0,4},{4,12},{12,8},{8,0},{1,5},{5,13},{13,9},{9,1},{2,6},{6,14},{... | collective-permute-start | bytes 786440 | tf_op jit(solution)/shard_map/ppermute | solution.py:552
  78.7 3.7 %collective-permute-done.16.s2 = bf16[64,16,128]{2,1,0:T(8,128)(2,1)S(1)} collective-permute-done((bf16[64,16,128]{2,1,0:T(8,128)(2,1)S(1)}, bf16[64,16,128]{2,1,0:T(8,128)(2,1)S(1)}, u32[]{:S(2)}, u32[]{:S(2)}) %collective-permute-start.16) | collective-permute-done | bytes 262176 | tf_op jit(solution)/shard_map/ppermute | solution.py:552
  89.4 3.3 %collective-permute-start.19 = (bf16[64,16,128]{2,1,0:T(8,128)(2,1)S(1)}, bf16[64,16,128]{2,1,0:T(8,128)(2,1)S(1)}, u32[]{:S(2)}, u32[]{:S(2)}) collective-permute-start(bf16[64,16,128]{2,1,0:T(8,128)(2,1)S(1)} %get-tuple-element.104), channel_id=1, source_target_pairs={{0,4},{4,12},{12,8},{8,0},{1,5},{5,13},{13,9},{9,1},{2,6},{6,14},{... | collective-permute-start | bytes 786440 | tf_op jit(solution)/shard_map/ppermute | solution.py:552
  104.2 3.4 %collective-permute-done.27 = bf16[64,16,128]{2,1,0:T(8,128)(2,1)S(1)} collective-permute-done((bf16[64,16,128]{2,1,0:T(8,128)(2,1)S(1)}, bf16[64,16,128]{2,1,0:T(8,128)(2,1)S(1)}, u32[]{:S(2)}, u32[]{:S(2)}) %collective-permute-start.27) | collective-permute-done | bytes 262176 | tf_op jit(solution)/shard_map/ppermute | solution.py:552
  110.3 3.2 %collective-permute-done.26.c_ref = bf16[64,16,128]{2,1,0:T(8,128)(2,1)S(1)} collective-permute-done((bf16[64,16,128]{2,1,0:T(8,128)(2,1)S(1)}, bf16[64,16,128]{2,1,0:T(8,128)(2,1)S(1)}, u32[]{:S(2)}, u32[]{:S(2)}) %collective-permute-start.26) | collective-permute-done | bytes 262176 | tf_op jit(solution)/shard_map/ppermute | solution.py:558
  113.5 3.6 %mid_part.6 = (bf16[64,16,128]{2,1,0:T(8,128)(2,1)S(1)}, bf16[64,16,128]{2,1,0:T(8,128)(2,1)}, f32[128,128]{1,0:T(8,128)S(1)}, f32[128,128]{1,0:T(8,128)S(1)}) custom-call(bf16[64,16,128]{2,1,0:T(8,128)(2,1)S(1)} %get-tuple-element.106.a_ref, bf16[2,64,16,128]{3,2,1,0:T(8,128)(2,1)S(1)} %collective-permute-done.17.b_ref, ...), custom_call_target="tpu_custom_call" | custom-call | flops 201326592 | bytes 2097152 | tf_op jit(solution)/shard_map/mid_part/pallas_call | solution.py:443
  117.0 3.6 %mid_part.7 = (bf16[64,16,128]{2,1,0:T(8,128)(2,1)}, bf16[64,16,128]{2,1,0:T(8,128)(2,1)}, f32[128,128]{1,0:T(8,128)S(1)}, f32[128,128]{1,0:T(8,128)S(1)}) custom-call(bf16[64,16,128]{2,1,0:T(8,128)(2,1)S(1)} %get-tuple-element.128.a_ref, bf16[2,64,16,128]{3,2,1,0:T(8,128)(2,1)S(1)} %collective-permute-done.25.b_ref, ...), custom_call_target="tpu_custom_call" | custom-call | flops 201326592 | bytes 2097152 | tf_op jit(solution)/shard_map/mid_part/pallas_call | solution.py:443
  126.8 4.0 %collective-permute-done.28.refs_1_.refs_5_ = bf16[64,16,128]{2,1,0:T(8,128)(2,1)} collective-permute-done((bf16[64,16,128]{2,1,0:T(8,128)(2,1)}, bf16[64,16,128]{2,1,0:T(8,128)(2,1)}, u32[]{:S(2)}, u32[]{:S(2)}) %collective-permute-start.28) | collective-permute-done | bytes 262176 | tf_op jit(solution)/shard_map/ppermute | solution.py:558
  130.9 3.5 %collective-permute-done.32.refs_1_ = bf16[64,16,128]{2,1,0:T(8,128)(2,1)} collective-permute-done((bf16[64,16,128]{2,1,0:T(8,128)(2,1)S(1)}, bf16[64,16,128]{2,1,0:T(8,128)(2,1)}, u32[]{:S(2)}, u32[]{:S(2)}) %collective-permute-start.32) | collective-permute-done | bytes 262176 | tf_op jit(solution)/shard_map/ppermute | solution.py:558
  140.1 3.7 %dright_part.6 = (bf16[64,16,128]{2,1,0:T(8,128)(2,1)}, bf16[64,16,128]{2,1,0:T(8,128)(2,1)S(1)}, bf16[64,16,128]{2,1,0:T(8,128)(2,1)S(1)}, bf16[64,16,128]{2,1,0:T(8,128)(2,1)S(1)}) custom-call(bf16[64,16,128]{2,1,0:T(8,128)(2,1)} %get-tuple-element.133.refs_0_.refs_4_, bf16[64,16,128]{2,1,0:T(8,128)(2,1)} %collective-permute-done.28.refs_1_.refs_5_, ...), custom_call_target="tpu_custom_call" | custom-call | flops 268435456 | bytes 6291456 | tf_op jit(solution)/shard_map/dright_part/pallas_call | solution.py:459
  144.3 3.8 %dright_part.7 = (bf16[64,16,128]{2,1,0:T(8,128)(2,1)}, bf16[64,16,128]{2,1,0:T(8,128)(2,1)S(1)}, bf16[64,16,128]{2,1,0:T(8,128)(2,1)S(1)}, bf16[64,16,128]{2,1,0:T(8,128)(2,1)S(1)}) custom-call(bf16[64,16,128]{2,1,0:T(8,128)(2,1)S(1)} %get-tuple-element.138.refs_0_, bf16[64,16,128]{2,1,0:T(8,128)(2,1)} %collective-permute-done.32.refs_1_, ...), custom_call_target="tpu_custom_call" | custom-call | flops 268435456 | bytes 6291456 | tf_op jit(solution)/shard_map/dright_part/pallas_call | solution.py:459
  148.8 3.0 %dleft_part.3.dleft_ref = f32[64,64,128]{2,1,0:T(8,128)S(1)} custom-call(bf16[64,16,128]{2,1,0:T(8,128)(2,1)S(1)} %get-tuple-element.138.refs_0_, bf16[64,16,128]{2,1,0:T(8,128)(2,1)} %collective-permute-done.32.refs_1_, bf16[64,16,128]{2,1,0:T(8,128)(2,1)S(1)} %collective-permute-done.33.refs_2_, bf16[64,16,128]{2,1,0:T(8,128)(2,1)S(1)} %collective-permute-done.34.refs_3_, ...), custom_call_target="tpu_custom_call" | custom-call | flops 268435456 | bytes 8388608 | tf_op jit(solution)/shard_map/dleft_part/pallas_call | solution.py:474
  151.9 6.0 %final_a_part.1 = (f32[128,4096]{1,0:T(8,128)S(1)}, f32[128,256]{1,0:T(8,128)S(1)}) custom-call(bf16[64,64,128]{2,1,0:T(8,128)(2,1)S(1)} %copy-done.1, f32[64,64,128]{2,1,0:T(8,128)S(1)} %dleft_part.3.dleft_ref, s32[1,256]{1,0:T(1,128)S(1)} %bitcast.43, f32[1,128]{1,0:T(1,128)S(1)} %bitcast.32, bf16[128,512]{1,0:T(8,128)(2,1)S(1)} %copy-done.4, ...), custom_call_target="tpu_custom_call" | custom-call | flops 939524096 | bytes 8388608 | tf_op jit(solution)/shard_map/final_a_part/pallas_call | solution.py:487
  166.4 6.4 %collective-permute-done.40 = bf16[64,16,128]{2,1,0:T(8,128)(2,1)S(1)} collective-permute-done((bf16[64,16,128]{2,1,0:T(8,128)(2,1)S(1)}, bf16[64,16,128]{2,1,0:T(8,128)(2,1)S(1)}, u32[]{:S(2)}, u32[]{:S(2)}) %collective-permute-start.40) | collective-permute-done | bytes 262176 | tf_op jit(solution)/shard_map/ppermute | solution.py:552
  173.4 5.0 %collective-permute-done.36 = bf16[64,16,128]{2,1,0:T(8,128)(2,1)S(1)} collective-permute-done((bf16[64,16,128]{2,1,0:T(8,128)(2,1)S(1)}, bf16[64,16,128]{2,1,0:T(8,128)(2,1)S(1)}, u32[]{:S(2)}, u32[]{:S(2)}) %collective-permute-start.36) | collective-permute-done | bytes 262176 | tf_op jit(solution)/shard_map/ppermute | solution.py:552
  179.7 5.1 %collective-permute-done.45 = f32[64,768]{1,0:T(8,128)S(1)} collective-permute-done((f32[64,768]{1,0:T(8,128)S(1)}, f32[64,768]{1,0:T(8,128)S(1)}, u32[]{:S(2)}, u32[]{:S(2)}) %collective-permute-start.45) | collective-permute-done | bytes 196640 | tf_op jit(solution)/shard_map/ppermute | solution.py:558
  192.2 3.7 %collective-permute-done.47 = f32[64,256]{1,0:T(8,128)S(1)} collective-permute-done((f32[64,256]{1,0:T(8,128)S(1)}, f32[64,256]{1,0:T(8,128)S(1)}, u32[]{:S(2)}, u32[]{:S(2)}) %collective-permute-start.47) | collective-permute-done | bytes 65568 | tf_op jit(solution)/shard_map/ppermute | solution.py:558
  197.9 2.7 %collective-permute-done.48 = bf16[64,768]{1,0:T(8,128)(2,1)S(1)} collective-permute-done((bf16[64,768]{1,0:T(8,128)(2,1)S(1)}, bf16[64,768]{1,0:T(8,128)(2,1)S(1)}, u32[]{:S(2)}, u32[]{:S(2)}) %collective-permute-start.48) | collective-permute-done | bytes 98336 | tf_op jit(solution)/shard_map/ppermute | solution.py:555
  202.3 3.9 %collective-permute-done.49 = bf16[64,768]{1,0:T(8,128)(2,1)S(1)} collective-permute-done((bf16[64,768]{1,0:T(8,128)(2,1)S(1)}, bf16[64,768]{1,0:T(8,128)(2,1)S(1)}, u32[]{:S(2)}, u32[]{:S(2)}) %collective-permute-start.49) | collective-permute-done | bytes 98336 | tf_op jit(solution)/shard_map/ppermute | solution.py:555
  (188 shorter events, 86.0 us)
Async XLA Ops:
  5.8 11.2 %collective-permute-start.3 = (bf16[64,16,128]{2,1,0:T(8,128)(2,1)S(1)}, bf16[64,16,128]{2,1,0:T(8,128)(2,1)S(1)}, u32[]{:S(2)}, u32[]{:S(2)}) collective-permute-start(bf16[64,16,128]{2,1,0:T(8,128)(2,1)S(1)} %right_part.6.s0), channel_id=1, source_target_pairs={{0,4},{4,12},{12,8},{8,0},{1,5},{5,13},{13,9},{9,1},{2,6},{6,14},{... | collective-permute-start | bytes 786440 | tf_op jit(solution)/shard_map/ppermute | solution.py:552
  9.9 12.8 %collective-permute-start = (bf16[64,16,128]{2,1,0:T(8,128)(2,1)S(1)}, bf16[64,16,128]{2,1,0:T(8,128)(2,1)S(1)}, u32[]{:S(2)}, u32[]{:S(2)}) collective-permute-start(bf16[64,16,128]{2,1,0:T(8,128)(2,1)S(1)} %right_part.5.s0), channel_id=1, source_target_pairs={{0,4},{4,12},{12,8},{8,0},{1,5},{5,13},{13,9},{9,1},{2,6},{6,14},{... | collective-permute-start | bytes 786440 | tf_op jit(solution)/shard_map/ppermute | solution.py:552
  17.0 11.2 %collective-permute-start.4 = (bf16[64,16,128]{2,1,0:T(8,128)(2,1)S(1)}, bf16[64,16,128]{2,1,0:T(8,128)(2,1)S(1)}, u32[]{:S(2)}, u32[]{:S(2)}) collective-permute-start(bf16[64,16,128]{2,1,0:T(8,128)(2,1)S(1)} %collective-permute-done.3.s1), channel_id=1, source_target_pairs={{0,4},{4,12},{12,8},{8,0},{1,5},{5,13},{13,9},{9,1},{2,6},{6,14},{... | collective-permute-start | bytes 786440 | tf_op jit(solution)/shard_map/ppermute | solution.py:552
  22.7 11.2 %collective-permute-start.1 = (bf16[64,16,128]{2,1,0:T(8,128)(2,1)S(1)}, bf16[64,16,128]{2,1,0:T(8,128)(2,1)S(1)}, u32[]{:S(2)}, u32[]{:S(2)}) collective-permute-start(bf16[64,16,128]{2,1,0:T(8,128)(2,1)S(1)} %collective-permute-done.s1), channel_id=1, source_target_pairs={{0,4},{4,12},{12,8},{8,0},{1,5},{5,13},{13,9},{9,1},{2,6},{6,14},{... | collective-permute-start | bytes 786440 | tf_op jit(solution)/shard_map/ppermute | solution.py:552
  28.3 11.2 %collective-permute-start.5 = (bf16[64,16,128]{2,1,0:T(8,128)(2,1)S(1)}, bf16[64,16,128]{2,1,0:T(8,128)(2,1)S(1)}, u32[]{:S(2)}, u32[]{:S(2)}) collective-permute-start(bf16[64,16,128]{2,1,0:T(8,128)(2,1)S(1)} %collective-permute-done.4.s2), channel_id=1, source_target_pairs={{0,4},{4,12},{12,8},{8,0},{1,5},{5,13},{13,9},{9,1},{2,6},{6,14},{... | collective-permute-start | bytes 786440 | tf_op jit(solution)/shard_map/ppermute | solution.py:552
  33.9 10.4 %collective-permute-start.14 = (bf16[64,16,128]{2,1,0:T(8,128)(2,1)S(1)}, bf16[64,16,128]{2,1,0:T(8,128)(2,1)S(1)}, u32[]{:S(2)}, u32[]{:S(2)}) collective-permute-start(bf16[64,16,128]{2,1,0:T(8,128)(2,1)S(1)} %collective-permute-done.1.s2), channel_id=1, source_target_pairs={{0,4},{4,12},{12,8},{8,0},{1,5},{5,13},{13,9},{9,1},{2,6},{6,14},{... | collective-permute-start | bytes 786440 | tf_op jit(solution)/shard_map/ppermute | solution.py:552
  47.3 14.8 %collective-permute-start.9 = (bf16[64,16,128]{2,1,0:T(8,128)(2,1)S(1)}, bf16[64,16,128]{2,1,0:T(8,128)(2,1)S(1)}, u32[]{:S(2)}, u32[]{:S(2)}) collective-permute-start(bf16[64,16,128]{2,1,0:T(8,128)(2,1)S(1)} %right_part.7.s0), channel_id=1, source_target_pairs={{0,4},{4,12},{12,8},{8,0},{1,5},{5,13},{13,9},{9,1},{2,6},{6,14},{... | collective-permute-start | bytes 786440 | tf_op jit(solution)/shard_map/ppermute | solution.py:552
  50.7 11.3 %collective-permute-start.8 = (bf16[64,16,128]{2,1,0:T(8,128)(2,1)S(1)}, bf16[64,16,128]{2,1,0:T(8,128)(2,1)S(1)}, u32[]{:S(2)}, u32[]{:S(2)}) collective-permute-start(bf16[64,16,128]{2,1,0:T(8,128)(2,1)S(1)} %fusion.3), channel_id=1, source_target_pairs={{0,2},{1,3},{2,0},{3,1},{4,6},{5,7},{6,4},{7,5},{8,10},{9,11},{10,... | collective-permute-start | bytes 786440 | tf_op jit(solution)/shard_map/ppermute | solution.py:558
  52.4 14.9 %collective-permute-start.20 = (bf16[64,16,128]{2,1,0:T(8,128)(2,1)S(1)}, bf16[64,16,128]{2,1,0:T(8,128)(2,1)S(1)}, u32[]{:S(2)}, u32[]{:S(2)}) collective-permute-start(bf16[64,16,128]{2,1,0:T(8,128)(2,1)S(1)} %fusion.2), channel_id=1, source_target_pairs={{0,2},{1,3},{2,0},{3,1},{4,6},{5,7},{6,4},{7,5},{8,10},{9,11},{10,... | collective-permute-start | bytes 786440 | tf_op jit(solution)/shard_map/ppermute | solution.py:558
  56.4 10.8 %collective-permute-start.7 = (bf16[64,16,128]{2,1,0:T(8,128)(2,1)S(1)}, bf16[64,16,128]{2,1,0:T(8,128)(2,1)S(1)}, u32[]{:S(2)}, u32[]{:S(2)}) collective-permute-start(bf16[64,16,128]{2,1,0:T(8,128)(2,1)S(1)} %collective-permute-done.2.s1), channel_id=1, source_target_pairs={{0,4},{4,12},{12,8},{8,0},{1,5},{5,13},{13,9},{9,1},{2,6},{6,14},{... | collective-permute-start | bytes 786440 | tf_op jit(solution)/shard_map/ppermute | solution.py:552
  72.3 10.1 %collective-permute-start.16 = (bf16[64,16,128]{2,1,0:T(8,128)(2,1)S(1)}, bf16[64,16,128]{2,1,0:T(8,128)(2,1)S(1)}, u32[]{:S(2)}, u32[]{:S(2)}) collective-permute-start(bf16[64,16,128]{2,1,0:T(8,128)(2,1)S(1)} %collective-permute-done.9.s1), channel_id=1, source_target_pairs={{0,4},{4,12},{12,8},{8,0},{1,5},{5,13},{13,9},{9,1},{2,6},{6,14},{... | collective-permute-start | bytes 786440 | tf_op jit(solution)/shard_map/ppermute | solution.py:552
  73.1 10.1 %collective-permute-start.12 = (bf16[64,16,128]{2,1,0:T(8,128)(2,1)S(1)}, bf16[64,16,128]{2,1,0:T(8,128)(2,1)S(1)}, u32[]{:S(2)}, u32[]{:S(2)}) collective-permute-start(bf16[64,16,128]{2,1,0:T(8,128)(2,1)S(1)} %get-tuple-element.121.refs_0_), channel_id=1, source_target_pairs={{0,1},{1,0},{2,3},{3,2},{4,5},{5,4},{6,7},{7,6},{8,9},{9,8},{10,11... | collective-permute-start | bytes 786440 | tf_op jit(solution)/shard_map/ppermute | solution.py:561
  73.6 12.8 %collective-permute-start.10 = (bf16[64,16,128]{2,1,0:T(8,128)(2,1)S(1)}, bf16[64,16,128]{2,1,0:T(8,128)(2,1)S(1)}, u32[]{:S(2)}, u32[]{:S(2)}) collective-permute-start(bf16[64,16,128]{2,1,0:T(8,128)(2,1)S(1)} %collective-permute-done.7.s2), channel_id=1, source_target_pairs={{0,4},{4,12},{12,8},{8,0},{1,5},{5,13},{13,9},{9,1},{2,6},{6,14},{... | collective-permute-start | bytes 786440 | tf_op jit(solution)/shard_map/ppermute | solution.py:552
  78.7 13.9 %collective-permute-start.24 = (bf16[64,16,128]{2,1,0:T(8,128)(2,1)S(1)}, bf16[64,16,128]{2,1,0:T(8,128)(2,1)S(1)}, u32[]{:S(2)}, u32[]{:S(2)}) collective-permute-start(bf16[64,16,128]{2,1,0:T(8,128)(2,1)S(1)} %collective-permute-done.22.refs_1_.refs_5_), channel_id=1, source_target_pairs={{0,1},{1,0},{2,3},{3,2},{4,5},{5,4},{6,7},{7,6},{8,9},{9,8},{10,11... | collective-permute-start | bytes 786440 | tf_op jit(solution)/shard_map/ppermute | solution.py:561
  82.4 10.2 %collective-permute-start.23 = (bf16[64,16,128]{2,1,0:T(8,128)(2,1)S(1)}, bf16[64,16,128]{2,1,0:T(8,128)(2,1)S(1)}, u32[]{:S(2)}, u32[]{:S(2)}) collective-permute-start(bf16[64,16,128]{2,1,0:T(8,128)(2,1)S(1)} %get-tuple-element.114.refs_0_.refs_4_), channel_id=1, source_target_pairs={{0,1},{1,0},{2,3},{3,2},{4,5},{5,4},{6,7},{7,6},{8,9},{9,8},{10,11... | collective-permute-start | bytes 786440 | tf_op jit(solution)/shard_map/ppermute | solution.py:561
  82.4 13.0 %collective-permute-start.21 = (bf16[64,16,128]{2,1,0:T(8,128)(2,1)S(1)}, bf16[64,16,128]{2,1,0:T(8,128)(2,1)S(1)}, u32[]{:S(2)}, u32[]{:S(2)}) collective-permute-start(bf16[64,16,128]{2,1,0:T(8,128)(2,1)S(1)} %collective-permute-done.16.s2), channel_id=1, source_target_pairs={{0,4},{4,12},{12,8},{8,0},{1,5},{5,13},{13,9},{9,1},{2,6},{6,14},{... | collective-permute-start | bytes 786440 | tf_op jit(solution)/shard_map/ppermute | solution.py:552
  89.4 10.4 %collective-permute-start.17 = (bf16[2,64,16,128]{3,2,1,0:T(8,128)(2,1)S(1)}, bf16[2,64,16,128]{3,2,1,0:T(8,128)(2,1)S(1)}, u32[]{:S(2)}, u32[]{:S(2)}) collective-permute-start(bf16[2,64,16,128]{3,2,1,0:T(8,128)(2,1)S(1)} %get-tuple-element.107), channel_id=1, source_target_pairs={{0,1},{1,0},{2,3},{3,2},{4,5},{5,4},{6,7},{7,6},{8,9},{9,8},{10,11... | collective-permute-start | bytes 1572872 | tf_op jit(solution)/shard_map/ppermute | solution.py:561
  99.9 13.6 %collective-permute-start.18 = (bf16[64,16,128]{2,1,0:T(8,128)(2,1)S(1)}, bf16[64,16,128]{2,1,0:T(8,128)(2,1)S(1)}, u32[]{:S(2)}, u32[]{:S(2)}) collective-permute-start(bf16[64,16,128]{2,1,0:T(8,128)(2,1)S(1)} %fusion.1), channel_id=1, source_target_pairs={{0,2},{1,3},{2,0},{3,1},{4,6},{5,7},{6,4},{7,5},{8,10},{9,11},{10,... | collective-permute-start | bytes 786440 | tf_op jit(solution)/shard_map/ppermute | solution.py:558
  100.4 24.8 %collective-permute-start.38 = (bf16[64,16,128]{2,1,0:T(8,128)(2,1)}, bf16[64,16,128]{2,1,0:T(8,128)(2,1)}, u32[]{:S(2)}, u32[]{:S(2)}) collective-permute-start(bf16[64,16,128]{2,1,0:T(8,128)(2,1)} %add_convert_fusion.7), channel_id=1, source_target_pairs={{0,4},{4,12},{12,8},{8,0},{1,5},{5,13},{13,9},{9,1},{2,6},{6,14},{... | collective-permute-start | bytes 786440 | tf_op jit(solution)/shard_map/ppermute | solution.py:552
  102.7 10.8 %collective-permute-start.26 = (bf16[64,16,128]{2,1,0:T(8,128)(2,1)S(1)}, bf16[64,16,128]{2,1,0:T(8,128)(2,1)S(1)}, u32[]{:S(2)}, u32[]{:S(2)}) collective-permute-start(bf16[64,16,128]{2,1,0:T(8,128)(2,1)S(1)} %fusion), channel_id=1, source_target_pairs={{0,2},{1,3},{2,0},{3,1},{4,6},{5,7},{6,4},{7,5},{8,10},{9,11},{10,... | collective-permute-start | bytes 786440 | tf_op jit(solution)/shard_map/ppermute | solution.py:558
  121.8 12.6 %collective-permute-start.32 = (bf16[64,16,128]{2,1,0:T(8,128)(2,1)S(1)}, bf16[64,16,128]{2,1,0:T(8,128)(2,1)}, u32[]{:S(2)}, u32[]{:S(2)}) collective-permute-start(bf16[64,16,128]{2,1,0:T(8,128)(2,1)S(1)} %get-tuple-element.138.refs_0_), channel_id=1, source_target_pairs={{0,2},{1,3},{2,0},{3,1},{4,6},{5,7},{6,4},{7,5},{8,10},{9,11},{10,... | collective-permute-start | bytes 786440 | tf_op jit(solution)/shard_map/ppermute | solution.py:558
  123.3 11.1 %collective-permute-start.31 = (bf16[64,16,128]{2,1,0:T(8,128)(2,1)}, bf16[64,16,128]{2,1,0:T(8,128)(2,1)}, u32[]{:S(2)}, u32[]{:S(2)}) collective-permute-start(bf16[64,16,128]{2,1,0:T(8,128)(2,1)} %add_convert_fusion.6), channel_id=1, source_target_pairs={{0,4},{4,12},{12,8},{8,0},{1,5},{5,13},{13,9},{9,1},{2,6},{6,14},{... | collective-permute-start | bytes 786440 | tf_op jit(solution)/shard_map/ppermute | solution.py:552
  125.2 14.8 %collective-permute-start.29 = (bf16[64,16,128]{2,1,0:T(8,128)(2,1)}, bf16[64,16,128]{2,1,0:T(8,128)(2,1)S(1)}, u32[]{:S(2)}, u32[]{:S(2)}) collective-permute-start(bf16[64,16,128]{2,1,0:T(8,128)(2,1)} %get-tuple-element.133.refs_0_.refs_4_), channel_id=1, source_target_pairs={{0,1},{1,0},{2,3},{3,2},{4,5},{5,4},{6,7},{7,6},{8,9},{9,8},{10,11... | collective-permute-start | bytes 786440 | tf_op jit(solution)/shard_map/ppermute | solution.py:561
  125.2 19.1 %collective-permute-start.33 = (bf16[64,16,128]{2,1,0:T(8,128)(2,1)S(1)}, bf16[64,16,128]{2,1,0:T(8,128)(2,1)S(1)}, u32[]{:S(2)}, u32[]{:S(2)}) collective-permute-start(bf16[64,16,128]{2,1,0:T(8,128)(2,1)S(1)} %get-tuple-element.138.refs_0_), channel_id=1, source_target_pairs={{0,1},{1,0},{2,3},{3,2},{4,5},{5,4},{6,7},{7,6},{8,9},{9,8},{10,11... | collective-permute-start | bytes 786440 | tf_op jit(solution)/shard_map/ppermute | solution.py:561
  135.5 22.4 %collective-permute-start.43 = (bf16[64,16,128]{2,1,0:T(8,128)(2,1)S(1)}, bf16[64,16,128]{2,1,0:T(8,128)(2,1)S(1)}, u32[]{:S(2)}, u32[]{:S(2)}) collective-permute-start(bf16[64,16,128]{2,1,0:T(8,128)(2,1)S(1)} %add_convert_fusion.2), channel_id=1, source_target_pairs={{0,4},{4,12},{12,8},{8,0},{1,5},{5,13},{13,9},{9,1},{2,6},{6,14},{... | collective-permute-start | bytes 786440 | tf_op jit(solution)/shard_map/ppermute | solution.py:552
  137.9 22.2 %collective-permute-start.42 = (bf16[64,16,128]{2,1,0:T(8,128)(2,1)S(1)}, bf16[64,16,128]{2,1,0:T(8,128)(2,1)S(1)}, u32[]{:S(2)}, u32[]{:S(2)}) collective-permute-start(bf16[64,16,128]{2,1,0:T(8,128)(2,1)S(1)} %add_convert_fusion.5), channel_id=1, source_target_pairs={{0,4},{4,12},{12,8},{8,0},{1,5},{5,13},{13,9},{9,1},{2,6},{6,14},{... | collective-permute-start | bytes 786440 | tf_op jit(solution)/shard_map/ppermute | solution.py:552
  143.7 20.3 %collective-permute-start.35 = (bf16[64,16,128]{2,1,0:T(8,128)(2,1)S(1)}, bf16[64,16,128]{2,1,0:T(8,128)(2,1)S(1)}, u32[]{:S(2)}, u32[]{:S(2)}) collective-permute-start(bf16[64,16,128]{2,1,0:T(8,128)(2,1)S(1)} %get-tuple-element.137), channel_id=1, source_target_pairs={{0,4},{4,12},{12,8},{8,0},{1,5},{5,13},{13,9},{9,1},{2,6},{6,14},{... | collective-permute-start | bytes 786440 | tf_op jit(solution)/shard_map/ppermute | solution.py:552
  148.1 14.2 %collective-permute-start.39 = (bf16[64,16,128]{2,1,0:T(8,128)(2,1)S(1)}, bf16[64,16,128]{2,1,0:T(8,128)(2,1)S(1)}, u32[]{:S(2)}, u32[]{:S(2)}) collective-permute-start(bf16[64,16,128]{2,1,0:T(8,128)(2,1)S(1)} %get-tuple-element.153), channel_id=1, source_target_pairs={{0,4},{4,12},{12,8},{8,0},{1,5},{5,13},{13,9},{9,1},{2,6},{6,14},{... | collective-permute-start | bytes 786440 | tf_op jit(solution)/shard_map/ppermute | solution.py:552
  162.4 10.5 %collective-permute-start.40 = (bf16[64,16,128]{2,1,0:T(8,128)(2,1)S(1)}, bf16[64,16,128]{2,1,0:T(8,128)(2,1)S(1)}, u32[]{:S(2)}, u32[]{:S(2)}) collective-permute-start(bf16[64,16,128]{2,1,0:T(8,128)(2,1)S(1)} %add_convert_fusion.1), channel_id=1, source_target_pairs={{0,4},{4,12},{12,8},{8,0},{1,5},{5,13},{13,9},{9,1},{2,6},{6,14},{... | collective-permute-start | bytes 786440 | tf_op jit(solution)/shard_map/ppermute | solution.py:552
  164.1 14.3 %collective-permute-start.36 = (bf16[64,16,128]{2,1,0:T(8,128)(2,1)S(1)}, bf16[64,16,128]{2,1,0:T(8,128)(2,1)S(1)}, u32[]{:S(2)}, u32[]{:S(2)}) collective-permute-start(bf16[64,16,128]{2,1,0:T(8,128)(2,1)S(1)} %add_convert_fusion.4), channel_id=1, source_target_pairs={{0,4},{4,12},{12,8},{8,0},{1,5},{5,13},{13,9},{9,1},{2,6},{6,14},{... | collective-permute-start | bytes 786440 | tf_op jit(solution)/shard_map/ppermute | solution.py:552
  166.3 12.7 %collective-permute-start.44 = (f32[64,768]{1,0:T(8,128)S(1)}, f32[64,768]{1,0:T(8,128)S(1)}, u32[]{:S(2)}, u32[]{:S(2)}) collective-permute-start(f32[64,768]{1,0:T(8,128)S(1)} %constant_dynamic-slice_fusion.1), channel_id=1, source_target_pairs={{0,1},{1,0},{2,3},{3,2},{4,5},{5,4},{6,7},{7,6},{8,9},{9,8},{10,11... | collective-permute-start | bytes 589832 | tf_op jit(solution)/shard_map/ppermute | solution.py:561
  172.9 11.9 %collective-permute-start.41 = (bf16[64,16,128]{2,1,0:T(8,128)(2,1)S(1)}, bf16[64,16,128]{2,1,0:T(8,128)(2,1)S(1)}, u32[]{:S(2)}, u32[]{:S(2)}) collective-permute-start(bf16[64,16,128]{2,1,0:T(8,128)(2,1)S(1)} %add_convert_fusion), channel_id=1, source_target_pairs={{0,4},{4,12},{12,8},{8,0},{1,5},{5,13},{13,9},{9,1},{2,6},{6,14},{... | collective-permute-start | bytes 786440 | tf_op jit(solution)/shard_map/ppermute | solution.py:552
  (50 other events, 363.1 us)

commit v6 on v5

--- a/solution.py
+++ b/solution.py
@@ -106,7 +106,7 @@
 
 
 SUB = 16
-PART = 16
+PAIR = 32
 HALF = 64
 WIDTH = 128
 LANES = SUB * HALF
@@ -222,7 +222,7 @@
 def right_kernel(at, x_ref, gain_ref, w_ref, token_ref, exponent_ref, out_ref, buf):
     normed = normed_cells(x_ref, gain_ref)[0]
     proj = mm(w_ref[...], normed, TN)
-    raw = mask_lanes(token_ref, at + pl.program_id(0)) * jax.nn.sigmoid(proj[:WIDTH]) * proj[WIDTH:]
+    raw = mask_lanes(token_ref, at) * jax.nn.sigmoid(proj[:WIDTH]) * proj[WIDTH:]
     bound = bound_lanes(exponent_ref)
     stage_rows(jnp.clip(raw, -bound, bound), buf)
     for p in range(HALF):
@@ -241,19 +241,21 @@
         out_ref[p, 1] = jnp.where(first, 0.0, row).astype(BF16)
 
 
-def tri_kernel(s0, s1, s2, s3, left_ref, keep_ref, near_ref, send_ref, panel_ref):
+def tri_kernel(*refs):
+    *slot_refs, left_ref, keep_ref, near_ref, send_ref, panel_ref = refs
     z, q = lax.axis_index("row"), lax.axis_index("col")
-    for m, ref in enumerate((s0, s1, s2, s3)):
-        place = ((z ^ (z >> 1)) - m + 4) & 3
+    for k, ref in enumerate(slot_refs):
+        place = ((z ^ (z >> 1)) - (k % 4) + 4) & 3
         other = place ^ (place >> 1) ^ q
-        panel_ref[(other & 1) * 2 + (other >> 1)] = ref[...]
+        at = (k // 4) * SUB
+        panel_ref[(other & 1) * 2 + (other >> 1), :, at : at + SUB] = ref[...]
     for p in range(GROUP):
         right = jnp.concatenate([panel_ref[r, p] for r in range(4)], axis=0)
         tri = mm(right, left_ref[p].reshape(WIDTH, WIDTH), NT).astype(BF16)
-        keep_ref[p] = tri[:SUB]
-        near_ref[p] = tri[SUB : 2 * SUB]
-        send_ref[0, p] = tri[2 * SUB : 3 * SUB]
-        send_ref[1, p] = tri[3 * SUB :]
+        keep_ref[p] = tri[:PAIR]
+        near_ref[p] = tri[PAIR : 2 * PAIR]
+        send_ref[0, p] = tri[2 * PAIR : 3 * PAIR]
+        send_ref[1, p] = tri[3 * PAIR :]
 
 
 def mid_kernel(
@@ -278,11 +280,17 @@
     outproj = mm(out_w_ref[...], tnorm, TN)
     d_open = upstream * outproj
     d_outproj = (upstream * opened).astype(BF16)
-    g_out_ref[...] = g_out_so_far[...] + mm(tnorm, d_outproj, NT)
+
+    @pl.when(pl.program_id(0) == 0)
+    def start():
+        g_out_ref[...] = g_out_so_far[...]
+        g_gate_ref[...] = g_gate_so_far[...]
+
+    g_out_ref[...] += mm(tnorm, d_outproj, NT)
     d_tnorm = mm(out_w_ref[...], d_outproj, NN)
     d_tri = norm_back_channels(d_tnorm, tcentred, tinverse, gain_out)
     d_gatepre = (d_open * opened * (1.0 - opened)).astype(BF16)
-    g_gate_ref[...] = g_gate_so_far[...] + mm(normed, d_gatepre, NT)
+    g_gate_ref[...] += mm(normed, d_gatepre, NT)
     stage_rows(d_tri, buf)
     for p in range(HALF):
         dtri_ref[p] = panel_row(buf, p).astype(BF16)
@@ -291,29 +299,25 @@
         dgate_ref[i] = panel_row(buf, i).astype(BF16)
 
 
-def dright_kernel(*refs):
-    *grads_refs, left_ref, p0, p1, p2, p3, held = refs
+def dright_kernel(d0, d1, d2, d3, left_ref, *refs):
+    *part_refs, held = refs
     z, q = lax.axis_index("row"), lax.axis_index("col")
-    for k, ref in enumerate(grads_refs):
-        r = k % 4
+    for r, ref in enumerate((d0, d1, d2, d3)):
         block_at = q ^ ((r % 2) * 2 + r // 2)
-        slot = ((z ^ (z >> 1)) - (block_at ^ (block_at >> 1)) + 4) & 3
-        held[slot, :, (k // 4) * SUB : (k // 4 + 1) * SUB] = ref[...]
+        held[((z ^ (z >> 1)) - (block_at ^ (block_at >> 1)) + 4) & 3] = ref[...]
     for p in range(GROUP):
         grads = jnp.concatenate([held[m, p] for m in range(4)], axis=0)
         part = mm(grads, left_ref[p].reshape(WIDTH, WIDTH), NN).astype(BF16)
-        for m, ref in enumerate((p0, p1, p2, p3)):
-            ref[p] = part[m * PART : (m + 1) * PART]
-
-
-def dleft_kernel(*refs):
-    so_far, out_ref = refs[-2:]
-    parts = (len(refs) - 2) // 5
-    grad_refs, panel_refs = refs[: 4 * parts], refs[4 * parts : 5 * parts]
+        for k, ref in enumerate(part_refs):
+            at = (k % 4) * PAIR + (k // 4) * SUB
+            ref[p] = part[at : at + SUB]
+
+
+def dleft_kernel(d0, d1, d2, d3, panel_ref, so_far, out_ref):
     first = first_half(HALF)
     for p in range(GROUP):
-        grads = jnp.concatenate([d[p] for d in grad_refs], axis=0)
-        right = jnp.concatenate([r[q, p] for r in panel_refs for q in range(4)], axis=0)
+        grads = jnp.concatenate([d[p] for d in (d0, d1, d2, d3)], axis=0)
+        right = jnp.concatenate([panel_ref[r, p] for r in range(4)], axis=0)
         both = mm(grads, right, TN)
         out_ref[p] = so_far[p] + jnp.where(first, both[:HALF], both[HALF:])
 
@@ -325,14 +329,14 @@
 
 
 def final_a_kernel(
-    x_ref, dleft_ref, token_ref, gain_ref, w_ref, gate_ref, q0, q1, q2, q3, out_ref, g_ref, buf, wide
+    x_ref, dleft_ref, token_ref, gain_ref, w_ref, gate_ref, q0, q1, out_ref, g_ref, buf, wide
 ):
     s = pl.program_id(0)
     normed = normed_cells(x_ref, gain_ref)[0]
     proj = mm(w_ref[...], normed, TN)
     d_left = channels_of(dleft_ref[...], buf, wide)
     d_proj = gate_grads(d_left, mask_lanes(token_ref, s), jax.nn.sigmoid(proj[:WIDTH]), proj[WIDTH:])
-    d_gate = jnp.concatenate([q[...] for q in (q0, q1, q2, q3)], axis=1).reshape(LANES, WIDTH)
+    d_gate = jnp.concatenate([q0[...], q1[...]], axis=1).reshape(LANES, WIDTH)
     out_ref[...] = mm(w_ref[...], d_proj, NN) + mm(gate_ref[...], d_gate, NT)
 
     @pl.when(s == 0)
@@ -346,20 +350,15 @@
     at, x_ref, part_ref, a_ref, b_ref, token_ref, exponent_ref, gain_ref, w_ref, so_far, into_ref,
     out_ref, g_ref, buf, wide,
 ):
-    step = pl.program_id(0)
     normed, centred, inverse, gain = normed_cells(x_ref, gain_ref)
     proj = mm(w_ref[...], normed, TN)
-    mask = mask_lanes(token_ref, at + step)
+    mask = mask_lanes(token_ref, at)
     sig = jax.nn.sigmoid(proj[:WIDTH])
     inside = jnp.abs(mask * sig * proj[WIDTH:]) <= bound_lanes(exponent_ref)
     d_right = channels_of(a_ref[...].astype(F32) + b_ref[...].astype(F32), buf, wide)
     d_proj = gate_grads(jnp.where(inside, d_right, 0.0), mask, sig, proj[WIDTH:])
 
-    @pl.when(step == 0)
-    def start():
-        g_ref[...] = so_far[...]
-
-    g_ref[...] += mm(normed, d_proj, NT)
+    g_ref[...] = so_far[...] + mm(normed, d_proj, NT)
     d_normed = part_ref[...] + mm(w_ref[...], d_proj, NN)
     d_pair = norm_back_channels(d_normed, centred, inverse, gain).astype(BF16)
     out_ref[...] = to_cells(d_pair).astype(BF16).reshape(SUB, HALF, WIDTH)
@@ -377,31 +376,29 @@
 WIDE = pltpu.VMEM((WIDTH, LANES), F32)
 PANEL = jax.ShapeDtypeStruct((HALF, SUB, WIDTH), BF16)
 PANEL_SPEC = pl.BlockSpec((GROUP, SUB, WIDTH), lambda i: (i, 0, 0))
-FOUR = jax.ShapeDtypeStruct((4, HALF, SUB, WIDTH), BF16)
-FOUR_SPEC = pl.BlockSpec((4, GROUP, SUB, WIDTH), lambda i: (0, i, 0, 0))
-TWO = jax.ShapeDtypeStruct((2, HALF, SUB, WIDTH), BF16)
-TWO_SPEC = pl.BlockSpec((2, GROUP, SUB, WIDTH), lambda i: (0, i, 0, 0))
+FOUR = jax.ShapeDtypeStruct((4, HALF, PAIR, WIDTH), BF16)
+FOUR_SPEC = pl.BlockSpec((4, GROUP, PAIR, WIDTH), lambda i: (0, i, 0, 0))
+TWO = jax.ShapeDtypeStruct((2, HALF, PAIR, WIDTH), BF16)
+TWO_SPEC = pl.BlockSpec((2, GROUP, PAIR, WIDTH), lambda i: (0, i, 0, 0))
 LEFT_SPEC = pl.BlockSpec((GROUP, 2, HALF, WIDTH), lambda i: (i, 0, 0, 0))
-LONG = jax.ShapeDtypeStruct((HALF, PART, WIDTH), BF16)
-LONG_SPEC = pl.BlockSpec((GROUP, PART, WIDTH), lambda i: (i, 0, 0))
+LONG = jax.ShapeDtypeStruct((HALF, PAIR, WIDTH), BF16)
+LONG_SPEC = pl.BlockSpec((GROUP, PAIR, WIDTH), lambda i: (i, 0, 0))
 WHOLE_PANEL = pl.BlockSpec(PANEL.shape, lambda i: (0, 0, 0))
 
 
 def right_part(s, pair, gain, w_proj, tokens, exponents):
-    steps = PART // SUB
-    return pl.pallas_call(
-        functools.partial(right_kernel, s * steps),
-        grid=(steps,),
-        out_shape=LONG,
+    return pl.pallas_call(
+        functools.partial(right_kernel, s),
+        grid=(1,),
+        out_shape=PANEL,
         in_specs=[
-            pl.BlockSpec((SUB, HALF, WIDTH), lambda i: (s * steps + i, 0, 0)),
-            whole(gain), block((WIDTH, 2 * WIDTH), (0, 1)), whole(tokens),
-            pl.BlockSpec((SUB, HALF), lambda i: (s * steps + i, 0)),
+            block((SUB, HALF, WIDTH), (s, 0, 0)), whole(gain), block((WIDTH, 2 * WIDTH), (0, 1)),
+            whole(tokens), block((SUB, HALF), (s, 0)),
         ],
-        out_specs=pl.BlockSpec((HALF, SUB, WIDTH), lambda i: (0, i, 0)),
+        out_specs=WHOLE_PANEL,
         scratch_shapes=[BUF],
         compiler_params=params(),
-        cost_estimate=cost(8 * LANES * WIDTH * WIDTH, 1 << 20, 2 * LANES * WIDTH),
+        cost_estimate=cost(4 * LANES * WIDTH * WIDTH, 1 << 19, LANES * WIDTH),
         name="right_part",
     )(pair, gain, w_proj, tokens, exponents)
 
@@ -423,34 +420,36 @@
     )(pair, gain, w_proj, tokens)
 
 
-def tri_part(at, slots, left):
+def tri_part(slots, left):
     return pl.pallas_call(
         tri_kernel,
         grid=(HALF // GROUP,),
-        out_shape=(PANEL, PANEL, TWO, FOUR),
-        in_specs=[pl.BlockSpec((GROUP, SUB, WIDTH), lambda i: (i, at, 0))] * 4 + [LEFT_SPEC],
-        out_specs=(PANEL_SPEC, PANEL_SPEC, TWO_SPEC, FOUR_SPEC),
-        compiler_params=params(),
-        cost_estimate=cost(2 * HALF * HALF * WIDTH * WIDTH, 5 << 20),
+        out_shape=(LONG, LONG, TWO, FOUR),
+        in_specs=[PANEL_SPEC] * 8 + [LEFT_SPEC],
+        out_specs=(LONG_SPEC, LONG_SPEC, TWO_SPEC, FOUR_SPEC),
+        compiler_params=params(),
+        cost_estimate=cost(4 * HALF * HALF * WIDTH * WIDTH, 8 << 20),
         name="tri_part",
     )(*slots, left)
 
 
 def mid_part(s, parts, pair, grad, gain_in, gain_out, w_gate, w_out, g_out, g_gate):
     square = jax.ShapeDtypeStruct((WIDTH, WIDTH), F32)
-    columns = block((HALF, SUB, WIDTH), (0, s, 0))
+    steps = PAIR // SUB
+    columns = pl.BlockSpec((HALF, SUB, WIDTH), lambda i: (0, s * steps + i, 0))
+    panel = pl.BlockSpec((HALF, SUB, WIDTH), lambda i: (0, i, 0))
     small = [gain_in, gain_out, w_gate, w_out, g_out, g_gate]
     return pl.pallas_call(
         mid_kernel,
-        grid=(1,),
-        out_shape=(PANEL, pltpu.HBM(PANEL.shape, BF16), square, square),
-        in_specs=[WHOLE_PANEL, block((1, HALF, SUB, WIDTH), (0, 0, 0, 0)), WHOLE_PANEL]
+        grid=(steps,),
+        out_shape=(LONG, LONG, square, square),
+        in_specs=[panel, pl.BlockSpec((1, HALF, SUB, WIDTH), lambda i: (0, 0, i, 0)), panel]
         + [columns] * 2
         + [whole(a) for a in small],
-        out_specs=(WHOLE_PANEL, WHOLE_PANEL, block(square.shape, (0, 0)), block(square.shape, (0, 0))),
+        out_specs=(panel, panel, block(square.shape, (0, 0)), block(square.shape, (0, 0))),
         scratch_shapes=[BUF, WIDE],
         compiler_params=params(),
-        cost_estimate=cost(12 * LANES * WIDTH * WIDTH, 2 << 20, LANES * WIDTH),
+        cost_estimate=cost(24 * LANES * WIDTH * WIDTH, 4 << 20, 2 * LANES * WIDTH),
         name="mid_part",
     )(*parts, pair, grad, *small)
 
@@ -459,28 +458,28 @@
     return pl.pallas_call(
         dright_kernel,
         grid=(HALF // GROUP,),
-        out_shape=(pltpu.HBM(LONG.shape, BF16), LONG, LONG, LONG),
-        in_specs=[PANEL_SPEC] * len(blocks) + [LEFT_SPEC],
-        out_specs=(LONG_SPEC,) * 4,
-        scratch_shapes=[pltpu.VMEM((4, GROUP, PART, WIDTH), BF16)],
+        out_shape=(PANEL,) * 8,
+        in_specs=[LONG_SPEC] * 4 + [LEFT_SPEC],
+        out_specs=(PANEL_SPEC,) * 8,
+        scratch_shapes=[pltpu.VMEM((4, GROUP, PAIR, WIDTH), BF16)],
         compiler_params=params(),
         cost_estimate=cost(4 * HALF * HALF * WIDTH * WIDTH, 6 << 20),
         name="dright_part",
     )(*blocks, left)
 
 
-def dleft_part(grads, panels, so_far):
+def dleft_part(grads, panel, so_far):
     rows = pl.BlockSpec((GROUP, HALF, WIDTH), lambda i: (i, 0, 0))
     return pl.pallas_call(
         dleft_kernel,
         grid=(HALF // GROUP,),
         out_shape=jax.ShapeDtypeStruct((HALF, HALF, WIDTH), F32),
-        in_specs=[PANEL_SPEC] * len(grads) + [FOUR_SPEC] * len(panels) + [rows],
+        in_specs=[LONG_SPEC] * 4 + [FOUR_SPEC, rows],
         out_specs=rows,
         compiler_params=params(),
         cost_estimate=cost(4 * HALF * HALF * WIDTH * WIDTH, 8 << 20),
         name="dleft_part",
-    )(*grads, *panels, so_far)
+    )(*grads, panel, so_far)
 
 
 def final_a_part(pair, dleft, tokens, gain, w_proj, w_gate, gates):
@@ -496,7 +495,7 @@
             pl.BlockSpec((HALF, SUB, WIDTH), lambda i: (0, i, 0)),
             whole(tokens), whole(gain), block((WIDTH, 2 * WIDTH), (0, 0)), whole(w_gate),
         ]
-        + [pl.BlockSpec((SUB, SUB, WIDTH), lambda i: (i, 0, 0))] * 4,
+        + [pl.BlockSpec((SUB, PAIR, WIDTH), lambda i: (i, 0, 0))] * 2,
         out_specs=(
             pl.BlockSpec((WIDTH, LANES), lambda i: (0, i)),
             block((WIDTH, 2 * WIDTH), (0, 0)),
@@ -509,29 +508,24 @@
 
 
 def final_b_part(s, pair, part, sums, tokens, exponents, gain, w_proj, so_far, into):
-    steps = PART // SUB
-    rows = pl.BlockSpec((SUB, HALF, WIDTH), lambda i: (s * steps + i, 0, 0))
-    panel = pl.BlockSpec((HALF, SUB, WIDTH), lambda i: (0, i, 0))
-    return pl.pallas_call(
-        functools.partial(final_b_kernel, s * steps),
-        grid=(steps,),
+    rows = block((SUB, HALF, WIDTH), (s, 0, 0))
+    return pl.pallas_call(
+        functools.partial(final_b_kernel, s),
+        grid=(1,),
         out_shape=(
             jax.ShapeDtypeStruct((HALF, HALF, WIDTH), BF16),
             jax.ShapeDtypeStruct((WIDTH, 2 * WIDTH), F32),
         ),
         in_specs=[
-            rows,
-            pl.BlockSpec((WIDTH, LANES), lambda i: (0, s * steps + i)),
-            panel, panel, whole(tokens),
-            pl.BlockSpec((SUB, HALF), lambda i: (s * steps + i, 0)),
-            whole(gain), block((WIDTH, 2 * WIDTH), (0, 1)), whole(so_far),
+            rows, block((WIDTH, LANES), (0, s)), WHOLE_PANEL, WHOLE_PANEL, whole(tokens),
+            block((SUB, HALF), (s, 0)), whole(gain), block((WIDTH, 2 * WIDTH), (0, 1)), whole(so_far),
             pl.BlockSpec(memory_space=pl.ANY),
         ],
         out_specs=(rows, block((WIDTH, 2 * WIDTH), (0, 0))),
         scratch_shapes=[BUF, WIDE],
         input_output_aliases={9: 0} if into.shape == pair.shape else {},
         compiler_params=params(),
-        cost_estimate=cost(28 * LANES * WIDTH * WIDTH, 4 << 20, 2 * LANES * WIDTH),
+        cost_estimate=cost(14 * LANES * WIDTH * WIDTH, 2 << 20, LANES * WIDTH),
         name="final_b_part",
     )(pair, part, *sums, tokens, exponents, gain, w_proj, so_far, into)
 
@@ -564,7 +558,10 @@
         return (a.astype(F32) + b.astype(F32)).astype(BF16)
 
     def right(s):
-        return right_part(s, pair_tiles, gain_in, w_proj, tokens, exponents)
+        operands = (pair_tiles, gain_in, w_proj, tokens, exponents)
+        if s == 0:
+            operands = [pltpu.with_memory_space_constraint(a, pltpu.HBM) for a in operands]
+        return right_part(s, *operands)
 
     a0, b0 = right(0), right(1)
     left = left_part(pair_tiles, gain_in, w_proj, tokens)
@@ -574,12 +571,13 @@
     a3, b3 = forward(after(a2, c0)), forward(after(b2, d0))
     c1, d1 = forward(after(c0, b2)), forward(after(d0, a3))
 
+    g_out = g_gate = jnp.zeros((width, width), F32)
+    d_left = jnp.zeros((HALF, HALF, WIDTH), F32)
+
     def triangle(slots):
-        keep, near, send, panel = tri_part(0, slots, left)
+        keep, near, send, panel = tri_part(slots, left)
         got = over_core(send)
         return keep, got, plus(near, got[1]), panel
-
-    g_out = g_gate = jnp.zeros((width, width), F32)
 
     def middle(s, tri, mine):
         return mid_part(
@@ -590,51 +588,35 @@
         far = over_x(d_tri)
         return [d_tri, far, over_core(d_tri), over_core(far)]
 
-    def dright(blocks, *others):
-        return dright_part([blocks[0], blocks[1], blocks[2], after(blocks[3], *others)], left)
-
-    tri_a, tri_b = triangle([a0, a1, a2, a3]), triangle([b0, b1, b2, b3])
-    x_a, x_b = over_x(tri_a[2]), over_x(tri_b[2])
-    c2, d2 = forward(after(c1, tri_a[2])), forward(after(d1, tri_b[2]))
-    dtri_a, gate_a, g_out, g_gate = middle(0, tri_a, after(x_a, d1))
-    blocks_a = spread(dtri_a)
-    dtri_b, gate_b, g_out, g_gate = middle(1, tri_b, after(x_b, c2))
-    blocks_b = spread(dtri_b)
-    c3, d3 = forward(after(c2, dtri_a)), forward(after(d2, dtri_b))
-    part_a = dright(blocks_a, d2)
-    part_b = dright(blocks_b, c3)
+    ab = triangle([a0, a1, a2, a3, b0, b1, b2, b3])
+    x_ab = over_x(ab[2])
+    c2, d2 = forward(after(c1, ab[0])), forward(after(d1, ab[2]))
+    dtri_ab, gate_ab, g_out, g_gate = middle(0, ab, after(x_ab, c2))
+    blocks_ab = spread(dtri_ab)
+    c3, d3 = forward(c2), forward(after(d2, dtri_ab))
+
+    cd = triangle([c0, c1, c2, c3, d0, d1, d2, d3])
+    x_cd = over_x(cd[2])
+    part = dright_part([after(blocks_ab[0], cd[2])] + blocks_ab[1:], left)
+    part_a, part_b = part[:4], part[4:]
     r_a, r_b = forward(part_a[1]), forward(part_b[1])
-
-    tri_c = triangle([c0, c1, c2, after(c3, part_a[1])])
-    tri_d = triangle([d0, d1, d2, after(d3, part_b[1])])
-    x_c, x_d = over_x(tri_c[2]), over_x(tri_d[2])
+    d_left = dleft_part([after(blocks_ab[0], part_b[1])] + blocks_ab[1:], ab[3], d_left)
     r_a = plus(r_a, part_a[2])
-    r_a2 = forward(after(r_a, tri_c[2]))
+    r_a2 = forward(r_a)
     r_b = plus(r_b, part_b[2])
-    r_b2 = forward(after(r_b, tri_d[2]))
-    d_left = dleft_part(
-        [after(blocks_a[0], tri_d[2])] + blocks_a[1:] + blocks_b,
-        [tri_a[3], tri_b[3]],
-        jnp.zeros((HALF, HALF, WIDTH), F32),
-    )
-    dtri_c, gate_c, g_out, g_gate = middle(2, tri_c, after(x_c, r_a, d_left))
-    blocks_c = spread(dtri_c)
-    dtri_d, gate_d, g_out, g_gate = middle(3, tri_d, after(x_d, r_b))
-    blocks_d = spread(dtri_d)
+    dtri_cd, gate_cd, g_out, g_gate = middle(1, cd, after(x_cd, r_a, d_left))
+    blocks_cd = spread(dtri_cd)
+    r_b2 = forward(after(r_b, dtri_cd))
     r_a2 = plus(r_a2, part_a[3])
-    r_a3 = forward(after(r_a2, dtri_c))
+    r_a3 = forward(r_a2)
     r_b2 = plus(r_b2, part_b[3])
-    r_b3 = forward(after(r_b2, dtri_d))
-    part_c = dright(blocks_c, r_a2)
-    part_d = dright(blocks_d, r_b2)
+    r_b3 = forward(r_b2)
+    part = dright_part([after(blocks_cd[0], r_a2, r_b2)] + blocks_cd[1:], left)
+    part_c, part_d = part[:4], part[4:]
 
     r_c, r_d = forward(part_c[1]), forward(part_d[1])
-    d_left = dleft_part(
-        [after(blocks_c[0], part_d[1])] + blocks_c[1:] + blocks_d, [tri_c[3], tri_d[3]], d_left
-    )
-    partial, g_a = final_a_part(
-        pair_tiles, d_left, tokens, gain_in, w_proj, w_gate, [gate_a, gate_b, gate_c, gate_d]
-    )
+    d_left = dleft_part([after(blocks_cd[0], part_d[1])] + blocks_cd[1:], cd[3], d_left)
+    partial, g_a = final_a_part(pair_tiles, d_left, tokens, gain_in, w_proj, w_gate, [gate_ab, gate_cd])
     r_c = forward(plus(r_c, part_c[2]))
     r_d = forward(plus(r_d, part_d[2]))
     zero = jnp.zeros((width, 2 * width), F32)

time: 210 us -> 216 us (1.029)
  waiting for transfers between devices: 76.1 us -> 93.9 us
  Pallas kernels: 61.1 us -> 51.3 us
  starting transfers between devices: 56.3 us -> 52.6 us
    ppermute x24, waiting for transfers between devices: 45.4 us -> 57.8 us  [forward(): return lax.ppermute(a, 'row', [(0, 1), (1, 3), (3, 2), (2, 0)])]
    pallas_call x20 -> x14, Pallas kernels: 46.3 us -> 36.3 us  [the longest x2 13.1 us: mid_part(): pl.pallas_call(mid_kernel, grid=(steps,), out_shape=(LONG, LONG, square,...]
    ppermute x10 -> x6, waiting for transfers between devices: 21.3 us -> 25.1 us  [over_x(): return lax.ppermute(a, 'col', [(k, k ^ 2) for k in range(4)])]
    ppermute x24, starting transfers between devices: 40.7 us -> 38.3 us  [forward(): return lax.ppermute(a, 'row', [(0, 1), (1, 3), (3, 2), (2, 0)])]
    unnamed x65 -> x61, local copies, waits for them, and re-layouts: 8.2 us -> 10.1 us
    ppermute x15 -> x9, waiting for transfers between devices: 2.71 us -> 4.59 us  [over_core(): return lax.ppermute(a, 'col', [(k, k ^ 1) for k in range(4)])]
    ppermute x10 -> x6, starting transfers between devices: 10.6 us -> 9.47 us  [over_x(): return lax.ppermute(a, 'col', [(k, k ^ 2) for k in range(4)])]
    convert_element_type x12 -> x10, other arithmetic: 4.33 us -> 4.51 us  [plus(): return (a.astype(F32) + b.astype(F32)).astype(BF16)]
  transfers between devices with their start and end apart: 51 -> 41, of which waited for: 25 -> 24; matrix products, arithmetic and copies ran while one was open for 3% -> 2% of each run, Pallas kernels for 28% -> 20%
where the time goes in v6:
time: 216 us; the launch traced here: 215 us
  waiting for transfers between devices  93.9 us (43%)
  starting transfers between devices  52.6 us (24%)
  Pallas kernels  51.3 us (24%)
  local copies, waits for them, and re-layouts  10.4 us (5%)
  other arithmetic  6.07 us (3%)
    ppermute x24, waiting for transfers between devices, forward(): return lax.ppermute(a, 'row', [(0, 1), (1, 3), (3, 2), (2, 0)])  57.8 us
    ppermute x24, starting transfers between devices, forward(): return lax.ppermute(a, 'row', [(0, 1), (1, 3), (3, 2), (2, 0)])  38.3 us
    ppermute x6, waiting for transfers between devices, over_x(): return lax.ppermute(a, 'col', [(k, k ^ 2) for k in range(4)])  25.1 us
    pallas_call x2, Pallas kernels, mid_part(): pl.pallas_call(mid_kernel, grid=(steps,), out_shape=(LONG, LONG, square,...  13.1 us
    unnamed x61, local copies, waits for them, and re-layouts  10.1 us
    ppermute x6, starting transfers between devices, over_x(): return lax.ppermute(a, 'col', [(k, k ^ 2) for k in range(4)])  9.47 us
    pallas_call x4, Pallas kernels, final_b_part(): pl.pallas_call(functools.partial(final_b_kernel, s), grid=(1,), out_shape...  8.48 us
    ppermute x2, waiting for transfers between devices, over_row(): return lax.ppermute(a, 'row', [(k, k ^ bit) for k in range(4)])  6.43 us
  transfers between devices with their start and end apart: 41, of which 24 were waited for; matrix products, arithmetic and copies ran while one was open for 2% of the time, Pallas kernels for 20%

profile of v6, /device:TPU:0, one launch (start us, length us, event | category | flops | bytes accessed | tf_op | source)
XLA Modules:
  0.0 215.4 jit_solution(2369803900520914476)
XLA Ops:
  5.9 3.1 %collective-permute-start = (bf16[64,16,128]{2,1,0:T(8,128)(2,1)S(1)}, bf16[64,16,128]{2,1,0:T(8,128)(2,1)S(1)}, u32[]{:S(2)}, u32[]{:S(2)}) collective-permute-start(bf16[64,16,128]{2,1,0:T(8,128)(2,1)S(1)} %right_part.5.refs_4_), channel_id=1, source_target_pairs={{0,4},{4,12},{12,8},{8,0},{1,5},{5,13},{13,9},{9,1},{2,6},{6,14},{... | collective-permute-start | bytes 786440 | tf_op jit(solution)/shard_map/ppermute | solution.py:546
  10.9 2.6 %collective-permute-start.3 = (bf16[64,16,128]{2,1,0:T(8,128)(2,1)S(1)}, bf16[64,16,128]{2,1,0:T(8,128)(2,1)S(1)}, u32[]{:S(2)}, u32[]{:S(2)}) collective-permute-start(bf16[64,16,128]{2,1,0:T(8,128)(2,1)S(1)} %right_part.6.refs_0_), channel_id=1, source_target_pairs={{0,4},{4,12},{12,8},{8,0},{1,5},{5,13},{13,9},{9,1},{2,6},{6,14},{... | collective-permute-start | bytes 786440 | tf_op jit(solution)/shard_map/ppermute | solution.py:546
  13.5 4.3 %left_part.1.refs_8_.left_ref = bf16[64,2,64,128]{3,2,1,0:T(8,128)(2,1)S(1)} custom-call(bf16[64,64,128]{2,1,0:T(8,128)(2,1)S(1)} %copy-done.1, f32[1,128]{1,0:T(1,128)S(1)} %bitcast.25, bf16[128,512]{1,0:T(8,128)(2,1)S(1)} %copy-done.3, s32[1,256]{1,0:T(1,128)S(1)} %bitcast.15), custom_call_target="tpu_custom_call" | custom-call | flops 268435456 | bytes 3145728 | tf_op jit(solution)/shard_map/left_part/pallas_call | solution.py:407
  18.3 4.4 %collective-permute-done.3.refs_1_ = bf16[64,16,128]{2,1,0:T(8,128)(2,1)S(1)} collective-permute-done((bf16[64,16,128]{2,1,0:T(8,128)(2,1)S(1)}, bf16[64,16,128]{2,1,0:T(8,128)(2,1)S(1)}, u32[]{:S(2)}, u32[]{:S(2)}) %collective-permute-start.3) | collective-permute-done | bytes 262176 | tf_op jit(solution)/shard_map/ppermute | solution.py:546
  25.8 2.5 %collective-permute-done.1.refs_6_ = bf16[64,16,128]{2,1,0:T(8,128)(2,1)S(1)} collective-permute-done((bf16[64,16,128]{2,1,0:T(8,128)(2,1)S(1)}, bf16[64,16,128]{2,1,0:T(8,128)(2,1)S(1)}, u32[]{:S(2)}, u32[]{:S(2)}) %collective-permute-start.1) | collective-permute-done | bytes 262176 | tf_op jit(solution)/shard_map/ppermute | solution.py:546
  29.5 4.5 %collective-permute-done.4.refs_2_ = bf16[64,16,128]{2,1,0:T(8,128)(2,1)S(1)} collective-permute-done((bf16[64,16,128]{2,1,0:T(8,128)(2,1)S(1)}, bf16[64,16,128]{2,1,0:T(8,128)(2,1)S(1)}, u32[]{:S(2)}, u32[]{:S(2)}) %collective-permute-start.4) | collective-permute-done | bytes 262176 | tf_op jit(solution)/shard_map/ppermute | solution.py:546
  35.1 4.5 %collective-permute-done.6.refs_7_ = bf16[64,16,128]{2,1,0:T(8,128)(2,1)S(1)} collective-permute-done((bf16[64,16,128]{2,1,0:T(8,128)(2,1)S(1)}, bf16[64,16,128]{2,1,0:T(8,128)(2,1)S(1)}, u32[]{:S(2)}, u32[]{:S(2)}) %collective-permute-start.6) | collective-permute-done | bytes 262176 | tf_op jit(solution)/shard_map/ppermute | solution.py:546
  39.6 4.8 %collective-permute-done.5.refs_3_ = bf16[64,16,128]{2,1,0:T(8,128)(2,1)S(1)} collective-permute-done((bf16[64,16,128]{2,1,0:T(8,128)(2,1)S(1)}, bf16[64,16,128]{2,1,0:T(8,128)(2,1)S(1)}, u32[]{:S(2)}, u32[]{:S(2)}) %collective-permute-start.5) | collective-permute-done | bytes 262176 | tf_op jit(solution)/shard_map/ppermute | solution.py:546
  52.7 4.1 %collective-permute-done.2.refs_1_ = bf16[64,16,128]{2,1,0:T(8,128)(2,1)S(1)} collective-permute-done((bf16[64,16,128]{2,1,0:T(8,128)(2,1)S(1)}, bf16[64,16,128]{2,1,0:T(8,128)(2,1)S(1)}, u32[]{:S(2)}, u32[]{:S(2)}) %collective-permute-start.2) | collective-permute-done | bytes 262176 | tf_op jit(solution)/shard_map/ppermute | solution.py:546
  57.6 4.8 %collective-permute-done.9.refs_5_ = bf16[64,16,128]{2,1,0:T(8,128)(2,1)S(1)} collective-permute-done((bf16[64,16,128]{2,1,0:T(8,128)(2,1)S(1)}, bf16[64,16,128]{2,1,0:T(8,128)(2,1)S(1)}, u32[]{:S(2)}, u32[]{:S(2)}) %collective-permute-start.9) | collective-permute-done | bytes 262176 | tf_op jit(solution)/shard_map/ppermute | solution.py:546
  63.2 4.8 %collective-permute-done.7.refs_2_ = bf16[64,16,128]{2,1,0:T(8,128)(2,1)S(1)} collective-permute-done((bf16[64,16,128]{2,1,0:T(8,128)(2,1)S(1)}, bf16[64,16,128]{2,1,0:T(8,128)(2,1)S(1)}, u32[]{:S(2)}, u32[]{:S(2)}) %collective-permute-start.7) | collective-permute-done | bytes 262176 | tf_op jit(solution)/shard_map/ppermute | solution.py:546
  68.9 6.3 %mid_part.2 = (bf16[64,32,128]{2,1,0:T(8,128)(2,1)S(1)}, bf16[64,32,128]{2,1,0:T(8,128)(2,1)S(1)}, f32[128,128]{1,0:T(8,128)S(1)}, f32[128,128]{1,0:T(8,128)S(1)}) custom-call(bf16[64,32,128]{2,1,0:T(8,128)(2,1)S(1)} %get-tuple-element.66.a_ref, bf16[2,64,32,128]{3,2,1,0:T(8,128)(2,1)S(1)} %collective-permute-done.10.b_ref, ...), custom_call_target="tpu_custom_call" | custom-call | flops 402653184 | bytes 4194304 | tf_op jit(solution)/shard_map/mid_part/pallas_call | solution.py:442
  76.0 3.4 %collective-permute-start.13 = (bf16[64,16,128]{2,1,0:T(8,128)(2,1)S(1)}, bf16[64,16,128]{2,1,0:T(8,128)(2,1)S(1)}, u32[]{:S(2)}, u32[]{:S(2)}) collective-permute-start(bf16[64,16,128]{2,1,0:T(8,128)(2,1)S(1)} %collective-permute-done.11.refs_6_), channel_id=1, source_target_pairs={{0,4},{4,12},{12,8},{8,0},{1,5},{5,13},{13,9},{9,1},{2,6},{6,14},{... | collective-permute-start | bytes 786440 | tf_op jit(solution)/shard_map/ppermute | solution.py:546
  79.4 5.0 %collective-permute-done.13.refs_7_ = bf16[64,16,128]{2,1,0:T(8,128)(2,1)S(1)} collective-permute-done((bf16[64,16,128]{2,1,0:T(8,128)(2,1)S(1)}, bf16[64,16,128]{2,1,0:T(8,128)(2,1)S(1)}, u32[]{:S(2)}, u32[]{:S(2)}) %collective-permute-start.13) | collective-permute-done | bytes 262176 | tf_op jit(solution)/shard_map/ppermute | solution.py:546
  89.8 12.6 %collective-permute-done.16.d1 = bf16[64,32,128]{2,1,0:T(8,128)(2,1)S(1)} collective-permute-done((bf16[64,32,128]{2,1,0:T(8,128)(2,1)S(1)}, bf16[64,32,128]{2,1,0:T(8,128)(2,1)S(1)}, u32[]{:S(2)}, u32[]{:S(2)}) %collective-permute-start.16) | collective-permute-done | bytes 524320 | tf_op jit(solution)/shard_map/ppermute | solution.py:552
  115.4 3.9 %collective-permute-done.19 = bf16[64,16,128]{2,1,0:T(8,128)(2,1)S(1)} collective-permute-done((bf16[64,16,128]{2,1,0:T(8,128)(2,1)S(1)}, bf16[64,16,128]{2,1,0:T(8,128)(2,1)S(1)}, u32[]{:S(2)}, u32[]{:S(2)}) %collective-permute-start.19) | collective-permute-done | bytes 262176 | tf_op jit(solution)/shard_map/ppermute | solution.py:546
  120.2 6.9 %mid_part.3 = (bf16[64,32,128]{2,1,0:T(8,128)(2,1)}, bf16[64,32,128]{2,1,0:T(8,128)(2,1)S(1)}, f32[128,128]{1,0:T(8,128)S(1)}, f32[128,128]{1,0:T(8,128)S(1)}) custom-call(bf16[64,32,128]{2,1,0:T(8,128)(2,1)S(1)} %get-tuple-element.75.a_ref, bf16[2,64,32,128]{3,2,1,0:T(8,128)(2,1)S(1)} %collective-permute-done.14.b_ref, ...), custom_call_target="tpu_custom_call" | custom-call | flops 402653184 | bytes 4194304 | tf_op jit(solution)/shard_map/mid_part/pallas_call | solution.py:442
  131.8 3.0 %collective-permute-start.22 = (bf16[64,16,128]{2,1,0:T(8,128)(2,1)S(1)}, bf16[64,16,128]{2,1,0:T(8,128)(2,1)S(1)}, u32[]{:S(2)}, u32[]{:S(2)}) collective-permute-start(bf16[64,16,128]{2,1,0:T(8,128)(2,1)S(1)} %add_convert_fusion.5), channel_id=1, source_target_pairs={{0,4},{4,12},{12,8},{8,0},{1,5},{5,13},{13,9},{9,1},{2,6},{6,14},{... | collective-permute-start | bytes 786440 | tf_op jit(solution)/shard_map/ppermute | solution.py:546
  134.8 5.7 %collective-permute-done.23.d1 = bf16[64,32,128]{2,1,0:T(8,128)(2,1)} collective-permute-done((bf16[64,32,128]{2,1,0:T(8,128)(2,1)}, bf16[64,32,128]{2,1,0:T(8,128)(2,1)}, u32[]{:S(2)}, u32[]{:S(2)}) %collective-permute-start.23) | collective-permute-done | bytes 524320 | tf_op jit(solution)/shard_map/ppermute | solution.py:552
  143.8 3.1 %collective-permute-start.32 = (bf16[64,16,128]{2,1,0:T(8,128)(2,1)S(1)}, bf16[64,16,128]{2,1,0:T(8,128)(2,1)S(1)}, u32[]{:S(2)}, u32[]{:S(2)}) collective-permute-start(bf16[64,16,128]{2,1,0:T(8,128)(2,1)S(1)} %add_convert_fusion.4), channel_id=1, source_target_pairs={{0,4},{4,12},{12,8},{8,0},{1,5},{5,13},{13,9},{9,1},{2,6},{6,14},{... | collective-permute-start | bytes 786440 | tf_op jit(solution)/shard_map/ppermute | solution.py:546
  147.0 3.2 %dright_part.3 = (bf16[64,16,128]{2,1,0:T(8,128)(2,1)S(1)}, bf16[64,16,128]{2,1,0:T(8,128)(2,1)S(1)}, bf16[64,16,128]{2,1,0:T(8,128)(2,1)S(1)}, bf16[64,16,128]{...) custom-call(bf16[64,32,128]{2,1,0:T(8,128)(2,1)} %get-tuple-element., ...), custom_call_target="tpu_custom_call" | custom-call | flops 268435456 | bytes 6291456 | tf_op jit(solution)/shard_map/dright_part/pallas_call | solution.py:458
  151.2 3.2 %dleft_part.3.dleft_ref = f32[64,64,128]{2,1,0:T(8,128)S(1)} custom-call(bf16[64,32,128]{2,1,0:T(8,128)(2,1)} %get-tuple-element.94.d0, bf16[64,32,128]{2,1,0:T(8,128)(2,1)} %collective-permute-done.23.d1, bf16[64,32,128]{2,1,0:T(8,128)(2,1)S(1)} %collective-permute-done.24.d2, bf16[64,32,128]{2,1,0:T(8,128)(2,1)S(1)} %collective-permute-done.25.d3, ...), custom_call_target="tpu_custom_call" | custom-call | flops 268435456 | bytes 8388608 | tf_op jit(solution)/shard_map/dleft_part/pallas_call | solution.py:473
  154.4 5.9 %final_a_part.1 = (f32[128,4096]{1,0:T(8,128)S(1)}, f32[128,256]{1,0:T(8,128)S(1)}) custom-call(bf16[64,64,128]{2,1,0:T(8,128)(2,1)S(1)} %copy-done.1, f32[64,64,128]{2,1,0:T(8,128)S(1)} %dleft_part.3.dleft_ref, s32[1,256]{1,0:T(1,128)S(1)} %bitcast.18, f32[1,128]{1,0:T(1,128)S(1)} %bitcast.30, bf16[128,512]{1,0:T(8,128)(2,1)S(1)} %copy-done.3, ...), custom_call_target="tpu_custom_call" | custom-call | flops 939524096 | bytes 8388608 | tf_op jit(solution)/shard_map/final_a_part/pallas_call | solution.py:486
  164.6 3.4 %collective-permute-done.29 = bf16[64,16,128]{2,1,0:T(8,128)(2,1)S(1)} collective-permute-done((bf16[64,16,128]{2,1,0:T(8,128)(2,1)S(1)}, bf16[64,16,128]{2,1,0:T(8,128)(2,1)S(1)}, u32[]{:S(2)}, u32[]{:S(2)}) %collective-permute-start.29) | collective-permute-done | bytes 262176 | tf_op jit(solution)/shard_map/ppermute | solution.py:546
  169.1 3.4 %collective-permute-start.27 = (bf16[64,16,128]{2,1,0:T(8,128)(2,1)S(1)}, bf16[64,16,128]{2,1,0:T(8,128)(2,1)S(1)}, u32[]{:S(2)}, u32[]{:S(2)}) collective-permute-start(bf16[64,16,128]{2,1,0:T(8,128)(2,1)S(1)} %add_convert_fusion.3), channel_id=1, source_target_pairs={{0,4},{4,12},{12,8},{8,0},{1,5},{5,13},{13,9},{9,1},{2,6},{6,14},{... | collective-permute-start | bytes 786440 | tf_op jit(solution)/shard_map/ppermute | solution.py:546
  172.7 5.7 %collective-permute-done.30 = bf16[64,16,128]{2,1,0:T(8,128)(2,1)S(1)} collective-permute-done((bf16[64,16,128]{2,1,0:T(8,128)(2,1)S(1)}, bf16[64,16,128]{2,1,0:T(8,128)(2,1)S(1)}, u32[]{:S(2)}, u32[]{:S(2)}) %collective-permute-start.30) | collective-permute-done | bytes 262176 | tf_op jit(solution)/shard_map/ppermute | solution.py:546
  179.3 4.6 %collective-permute-done.27 = bf16[64,16,128]{2,1,0:T(8,128)(2,1)S(1)} collective-permute-done((bf16[64,16,128]{2,1,0:T(8,128)(2,1)S(1)}, bf16[64,16,128]{2,1,0:T(8,128)(2,1)S(1)}, u32[]{:S(2)}, u32[]{:S(2)}) %collective-permute-start.27) | collective-permute-done | bytes 262176 | tf_op jit(solution)/shard_map/ppermute | solution.py:546
  186.7 4.2 %collective-permute-done.35 = f32[64,768]{1,0:T(8,128)S(1)} collective-permute-done((f32[64,768]{1,0:T(8,128)S(1)}, f32[64,768]{1,0:T(8,128)S(1)}, u32[]{:S(2)}, u32[]{:S(2)}) %collective-permute-start.35) | collective-permute-done | bytes 196640 | tf_op jit(solution)/shard_map/ppermute | solution.py:552
  198.9 2.7 %collective-permute-done.37 = f32[64,256]{1,0:T(8,128)S(1)} collective-permute-done((f32[64,256]{1,0:T(8,128)S(1)}, f32[64,256]{1,0:T(8,128)S(1)}, u32[]{:S(2)}, u32[]{:S(2)}) %collective-permute-start.37) | collective-permute-done | bytes 65568 | tf_op jit(solution)/shard_map/ppermute | solution.py:552
  201.7 2.6 %collective-permute-start.38 = (bf16[64,768]{1,0:T(8,128)(2,1)S(1)}, bf16[64,768]{1,0:T(8,128)(2,1)S(1)}, u32[]{:S(2)}, u32[]{:S(2)}) collective-permute-start(bf16[64,768]{1,0:T(8,128)(2,1)S(1)} %pad_maximum_fusion), channel_id=1, source_target_pairs={{0,4},{4,0},{8,12},{12,8},{1,5},{5,1},{9,13},{13,9},{2,6},{6,2},{1... | collective-permute-start | bytes 294920 | tf_op jit(solution)/shard_map/ppermute | solution.py:549
  204.3 2.6 %collective-permute-done.38 = bf16[64,768]{1,0:T(8,128)(2,1)S(1)} collective-permute-done((bf16[64,768]{1,0:T(8,128)(2,1)S(1)}, bf16[64,768]{1,0:T(8,128)(2,1)S(1)}, u32[]{:S(2)}, u32[]{:S(2)}) %collective-permute-start.38) | collective-permute-done | bytes 98336 | tf_op jit(solution)/shard_map/ppermute | solution.py:549
  208.6 3.8 %collective-permute-done.39 = bf16[64,768]{1,0:T(8,128)(2,1)S(1)} collective-permute-done((bf16[64,768]{1,0:T(8,128)(2,1)S(1)}, bf16[64,768]{1,0:T(8,128)(2,1)S(1)}, u32[]{:S(2)}, u32[]{:S(2)}) %collective-permute-start.39) | collective-permute-done | bytes 98336 | tf_op jit(solution)/shard_map/ppermute | solution.py:549
  (156 shorter events, 74.9 us)
Async XLA Ops:
  5.9 11.9 %collective-permute-start = (bf16[64,16,128]{2,1,0:T(8,128)(2,1)S(1)}, bf16[64,16,128]{2,1,0:T(8,128)(2,1)S(1)}, u32[]{:S(2)}, u32[]{:S(2)}) collective-permute-start(bf16[64,16,128]{2,1,0:T(8,128)(2,1)S(1)} %right_part.5.refs_4_), channel_id=1, source_target_pairs={{0,4},{4,12},{12,8},{8,0},{1,5},{5,13},{13,9},{9,1},{2,6},{6,14},{... | collective-permute-start | bytes 786440 | tf_op jit(solution)/shard_map/ppermute | solution.py:546
  10.9 11.8 %collective-permute-start.3 = (bf16[64,16,128]{2,1,0:T(8,128)(2,1)S(1)}, bf16[64,16,128]{2,1,0:T(8,128)(2,1)S(1)}, u32[]{:S(2)}, u32[]{:S(2)}) collective-permute-start(bf16[64,16,128]{2,1,0:T(8,128)(2,1)S(1)} %right_part.6.refs_0_), channel_id=1, source_target_pairs={{0,4},{4,12},{12,8},{8,0},{1,5},{5,13},{13,9},{9,1},{2,6},{6,14},{... | collective-permute-start | bytes 786440 | tf_op jit(solution)/shard_map/ppermute | solution.py:546
  17.8 10.5 %collective-permute-start.1 = (bf16[64,16,128]{2,1,0:T(8,128)(2,1)S(1)}, bf16[64,16,128]{2,1,0:T(8,128)(2,1)S(1)}, u32[]{:S(2)}, u32[]{:S(2)}) collective-permute-start(bf16[64,16,128]{2,1,0:T(8,128)(2,1)S(1)} %collective-permute-done.refs_5_), channel_id=1, source_target_pairs={{0,4},{4,12},{12,8},{8,0},{1,5},{5,13},{13,9},{9,1},{2,6},{6,14},{... | collective-permute-start | bytes 786440 | tf_op jit(solution)/shard_map/ppermute | solution.py:546
  22.7 11.2 %collective-permute-start.4 = (bf16[64,16,128]{2,1,0:T(8,128)(2,1)S(1)}, bf16[64,16,128]{2,1,0:T(8,128)(2,1)S(1)}, u32[]{:S(2)}, u32[]{:S(2)}) collective-permute-start(bf16[64,16,128]{2,1,0:T(8,128)(2,1)S(1)} %collective-permute-done.3.refs_1_), channel_id=1, source_target_pairs={{0,4},{4,12},{12,8},{8,0},{1,5},{5,13},{13,9},{9,1},{2,6},{6,14},{... | collective-permute-start | bytes 786440 | tf_op jit(solution)/shard_map/ppermute | solution.py:546
  28.3 11.2 %collective-permute-start.6 = (bf16[64,16,128]{2,1,0:T(8,128)(2,1)S(1)}, bf16[64,16,128]{2,1,0:T(8,128)(2,1)S(1)}, u32[]{:S(2)}, u32[]{:S(2)}) collective-permute-start(bf16[64,16,128]{2,1,0:T(8,128)(2,1)S(1)} %collective-permute-done.1.refs_6_), channel_id=1, source_target_pairs={{0,4},{4,12},{12,8},{8,0},{1,5},{5,13},{13,9},{9,1},{2,6},{6,14},{... | collective-permute-start | bytes 786440 | tf_op jit(solution)/shard_map/ppermute | solution.py:546
  33.9 10.4 %collective-permute-start.5 = (bf16[64,16,128]{2,1,0:T(8,128)(2,1)S(1)}, bf16[64,16,128]{2,1,0:T(8,128)(2,1)S(1)}, u32[]{:S(2)}, u32[]{:S(2)}) collective-permute-start(bf16[64,16,128]{2,1,0:T(8,128)(2,1)S(1)} %collective-permute-done.4.refs_2_), channel_id=1, source_target_pairs={{0,4},{4,12},{12,8},{8,0},{1,5},{5,13},{13,9},{9,1},{2,6},{6,14},{... | collective-permute-start | bytes 786440 | tf_op jit(solution)/shard_map/ppermute | solution.py:546
  46.7 10.1 %collective-permute-start.2 = (bf16[64,16,128]{2,1,0:T(8,128)(2,1)S(1)}, bf16[64,16,128]{2,1,0:T(8,128)(2,1)S(1)}, u32[]{:S(2)}, u32[]{:S(2)}) collective-permute-start(bf16[64,16,128]{2,1,0:T(8,128)(2,1)S(1)} %right_part.4.refs_0_), channel_id=1, source_target_pairs={{0,4},{4,12},{12,8},{8,0},{1,5},{5,13},{13,9},{9,1},{2,6},{6,14},{... | collective-permute-start | bytes 786440 | tf_op jit(solution)/shard_map/ppermute | solution.py:546
  49.5 19.4 %collective-permute-start.12 = (bf16[64,32,128]{2,1,0:T(8,128)(2,1)S(1)}, bf16[64,32,128]{2,1,0:T(8,128)(2,1)S(1)}, u32[]{:S(2)}, u32[]{:S(2)}) collective-permute-start(bf16[64,32,128]{2,1,0:T(8,128)(2,1)S(1)} %fusion.1), channel_id=1, source_target_pairs={{0,2},{1,3},{2,0},{3,1},{4,6},{5,7},{6,4},{7,5},{8,10},{9,11},{10,... | collective-permute-start | bytes 1572872 | tf_op jit(solution)/shard_map/ppermute | solution.py:552
  51.1 11.3 %collective-permute-start.9 = (bf16[64,16,128]{2,1,0:T(8,128)(2,1)S(1)}, bf16[64,16,128]{2,1,0:T(8,128)(2,1)S(1)}, u32[]{:S(2)}, u32[]{:S(2)}) collective-permute-start(bf16[64,16,128]{2,1,0:T(8,128)(2,1)S(1)} %right_part.7.refs_4_), channel_id=1, source_target_pairs={{0,4},{4,12},{12,8},{8,0},{1,5},{5,13},{13,9},{9,1},{2,6},{6,14},{... | collective-permute-start | bytes 786440 | tf_op jit(solution)/shard_map/ppermute | solution.py:546
  56.8 11.2 %collective-permute-start.7 = (bf16[64,16,128]{2,1,0:T(8,128)(2,1)S(1)}, bf16[64,16,128]{2,1,0:T(8,128)(2,1)S(1)}, u32[]{:S(2)}, u32[]{:S(2)}) collective-permute-start(bf16[64,16,128]{2,1,0:T(8,128)(2,1)S(1)} %collective-permute-done.2.refs_1_), channel_id=1, source_target_pairs={{0,4},{4,12},{12,8},{8,0},{1,5},{5,13},{13,9},{9,1},{2,6},{6,14},{... | collective-permute-start | bytes 786440 | tf_op jit(solution)/shard_map/ppermute | solution.py:546
  62.4 13.6 %collective-permute-start.11 = (bf16[64,16,128]{2,1,0:T(8,128)(2,1)S(1)}, bf16[64,16,128]{2,1,0:T(8,128)(2,1)S(1)}, u32[]{:S(2)}, u32[]{:S(2)}) collective-permute-start(bf16[64,16,128]{2,1,0:T(8,128)(2,1)S(1)} %collective-permute-done.9.refs_5_), channel_id=1, source_target_pairs={{0,4},{4,12},{12,8},{8,0},{1,5},{5,13},{13,9},{9,1},{2,6},{6,14},{... | collective-permute-start | bytes 786440 | tf_op jit(solution)/shard_map/ppermute | solution.py:546
  68.0 11.4 %collective-permute-start.8 = (bf16[64,16,128]{2,1,0:T(8,128)(2,1)S(1)}, bf16[64,16,128]{2,1,0:T(8,128)(2,1)S(1)}, u32[]{:S(2)}, u32[]{:S(2)}) collective-permute-start(bf16[64,16,128]{2,1,0:T(8,128)(2,1)S(1)} %collective-permute-done.7.refs_2_), channel_id=1, source_target_pairs={{0,4},{4,12},{12,8},{8,0},{1,5},{5,13},{13,9},{9,1},{2,6},{6,14},{... | collective-permute-start | bytes 786440 | tf_op jit(solution)/shard_map/ppermute | solution.py:546
  76.0 8.4 %collective-permute-start.13 = (bf16[64,16,128]{2,1,0:T(8,128)(2,1)S(1)}, bf16[64,16,128]{2,1,0:T(8,128)(2,1)S(1)}, u32[]{:S(2)}, u32[]{:S(2)}) collective-permute-start(bf16[64,16,128]{2,1,0:T(8,128)(2,1)S(1)} %collective-permute-done.11.refs_6_), channel_id=1, source_target_pairs={{0,4},{4,12},{12,8},{8,0},{1,5},{5,13},{13,9},{9,1},{2,6},{6,14},{... | collective-permute-start | bytes 786440 | tf_op jit(solution)/shard_map/ppermute | solution.py:546
  88.0 14.3 %collective-permute-start.14 = (bf16[2,64,32,128]{3,2,1,0:T(8,128)(2,1)S(1)}, bf16[2,64,32,128]{3,2,1,0:T(8,128)(2,1)S(1)}, u32[]{:S(2)}, u32[]{:S(2)}) collective-permute-start(bf16[2,64,32,128]{3,2,1,0:T(8,128)(2,1)S(1)} %get-tuple-element.76), channel_id=1, source_target_pairs={{0,1},{1,0},{2,3},{3,2},{4,5},{5,4},{6,7},{7,6},{8,9},{9,8},{10,11... | collective-permute-start | bytes 3145736 | tf_op jit(solution)/shard_map/ppermute | solution.py:555
  88.0 14.3 %collective-permute-start.16 = (bf16[64,32,128]{2,1,0:T(8,128)(2,1)S(1)}, bf16[64,32,128]{2,1,0:T(8,128)(2,1)S(1)}, u32[]{:S(2)}, u32[]{:S(2)}) collective-permute-start(bf16[64,32,128]{2,1,0:T(8,128)(2,1)S(1)} %get-tuple-element.82.d0), channel_id=1, source_target_pairs={{0,2},{1,3},{2,0},{3,1},{4,6},{5,7},{6,4},{7,5},{8,10},{9,11},{10,... | collective-permute-start | bytes 1572872 | tf_op jit(solution)/shard_map/ppermute | solution.py:552
  89.6 14.6 %collective-permute-start.17 = (bf16[64,32,128]{2,1,0:T(8,128)(2,1)S(1)}, bf16[64,32,128]{2,1,0:T(8,128)(2,1)S(1)}, u32[]{:S(2)}, u32[]{:S(2)}) collective-permute-start(bf16[64,32,128]{2,1,0:T(8,128)(2,1)S(1)} %get-tuple-element.82.d0), channel_id=1, source_target_pairs={{0,1},{1,0},{2,3},{3,2},{4,5},{5,4},{6,7},{7,6},{8,9},{9,8},{10,11... | collective-permute-start | bytes 1572872 | tf_op jit(solution)/shard_map/ppermute | solution.py:555
  102.5 17.7 %collective-permute-start.15 = (bf16[64,32,128]{2,1,0:T(8,128)(2,1)S(1)}, bf16[64,32,128]{2,1,0:T(8,128)(2,1)S(1)}, u32[]{:S(2)}, u32[]{:S(2)}) collective-permute-start(bf16[64,32,128]{2,1,0:T(8,128)(2,1)S(1)} %fusion), channel_id=1, source_target_pairs={{0,2},{1,3},{2,0},{3,1},{4,6},{5,7},{6,4},{7,5},{8,10},{9,11},{10,... | collective-permute-start | bytes 1572872 | tf_op jit(solution)/shard_map/ppermute | solution.py:552
  109.3 10.1 %collective-permute-start.19 = (bf16[64,16,128]{2,1,0:T(8,128)(2,1)S(1)}, bf16[64,16,128]{2,1,0:T(8,128)(2,1)S(1)}, u32[]{:S(2)}, u32[]{:S(2)}) collective-permute-start(bf16[64,16,128]{2,1,0:T(8,128)(2,1)S(1)} %get-tuple-element.79), channel_id=1, source_target_pairs={{0,4},{4,12},{12,8},{8,0},{1,5},{5,13},{13,9},{9,1},{2,6},{6,14},{... | collective-permute-start | bytes 786440 | tf_op jit(solution)/shard_map/ppermute | solution.py:546
  111.4 19.2 %collective-permute-start.21 = (bf16[64,16,128]{2,1,0:T(8,128)(2,1)}, bf16[64,16,128]{2,1,0:T(8,128)(2,1)}, u32[]{:S(2)}, u32[]{:S(2)}) collective-permute-start(bf16[64,16,128]{2,1,0:T(8,128)(2,1)} %get-tuple-element.81), channel_id=1, source_target_pairs={{0,4},{4,12},{12,8},{8,0},{1,5},{5,13},{13,9},{9,1},{2,6},{6,14},{... | collective-permute-start | bytes 786440 | tf_op jit(solution)/shard_map/ppermute | solution.py:546
  127.9 12.6 %collective-permute-start.23 = (bf16[64,32,128]{2,1,0:T(8,128)(2,1)}, bf16[64,32,128]{2,1,0:T(8,128)(2,1)}, u32[]{:S(2)}, u32[]{:S(2)}) collective-permute-start(bf16[64,32,128]{2,1,0:T(8,128)(2,1)} %get-tuple-element.94.d0), channel_id=1, source_target_pairs={{0,2},{1,3},{2,0},{3,1},{4,6},{5,7},{6,4},{7,5},{8,10},{9,11},{10,... | collective-permute-start | bytes 1572872 | tf_op jit(solution)/shard_map/ppermute | solution.py:552
  129.4 11.1 %collective-permute-start.20 = (bf16[64,16,128]{2,1,0:T(8,128)(2,1)}, bf16[64,16,128]{2,1,0:T(8,128)(2,1)S(1)}, u32[]{:S(2)}, u32[]{:S(2)}) collective-permute-start(bf16[64,16,128]{2,1,0:T(8,128)(2,1)} %add_convert_fusion.7), channel_id=1, source_target_pairs={{0,4},{4,12},{12,8},{8,0},{1,5},{5,13},{13,9},{9,1},{2,6},{6,14},{... | collective-permute-start | bytes 786440 | tf_op jit(solution)/shard_map/ppermute | solution.py:546
  131.7 15.2 %collective-permute-start.24 = (bf16[64,32,128]{2,1,0:T(8,128)(2,1)}, bf16[64,32,128]{2,1,0:T(8,128)(2,1)S(1)}, u32[]{:S(2)}, u32[]{:S(2)}) collective-permute-start(bf16[64,32,128]{2,1,0:T(8,128)(2,1)} %get-tuple-element.94.d0), channel_id=1, source_target_pairs={{0,1},{1,0},{2,3},{3,2},{4,5},{5,4},{6,7},{7,6},{8,9},{9,8},{10,11... | collective-permute-start | bytes 1572872 | tf_op jit(solution)/shard_map/ppermute | solution.py:555
  131.8 11.0 %collective-permute-start.22 = (bf16[64,16,128]{2,1,0:T(8,128)(2,1)S(1)}, bf16[64,16,128]{2,1,0:T(8,128)(2,1)S(1)}, u32[]{:S(2)}, u32[]{:S(2)}) collective-permute-start(bf16[64,16,128]{2,1,0:T(8,128)(2,1)S(1)} %add_convert_fusion.5), channel_id=1, source_target_pairs={{0,4},{4,12},{12,8},{8,0},{1,5},{5,13},{13,9},{9,1},{2,6},{6,14},{... | collective-permute-start | bytes 786440 | tf_op jit(solution)/shard_map/ppermute | solution.py:546
  141.6 18.8 %collective-permute-start.33 = (bf16[64,16,128]{2,1,0:T(8,128)(2,1)S(1)}, bf16[64,16,128]{2,1,0:T(8,128)(2,1)S(1)}, u32[]{:S(2)}, u32[]{:S(2)}) collective-permute-start(bf16[64,16,128]{2,1,0:T(8,128)(2,1)S(1)} %add_convert_fusion.6), channel_id=1, source_target_pairs={{0,4},{4,12},{12,8},{8,0},{1,5},{5,13},{13,9},{9,1},{2,6},{6,14},{... | collective-permute-start | bytes 786440 | tf_op jit(solution)/shard_map/ppermute | solution.py:546
  143.8 18.6 %collective-permute-start.32 = (bf16[64,16,128]{2,1,0:T(8,128)(2,1)S(1)}, bf16[64,16,128]{2,1,0:T(8,128)(2,1)S(1)}, u32[]{:S(2)}, u32[]{:S(2)}) collective-permute-start(bf16[64,16,128]{2,1,0:T(8,128)(2,1)S(1)} %add_convert_fusion.4), channel_id=1, source_target_pairs={{0,4},{4,12},{12,8},{8,0},{1,5},{5,13},{13,9},{9,1},{2,6},{6,14},{... | collective-permute-start | bytes 786440 | tf_op jit(solution)/shard_map/ppermute | solution.py:546
  150.1 18.9 %collective-permute-start.26 = (bf16[64,16,128]{2,1,0:T(8,128)(2,1)S(1)}, bf16[64,16,128]{2,1,0:T(8,128)(2,1)S(1)}, u32[]{:S(2)}, u32[]{:S(2)}) collective-permute-start(bf16[64,16,128]{2,1,0:T(8,128)(2,1)S(1)} %get-tuple-element.93), channel_id=1, source_target_pairs={{0,4},{4,12},{12,8},{8,0},{1,5},{5,13},{13,9},{9,1},{2,6},{6,14},{... | collective-permute-start | bytes 786440 | tf_op jit(solution)/shard_map/ppermute | solution.py:546
  151.1 17.0 %collective-permute-start.29 = (bf16[64,16,128]{2,1,0:T(8,128)(2,1)S(1)}, bf16[64,16,128]{2,1,0:T(8,128)(2,1)S(1)}, u32[]{:S(2)}, u32[]{:S(2)}) collective-permute-start(bf16[64,16,128]{2,1,0:T(8,128)(2,1)S(1)} %get-tuple-element.103), channel_id=1, source_target_pairs={{0,4},{4,12},{12,8},{8,0},{1,5},{5,13},{13,9},{9,1},{2,6},{6,14},{... | collective-permute-start | bytes 786440 | tf_op jit(solution)/shard_map/ppermute | solution.py:546
  168.2 10.2 %collective-permute-start.30 = (bf16[64,16,128]{2,1,0:T(8,128)(2,1)S(1)}, bf16[64,16,128]{2,1,0:T(8,128)(2,1)S(1)}, u32[]{:S(2)}, u32[]{:S(2)}) collective-permute-start(bf16[64,16,128]{2,1,0:T(8,128)(2,1)S(1)} %add_convert_fusion.1), channel_id=1, source_target_pairs={{0,4},{4,12},{12,8},{8,0},{1,5},{5,13},{13,9},{9,1},{2,6},{6,14},{... | collective-permute-start | bytes 786440 | tf_op jit(solution)/shard_map/ppermute | solution.py:546
  169.1 14.8 %collective-permute-start.27 = (bf16[64,16,128]{2,1,0:T(8,128)(2,1)S(1)}, bf16[64,16,128]{2,1,0:T(8,128)(2,1)S(1)}, u32[]{:S(2)}, u32[]{:S(2)}) collective-permute-start(bf16[64,16,128]{2,1,0:T(8,128)(2,1)S(1)} %add_convert_fusion.3), channel_id=1, source_target_pairs={{0,4},{4,12},{12,8},{8,0},{1,5},{5,13},{13,9},{9,1},{2,6},{6,14},{... | collective-permute-start | bytes 786440 | tf_op jit(solution)/shard_map/ppermute | solution.py:546
  172.6 12.5 %collective-permute-start.34 = (f32[64,768]{1,0:T(8,128)S(1)}, f32[64,768]{1,0:T(8,128)S(1)}, u32[]{:S(2)}, u32[]{:S(2)}) collective-permute-start(f32[64,768]{1,0:T(8,128)S(1)} %constant_dynamic-slice_fusion.1), channel_id=1, source_target_pairs={{0,1},{1,0},{2,3},{3,2},{4,5},{5,4},{6,7},{7,6},{8,9},{9,8},{10,11... | collective-permute-start | bytes 589832 | tf_op jit(solution)/shard_map/ppermute | solution.py:555
  178.4 12.5 %collective-permute-start.31 = (bf16[64,16,128]{2,1,0:T(8,128)(2,1)S(1)}, bf16[64,16,128]{2,1,0:T(8,128)(2,1)S(1)}, u32[]{:S(2)}, u32[]{:S(2)}) collective-permute-start(bf16[64,16,128]{2,1,0:T(8,128)(2,1)S(1)} %add_convert_fusion), channel_id=1, source_target_pairs={{0,4},{4,12},{12,8},{8,0},{1,5},{5,13},{13,9},{9,1},{2,6},{6,14},{... | collective-permute-start | bytes 786440 | tf_op jit(solution)/shard_map/ppermute | solution.py:546
  184.0 9.9 %collective-permute-start.28 = (bf16[64,16,128]{2,1,0:T(8,128)(2,1)S(1)}, bf16[64,16,128]{2,1,0:T(8,128)(2,1)S(1)}, u32[]{:S(2)}, u32[]{:S(2)}) collective-permute-start(bf16[64,16,128]{2,1,0:T(8,128)(2,1)S(1)} %add_convert_fusion.2), channel_id=1, source_target_pairs={{0,4},{4,12},{12,8},{8,0},{1,5},{5,13},{13,9},{9,1},{2,6},{6,14},{... | collective-permute-start | bytes 786440 | tf_op jit(solution)/shard_map/ppermute | solution.py:546
  (38 other events, 318.9 us)

commit v7 on v6

--- a/solution.py
+++ b/solution.py
@@ -557,14 +557,14 @@
     def plus(a, b):
         return (a.astype(F32) + b.astype(F32)).astype(BF16)
 
+    def in_hbm(*arrays):
+        return [pltpu.with_memory_space_constraint(a, pltpu.HBM) for a in arrays]
+
     def right(s):
-        operands = (pair_tiles, gain_in, w_proj, tokens, exponents)
-        if s == 0:
-            operands = [pltpu.with_memory_space_constraint(a, pltpu.HBM) for a in operands]
-        return right_part(s, *operands)
+        return right_part(s, *in_hbm(pair_tiles, gain_in, w_proj, tokens, exponents))
 
     a0, b0 = right(0), right(1)
-    left = left_part(pair_tiles, gain_in, w_proj, tokens)
+    left = left_part(*in_hbm(pair_tiles, gain_in, w_proj, tokens))
     a1, b1 = forward(a0), forward(b0)
     a2, b2 = forward(a1), forward(after(b1, left))
     c0, d0 = right(2), right(3)
@@ -589,13 +589,13 @@
         return [d_tri, far, over_core(d_tri), over_core(far)]
 
     ab = triangle([a0, a1, a2, a3, b0, b1, b2, b3])
-    x_ab = over_x(ab[2])
+    x_ab = over_x(after(ab[2], c1))
     c2, d2 = forward(after(c1, ab[0])), forward(after(d1, ab[2]))
-    dtri_ab, gate_ab, g_out, g_gate = middle(0, ab, after(x_ab, c2))
+    dtri_ab, gate_ab, g_out, g_gate = middle(0, ab, after(x_ab, c2, d1))
     blocks_ab = spread(dtri_ab)
     c3, d3 = forward(c2), forward(after(d2, dtri_ab))
 
-    cd = triangle([c0, c1, c2, c3, d0, d1, d2, d3])
+    cd = triangle([c0, c1, c2, c3, d0, d1, d2, after(d3, blocks_ab[1])])
     x_cd = over_x(cd[2])
     part = dright_part([after(blocks_ab[0], cd[2])] + blocks_ab[1:], left)
     part_a, part_b = part[:4], part[4:]
@@ -616,9 +616,12 @@
 
     r_c, r_d = forward(part_c[1]), forward(part_d[1])
     d_left = dleft_part([after(blocks_cd[0], part_d[1])] + blocks_cd[1:], cd[3], d_left)
-    partial, g_a = final_a_part(pair_tiles, d_left, tokens, gain_in, w_proj, w_gate, [gate_ab, gate_cd])
-    r_c = forward(plus(r_c, part_c[2]))
-    r_d = forward(plus(r_d, part_d[2]))
+    r_c = plus(r_c, part_c[2])
+    partial, g_a = final_a_part(
+        pair_tiles, after(d_left, r_c), tokens, gain_in, w_proj, w_gate, [gate_ab, gate_cd]
+    )
+    r_c = forward(r_c)
+    r_d = plus(r_d, part_d[2])
     zero = jnp.zeros((width, 2 * width), F32)
 
     def final(s, sums, so_far, into):
@@ -626,10 +629,12 @@
             s, pair_tiles, partial, sums, tokens, exponents, gain_in, w_proj, so_far, into
         )
 
-    d_pair, g_first = final(0, (part_a[0], r_a3), zero, gain_in)
-    d_pair, g_first = final(1, (part_b[0], r_b3), g_first, d_pair)
-    r_c = forward(plus(r_c, part_c[3]))
-    r_d = forward(plus(r_d, part_d[3]))
+    d_pair, g_first = final(0, (part_a[0], after(r_a3, r_d)), zero, gain_in)
+    r_d = forward(r_d)
+    r_c = plus(r_c, part_c[3])
+    d_pair, g_first = final(1, (part_b[0], after(r_b3, r_c)), g_first, d_pair)
+    r_c = forward(r_c)
+    r_d = plus(r_d, part_d[3])
 
     def halved(a):
         half = a.shape[0] // 2
@@ -638,7 +643,8 @@
         )
         return a + over_x(a)
 
-    early = halved(jnp.concatenate([g_out, g_gate, g_a, g_first], axis=1))
+    early = halved(after(jnp.concatenate([g_out, g_gate, g_a, g_first], axis=1), r_d))
+    r_d = forward(r_d)
     d_pair, g_last = final(2, (part_c[0], after(r_c, early)), zero, d_pair)
     d_pair, g_last = final(3, (part_d[0], r_d), g_last, d_pair)
     late = halved(g_last)

time: 216 us -> 226 us (1.046)
  local copies, waits for them, and re-layouts: 10.4 us -> 16.4 us
  waiting for transfers between devices: 93.9 us -> 99.7 us
  starting transfers between devices: 52.6 us -> 49.6 us
    ppermute x24, waiting for transfers between devices: 57.8 us -> 67.6 us  [forward(): return lax.ppermute(a, 'row', [(0, 1), (1, 3), (3, 2), (2, 0)])]
    ppermute x6, waiting for transfers between devices: 25.1 us -> 18.8 us  [over_x(): return lax.ppermute(a, 'col', [(k, k ^ 2) for k in range(4)])]
    unnamed x61 -> x86, local copies, waits for them, and re-layouts: 10.1 us -> 15.4 us
    pallas_call x4, Pallas kernels: 4.8 us -> 7.77 us  [right_part(): pl.pallas_call(functools.partial(right_kernel, s), grid=(1,), out_shape=P...]
  transfers between devices with their start and end apart: 41 -> 41, of which waited for: 24 -> 26; matrix products, arithmetic and copies ran while one was open for 2% -> 2% of each run, Pallas kernels for 20% -> 15%
where the time goes in v7:
time: 226 us; the launch traced here: 225 us
  waiting for transfers between devices  99.7 us (44%)
  Pallas kernels  51.1 us (23%)
  starting transfers between devices  49.6 us (22%)
  local copies, waits for them, and re-layouts  16.4 us (7%)
  other arithmetic  7.27 us (3%)
    ppermute x24, waiting for transfers between devices, forward(): return lax.ppermute(a, 'row', [(0, 1), (1, 3), (3, 2), (2, 0)])  67.6 us
    ppermute x24, starting transfers between devices, forward(): return lax.ppermute(a, 'row', [(0, 1), (1, 3), (3, 2), (2, 0)])  36.8 us
    ppermute x6, waiting for transfers between devices, over_x(): return lax.ppermute(a, 'col', [(k, k ^ 2) for k in range(4)])  18.8 us
    unnamed x86, local copies, waits for them, and re-layouts  15.4 us
    pallas_call x2, Pallas kernels, mid_part(): pl.pallas_call(mid_kernel, grid=(steps,), out_shape=(LONG, LONG, square,...  12.5 us
    pallas_call x4, Pallas kernels, final_b_part(): pl.pallas_call(functools.partial(final_b_kernel, s), grid=(1,), out_shape...  8.42 us
    ppermute x6, starting transfers between devices, over_x(): return lax.ppermute(a, 'col', [(k, k ^ 2) for k in range(4)])  8.29 us
    pallas_call x4, Pallas kernels, right_part(): pl.pallas_call(functools.partial(right_kernel, s), grid=(1,), out_shape=P...  7.77 us
  transfers between devices with their start and end apart: 41, of which 26 were waited for; matrix products, arithmetic and copies ran while one was open for 2% of the time, Pallas kernels for 15%

profile of v7, /device:TPU:0, one launch (start us, length us, event | category | flops | bytes accessed | tf_op | source)
XLA Modules:
  0.0 225.3 jit_solution(14241614936325808133)
XLA Ops:
  2.6 3.1 %collective-permute-start = (bf16[64,16,128]{2,1,0:T(8,128)(2,1)S(1)}, bf16[64,16,128]{2,1,0:T(8,128)(2,1)S(1)}, u32[]{:S(2)}, u32[]{:S(2)}) collective-permute-start(bf16[64,16,128]{2,1,0:T(8,128)(2,1)S(1)} %right_part.5.refs_4_), channel_id=1, source_target_pairs={{0,4},{4,12},{12,8},{8,0},{1,5},{5,13},{13,9},{9,1},{2,6},{6,14},{... | collective-permute-start | bytes 786440 | tf_op jit(solution)/shard_map/ppermute | solution.py:546
  7.6 2.6 %collective-permute-start.3 = (bf16[64,16,128]{2,1,0:T(8,128)(2,1)S(1)}, bf16[64,16,128]{2,1,0:T(8,128)(2,1)S(1)}, u32[]{:S(2)}, u32[]{:S(2)}) collective-permute-start(bf16[64,16,128]{2,1,0:T(8,128)(2,1)S(1)} %right_part.6.refs_0_), channel_id=1, source_target_pairs={{0,4},{4,12},{12,8},{8,0},{1,5},{5,13},{13,9},{9,1},{2,6},{6,14},{... | collective-permute-start | bytes 786440 | tf_op jit(solution)/shard_map/ppermute | solution.py:546
  10.2 5.2 %left_part.1.refs_8_.left_ref = bf16[64,2,64,128]{3,2,1,0:T(8,128)(2,1)S(1)} custom-call(bf16[64,64,128]{2,1,0:T(8,128)(2,1)} %x_ref.23, f32[1,128]{1,0:T(1,128)} %bitcast.25, bf16[128,512]{1,0:T(8,128)(2,1)} %w_ref.19, s32[1,256]{1,0:T(1,128)} %bitcast.15), custom_call_target="tpu_custom_call" | custom-call | flops 268435456 | bytes 3145728 | tf_op jit(solution)/shard_map/left_part/pallas_call | solution.py:407
  16.0 2.9 %collective-permute-done.3.refs_1_ = bf16[64,16,128]{2,1,0:T(8,128)(2,1)S(1)} collective-permute-done((bf16[64,16,128]{2,1,0:T(8,128)(2,1)S(1)}, bf16[64,16,128]{2,1,0:T(8,128)(2,1)S(1)}, u32[]{:S(2)}, u32[]{:S(2)}) %collective-permute-start.3) | collective-permute-done | bytes 262176 | tf_op jit(solution)/shard_map/ppermute | solution.py:546
  25.7 2.3 %collective-permute-start.6 = (bf16[64,16,128]{2,1,0:T(8,128)(2,1)S(1)}, bf16[64,16,128]{2,1,0:T(8,128)(2,1)S(1)}, u32[]{:S(2)}, u32[]{:S(2)}) collective-permute-start(bf16[64,16,128]{2,1,0:T(8,128)(2,1)S(1)} %collective-permute-done.1.refs_6_), channel_id=1, source_target_pairs={{0,4},{4,12},{12,8},{8,0},{1,5},{5,13},{13,9},{9,1},{2,6},{6,14},{... | collective-permute-start | bytes 786440 | tf_op jit(solution)/shard_map/ppermute | solution.py:546
  28.0 3.3 %collective-permute-done.4.refs_2_ = bf16[64,16,128]{2,1,0:T(8,128)(2,1)S(1)} collective-permute-done((bf16[64,16,128]{2,1,0:T(8,128)(2,1)S(1)}, bf16[64,16,128]{2,1,0:T(8,128)(2,1)S(1)}, u32[]{:S(2)}, u32[]{:S(2)}) %collective-permute-start.4) | collective-permute-done | bytes 262176 | tf_op jit(solution)/shard_map/ppermute | solution.py:546
  31.8 5.1 %collective-permute-done.6.refs_7_ = bf16[64,16,128]{2,1,0:T(8,128)(2,1)S(1)} collective-permute-done((bf16[64,16,128]{2,1,0:T(8,128)(2,1)S(1)}, bf16[64,16,128]{2,1,0:T(8,128)(2,1)S(1)}, u32[]{:S(2)}, u32[]{:S(2)}) %collective-permute-start.6) | collective-permute-done | bytes 262176 | tf_op jit(solution)/shard_map/ppermute | solution.py:546
  36.9 4.2 %collective-permute-done.5.refs_3_ = bf16[64,16,128]{2,1,0:T(8,128)(2,1)S(1)} collective-permute-done((bf16[64,16,128]{2,1,0:T(8,128)(2,1)S(1)}, bf16[64,16,128]{2,1,0:T(8,128)(2,1)S(1)}, u32[]{:S(2)}, u32[]{:S(2)}) %collective-permute-start.5) | collective-permute-done | bytes 262176 | tf_op jit(solution)/shard_map/ppermute | solution.py:546
  41.1 2.2 tri_part.2
  46.2 6.8 %collective-permute-done.2.refs_1_ = bf16[64,16,128]{2,1,0:T(8,128)(2,1)S(1)} collective-permute-done((bf16[64,16,128]{2,1,0:T(8,128)(2,1)S(1)}, bf16[64,16,128]{2,1,0:T(8,128)(2,1)S(1)}, u32[]{:S(2)}, u32[]{:S(2)}) %collective-permute-start.2) | collective-permute-done | bytes 262176 | tf_op jit(solution)/shard_map/ppermute | solution.py:546
  55.3 3.4 %collective-permute-start.7 = (bf16[64,16,128]{2,1,0:T(8,128)(2,1)S(1)}, bf16[64,16,128]{2,1,0:T(8,128)(2,1)S(1)}, u32[]{:S(2)}, u32[]{:S(2)}) collective-permute-start(bf16[64,16,128]{2,1,0:T(8,128)(2,1)S(1)} %collective-permute-done.2.refs_1_), channel_id=1, source_target_pairs={{0,4},{4,12},{12,8},{8,0},{1,5},{5,13},{13,9},{9,1},{2,6},{6,14},{... | collective-permute-start | bytes 786440 | tf_op jit(solution)/shard_map/ppermute | solution.py:546
  58.7 6.0 %collective-permute-done.9.refs_5_ = bf16[64,16,128]{2,1,0:T(8,128)(2,1)S(1)} collective-permute-done((bf16[64,16,128]{2,1,0:T(8,128)(2,1)S(1)}, bf16[64,16,128]{2,1,0:T(8,128)(2,1)S(1)}, u32[]{:S(2)}, u32[]{:S(2)}) %collective-permute-start.9) | collective-permute-done | bytes 262176 | tf_op jit(solution)/shard_map/ppermute | solution.py:546
  65.5 4.8 %collective-permute-done.7.refs_2_ = bf16[64,16,128]{2,1,0:T(8,128)(2,1)S(1)} collective-permute-done((bf16[64,16,128]{2,1,0:T(8,128)(2,1)S(1)}, bf16[64,16,128]{2,1,0:T(8,128)(2,1)S(1)}, u32[]{:S(2)}, u32[]{:S(2)}) %collective-permute-start.7) | collective-permute-done | bytes 262176 | tf_op jit(solution)/shard_map/ppermute | solution.py:546
  70.4 6.2 %mid_part.2 = (bf16[64,32,128]{2,1,0:T(8,128)(2,1)S(1)}, bf16[64,32,128]{2,1,0:T(8,128)(2,1)S(1)}, f32[128,128]{1,0:T(8,128)S(1)}, f32[128,128]{1,0:T(8,128)S(1)}) custom-call(bf16[64,32,128]{2,1,0:T(8,128)(2,1)S(1)} %get-tuple-element.72.a_ref, bf16[2,64,32,128]{3,2,1,0:T(8,128)(2,1)S(1)} %collective-permute-done.10.b_ref, ...), custom_call_target="tpu_custom_call" | custom-call | flops 402653184 | bytes 4194304 | tf_op jit(solution)/shard_map/mid_part/pallas_call | solution.py:442
  78.8 3.4 %collective-permute-start.8 = (bf16[64,16,128]{2,1,0:T(8,128)(2,1)S(1)}, bf16[64,16,128]{2,1,0:T(8,128)(2,1)S(1)}, u32[]{:S(2)}, u32[]{:S(2)}) collective-permute-start(bf16[64,16,128]{2,1,0:T(8,128)(2,1)S(1)} %collective-permute-done.7.refs_2_), channel_id=1, source_target_pairs={{0,4},{4,12},{12,8},{8,0},{1,5},{5,13},{13,9},{9,1},{2,6},{6,14},{... | collective-permute-start | bytes 786440 | tf_op jit(solution)/shard_map/ppermute | solution.py:546
  82.1 4.2 %collective-permute-done.13.refs_7_ = bf16[64,16,128]{2,1,0:T(8,128)(2,1)S(1)} collective-permute-done((bf16[64,16,128]{2,1,0:T(8,128)(2,1)S(1)}, bf16[64,16,128]{2,1,0:T(8,128)(2,1)S(1)}, u32[]{:S(2)}, u32[]{:S(2)}) %collective-permute-start.13) | collective-permute-done | bytes 262176 | tf_op jit(solution)/shard_map/ppermute | solution.py:546
  89.2 2.2 tri_part.3
  101.8 6.3 %collective-permute-done.19 = bf16[64,16,128]{2,1,0:T(8,128)(2,1)S(1)} collective-permute-done((bf16[64,16,128]{2,1,0:T(8,128)(2,1)S(1)}, bf16[64,16,128]{2,1,0:T(8,128)(2,1)S(1)}, u32[]{:S(2)}, u32[]{:S(2)}) %collective-permute-start.19) | collective-permute-done | bytes 262176 | tf_op jit(solution)/shard_map/ppermute | solution.py:546
  109.6 6.2 %mid_part.3 = (bf16[64,32,128]{2,1,0:T(8,128)(2,1)S(1)}, bf16[64,32,128]{2,1,0:T(8,128)(2,1)S(1)}, f32[128,128]{1,0:T(8,128)S(1)}, f32[128,128]{1,0:T(8,128)S(1)}) custom-call(bf16[64,32,128]{2,1,0:T(8,128)(2,1)S(1)} %get-tuple-element.83.a_ref, bf16[2,64,32,128]{3,2,1,0:T(8,128)(2,1)S(1)} %collective-permute-done.15.b_ref, ...), custom_call_target="tpu_custom_call" | custom-call | flops 402653184 | bytes 4194304 | tf_op jit(solution)/shard_map/mid_part/pallas_call | solution.py:442
  118.9 3.4 %collective-permute-start.20 = (bf16[64,16,128]{2,1,0:T(8,128)(2,1)S(1)}, bf16[64,16,128]{2,1,0:T(8,128)(2,1)S(1)}, u32[]{:S(2)}, u32[]{:S(2)}) collective-permute-start(bf16[64,16,128]{2,1,0:T(8,128)(2,1)S(1)} %add_convert_fusion.7), channel_id=1, source_target_pairs={{0,4},{4,12},{12,8},{8,0},{1,5},{5,13},{13,9},{9,1},{2,6},{6,14},{... | collective-permute-start | bytes 786440 | tf_op jit(solution)/shard_map/ppermute | solution.py:546
  122.3 7.4 %collective-permute-done.23.d1 = bf16[64,32,128]{2,1,0:T(8,128)(2,1)S(1)} collective-permute-done((bf16[64,32,128]{2,1,0:T(8,128)(2,1)S(1)}, bf16[64,32,128]{2,1,0:T(8,128)(2,1)S(1)}, u32[]{:S(2)}, u32[]{:S(2)}) %collective-permute-start.23) | collective-permute-done | bytes 524320 | tf_op jit(solution)/shard_map/ppermute | solution.py:552
  132.7 6.8 %collective-permute-done.22 = bf16[64,16,128]{2,1,0:T(8,128)(2,1)S(1)} collective-permute-done((bf16[64,16,128]{2,1,0:T(8,128)(2,1)S(1)}, bf16[64,16,128]{2,1,0:T(8,128)(2,1)S(1)}, u32[]{:S(2)}, u32[]{:S(2)}) %collective-permute-start.22) | collective-permute-done | bytes 262176 | tf_op jit(solution)/shard_map/ppermute | solution.py:546
  140.3 2.3 %dright_part.3 = (bf16[64,16,128]{2,1,0:T(8,128)(2,1)S(1)}, bf16[64,16,128]{2,1,0:T(8,128)(2,1)}, bf16[64,16,128]{2,1,0:T(8,128)(2,1)S(1)}, bf16[64,16,128]{2,1,...) custom-call(bf16[64,32,128]{2,1,0:T(8,128)(2,1)S(1)} %get-tuple-elem, ...), custom_call_target="tpu_custom_call" | custom-call | flops 268435456 | bytes 6291456 | tf_op jit(solution)/shard_map/dright_part/pallas_call | solution.py:458
  148.4 3.4 %collective-permute-start.33 = (bf16[64,16,128]{2,1,0:T(8,128)(2,1)}, bf16[64,16,128]{2,1,0:T(8,128)(2,1)S(1)}, u32[]{:S(2)}, u32[]{:S(2)}) collective-permute-start(bf16[64,16,128]{2,1,0:T(8,128)(2,1)} %add_convert_fusion.6), channel_id=1, source_target_pairs={{0,4},{4,12},{12,8},{8,0},{1,5},{5,13},{13,9},{9,1},{2,6},{6,14},{... | collective-permute-start | bytes 786440 | tf_op jit(solution)/shard_map/ppermute | solution.py:546
  161.9 12.9 %collective-permute-done.27 = bf16[64,16,128]{2,1,0:T(8,128)(2,1)S(1)} collective-permute-done((bf16[64,16,128]{2,1,0:T(8,128)(2,1)}, bf16[64,16,128]{2,1,0:T(8,128)(2,1)S(1)}, u32[]{:S(2)}, u32[]{:S(2)}) %collective-permute-start.27) | collective-permute-done | bytes 262176 | tf_op jit(solution)/shard_map/ppermute | solution.py:546
  175.9 5.9 %final_a_part.1 = (f32[128,4096]{1,0:T(8,128)S(1)}, f32[128,256]{1,0:T(8,128)S(1)}) custom-call(bf16[64,64,128]{2,1,0:T(8,128)(2,1)S(1)} %copy-done, f32[64,64,128]{2,1,0:T(8,128)S(1)} %dleft_part.3.dleft_ref, s32[1,256]{1,0:T(1,128)S(1)} %bitcast.18, f32[1,128]{1,0:T(1,128)S(1)} %bitcast.30, bf16[128,512]{1,0:T(8,128)(2,1)S(1)} %copy-done.1, ...), custom_call_target="tpu_custom_call" | custom-call | flops 939524096 | bytes 8388608 | tf_op jit(solution)/shard_map/final_a_part/pallas_call | solution.py:486
  188.5 3.3 %collective-permute-start.31 = (bf16[64,16,128]{2,1,0:T(8,128)(2,1)}, bf16[64,16,128]{2,1,0:T(8,128)(2,1)S(1)}, u32[]{:S(2)}, u32[]{:S(2)}) collective-permute-start(bf16[64,16,128]{2,1,0:T(8,128)(2,1)} %add_convert_fusion), channel_id=1, source_target_pairs={{0,4},{4,12},{12,8},{8,0},{1,5},{5,13},{13,9},{9,1},{2,6},{6,14},{... | collective-permute-start | bytes 786440 | tf_op jit(solution)/shard_map/ppermute | solution.py:546
  194.4 5.5 %collective-permute-done.35 = f32[64,768]{1,0:T(8,128)S(1)} collective-permute-done((f32[64,768]{1,0:T(8,128)S(1)}, f32[64,768]{1,0:T(8,128)S(1)}, u32[]{:S(2)}, u32[]{:S(2)}) %collective-permute-start.35) | collective-permute-done | bytes 196640 | tf_op jit(solution)/shard_map/ppermute | solution.py:552
  208.9 2.8 %collective-permute-done.37 = f32[64,256]{1,0:T(8,128)S(1)} collective-permute-done((f32[64,256]{1,0:T(8,128)S(1)}, f32[64,256]{1,0:T(8,128)S(1)}, u32[]{:S(2)}, u32[]{:S(2)}) %collective-permute-start.37) | collective-permute-done | bytes 65568 | tf_op jit(solution)/shard_map/ppermute | solution.py:552
  211.7 2.4 %collective-permute-start.38 = (bf16[64,768]{1,0:T(8,128)(2,1)S(1)}, bf16[64,768]{1,0:T(8,128)(2,1)S(1)}, u32[]{:S(2)}, u32[]{:S(2)}) collective-permute-start(bf16[64,768]{1,0:T(8,128)(2,1)S(1)} %pad_maximum_fusion.1), channel_id=1, source_target_pairs={{0,4},{4,0},{8,12},{12,8},{1,5},{5,1},{9,13},{13,9},{2,6},{6,2},{1... | collective-permute-start | bytes 294920 | tf_op jit(solution)/shard_map/ppermute | solution.py:549
  214.1 2.6 %collective-permute-done.38 = bf16[64,768]{1,0:T(8,128)(2,1)S(1)} collective-permute-done((bf16[64,768]{1,0:T(8,128)(2,1)S(1)}, bf16[64,768]{1,0:T(8,128)(2,1)S(1)}, u32[]{:S(2)}, u32[]{:S(2)}) %collective-permute-start.38) | collective-permute-done | bytes 98336 | tf_op jit(solution)/shard_map/ppermute | solution.py:549
  218.2 4.1 %collective-permute-done.39 = bf16[64,768]{1,0:T(8,128)(2,1)S(1)} collective-permute-done((bf16[64,768]{1,0:T(8,128)(2,1)S(1)}, bf16[64,768]{1,0:T(8,128)(2,1)S(1)}, u32[]{:S(2)}, u32[]{:S(2)}) %collective-permute-start.39) | collective-permute-done | bytes 98336 | tf_op jit(solution)/shard_map/ppermute | solution.py:549
  (181 shorter events, 80.6 us)
Async XLA Ops:
  2.6 12.9 %collective-permute-start = (bf16[64,16,128]{2,1,0:T(8,128)(2,1)S(1)}, bf16[64,16,128]{2,1,0:T(8,128)(2,1)S(1)}, u32[]{:S(2)}, u32[]{:S(2)}) collective-permute-start(bf16[64,16,128]{2,1,0:T(8,128)(2,1)S(1)} %right_part.5.refs_4_), channel_id=1, source_target_pairs={{0,4},{4,12},{12,8},{8,0},{1,5},{5,13},{13,9},{9,1},{2,6},{6,14},{... | collective-permute-start | bytes 786440 | tf_op jit(solution)/shard_map/ppermute | solution.py:546
  7.6 11.2 %collective-permute-start.3 = (bf16[64,16,128]{2,1,0:T(8,128)(2,1)S(1)}, bf16[64,16,128]{2,1,0:T(8,128)(2,1)S(1)}, u32[]{:S(2)}, u32[]{:S(2)}) collective-permute-start(bf16[64,16,128]{2,1,0:T(8,128)(2,1)S(1)} %right_part.6.refs_0_), channel_id=1, source_target_pairs={{0,4},{4,12},{12,8},{8,0},{1,5},{5,13},{13,9},{9,1},{2,6},{6,14},{... | collective-permute-start | bytes 786440 | tf_op jit(solution)/shard_map/ppermute | solution.py:546
  15.5 10.2 %collective-permute-start.1 = (bf16[64,16,128]{2,1,0:T(8,128)(2,1)S(1)}, bf16[64,16,128]{2,1,0:T(8,128)(2,1)S(1)}, u32[]{:S(2)}, u32[]{:S(2)}) collective-permute-start(bf16[64,16,128]{2,1,0:T(8,128)(2,1)S(1)} %collective-permute-done.refs_5_), channel_id=1, source_target_pairs={{0,4},{4,12},{12,8},{8,0},{1,5},{5,13},{13,9},{9,1},{2,6},{6,14},{... | collective-permute-start | bytes 786440 | tf_op jit(solution)/shard_map/ppermute | solution.py:546
  18.8 12.5 %collective-permute-start.4 = (bf16[64,16,128]{2,1,0:T(8,128)(2,1)S(1)}, bf16[64,16,128]{2,1,0:T(8,128)(2,1)S(1)}, u32[]{:S(2)}, u32[]{:S(2)}) collective-permute-start(bf16[64,16,128]{2,1,0:T(8,128)(2,1)S(1)} %collective-permute-done.3.refs_1_), channel_id=1, source_target_pairs={{0,4},{4,12},{12,8},{8,0},{1,5},{5,13},{13,9},{9,1},{2,6},{6,14},{... | collective-permute-start | bytes 786440 | tf_op jit(solution)/shard_map/ppermute | solution.py:546
  25.7 11.2 %collective-permute-start.6 = (bf16[64,16,128]{2,1,0:T(8,128)(2,1)S(1)}, bf16[64,16,128]{2,1,0:T(8,128)(2,1)S(1)}, u32[]{:S(2)}, u32[]{:S(2)}) collective-permute-start(bf16[64,16,128]{2,1,0:T(8,128)(2,1)S(1)} %collective-permute-done.1.refs_6_), channel_id=1, source_target_pairs={{0,4},{4,12},{12,8},{8,0},{1,5},{5,13},{13,9},{9,1},{2,6},{6,14},{... | collective-permute-start | bytes 786440 | tf_op jit(solution)/shard_map/ppermute | solution.py:546
  31.3 9.8 %collective-permute-start.5 = (bf16[64,16,128]{2,1,0:T(8,128)(2,1)S(1)}, bf16[64,16,128]{2,1,0:T(8,128)(2,1)S(1)}, u32[]{:S(2)}, u32[]{:S(2)}) collective-permute-start(bf16[64,16,128]{2,1,0:T(8,128)(2,1)S(1)} %collective-permute-done.4.refs_2_), channel_id=1, source_target_pairs={{0,4},{4,12},{12,8},{8,0},{1,5},{5,13},{13,9},{9,1},{2,6},{6,14},{... | collective-permute-start | bytes 786440 | tf_op jit(solution)/shard_map/ppermute | solution.py:546
  43.4 9.6 %collective-permute-start.2 = (bf16[64,16,128]{2,1,0:T(8,128)(2,1)S(1)}, bf16[64,16,128]{2,1,0:T(8,128)(2,1)S(1)}, u32[]{:S(2)}, u32[]{:S(2)}) collective-permute-start(bf16[64,16,128]{2,1,0:T(8,128)(2,1)S(1)} %right_part.4.refs_0_), channel_id=1, source_target_pairs={{0,4},{4,12},{12,8},{8,0},{1,5},{5,13},{13,9},{9,1},{2,6},{6,14},{... | collective-permute-start | bytes 786440 | tf_op jit(solution)/shard_map/ppermute | solution.py:546
  53.0 17.3 %collective-permute-start.12 = (bf16[64,32,128]{2,1,0:T(8,128)(2,1)S(1)}, bf16[64,32,128]{2,1,0:T(8,128)(2,1)S(1)}, u32[]{:S(2)}, u32[]{:S(2)}) collective-permute-start(bf16[64,32,128]{2,1,0:T(8,128)(2,1)S(1)} %fusion.1), channel_id=1, source_target_pairs={{0,2},{1,3},{2,0},{3,1},{4,6},{5,7},{6,4},{7,5},{8,10},{9,11},{10,... | collective-permute-start | bytes 1572872 | tf_op jit(solution)/shard_map/ppermute | solution.py:552
  54.5 10.1 %collective-permute-start.9 = (bf16[64,16,128]{2,1,0:T(8,128)(2,1)S(1)}, bf16[64,16,128]{2,1,0:T(8,128)(2,1)S(1)}, u32[]{:S(2)}, u32[]{:S(2)}) collective-permute-start(bf16[64,16,128]{2,1,0:T(8,128)(2,1)S(1)} %right_part.7.refs_4_), channel_id=1, source_target_pairs={{0,4},{4,12},{12,8},{8,0},{1,5},{5,13},{13,9},{9,1},{2,6},{6,14},{... | collective-permute-start | bytes 786440 | tf_op jit(solution)/shard_map/ppermute | solution.py:546
  55.3 15.0 %collective-permute-start.7 = (bf16[64,16,128]{2,1,0:T(8,128)(2,1)S(1)}, bf16[64,16,128]{2,1,0:T(8,128)(2,1)S(1)}, u32[]{:S(2)}, u32[]{:S(2)}) collective-permute-start(bf16[64,16,128]{2,1,0:T(8,128)(2,1)S(1)} %collective-permute-done.2.refs_1_), channel_id=1, source_target_pairs={{0,4},{4,12},{12,8},{8,0},{1,5},{5,13},{13,9},{9,1},{2,6},{6,14},{... | collective-permute-start | bytes 786440 | tf_op jit(solution)/shard_map/ppermute | solution.py:546
  64.7 13.2 %collective-permute-start.11 = (bf16[64,16,128]{2,1,0:T(8,128)(2,1)S(1)}, bf16[64,16,128]{2,1,0:T(8,128)(2,1)S(1)}, u32[]{:S(2)}, u32[]{:S(2)}) collective-permute-start(bf16[64,16,128]{2,1,0:T(8,128)(2,1)S(1)} %collective-permute-done.9.refs_5_), channel_id=1, source_target_pairs={{0,4},{4,12},{12,8},{8,0},{1,5},{5,13},{13,9},{9,1},{2,6},{6,14},{... | collective-permute-start | bytes 786440 | tf_op jit(solution)/shard_map/ppermute | solution.py:546
  77.4 10.6 %collective-permute-start.14 = (bf16[64,32,128]{2,1,0:T(8,128)(2,1)S(1)}, bf16[64,32,128]{2,1,0:T(8,128)(2,1)S(1)}, u32[]{:S(2)}, u32[]{:S(2)}) collective-permute-start(bf16[64,32,128]{2,1,0:T(8,128)(2,1)S(1)} %get-tuple-element.90.d0), channel_id=1, source_target_pairs={{0,2},{1,3},{2,0},{3,1},{4,6},{5,7},{6,4},{7,5},{8,10},{9,11},{10,... | collective-permute-start | bytes 1572872 | tf_op jit(solution)/shard_map/ppermute | solution.py:552
  77.9 8.4 %collective-permute-start.13 = (bf16[64,16,128]{2,1,0:T(8,128)(2,1)S(1)}, bf16[64,16,128]{2,1,0:T(8,128)(2,1)S(1)}, u32[]{:S(2)}, u32[]{:S(2)}) collective-permute-start(bf16[64,16,128]{2,1,0:T(8,128)(2,1)S(1)} %collective-permute-done.11.refs_6_), channel_id=1, source_target_pairs={{0,4},{4,12},{12,8},{8,0},{1,5},{5,13},{13,9},{9,1},{2,6},{6,14},{... | collective-permute-start | bytes 786440 | tf_op jit(solution)/shard_map/ppermute | solution.py:546
  78.8 10.4 %collective-permute-start.8 = (bf16[64,16,128]{2,1,0:T(8,128)(2,1)S(1)}, bf16[64,16,128]{2,1,0:T(8,128)(2,1)S(1)}, u32[]{:S(2)}, u32[]{:S(2)}) collective-permute-start(bf16[64,16,128]{2,1,0:T(8,128)(2,1)S(1)} %collective-permute-done.7.refs_2_), channel_id=1, source_target_pairs={{0,4},{4,12},{12,8},{8,0},{1,5},{5,13},{13,9},{9,1},{2,6},{6,14},{... | collective-permute-start | bytes 786440 | tf_op jit(solution)/shard_map/ppermute | solution.py:546
  95.5 14.0 %collective-permute-start.16 = (bf16[64,32,128]{2,1,0:T(8,128)(2,1)S(1)}, bf16[64,32,128]{2,1,0:T(8,128)(2,1)S(1)}, u32[]{:S(2)}, u32[]{:S(2)}) collective-permute-start(bf16[64,32,128]{2,1,0:T(8,128)(2,1)S(1)} %fusion), channel_id=1, source_target_pairs={{0,2},{1,3},{2,0},{3,1},{4,6},{5,7},{6,4},{7,5},{8,10},{9,11},{10,... | collective-permute-start | bytes 1572872 | tf_op jit(solution)/shard_map/ppermute | solution.py:552
  99.2 9.0 %collective-permute-start.19 = (bf16[64,16,128]{2,1,0:T(8,128)(2,1)S(1)}, bf16[64,16,128]{2,1,0:T(8,128)(2,1)S(1)}, u32[]{:S(2)}, u32[]{:S(2)}) collective-permute-start(bf16[64,16,128]{2,1,0:T(8,128)(2,1)S(1)} %get-tuple-element.87), channel_id=1, source_target_pairs={{0,4},{4,12},{12,8},{8,0},{1,5},{5,13},{13,9},{9,1},{2,6},{6,14},{... | collective-permute-start | bytes 786440 | tf_op jit(solution)/shard_map/ppermute | solution.py:546
  116.6 13.1 %collective-permute-start.23 = (bf16[64,32,128]{2,1,0:T(8,128)(2,1)S(1)}, bf16[64,32,128]{2,1,0:T(8,128)(2,1)S(1)}, u32[]{:S(2)}, u32[]{:S(2)}) collective-permute-start(bf16[64,32,128]{2,1,0:T(8,128)(2,1)S(1)} %get-tuple-element.102.d0), channel_id=1, source_target_pairs={{0,2},{1,3},{2,0},{3,1},{4,6},{5,7},{6,4},{7,5},{8,10},{9,11},{10,... | collective-permute-start | bytes 1572872 | tf_op jit(solution)/shard_map/ppermute | solution.py:552
  118.1 11.6 %collective-permute-start.21 = (bf16[64,16,128]{2,1,0:T(8,128)(2,1)S(1)}, bf16[64,16,128]{2,1,0:T(8,128)(2,1)S(1)}, u32[]{:S(2)}, u32[]{:S(2)}) collective-permute-start(bf16[64,16,128]{2,1,0:T(8,128)(2,1)S(1)} %get-tuple-element.89), channel_id=1, source_target_pairs={{0,4},{4,12},{12,8},{8,0},{1,5},{5,13},{13,9},{9,1},{2,6},{6,14},{... | collective-permute-start | bytes 786440 | tf_op jit(solution)/shard_map/ppermute | solution.py:546
  118.9 13.0 %collective-permute-start.20 = (bf16[64,16,128]{2,1,0:T(8,128)(2,1)S(1)}, bf16[64,16,128]{2,1,0:T(8,128)(2,1)S(1)}, u32[]{:S(2)}, u32[]{:S(2)}) collective-permute-start(bf16[64,16,128]{2,1,0:T(8,128)(2,1)S(1)} %add_convert_fusion.7), channel_id=1, source_target_pairs={{0,4},{4,12},{12,8},{8,0},{1,5},{5,13},{13,9},{9,1},{2,6},{6,14},{... | collective-permute-start | bytes 786440 | tf_op jit(solution)/shard_map/ppermute | solution.py:546
  122.3 18.0 %collective-permute-start.24 = (bf16[64,32,128]{2,1,0:T(8,128)(2,1)S(1)}, bf16[64,32,128]{2,1,0:T(8,128)(2,1)S(1)}, u32[]{:S(2)}, u32[]{:S(2)}) collective-permute-start(bf16[64,32,128]{2,1,0:T(8,128)(2,1)S(1)} %get-tuple-element.102.d0), channel_id=1, source_target_pairs={{0,1},{1,0},{2,3},{3,2},{4,5},{5,4},{6,7},{7,6},{8,9},{9,8},{10,11... | collective-permute-start | bytes 1572872 | tf_op jit(solution)/shard_map/ppermute | solution.py:555
  129.7 10.5 %collective-permute-start.25 = (bf16[64,32,128]{2,1,0:T(8,128)(2,1)S(1)}, bf16[64,32,128]{2,1,0:T(8,128)(2,1)S(1)}, u32[]{:S(2)}, u32[]{:S(2)}) collective-permute-start(bf16[64,32,128]{2,1,0:T(8,128)(2,1)S(1)} %collective-permute-done.23.d1), channel_id=1, source_target_pairs={{0,1},{1,0},{2,3},{3,2},{4,5},{5,4},{6,7},{7,6},{8,9},{9,8},{10,11... | collective-permute-start | bytes 1572872 | tf_op jit(solution)/shard_map/ppermute | solution.py:555
  129.8 9.7 %collective-permute-start.22 = (bf16[64,16,128]{2,1,0:T(8,128)(2,1)S(1)}, bf16[64,16,128]{2,1,0:T(8,128)(2,1)S(1)}, u32[]{:S(2)}, u32[]{:S(2)}) collective-permute-start(bf16[64,16,128]{2,1,0:T(8,128)(2,1)S(1)} %add_convert_fusion.5), channel_id=1, source_target_pairs={{0,4},{4,12},{12,8},{8,0},{1,5},{5,13},{13,9},{9,1},{2,6},{6,14},{... | collective-permute-start | bytes 786440 | tf_op jit(solution)/shard_map/ppermute | solution.py:546
  147.6 12.4 %collective-permute-start.26 = (bf16[64,16,128]{2,1,0:T(8,128)(2,1)}, bf16[64,16,128]{2,1,0:T(8,128)(2,1)}, u32[]{:S(2)}, u32[]{:S(2)}) collective-permute-start(bf16[64,16,128]{2,1,0:T(8,128)(2,1)} %get-tuple-element.104), channel_id=1, source_target_pairs={{0,4},{4,12},{12,8},{8,0},{1,5},{5,13},{13,9},{9,1},{2,6},{6,14},{... | collective-permute-start | bytes 786440 | tf_op jit(solution)/shard_map/ppermute | solution.py:546
  148.4 27.4 %collective-permute-start.33 = (bf16[64,16,128]{2,1,0:T(8,128)(2,1)}, bf16[64,16,128]{2,1,0:T(8,128)(2,1)S(1)}, u32[]{:S(2)}, u32[]{:S(2)}) collective-permute-start(bf16[64,16,128]{2,1,0:T(8,128)(2,1)} %add_convert_fusion.6), channel_id=1, source_target_pairs={{0,4},{4,12},{12,8},{8,0},{1,5},{5,13},{13,9},{9,1},{2,6},{6,14},{... | collective-permute-start | bytes 786440 | tf_op jit(solution)/shard_map/ppermute | solution.py:546
  151.8 33.0 %collective-permute-start.32 = (bf16[64,16,128]{2,1,0:T(8,128)(2,1)}, bf16[64,16,128]{2,1,0:T(8,128)(2,1)S(1)}, u32[]{:S(2)}, u32[]{:S(2)}) collective-permute-start(bf16[64,16,128]{2,1,0:T(8,128)(2,1)} %add_convert_fusion.4), channel_id=1, source_target_pairs={{0,4},{4,12},{12,8},{8,0},{1,5},{5,13},{13,9},{9,1},{2,6},{6,14},{... | collective-permute-start | bytes 786440 | tf_op jit(solution)/shard_map/ppermute | solution.py:546
  151.9 22.9 %collective-permute-start.27 = (bf16[64,16,128]{2,1,0:T(8,128)(2,1)}, bf16[64,16,128]{2,1,0:T(8,128)(2,1)S(1)}, u32[]{:S(2)}, u32[]{:S(2)}) collective-permute-start(bf16[64,16,128]{2,1,0:T(8,128)(2,1)} %copy-done.41), channel_id=1, source_target_pairs={{0,4},{4,12},{12,8},{8,0},{1,5},{5,13},{13,9},{9,1},{2,6},{6,14},{... | collective-permute-start | bytes 786440 | tf_op jit(solution)/shard_map/ppermute | solution.py:546
  161.0 23.0 %collective-permute-start.30 = (bf16[64,16,128]{2,1,0:T(8,128)(2,1)S(1)}, bf16[64,16,128]{2,1,0:T(8,128)(2,1)S(1)}, u32[]{:S(2)}, u32[]{:S(2)}) collective-permute-start(bf16[64,16,128]{2,1,0:T(8,128)(2,1)S(1)} %add_convert_fusion.3), channel_id=1, source_target_pairs={{0,4},{4,12},{12,8},{8,0},{1,5},{5,13},{13,9},{9,1},{2,6},{6,14},{... | collective-permute-start | bytes 786440 | tf_op jit(solution)/shard_map/ppermute | solution.py:546
  174.8 12.1 %collective-permute-start.28 = (bf16[64,16,128]{2,1,0:T(8,128)(2,1)S(1)}, bf16[64,16,128]{2,1,0:T(8,128)(2,1)S(1)}, u32[]{:S(2)}, u32[]{:S(2)}) collective-permute-start(bf16[64,16,128]{2,1,0:T(8,128)(2,1)S(1)} %add_convert_fusion.2), channel_id=1, source_target_pairs={{0,4},{4,12},{12,8},{8,0},{1,5},{5,13},{13,9},{9,1},{2,6},{6,14},{... | collective-permute-start | bytes 786440 | tf_op jit(solution)/shard_map/ppermute | solution.py:546
  188.5 11.5 %collective-permute-start.31 = (bf16[64,16,128]{2,1,0:T(8,128)(2,1)}, bf16[64,16,128]{2,1,0:T(8,128)(2,1)S(1)}, u32[]{:S(2)}, u32[]{:S(2)}) collective-permute-start(bf16[64,16,128]{2,1,0:T(8,128)(2,1)} %add_convert_fusion), channel_id=1, source_target_pairs={{0,4},{4,12},{12,8},{8,0},{1,5},{5,13},{13,9},{9,1},{2,6},{6,14},{... | collective-permute-start | bytes 786440 | tf_op jit(solution)/shard_map/ppermute | solution.py:546
  191.7 12.2 %collective-permute-start.29 = (bf16[64,16,128]{2,1,0:T(8,128)(2,1)}, bf16[64,16,128]{2,1,0:T(8,128)(2,1)S(1)}, u32[]{:S(2)}, u32[]{:S(2)}) collective-permute-start(bf16[64,16,128]{2,1,0:T(8,128)(2,1)} %add_convert_fusion.1), channel_id=1, source_target_pairs={{0,4},{4,12},{12,8},{8,0},{1,5},{5,13},{13,9},{9,1},{2,6},{6,14},{... | collective-permute-start | bytes 786440 | tf_op jit(solution)/shard_map/ppermute | solution.py:546
  192.8 7.1 %collective-permute-start.35 = (f32[64,768]{1,0:T(8,128)S(1)}, f32[64,768]{1,0:T(8,128)S(1)}, u32[]{:S(2)}, u32[]{:S(2)}) collective-permute-start(f32[64,768]{1,0:T(8,128)S(1)} %dynamic-slice_add_fusion), channel_id=1, source_target_pairs={{0,2},{1,3},{2,0},{3,1},{4,6},{5,7},{6,4},{7,5},{8,10},{9,11},{10,... | collective-permute-start | bytes 589832 | tf_op jit(solution)/shard_map/ppermute | solution.py:552
  216.7 5.6 %collective-permute-start.39 = (bf16[64,768]{1,0:T(8,128)(2,1)S(1)}, bf16[64,768]{1,0:T(8,128)(2,1)S(1)}, u32[]{:S(2)}, u32[]{:S(2)}) collective-permute-start(bf16[64,768]{1,0:T(8,128)(2,1)S(1)} %add_convert_fusion.8), channel_id=1, source_target_pairs={{0,8},{4,12},{8,0},{12,4},{1,9},{5,13},{9,1},{13,5},{2,10},{6,14},... | collective-permute-start | bytes 294920 | tf_op jit(solution)/shard_map/ppermute | solution.py:549
  (52 other events, 505.0 us)

commit v8 on v5

--- a/solution.py
+++ b/solution.py
@@ -563,11 +563,14 @@
     def plus(a, b):
         return (a.astype(F32) + b.astype(F32)).astype(BF16)
 
+    def in_hbm(*arrays):
+        return [pltpu.with_memory_space_constraint(a, pltpu.HBM) for a in arrays]
+
     def right(s):
-        return right_part(s, pair_tiles, gain_in, w_proj, tokens, exponents)
+        return right_part(s, *in_hbm(pair_tiles, gain_in, w_proj, tokens, exponents))
 
     a0, b0 = right(0), right(1)
-    left = left_part(pair_tiles, gain_in, w_proj, tokens)
+    left = left_part(*in_hbm(pair_tiles, gain_in, w_proj, tokens))
     a1, b1 = forward(a0), forward(b0)
     a2, b2 = forward(a1), forward(after(b1, left))
     c0, d0 = right(2), right(3)
@@ -593,8 +596,8 @@
     def dright(blocks, *others):
         return dright_part([blocks[0], blocks[1], blocks[2], after(blocks[3], *others)], left)
 
-    tri_a, tri_b = triangle([a0, a1, a2, a3]), triangle([b0, b1, b2, b3])
-    x_a, x_b = over_x(tri_a[2]), over_x(tri_b[2])
+    tri_a, tri_b = triangle([a0, a1, a2, a3]), triangle([b0, b1, b2, after(b3, c1)])
+    x_a, x_b = over_x(tri_a[2]), over_x(after(tri_b[2], d1))
     c2, d2 = forward(after(c1, tri_a[2])), forward(after(d1, tri_b[2]))
     dtri_a, gate_a, g_out, g_gate = middle(0, tri_a, after(x_a, d1))
     blocks_a = spread(dtri_a)
@@ -606,7 +609,7 @@
     r_a, r_b = forward(part_a[1]), forward(part_b[1])
 
     tri_c = triangle([c0, c1, c2, after(c3, part_a[1])])
-    tri_d = triangle([d0, d1, d2, after(d3, part_b[1])])
+    tri_d = triangle([d0, d1, d2, after(d3, part_b[1], tri_c[2])])
     x_c, x_d = over_x(tri_c[2]), over_x(tri_d[2])
     r_a = plus(r_a, part_a[2])
     r_a2 = forward(after(r_a, tri_c[2]))
@@ -629,14 +632,16 @@
     part_d = dright(blocks_d, r_b2)
 
     r_c, r_d = forward(part_c[1]), forward(part_d[1])
+    r_c = plus(r_c, part_c[2])
     d_left = dleft_part(
-        [after(blocks_c[0], part_d[1])] + blocks_c[1:] + blocks_d, [tri_c[3], tri_d[3]], d_left
-    )
+        [after(blocks_c[0], part_d[1], r_c)] + blocks_c[1:] + blocks_d, [tri_c[3], tri_d[3]], d_left
+    )
+    r_c = forward(r_c)
+    r_d = plus(r_d, part_d[2])
     partial, g_a = final_a_part(
-        pair_tiles, d_left, tokens, gain_in, w_proj, w_gate, [gate_a, gate_b, gate_c, gate_d]
-    )
-    r_c = forward(plus(r_c, part_c[2]))
-    r_d = forward(plus(r_d, part_d[2]))
+        pair_tiles, after(d_left, r_d), tokens, gain_in, w_proj, w_gate, [gate_a, gate_b, gate_c, gate_d]
+    )
+    r_d = forward(r_d)
     zero = jnp.zeros((width, 2 * width), F32)
 
     def final(s, sums, so_far, into):
@@ -644,10 +649,12 @@
             s, pair_tiles, partial, sums, tokens, exponents, gain_in, w_proj, so_far, into
         )
 
-    d_pair, g_first = final(0, (part_a[0], r_a3), zero, gain_in)
-    d_pair, g_first = final(1, (part_b[0], r_b3), g_first, d_pair)
-    r_c = forward(plus(r_c, part_c[3]))
-    r_d = forward(plus(r_d, part_d[3]))
+    r_c = plus(r_c, part_c[3])
+    d_pair, g_first = final(0, (part_a[0], after(r_a3, r_c)), zero, gain_in)
+    r_c = forward(r_c)
+    r_d = plus(r_d, part_d[3])
+    d_pair, g_first = final(1, (part_b[0], after(r_b3, r_d)), g_first, d_pair)
+    r_d = forward(r_d)
 
     def halved(a):
         half = a.shape[0] // 2

time: 210 us -> 233 us (1.11)
  waiting for transfers between devices: 76.1 us -> 87.8 us
  local copies, waits for them, and re-layouts: 8.5 us -> 12.5 us
  Pallas kernels: 61.1 us -> 64.6 us
  starting transfers between devices: 56.3 us -> 58.9 us
    ppermute x10, waiting for transfers between devices: 21.3 us -> 29.9 us  [over_x(): return lax.ppermute(a, 'col', [(k, k ^ 2) for k in range(4)])]
    pallas_call x4, Pallas kernels: 3.84 us -> 7.76 us  [right_part(): pl.pallas_call(functools.partial(right_kernel, s * steps), grid=(steps,),...]
    unnamed x65 -> x79, local copies, waits for them, and re-layouts: 8.2 us -> 9.9 us
  transfers between devices with their start and end apart: 51 -> 51, of which waited for: 25 -> 24; matrix products, arithmetic and copies ran while one was open for 3% -> 3% of each run, Pallas kernels for 28% -> 24%
where the time goes in v8:
time: 233 us; the launch traced here: 232 us
  waiting for transfers between devices  87.8 us (38%)
  Pallas kernels  64.6 us (28%)
  starting transfers between devices  58.9 us (25%)
  local copies, waits for them, and re-layouts  12.5 us (5%)
  other arithmetic  7.41 us (3%)
    ppermute x24, waiting for transfers between devices, forward(): return lax.ppermute(a, 'row', [(0, 1), (1, 3), (3, 2), (2, 0)])  47 us
    ppermute x24, starting transfers between devices, forward(): return lax.ppermute(a, 'row', [(0, 1), (1, 3), (3, 2), (2, 0)])  42.4 us
    ppermute x10, waiting for transfers between devices, over_x(): return lax.ppermute(a, 'col', [(k, k ^ 2) for k in range(4)])  29.9 us
    pallas_call x4, Pallas kernels, mid_part(): pl.pallas_call(mid_kernel, grid=(1,), out_shape=(PANEL, pltpu.HBM(PANEL.s...  15 us
    ppermute x10, starting transfers between devices, over_x(): return lax.ppermute(a, 'col', [(k, k ^ 2) for k in range(4)])  11.5 us
    unnamed x79, local copies, waits for them, and re-layouts  9.9 us
    pallas_call x4, Pallas kernels, dright_part(): pl.pallas_call(dright_kernel, grid=(HALF // GROUP,), out_shape=(pltpu.HBM...  9.82 us
    pallas_call x4, Pallas kernels, final_b_part(): pl.pallas_call(functools.partial(final_b_kernel, s * steps), grid=(steps,...  8.41 us
  transfers between devices with their start and end apart: 51, of which 24 were waited for; matrix products, arithmetic and copies ran while one was open for 3% of the time, Pallas kernels for 24%

profile of v8, /device:TPU:0, one launch (start us, length us, event | category | flops | bytes accessed | tf_op | source)
XLA Modules:
  0.0 232.4 jit_solution(15538634088001047308)
XLA Ops:
  2.6 3.1 %collective-permute-start.3 = (bf16[64,16,128]{2,1,0:T(8,128)(2,1)S(1)}, bf16[64,16,128]{2,1,0:T(8,128)(2,1)S(1)}, u32[]{:S(2)}, u32[]{:S(2)}) collective-permute-start(bf16[64,16,128]{2,1,0:T(8,128)(2,1)S(1)} %right_part.6.s0), channel_id=1, source_target_pairs={{0,4},{4,12},{12,8},{8,0},{1,5},{5,13},{13,9},{9,1},{2,6},{6,14},{... | collective-permute-start | bytes 786440 | tf_op jit(solution)/shard_map/ppermute | solution.py:552
  5.7 7.3 %collective-permute-done.3.s1 = bf16[64,16,128]{2,1,0:T(8,128)(2,1)S(1)} collective-permute-done((bf16[64,16,128]{2,1,0:T(8,128)(2,1)S(1)}, bf16[64,16,128]{2,1,0:T(8,128)(2,1)S(1)}, u32[]{:S(2)}, u32[]{:S(2)}) %collective-permute-start.3) | collective-permute-done | bytes 262176 | tf_op jit(solution)/shard_map/ppermute | solution.py:552
  15.8 3.4 %collective-permute-start = (bf16[64,16,128]{2,1,0:T(8,128)(2,1)S(1)}, bf16[64,16,128]{2,1,0:T(8,128)(2,1)S(1)}, u32[]{:S(2)}, u32[]{:S(2)}) collective-permute-start(bf16[64,16,128]{2,1,0:T(8,128)(2,1)S(1)} %right_part.5.s0), channel_id=1, source_target_pairs={{0,4},{4,12},{12,8},{8,0},{1,5},{5,13},{13,9},{9,1},{2,6},{6,14},{... | collective-permute-start | bytes 786440 | tf_op jit(solution)/shard_map/ppermute | solution.py:552
  24.0 5.2 %left_part.1.left_ref.refs_4_ = bf16[64,2,64,128]{3,2,1,0:T(8,128)(2,1)S(1)} custom-call(bf16[64,64,128]{2,1,0:T(8,128)(2,1)} %x_ref.27, f32[1,128]{1,0:T(1,128)} %bitcast.26, bf16[128,512]{1,0:T(8,128)(2,1)} %w_ref.19, s32[1,256]{1,0:T(1,128)} %bitcast.41), custom_call_target="tpu_custom_call" | custom-call | flops 268435456 | bytes 3145728 | tf_op jit(solution)/shard_map/left_part/pallas_call | solution.py:410
  29.2 3.4 %collective-permute-start.1 = (bf16[64,16,128]{2,1,0:T(8,128)(2,1)S(1)}, bf16[64,16,128]{2,1,0:T(8,128)(2,1)S(1)}, u32[]{:S(2)}, u32[]{:S(2)}) collective-permute-start(bf16[64,16,128]{2,1,0:T(8,128)(2,1)S(1)} %collective-permute-done.s1), channel_id=1, source_target_pairs={{0,4},{4,12},{12,8},{8,0},{1,5},{5,13},{13,9},{9,1},{2,6},{6,14},{... | collective-permute-start | bytes 786440 | tf_op jit(solution)/shard_map/ppermute | solution.py:552
  39.4 3.4 %collective-permute-start.14 = (bf16[64,16,128]{2,1,0:T(8,128)(2,1)S(1)}, bf16[64,16,128]{2,1,0:T(8,128)(2,1)S(1)}, u32[]{:S(2)}, u32[]{:S(2)}) collective-permute-start(bf16[64,16,128]{2,1,0:T(8,128)(2,1)S(1)} %collective-permute-done.1.s2), channel_id=1, source_target_pairs={{0,4},{4,12},{12,8},{8,0},{1,5},{5,13},{13,9},{9,1},{2,6},{6,14},{... | collective-permute-start | bytes 786440 | tf_op jit(solution)/shard_map/ppermute | solution.py:552
  42.8 5.7 %collective-permute-done.2.s1 = bf16[64,16,128]{2,1,0:T(8,128)(2,1)S(1)} collective-permute-done((bf16[64,16,128]{2,1,0:T(8,128)(2,1)S(1)}, bf16[64,16,128]{2,1,0:T(8,128)(2,1)S(1)}, u32[]{:S(2)}, u32[]{:S(2)}) %collective-permute-start.2) | collective-permute-done | bytes 262176 | tf_op jit(solution)/shard_map/ppermute | solution.py:552
  48.5 5.6 %collective-permute-done.14.s3 = bf16[64,16,128]{2,1,0:T(8,128)(2,1)S(1)} collective-permute-done((bf16[64,16,128]{2,1,0:T(8,128)(2,1)S(1)}, bf16[64,16,128]{2,1,0:T(8,128)(2,1)S(1)}, u32[]{:S(2)}, u32[]{:S(2)}) %collective-permute-start.14) | collective-permute-done | bytes 262176 | tf_op jit(solution)/shard_map/ppermute | solution.py:552
  59.4 5.7 %collective-permute-done.8.c_ref = bf16[64,16,128]{2,1,0:T(8,128)(2,1)S(1)} collective-permute-done((bf16[64,16,128]{2,1,0:T(8,128)(2,1)S(1)}, bf16[64,16,128]{2,1,0:T(8,128)(2,1)S(1)}, u32[]{:S(2)}, u32[]{:S(2)}) %collective-permute-start.8) | collective-permute-done | bytes 262176 | tf_op jit(solution)/shard_map/ppermute | solution.py:558
  65.1 3.5 %mid_part.4 = (bf16[64,16,128]{2,1,0:T(8,128)(2,1)S(1)}, bf16[64,16,128]{2,1,0:T(8,128)(2,1)}, f32[128,128]{1,0:T(8,128)S(1)}, f32[128,128]{1,0:T(8,128)S(1)}) custom-call(bf16[64,16,128]{2,1,0:T(8,128)(2,1)S(1)} %get-tuple-element.99.a_ref, bf16[2,64,16,128]{3,2,1,0:T(8,128)(2,1)S(1)} %collective-permute-done.6.b_ref, ...), custom_call_target="tpu_custom_call" | custom-call | flops 201326592 | bytes 2097152 | tf_op jit(solution)/shard_map/mid_part/pallas_call | solution.py:443
  71.6 6.2 %collective-permute-done.11.refs_1_ = bf16[64,16,128]{2,1,0:T(8,128)(2,1)S(1)} collective-permute-done((bf16[64,16,128]{2,1,0:T(8,128)(2,1)S(1)}, bf16[64,16,128]{2,1,0:T(8,128)(2,1)S(1)}, u32[]{:S(2)}, u32[]{:S(2)}) %collective-permute-start.11) | collective-permute-done | bytes 262176 | tf_op jit(solution)/shard_map/ppermute | solution.py:558
  79.2 3.0 %collective-permute-done.20.c_ref = bf16[64,16,128]{2,1,0:T(8,128)(2,1)S(1)} collective-permute-done((bf16[64,16,128]{2,1,0:T(8,128)(2,1)S(1)}, bf16[64,16,128]{2,1,0:T(8,128)(2,1)S(1)}, u32[]{:S(2)}, u32[]{:S(2)}) %collective-permute-start.20) | collective-permute-done | bytes 262176 | tf_op jit(solution)/shard_map/ppermute | solution.py:558
  82.2 3.5 %mid_part.5 = (bf16[64,16,128]{2,1,0:T(8,128)(2,1)S(1)}, bf16[64,16,128]{2,1,0:T(8,128)(2,1)}, f32[128,128]{1,0:T(8,128)S(1)}, f32[128,128]{1,0:T(8,128)S(1)}) custom-call(bf16[64,16,128]{2,1,0:T(8,128)(2,1)S(1)} %get-tuple-element.116.a_ref, bf16[2,64,16,128]{3,2,1,0:T(8,128)(2,1)S(1)} %collective-permute-done.15.b_ref, ...), custom_call_target="tpu_custom_call" | custom-call | flops 201326592 | bytes 2097152 | tf_op jit(solution)/shard_map/mid_part/pallas_call | solution.py:443
  96.9 5.5 %collective-permute-done.21.s3 = bf16[64,16,128]{2,1,0:T(8,128)(2,1)S(1)} collective-permute-done((bf16[64,16,128]{2,1,0:T(8,128)(2,1)S(1)}, bf16[64,16,128]{2,1,0:T(8,128)(2,1)S(1)}, u32[]{:S(2)}, u32[]{:S(2)}) %collective-permute-start.21) | collective-permute-done | bytes 262176 | tf_op jit(solution)/shard_map/ppermute | solution.py:552
  105.9 3.4 %collective-permute-start.27 = (bf16[64,16,128]{2,1,0:T(8,128)(2,1)}, bf16[64,16,128]{2,1,0:T(8,128)(2,1)}, u32[]{:S(2)}, u32[]{:S(2)}) collective-permute-start(bf16[64,16,128]{2,1,0:T(8,128)(2,1)} %get-tuple-element.124), channel_id=1, source_target_pairs={{0,4},{4,12},{12,8},{8,0},{1,5},{5,13},{13,9},{9,1},{2,6},{6,14},{... | collective-permute-start | bytes 786440 | tf_op jit(solution)/shard_map/ppermute | solution.py:552
  109.3 5.8 %collective-permute-done.19 = bf16[64,16,128]{2,1,0:T(8,128)(2,1)S(1)} collective-permute-done((bf16[64,16,128]{2,1,0:T(8,128)(2,1)S(1)}, bf16[64,16,128]{2,1,0:T(8,128)(2,1)S(1)}, u32[]{:S(2)}, u32[]{:S(2)}) %collective-permute-start.19) | collective-permute-done | bytes 262176 | tf_op jit(solution)/shard_map/ppermute | solution.py:552
  120.7 4.4 %collective-permute-done.18.c_ref = bf16[64,16,128]{2,1,0:T(8,128)(2,1)S(1)} collective-permute-done((bf16[64,16,128]{2,1,0:T(8,128)(2,1)S(1)}, bf16[64,16,128]{2,1,0:T(8,128)(2,1)S(1)}, u32[]{:S(2)}, u32[]{:S(2)}) %collective-permute-start.18) | collective-permute-done | bytes 262176 | tf_op jit(solution)/shard_map/ppermute | solution.py:558
  125.1 3.5 %mid_part.6 = (bf16[64,16,128]{2,1,0:T(8,128)(2,1)S(1)}, bf16[64,16,128]{2,1,0:T(8,128)(2,1)}, f32[128,128]{1,0:T(8,128)S(1)}, f32[128,128]{1,0:T(8,128)S(1)}) custom-call(bf16[64,16,128]{2,1,0:T(8,128)(2,1)S(1)} %get-tuple-element.112.a_ref, bf16[2,64,16,128]{3,2,1,0:T(8,128)(2,1)S(1)} %collective-permute-done.17.b_ref, ...), custom_call_target="tpu_custom_call" | custom-call | flops 201326592 | bytes 2097152 | tf_op jit(solution)/shard_map/mid_part/pallas_call | solution.py:443
  133.4 3.4 %collective-permute-start.31 = (bf16[64,16,128]{2,1,0:T(8,128)(2,1)S(1)}, bf16[64,16,128]{2,1,0:T(8,128)(2,1)S(1)}, u32[]{:S(2)}, u32[]{:S(2)}) collective-permute-start(bf16[64,16,128]{2,1,0:T(8,128)(2,1)S(1)} %add_convert_fusion.6), channel_id=1, source_target_pairs={{0,4},{4,12},{12,8},{8,0},{1,5},{5,13},{13,9},{9,1},{2,6},{6,14},{... | collective-permute-start | bytes 786440 | tf_op jit(solution)/shard_map/ppermute | solution.py:552
  141.9 4.5 %mid_part.7 = (bf16[64,16,128]{2,1,0:T(8,128)(2,1)S(1)}, bf16[64,16,128]{2,1,0:T(8,128)(2,1)}, f32[128,128]{1,0:T(8,128)S(1)}, f32[128,128]{1,0:T(8,128)S(1)}) custom-call(bf16[64,16,128]{2,1,0:T(8,128)(2,1)S(1)} %copy-done.28, bf16[2,64,16,128]{3,2,1,0:T(8,128)(2,1)S(1)} %copy-done.8, bf16[64,16,128]{2,1,0:T(8,128)(2,1)} %collective-permute-done.26.c_ref, ...), custom_call_target="tpu_custom_call" | custom-call | flops 201326592 | bytes 2097152 | tf_op jit(solution)/shard_map/mid_part/pallas_call | solution.py:443
  148.4 3.5 %dright_part.7 = (bf16[64,16,128]{2,1,0:T(8,128)(2,1)}, bf16[64,16,128]{2,1,0:T(8,128)(2,1)S(1)}, bf16[64,16,128]{2,1,0:T(8,128)(2,1)S(1)}, bf16[64,16,128]{2,1,0:T(8,128)(2,1)S(1)}) custom-call(bf16[64,16,128]{2,1,0:T(8,128)(2,1)S(1)} %get-tuple-element.150.refs_0_, bf16[64,16,128]{2,1,0:T(8,128)(2,1)} %collective-permute-done.32.refs_1_, ...), custom_call_target="tpu_custom_call" | custom-call | flops 268435456 | bytes 6291456 | tf_op jit(solution)/shard_map/dright_part/pallas_call | solution.py:459
  151.9 3.4 %collective-permute-start.36 = (bf16[64,16,128]{2,1,0:T(8,128)(2,1)S(1)}, bf16[64,16,128]{2,1,0:T(8,128)(2,1)S(1)}, u32[]{:S(2)}, u32[]{:S(2)}) collective-permute-start(bf16[64,16,128]{2,1,0:T(8,128)(2,1)S(1)} %get-tuple-element.148), channel_id=1, source_target_pairs={{0,4},{4,12},{12,8},{8,0},{1,5},{5,13},{13,9},{9,1},{2,6},{6,14},{... | collective-permute-start | bytes 786440 | tf_op jit(solution)/shard_map/ppermute | solution.py:552
  159.3 2.8 %collective-permute-start.37 = (bf16[64,16,128]{2,1,0:T(8,128)(2,1)S(1)}, bf16[64,16,128]{2,1,0:T(8,128)(2,1)S(1)}, u32[]{:S(2)}, u32[]{:S(2)}) collective-permute-start(bf16[64,16,128]{2,1,0:T(8,128)(2,1)S(1)} %get-tuple-element.144), channel_id=1, source_target_pairs={{0,4},{4,12},{12,8},{8,0},{1,5},{5,13},{13,9},{9,1},{2,6},{6,14},{... | collective-permute-start | bytes 786440 | tf_op jit(solution)/shard_map/ppermute | solution.py:552
  164.6 2.9 %dleft_part.3.dleft_ref = f32[64,64,128]{2,1,0:T(8,128)S(1)} custom-call(bf16[64,16,128]{2,1,0:T(8,128)(2,1)S(1)} %get-tuple-element.150.refs_0_, bf16[64,16,128]{2,1,0:T(8,128)(2,1)} %collective-permute-done.32.refs_1_, bf16[64,16,128]{2,1,0:T(8,128)(2,1)S(1)} %collective-permute-done.33.refs_2_, bf16[64,16,128]{2,1,0:T(8,128)(2,1)S(1)} %collective-permute-done.34.refs_3_, ...), custom_call_target="tpu_custom_call" | custom-call | flops 268435456 | bytes 8388608 | tf_op jit(solution)/shard_map/dleft_part/pallas_call | solution.py:474
  167.5 7.0 %collective-permute-done.37 = bf16[64,16,128]{2,1,0:T(8,128)(2,1)S(1)} collective-permute-done((bf16[64,16,128]{2,1,0:T(8,128)(2,1)S(1)}, bf16[64,16,128]{2,1,0:T(8,128)(2,1)S(1)}, u32[]{:S(2)}, u32[]{:S(2)}) %collective-permute-start.37) | collective-permute-done | bytes 262176 | tf_op jit(solution)/shard_map/ppermute | solution.py:552
  175.7 4.4 %collective-permute-done.40 = bf16[64,16,128]{2,1,0:T(8,128)(2,1)S(1)} collective-permute-done((bf16[64,16,128]{2,1,0:T(8,128)(2,1)S(1)}, bf16[64,16,128]{2,1,0:T(8,128)(2,1)S(1)}, u32[]{:S(2)}, u32[]{:S(2)}) %collective-permute-start.40) | collective-permute-done | bytes 262176 | tf_op jit(solution)/shard_map/ppermute | solution.py:552
  181.0 5.9 %final_a_part.1 = (f32[128,4096]{1,0:T(8,128)S(1)}, f32[128,256]{1,0:T(8,128)S(1)}) custom-call(bf16[64,64,128]{2,1,0:T(8,128)(2,1)S(1)} %copy-done, f32[64,64,128]{2,1,0:T(8,128)S(1)} %dleft_part.3.dleft_ref, s32[1,256]{1,0:T(1,128)S(1)} %bitcast.43, f32[1,128]{1,0:T(1,128)S(1)} %bitcast.32, bf16[128,512]{1,0:T(8,128)(2,1)S(1)} %copy-done.3, ...), custom_call_target="tpu_custom_call" | custom-call | flops 939524096 | bytes 8388608 | tf_op jit(solution)/shard_map/final_a_part/pallas_call | solution.py:487
  196.0 3.0 %collective-permute-start.39 = (bf16[64,16,128]{2,1,0:T(8,128)(2,1)}, bf16[64,16,128]{2,1,0:T(8,128)(2,1)S(1)}, u32[]{:S(2)}, u32[]{:S(2)}) collective-permute-start(bf16[64,16,128]{2,1,0:T(8,128)(2,1)} %add_convert_fusion.1), channel_id=1, source_target_pairs={{0,4},{4,12},{12,8},{8,0},{1,5},{5,13},{13,9},{9,1},{2,6},{6,14},{... | collective-permute-start | bytes 786440 | tf_op jit(solution)/shard_map/ppermute | solution.py:552
  200.7 6.2 %collective-permute-done.45 = f32[64,768]{1,0:T(8,128)S(1)} collective-permute-done((f32[64,768]{1,0:T(8,128)S(1)}, f32[64,768]{1,0:T(8,128)S(1)}, u32[]{:S(2)}, u32[]{:S(2)}) %collective-permute-start.45) | collective-permute-done | bytes 196640 | tf_op jit(solution)/shard_map/ppermute | solution.py:558
  214.9 3.1 %collective-permute-done.47 = f32[64,256]{1,0:T(8,128)S(1)} collective-permute-done((f32[64,256]{1,0:T(8,128)S(1)}, f32[64,256]{1,0:T(8,128)S(1)}, u32[]{:S(2)}, u32[]{:S(2)}) %collective-permute-start.47) | collective-permute-done | bytes 65568 | tf_op jit(solution)/shard_map/ppermute | solution.py:558
  219.0 3.7 %collective-permute-done.48 = bf16[64,768]{1,0:T(8,128)(2,1)S(1)} collective-permute-done((bf16[64,768]{1,0:T(8,128)(2,1)S(1)}, bf16[64,768]{1,0:T(8,128)(2,1)S(1)}, u32[]{:S(2)}, u32[]{:S(2)}) %collective-permute-start.48) | collective-permute-done | bytes 98336 | tf_op jit(solution)/shard_map/ppermute | solution.py:555
  225.0 4.4 %collective-permute-done.49 = bf16[64,768]{1,0:T(8,128)(2,1)S(1)} collective-permute-done((bf16[64,768]{1,0:T(8,128)(2,1)S(1)}, bf16[64,768]{1,0:T(8,128)(2,1)S(1)}, u32[]{:S(2)}, u32[]{:S(2)}) %collective-permute-start.49) | collective-permute-done | bytes 98336 | tf_op jit(solution)/shard_map/ppermute | solution.py:555
  (202 shorter events, 91.2 us)
Async XLA Ops:
  2.6 10.4 %collective-permute-start.3 = (bf16[64,16,128]{2,1,0:T(8,128)(2,1)S(1)}, bf16[64,16,128]{2,1,0:T(8,128)(2,1)S(1)}, u32[]{:S(2)}, u32[]{:S(2)}) collective-permute-start(bf16[64,16,128]{2,1,0:T(8,128)(2,1)S(1)} %right_part.6.s0), channel_id=1, source_target_pairs={{0,4},{4,12},{12,8},{8,0},{1,5},{5,13},{13,9},{9,1},{2,6},{6,14},{... | collective-permute-start | bytes 786440 | tf_op jit(solution)/shard_map/ppermute | solution.py:552
  13.0 10.1 %collective-permute-start.4 = (bf16[64,16,128]{2,1,0:T(8,128)(2,1)S(1)}, bf16[64,16,128]{2,1,0:T(8,128)(2,1)S(1)}, u32[]{:S(2)}, u32[]{:S(2)}) collective-permute-start(bf16[64,16,128]{2,1,0:T(8,128)(2,1)S(1)} %collective-permute-done.3.s1), channel_id=1, source_target_pairs={{0,4},{4,12},{12,8},{8,0},{1,5},{5,13},{13,9},{9,1},{2,6},{6,14},{... | collective-permute-start | bytes 786440 | tf_op jit(solution)/shard_map/ppermute | solution.py:552
  15.8 13.4 %collective-permute-start = (bf16[64,16,128]{2,1,0:T(8,128)(2,1)S(1)}, bf16[64,16,128]{2,1,0:T(8,128)(2,1)S(1)}, u32[]{:S(2)}, u32[]{:S(2)}) collective-permute-start(bf16[64,16,128]{2,1,0:T(8,128)(2,1)S(1)} %right_part.5.s0), channel_id=1, source_target_pairs={{0,4},{4,12},{12,8},{8,0},{1,5},{5,13},{13,9},{9,1},{2,6},{6,14},{... | collective-permute-start | bytes 786440 | tf_op jit(solution)/shard_map/ppermute | solution.py:552
  23.1 11.2 %collective-permute-start.5 = (bf16[64,16,128]{2,1,0:T(8,128)(2,1)S(1)}, bf16[64,16,128]{2,1,0:T(8,128)(2,1)S(1)}, u32[]{:S(2)}, u32[]{:S(2)}) collective-permute-start(bf16[64,16,128]{2,1,0:T(8,128)(2,1)S(1)} %collective-permute-done.4.s2), channel_id=1, source_target_pairs={{0,4},{4,12},{12,8},{8,0},{1,5},{5,13},{13,9},{9,1},{2,6},{6,14},{... | collective-permute-start | bytes 786440 | tf_op jit(solution)/shard_map/ppermute | solution.py:552
  29.2 9.3 %collective-permute-start.1 = (bf16[64,16,128]{2,1,0:T(8,128)(2,1)S(1)}, bf16[64,16,128]{2,1,0:T(8,128)(2,1)S(1)}, u32[]{:S(2)}, u32[]{:S(2)}) collective-permute-start(bf16[64,16,128]{2,1,0:T(8,128)(2,1)S(1)} %collective-permute-done.s1), channel_id=1, source_target_pairs={{0,4},{4,12},{12,8},{8,0},{1,5},{5,13},{13,9},{9,1},{2,6},{6,14},{... | collective-permute-start | bytes 786440 | tf_op jit(solution)/shard_map/ppermute | solution.py:552
  36.4 19.9 %collective-permute-start.6 = (bf16[2,64,16,128]{3,2,1,0:T(8,128)(2,1)S(1)}, bf16[2,64,16,128]{3,2,1,0:T(8,128)(2,1)S(1)}, u32[]{:S(2)}, u32[]{:S(2)}) collective-permute-start(bf16[2,64,16,128]{3,2,1,0:T(8,128)(2,1)S(1)} %get-tuple-element.97), channel_id=1, source_target_pairs={{0,1},{1,0},{2,3},{3,2},{4,5},{5,4},{6,7},{7,6},{8,9},{9,8},{10,11... | collective-permute-start | bytes 1572872 | tf_op jit(solution)/shard_map/ppermute | solution.py:561
  38.5 10.1 %collective-permute-start.2 = (bf16[64,16,128]{2,1,0:T(8,128)(2,1)S(1)}, bf16[64,16,128]{2,1,0:T(8,128)(2,1)S(1)}, u32[]{:S(2)}, u32[]{:S(2)}) collective-permute-start(bf16[64,16,128]{2,1,0:T(8,128)(2,1)S(1)} %right_part.4.s0), channel_id=1, source_target_pairs={{0,4},{4,12},{12,8},{8,0},{1,5},{5,13},{13,9},{9,1},{2,6},{6,14},{... | collective-permute-start | bytes 786440 | tf_op jit(solution)/shard_map/ppermute | solution.py:552
  39.4 14.8 %collective-permute-start.14 = (bf16[64,16,128]{2,1,0:T(8,128)(2,1)S(1)}, bf16[64,16,128]{2,1,0:T(8,128)(2,1)S(1)}, u32[]{:S(2)}, u32[]{:S(2)}) collective-permute-start(bf16[64,16,128]{2,1,0:T(8,128)(2,1)S(1)} %collective-permute-done.1.s2), channel_id=1, source_target_pairs={{0,4},{4,12},{12,8},{8,0},{1,5},{5,13},{13,9},{9,1},{2,6},{6,14},{... | collective-permute-start | bytes 786440 | tf_op jit(solution)/shard_map/ppermute | solution.py:552
  42.7 16.6 %collective-permute-start.9 = (bf16[64,16,128]{2,1,0:T(8,128)(2,1)S(1)}, bf16[64,16,128]{2,1,0:T(8,128)(2,1)S(1)}, u32[]{:S(2)}, u32[]{:S(2)}) collective-permute-start(bf16[64,16,128]{2,1,0:T(8,128)(2,1)S(1)} %right_part.7.s0), channel_id=1, source_target_pairs={{0,4},{4,12},{12,8},{8,0},{1,5},{5,13},{13,9},{9,1},{2,6},{6,14},{... | collective-permute-start | bytes 786440 | tf_op jit(solution)/shard_map/ppermute | solution.py:552
  56.1 14.1 %collective-permute-start.15 = (bf16[2,64,16,128]{3,2,1,0:T(8,128)(2,1)S(1)}, bf16[2,64,16,128]{3,2,1,0:T(8,128)(2,1)S(1)}, u32[]{:S(2)}, u32[]{:S(2)}) collective-permute-start(bf16[2,64,16,128]{3,2,1,0:T(8,128)(2,1)S(1)} %get-tuple-element.107), channel_id=1, source_target_pairs={{0,1},{1,0},{2,3},{3,2},{4,5},{5,4},{6,7},{7,6},{8,9},{9,8},{10,11... | collective-permute-start | bytes 1572872 | tf_op jit(solution)/shard_map/ppermute | solution.py:561
  57.9 20.5 %collective-permute-start.7 = (bf16[64,16,128]{2,1,0:T(8,128)(2,1)S(1)}, bf16[64,16,128]{2,1,0:T(8,128)(2,1)S(1)}, u32[]{:S(2)}, u32[]{:S(2)}) collective-permute-start(bf16[64,16,128]{2,1,0:T(8,128)(2,1)S(1)} %collective-permute-done.2.s1), channel_id=1, source_target_pairs={{0,4},{4,12},{12,8},{8,0},{1,5},{5,13},{13,9},{9,1},{2,6},{6,14},{... | collective-permute-start | bytes 786440 | tf_op jit(solution)/shard_map/ppermute | solution.py:552
  70.3 11.9 %collective-permute-start.20 = (bf16[64,16,128]{2,1,0:T(8,128)(2,1)S(1)}, bf16[64,16,128]{2,1,0:T(8,128)(2,1)S(1)}, u32[]{:S(2)}, u32[]{:S(2)}) collective-permute-start(bf16[64,16,128]{2,1,0:T(8,128)(2,1)S(1)} %fusion.2), channel_id=1, source_target_pairs={{0,2},{1,3},{2,0},{3,1},{4,6},{5,7},{6,4},{7,5},{8,10},{9,11},{10,... | collective-permute-start | bytes 786440 | tf_op jit(solution)/shard_map/ppermute | solution.py:558
  70.8 16.4 %collective-permute-start.16 = (bf16[64,16,128]{2,1,0:T(8,128)(2,1)S(1)}, bf16[64,16,128]{2,1,0:T(8,128)(2,1)S(1)}, u32[]{:S(2)}, u32[]{:S(2)}) collective-permute-start(bf16[64,16,128]{2,1,0:T(8,128)(2,1)S(1)} %collective-permute-done.9.s1), channel_id=1, source_target_pairs={{0,4},{4,12},{12,8},{8,0},{1,5},{5,13},{13,9},{9,1},{2,6},{6,14},{... | collective-permute-start | bytes 786440 | tf_op jit(solution)/shard_map/ppermute | solution.py:552
  77.9 9.4 %collective-permute-start.13 = (bf16[64,16,128]{2,1,0:T(8,128)(2,1)S(1)}, bf16[64,16,128]{2,1,0:T(8,128)(2,1)S(1)}, u32[]{:S(2)}, u32[]{:S(2)}) collective-permute-start(bf16[64,16,128]{2,1,0:T(8,128)(2,1)S(1)} %collective-permute-done.11.refs_1_), channel_id=1, source_target_pairs={{0,1},{1,0},{2,3},{3,2},{4,5},{5,4},{6,7},{7,6},{8,9},{9,8},{10,11... | collective-permute-start | bytes 786440 | tf_op jit(solution)/shard_map/ppermute | solution.py:561
  77.9 9.4 %collective-permute-start.12 = (bf16[64,16,128]{2,1,0:T(8,128)(2,1)S(1)}, bf16[64,16,128]{2,1,0:T(8,128)(2,1)S(1)}, u32[]{:S(2)}, u32[]{:S(2)}) collective-permute-start(bf16[64,16,128]{2,1,0:T(8,128)(2,1)S(1)} %get-tuple-element.128.refs_0_), channel_id=1, source_target_pairs={{0,1},{1,0},{2,3},{3,2},{4,5},{5,4},{6,7},{7,6},{8,9},{9,8},{10,11... | collective-permute-start | bytes 786440 | tf_op jit(solution)/shard_map/ppermute | solution.py:561
  78.4 11.0 %collective-permute-start.10 = (bf16[64,16,128]{2,1,0:T(8,128)(2,1)S(1)}, bf16[64,16,128]{2,1,0:T(8,128)(2,1)S(1)}, u32[]{:S(2)}, u32[]{:S(2)}) collective-permute-start(bf16[64,16,128]{2,1,0:T(8,128)(2,1)S(1)} %collective-permute-done.7.s2), channel_id=1, source_target_pairs={{0,4},{4,12},{12,8},{8,0},{1,5},{5,13},{13,9},{9,1},{2,6},{6,14},{... | collective-permute-start | bytes 786440 | tf_op jit(solution)/shard_map/ppermute | solution.py:552
  105.1 12.3 %collective-permute-start.25 = (bf16[2,64,16,128]{3,2,1,0:T(8,128)(2,1)S(1)}, bf16[2,64,16,128]{3,2,1,0:T(8,128)(2,1)S(1)}, u32[]{:S(2)}, u32[]{:S(2)}) collective-permute-start(bf16[2,64,16,128]{3,2,1,0:T(8,128)(2,1)S(1)} %get-tuple-element.127), channel_id=1, source_target_pairs={{0,1},{1,0},{2,3},{3,2},{4,5},{5,4},{6,7},{7,6},{8,9},{9,8},{10,11... | collective-permute-start | bytes 1572872 | tf_op jit(solution)/shard_map/ppermute | solution.py:561
  105.1 10.0 %collective-permute-start.19 = (bf16[64,16,128]{2,1,0:T(8,128)(2,1)S(1)}, bf16[64,16,128]{2,1,0:T(8,128)(2,1)S(1)}, u32[]{:S(2)}, u32[]{:S(2)}) collective-permute-start(bf16[64,16,128]{2,1,0:T(8,128)(2,1)S(1)} %get-tuple-element.110), channel_id=1, source_target_pairs={{0,4},{4,12},{12,8},{8,0},{1,5},{5,13},{13,9},{9,1},{2,6},{6,14},{... | collective-permute-start | bytes 786440 | tf_op jit(solution)/shard_map/ppermute | solution.py:552
  105.9 26.3 %collective-permute-start.27 = (bf16[64,16,128]{2,1,0:T(8,128)(2,1)}, bf16[64,16,128]{2,1,0:T(8,128)(2,1)}, u32[]{:S(2)}, u32[]{:S(2)}) collective-permute-start(bf16[64,16,128]{2,1,0:T(8,128)(2,1)} %get-tuple-element.124), channel_id=1, source_target_pairs={{0,4},{4,12},{12,8},{8,0},{1,5},{5,13},{13,9},{9,1},{2,6},{6,14},{... | collective-permute-start | bytes 786440 | tf_op jit(solution)/shard_map/ppermute | solution.py:552
  118.3 18.5 %collective-permute-start.26 = (bf16[64,16,128]{2,1,0:T(8,128)(2,1)}, bf16[64,16,128]{2,1,0:T(8,128)(2,1)}, u32[]{:S(2)}, u32[]{:S(2)}) collective-permute-start(bf16[64,16,128]{2,1,0:T(8,128)(2,1)} %fusion), channel_id=1, source_target_pairs={{0,2},{1,3},{2,0},{3,1},{4,6},{5,7},{6,4},{7,5},{8,10},{9,11},{10,... | collective-permute-start | bytes 786440 | tf_op jit(solution)/shard_map/ppermute | solution.py:558
  131.4 15.8 %collective-permute-start.35 = (bf16[64,16,128]{2,1,0:T(8,128)(2,1)}, bf16[64,16,128]{2,1,0:T(8,128)(2,1)S(1)}, u32[]{:S(2)}, u32[]{:S(2)}) collective-permute-start(bf16[64,16,128]{2,1,0:T(8,128)(2,1)} %add_convert_fusion.7), channel_id=1, source_target_pairs={{0,4},{4,12},{12,8},{8,0},{1,5},{5,13},{13,9},{9,1},{2,6},{6,14},{... | collective-permute-start | bytes 786440 | tf_op jit(solution)/shard_map/ppermute | solution.py:552
  133.3 15.1 %collective-permute-start.33 = (bf16[64,16,128]{2,1,0:T(8,128)(2,1)S(1)}, bf16[64,16,128]{2,1,0:T(8,128)(2,1)S(1)}, u32[]{:S(2)}, u32[]{:S(2)}) collective-permute-start(bf16[64,16,128]{2,1,0:T(8,128)(2,1)S(1)} %get-tuple-element.150.refs_0_), channel_id=1, source_target_pairs={{0,1},{1,0},{2,3},{3,2},{4,5},{5,4},{6,7},{7,6},{8,9},{9,8},{10,11... | collective-permute-start | bytes 786440 | tf_op jit(solution)/shard_map/ppermute | solution.py:561
  133.4 22.1 %collective-permute-start.31 = (bf16[64,16,128]{2,1,0:T(8,128)(2,1)S(1)}, bf16[64,16,128]{2,1,0:T(8,128)(2,1)S(1)}, u32[]{:S(2)}, u32[]{:S(2)}) collective-permute-start(bf16[64,16,128]{2,1,0:T(8,128)(2,1)S(1)} %add_convert_fusion.6), channel_id=1, source_target_pairs={{0,4},{4,12},{12,8},{8,0},{1,5},{5,13},{13,9},{9,1},{2,6},{6,14},{... | collective-permute-start | bytes 786440 | tf_op jit(solution)/shard_map/ppermute | solution.py:552
  136.8 11.6 %collective-permute-start.34 = (bf16[64,16,128]{2,1,0:T(8,128)(2,1)}, bf16[64,16,128]{2,1,0:T(8,128)(2,1)S(1)}, u32[]{:S(2)}, u32[]{:S(2)}) collective-permute-start(bf16[64,16,128]{2,1,0:T(8,128)(2,1)} %collective-permute-done.32.refs_1_), channel_id=1, source_target_pairs={{0,1},{1,0},{2,3},{3,2},{4,5},{5,4},{6,7},{7,6},{8,9},{9,8},{10,11... | collective-permute-start | bytes 786440 | tf_op jit(solution)/shard_map/ppermute | solution.py:561
  147.3 33.6 %collective-permute-start.43 = (bf16[64,16,128]{2,1,0:T(8,128)(2,1)S(1)}, bf16[64,16,128]{2,1,0:T(8,128)(2,1)S(1)}, u32[]{:S(2)}, u32[]{:S(2)}) collective-permute-start(bf16[64,16,128]{2,1,0:T(8,128)(2,1)S(1)} %add_convert_fusion.4), channel_id=1, source_target_pairs={{0,4},{4,12},{12,8},{8,0},{1,5},{5,13},{13,9},{9,1},{2,6},{6,14},{... | collective-permute-start | bytes 786440 | tf_op jit(solution)/shard_map/ppermute | solution.py:552
  151.9 11.4 %collective-permute-start.36 = (bf16[64,16,128]{2,1,0:T(8,128)(2,1)S(1)}, bf16[64,16,128]{2,1,0:T(8,128)(2,1)S(1)}, u32[]{:S(2)}, u32[]{:S(2)}) collective-permute-start(bf16[64,16,128]{2,1,0:T(8,128)(2,1)S(1)} %get-tuple-element.148), channel_id=1, source_target_pairs={{0,4},{4,12},{12,8},{8,0},{1,5},{5,13},{13,9},{9,1},{2,6},{6,14},{... | collective-permute-start | bytes 786440 | tf_op jit(solution)/shard_map/ppermute | solution.py:552
  155.5 34.9 %collective-permute-start.42 = (bf16[64,16,128]{2,1,0:T(8,128)(2,1)S(1)}, bf16[64,16,128]{2,1,0:T(8,128)(2,1)S(1)}, u32[]{:S(2)}, u32[]{:S(2)}) collective-permute-start(bf16[64,16,128]{2,1,0:T(8,128)(2,1)S(1)} %add_convert_fusion.5), channel_id=1, source_target_pairs={{0,4},{4,12},{12,8},{8,0},{1,5},{5,13},{13,9},{9,1},{2,6},{6,14},{... | collective-permute-start | bytes 786440 | tf_op jit(solution)/shard_map/ppermute | solution.py:552
  159.3 15.1 %collective-permute-start.37 = (bf16[64,16,128]{2,1,0:T(8,128)(2,1)S(1)}, bf16[64,16,128]{2,1,0:T(8,128)(2,1)S(1)}, u32[]{:S(2)}, u32[]{:S(2)}) collective-permute-start(bf16[64,16,128]{2,1,0:T(8,128)(2,1)S(1)} %get-tuple-element.144), channel_id=1, source_target_pairs={{0,4},{4,12},{12,8},{8,0},{1,5},{5,13},{13,9},{9,1},{2,6},{6,14},{... | collective-permute-start | bytes 786440 | tf_op jit(solution)/shard_map/ppermute | solution.py:552
  163.3 16.8 %collective-permute-start.40 = (bf16[64,16,128]{2,1,0:T(8,128)(2,1)S(1)}, bf16[64,16,128]{2,1,0:T(8,128)(2,1)S(1)}, u32[]{:S(2)}, u32[]{:S(2)}) collective-permute-start(bf16[64,16,128]{2,1,0:T(8,128)(2,1)S(1)} %add_convert_fusion.3), channel_id=1, source_target_pairs={{0,4},{4,12},{12,8},{8,0},{1,5},{5,13},{13,9},{9,1},{2,6},{6,14},{... | collective-permute-start | bytes 786440 | tf_op jit(solution)/shard_map/ppermute | solution.py:552
  174.6 15.1 %collective-permute-start.38 = (bf16[64,16,128]{2,1,0:T(8,128)(2,1)S(1)}, bf16[64,16,128]{2,1,0:T(8,128)(2,1)S(1)}, u32[]{:S(2)}, u32[]{:S(2)}) collective-permute-start(bf16[64,16,128]{2,1,0:T(8,128)(2,1)S(1)} %add_convert_fusion.2), channel_id=1, source_target_pairs={{0,4},{4,12},{12,8},{8,0},{1,5},{5,13},{13,9},{9,1},{2,6},{6,14},{... | collective-permute-start | bytes 786440 | tf_op jit(solution)/shard_map/ppermute | solution.py:552
  194.9 12.1 %collective-permute-start.41 = (bf16[64,16,128]{2,1,0:T(8,128)(2,1)}, bf16[64,16,128]{2,1,0:T(8,128)(2,1)S(1)}, u32[]{:S(2)}, u32[]{:S(2)}) collective-permute-start(bf16[64,16,128]{2,1,0:T(8,128)(2,1)} %add_convert_fusion), channel_id=1, source_target_pairs={{0,4},{4,12},{12,8},{8,0},{1,5},{5,13},{13,9},{9,1},{2,6},{6,14},{... | collective-permute-start | bytes 786440 | tf_op jit(solution)/shard_map/ppermute | solution.py:552
  196.0 14.3 %collective-permute-start.39 = (bf16[64,16,128]{2,1,0:T(8,128)(2,1)}, bf16[64,16,128]{2,1,0:T(8,128)(2,1)S(1)}, u32[]{:S(2)}, u32[]{:S(2)}) collective-permute-start(bf16[64,16,128]{2,1,0:T(8,128)(2,1)} %add_convert_fusion.1), channel_id=1, source_target_pairs={{0,4},{4,12},{12,8},{8,0},{1,5},{5,13},{13,9},{9,1},{2,6},{6,14},{... | collective-permute-start | bytes 786440 | tf_op jit(solution)/shard_map/ppermute | solution.py:552
  (57 other events, 541.2 us)

commit v9 on v8

--- a/solution.py
+++ b/solution.py
@@ -127,7 +127,7 @@
 
 
 def cost(flops, size, exps=0):
-    return pl.CostEstimate(flops=flops, bytes_accessed=size, transcendentals=exps)
+    return pl.CostEstimate(flops=flops // 1024, bytes_accessed=size // 1024, transcendentals=exps // 1024)
 
 
 def first_half(rows):
@@ -574,7 +574,7 @@
     a1, b1 = forward(a0), forward(b0)
     a2, b2 = forward(a1), forward(after(b1, left))
     c0, d0 = right(2), right(3)
-    a3, b3 = forward(after(a2, c0)), forward(after(b2, d0))
+    a3, b3 = forward(after(a2, b1, c0)), forward(after(b2, d0))
     c1, d1 = forward(after(c0, b2)), forward(after(d0, a3))
 
     def triangle(slots):
@@ -596,8 +596,8 @@
     def dright(blocks, *others):
         return dright_part([blocks[0], blocks[1], blocks[2], after(blocks[3], *others)], left)
 
-    tri_a, tri_b = triangle([a0, a1, a2, a3]), triangle([b0, b1, b2, after(b3, c1)])
-    x_a, x_b = over_x(tri_a[2]), over_x(after(tri_b[2], d1))
+    tri_a, tri_b = triangle([a0, a1, a2, after(a3, b3)]), triangle([b0, b1, b2, b3])
+    x_a, x_b = over_x(after(tri_a[2], c1)), over_x(tri_b[2])
     c2, d2 = forward(after(c1, tri_a[2])), forward(after(d1, tri_b[2]))
     dtri_a, gate_a, g_out, g_gate = middle(0, tri_a, after(x_a, d1))
     blocks_a = spread(dtri_a)
@@ -609,27 +609,24 @@
     r_a, r_b = forward(part_a[1]), forward(part_b[1])
 
     tri_c = triangle([c0, c1, c2, after(c3, part_a[1])])
-    tri_d = triangle([d0, d1, d2, after(d3, part_b[1], tri_c[2])])
+    r_a = plus(r_a, part_a[2])
+    tri_d = triangle([d0, d1, d2, after(d3, part_b[1], r_a, tri_c[2])])
     x_c, x_d = over_x(tri_c[2]), over_x(tri_d[2])
-    r_a = plus(r_a, part_a[2])
-    r_a2 = forward(after(r_a, tri_c[2]))
+    r_a = plus(forward(r_a), part_a[3])
     r_b = plus(r_b, part_b[2])
-    r_b2 = forward(after(r_b, tri_d[2]))
     d_left = dleft_part(
-        [after(blocks_a[0], tri_d[2])] + blocks_a[1:] + blocks_b,
+        [after(blocks_a[0], tri_d[2], r_b)] + blocks_a[1:] + blocks_b,
         [tri_a[3], tri_b[3]],
         jnp.zeros((HALF, HALF, WIDTH), F32),
     )
+    r_b = plus(forward(r_b), part_b[3])
     dtri_c, gate_c, g_out, g_gate = middle(2, tri_c, after(x_c, r_a, d_left))
     blocks_c = spread(dtri_c)
     dtri_d, gate_d, g_out, g_gate = middle(3, tri_d, after(x_d, r_b))
     blocks_d = spread(dtri_d)
-    r_a2 = plus(r_a2, part_a[3])
-    r_a3 = forward(after(r_a2, dtri_c))
-    r_b2 = plus(r_b2, part_b[3])
-    r_b3 = forward(after(r_b2, dtri_d))
-    part_c = dright(blocks_c, r_a2)
-    part_d = dright(blocks_d, r_b2)
+    r_a3, r_b3 = forward(r_a), forward(r_b)
+    part_c = dright(blocks_c, r_a3)
+    part_d = dright(blocks_d, r_b3, part_c[1])
 
     r_c, r_d = forward(part_c[1]), forward(part_d[1])
     r_c = plus(r_c, part_c[2])
@@ -656,21 +653,17 @@
     d_pair, g_first = final(1, (part_b[0], after(r_b3, r_d)), g_first, d_pair)
     r_d = forward(r_d)
 
-    def halved(a):
-        half = a.shape[0] // 2
-        a = lax.dynamic_slice_in_dim(a, core * half, half) + over_core(
-            lax.dynamic_slice_in_dim(a, (1 - core) * half, half)
-        )
-        return a + over_x(a)
-
-    early = halved(jnp.concatenate([g_out, g_gate, g_a, g_first], axis=1))
-    d_pair, g_last = final(2, (part_c[0], after(r_c, early)), zero, d_pair)
+    d_pair, g_last = final(2, (part_c[0], r_c), g_first, d_pair)
     d_pair, g_last = final(3, (part_d[0], r_d), g_last, d_pair)
-    late = halved(g_last)
-    sums = jnp.concatenate([early[:, : 4 * width], early[:, 4 * width :] + late], axis=1)
-    for bit in (1, 2):
+
+    sums = jnp.concatenate([g_out, g_gate, g_a, g_last], axis=1)
+    half = width // 2
+    sums = lax.dynamic_slice_in_dim(sums, core * half, half) + over_core(
+        lax.dynamic_slice_in_dim(sums, (1 - core) * half, half)
+    )
+    for send in (over_x, lambda a: over_row(a, 1), lambda a: over_row(a, 2)):
         mine = sums.astype(BF16)
-        sums = mine.astype(F32) + over_row(mine, bit).astype(F32)
+        sums = mine.astype(F32) + send(mine).astype(F32)
     sums = sums / crop_len
     theirs = over_core(sums)
     sums = jnp.concatenate(

time: 233 us -> 224 us (0.961)
  waiting for transfers between devices: 87.8 us -> 84.1 us
  Pallas kernels: 64.6 us -> 61 us
    ppermute x10 -> x9, waiting for transfers between devices: 29.9 us -> 18.4 us  [over_x(): return lax.ppermute(a, 'col', [(k, k ^ 2) for k in range(4)])]
    ppermute x24, waiting for transfers between devices: 47 us -> 55.9 us  [forward(): return lax.ppermute(a, 'row', [(0, 1), (1, 3), (3, 2), (2, 0)])]
    unnamed x79 -> x87, local copies, waits for them, and re-layouts: 9.9 us -> 11.6 us
    ppermute x10 -> x9, starting transfers between devices: 11.5 us -> 10.4 us  [over_x(): return lax.ppermute(a, 'col', [(k, k ^ 2) for k in range(4)])]
  transfers between devices with their start and end apart: 51 -> 49, of which waited for: 24 -> 28; matrix products, arithmetic and copies ran while one was open for 3% -> 3% of each run, Pallas kernels for 24% -> 24%
where the time goes in v9:
time: 224 us
  waiting for transfers between devices  84.1 us (38%)
  Pallas kernels  61 us (27%)
  starting transfers between devices  57.2 us (26%)
  local copies, waits for them, and re-layouts  13.5 us (6%)
  other arithmetic  6.8 us (3%)
    ppermute x24, waiting for transfers between devices, forward(): return lax.ppermute(a, 'row', [(0, 1), (1, 3), (3, 2), (2, 0)])  55.9 us
    ppermute x24, starting transfers between devices, forward(): return lax.ppermute(a, 'row', [(0, 1), (1, 3), (3, 2), (2, 0)])  41.3 us
    ppermute x9, waiting for transfers between devices, over_x(): return lax.ppermute(a, 'col', [(k, k ^ 2) for k in range(4)])  18.4 us
    pallas_call x4, Pallas kernels, mid_part(): pl.pallas_call(mid_kernel, grid=(1,), out_shape=(PANEL, pltpu.HBM(PANEL.s...  14.1 us
    unnamed x87, local copies, waits for them, and re-layouts  11.6 us
    ppermute x9, starting transfers between devices, over_x(): return lax.ppermute(a, 'col', [(k, k ^ 2) for k in range(4)])  10.4 us
    pallas_call x4, Pallas kernels, final_b_part(): pl.pallas_call(functools.partial(final_b_kernel, s * steps), grid=(steps,...  8.45 us
    pallas_call x4, Pallas kernels, dright_part(): pl.pallas_call(dright_kernel, grid=(HALF // GROUP,), out_shape=(pltpu.HBM...  8.43 us
  transfers between devices with their start and end apart: 49, of which 28 were waited for; matrix products, arithmetic and copies ran while one was open for 3% of the time, Pallas kernels for 24%

profile of v9, /device:TPU:0, one launch (start us, length us, event | category | flops | bytes accessed | tf_op | source)
XLA Modules:
  0.0 223.9 jit_solution(18369757169622219233)
XLA Ops:
  2.6 3.1 %collective-permute-start = (bf16[64,16,128]{2,1,0:T(8,128)(2,1)S(1)}, bf16[64,16,128]{2,1,0:T(8,128)(2,1)S(1)}, u32[]{:S(2)}, u32[]{:S(2)}) collective-permute-start(bf16[64,16,128]{2,1,0:T(8,128)(2,1)S(1)} %right_part.5.s0), channel_id=1, source_target_pairs={{0,4},{4,12},{12,8},{8,0},{1,5},{5,13},{13,9},{9,1},{2,6},{6,14},{... | collective-permute-start | bytes 786440 | tf_op jit(solution)/shard_map/ppermute | solution.py:552
  7.6 2.6 %collective-permute-start.3 = (bf16[64,16,128]{2,1,0:T(8,128)(2,1)S(1)}, bf16[64,16,128]{2,1,0:T(8,128)(2,1)S(1)}, u32[]{:S(2)}, u32[]{:S(2)}) collective-permute-start(bf16[64,16,128]{2,1,0:T(8,128)(2,1)S(1)} %right_part.6.s0), channel_id=1, source_target_pairs={{0,4},{4,12},{12,8},{8,0},{1,5},{5,13},{13,9},{9,1},{2,6},{6,14},{... | collective-permute-start | bytes 786440 | tf_op jit(solution)/shard_map/ppermute | solution.py:552
  10.2 5.2 %left_part.1.left_ref.refs_4_ = bf16[64,2,64,128]{3,2,1,0:T(8,128)(2,1)S(1)} custom-call(bf16[64,64,128]{2,1,0:T(8,128)(2,1)} %x_ref.27, f32[1,128]{1,0:T(1,128)} %bitcast.25, bf16[128,512]{1,0:T(8,128)(2,1)} %w_ref.19, s32[1,256]{1,0:T(1,128)} %bitcast.40), custom_call_target="tpu_custom_call" | custom-call | flops 262144 | bytes 3072 | tf_op jit(solution)/shard_map/left_part/pallas_call | solution.py:410
  16.0 2.9 %collective-permute-done.3.s1 = bf16[64,16,128]{2,1,0:T(8,128)(2,1)S(1)} collective-permute-done((bf16[64,16,128]{2,1,0:T(8,128)(2,1)S(1)}, bf16[64,16,128]{2,1,0:T(8,128)(2,1)S(1)}, u32[]{:S(2)}, u32[]{:S(2)}) %collective-permute-start.3) | collective-permute-done | bytes 262176 | tf_op jit(solution)/shard_map/ppermute | solution.py:552
  25.7 2.3 %collective-permute-start.6 = (bf16[64,16,128]{2,1,0:T(8,128)(2,1)S(1)}, bf16[64,16,128]{2,1,0:T(8,128)(2,1)S(1)}, u32[]{:S(2)}, u32[]{:S(2)}) collective-permute-start(bf16[64,16,128]{2,1,0:T(8,128)(2,1)S(1)} %collective-permute-done.1.s2), channel_id=1, source_target_pairs={{0,4},{4,12},{12,8},{8,0},{1,5},{5,13},{13,9},{9,1},{2,6},{6,14},{... | collective-permute-start | bytes 786440 | tf_op jit(solution)/shard_map/ppermute | solution.py:552
  27.9 3.4 %collective-permute-done.4.s2 = bf16[64,16,128]{2,1,0:T(8,128)(2,1)S(1)} collective-permute-done((bf16[64,16,128]{2,1,0:T(8,128)(2,1)S(1)}, bf16[64,16,128]{2,1,0:T(8,128)(2,1)S(1)}, u32[]{:S(2)}, u32[]{:S(2)}) %collective-permute-start.4) | collective-permute-done | bytes 262176 | tf_op jit(solution)/shard_map/ppermute | solution.py:552
  31.8 5.1 %collective-permute-done.6.s3 = bf16[64,16,128]{2,1,0:T(8,128)(2,1)S(1)} collective-permute-done((bf16[64,16,128]{2,1,0:T(8,128)(2,1)S(1)}, bf16[64,16,128]{2,1,0:T(8,128)(2,1)S(1)}, u32[]{:S(2)}, u32[]{:S(2)}) %collective-permute-start.6) | collective-permute-done | bytes 262176 | tf_op jit(solution)/shard_map/ppermute | solution.py:552
  36.9 4.2 %collective-permute-done.5.s3 = bf16[64,16,128]{2,1,0:T(8,128)(2,1)S(1)} collective-permute-done((bf16[64,16,128]{2,1,0:T(8,128)(2,1)S(1)}, bf16[64,16,128]{2,1,0:T(8,128)(2,1)S(1)}, u32[]{:S(2)}, u32[]{:S(2)}) %collective-permute-start.5) | collective-permute-done | bytes 262176 | tf_op jit(solution)/shard_map/ppermute | solution.py:552
  46.3 3.4 %collective-permute-start.10 = (bf16[64,16,128]{2,1,0:T(8,128)(2,1)S(1)}, bf16[64,16,128]{2,1,0:T(8,128)(2,1)S(1)}, u32[]{:S(2)}, u32[]{:S(2)}) collective-permute-start(bf16[64,16,128]{2,1,0:T(8,128)(2,1)S(1)} %right_part.7.s0), channel_id=1, source_target_pairs={{0,4},{4,12},{12,8},{8,0},{1,5},{5,13},{13,9},{9,1},{2,6},{6,14},{... | collective-permute-start | bytes 786440 | tf_op jit(solution)/shard_map/ppermute | solution.py:552
  49.8 3.5 %collective-permute-done.2.s1 = bf16[64,16,128]{2,1,0:T(8,128)(2,1)S(1)} collective-permute-done((bf16[64,16,128]{2,1,0:T(8,128)(2,1)S(1)}, bf16[64,16,128]{2,1,0:T(8,128)(2,1)S(1)}, u32[]{:S(2)}, u32[]{:S(2)}) %collective-permute-start.2) | collective-permute-done | bytes 262176 | tf_op jit(solution)/shard_map/ppermute | solution.py:552
  55.6 3.3 %collective-permute-done.10.s1 = bf16[64,16,128]{2,1,0:T(8,128)(2,1)S(1)} collective-permute-done((bf16[64,16,128]{2,1,0:T(8,128)(2,1)S(1)}, bf16[64,16,128]{2,1,0:T(8,128)(2,1)S(1)}, u32[]{:S(2)}, u32[]{:S(2)}) %collective-permute-start.10) | collective-permute-done | bytes 262176 | tf_op jit(solution)/shard_map/ppermute | solution.py:552
  60.8 3.5 %mid_part.4 = (bf16[64,16,128]{2,1,0:T(8,128)(2,1)S(1)}, bf16[64,16,128]{2,1,0:T(8,128)(2,1)}, f32[128,128]{1,0:T(8,128)S(1)}, f32[128,128]{1,0:T(8,128)S(1)}) custom-call(bf16[64,16,128]{2,1,0:T(8,128)(2,1)S(1)} %get-tuple-element.96.a_ref, bf16[2,64,16,128]{3,2,1,0:T(8,128)(2,1)S(1)} %collective-permute-done.7.b_ref, ...), custom_call_target="tpu_custom_call" | custom-call | flops 196608 | bytes 2048 | tf_op jit(solution)/shard_map/mid_part/pallas_call | solution.py:443
  67.3 6.2 %collective-permute-done.12.refs_1_ = bf16[64,16,128]{2,1,0:T(8,128)(2,1)S(1)} collective-permute-done((bf16[64,16,128]{2,1,0:T(8,128)(2,1)S(1)}, bf16[64,16,128]{2,1,0:T(8,128)(2,1)S(1)}, u32[]{:S(2)}, u32[]{:S(2)}) %collective-permute-start.12) | collective-permute-done | bytes 262176 | tf_op jit(solution)/shard_map/ppermute | solution.py:558
  76.4 3.5 %mid_part.5 = (bf16[64,16,128]{2,1,0:T(8,128)(2,1)S(1)}, bf16[64,16,128]{2,1,0:T(8,128)(2,1)}, f32[128,128]{1,0:T(8,128)S(1)}, f32[128,128]{1,0:T(8,128)S(1)}) custom-call(bf16[64,16,128]{2,1,0:T(8,128)(2,1)S(1)} %get-tuple-element.113.a_ref, bf16[2,64,16,128]{3,2,1,0:T(8,128)(2,1)S(1)} %collective-permute-done.15.b_ref, ...), custom_call_target="tpu_custom_call" | custom-call | flops 196608 | bytes 2048 | tf_op jit(solution)/shard_map/mid_part/pallas_call | solution.py:443
  86.8 3.4 %collective-permute-start.19 = (bf16[64,16,128]{2,1,0:T(8,128)(2,1)S(1)}, bf16[64,16,128]{2,1,0:T(8,128)(2,1)S(1)}, u32[]{:S(2)}, u32[]{:S(2)}) collective-permute-start(bf16[64,16,128]{2,1,0:T(8,128)(2,1)S(1)} %get-tuple-element.106), channel_id=1, source_target_pairs={{0,4},{4,12},{12,8},{8,0},{1,5},{5,13},{13,9},{9,1},{2,6},{6,14},{... | collective-permute-start | bytes 786440 | tf_op jit(solution)/shard_map/ppermute | solution.py:552
  93.1 3.8 %collective-permute-done.19 = bf16[64,16,128]{2,1,0:T(8,128)(2,1)S(1)} collective-permute-done((bf16[64,16,128]{2,1,0:T(8,128)(2,1)S(1)}, bf16[64,16,128]{2,1,0:T(8,128)(2,1)S(1)}, u32[]{:S(2)}, u32[]{:S(2)}) %collective-permute-start.19) | collective-permute-done | bytes 262176 | tf_op jit(solution)/shard_map/ppermute | solution.py:552
  97.1 4.5 %collective-permute-done.22.s3 = bf16[64,16,128]{2,1,0:T(8,128)(2,1)S(1)} collective-permute-done((bf16[64,16,128]{2,1,0:T(8,128)(2,1)S(1)}, bf16[64,16,128]{2,1,0:T(8,128)(2,1)S(1)}, u32[]{:S(2)}, u32[]{:S(2)}) %collective-permute-start.22) | collective-permute-done | bytes 262176 | tf_op jit(solution)/shard_map/ppermute | solution.py:552
  103.6 2.5 %collective-permute-start.27 = (bf16[64,16,128]{2,1,0:T(8,128)(2,1)S(1)}, bf16[64,16,128]{2,1,0:T(8,128)(2,1)S(1)}, u32[]{:S(2)}, u32[]{:S(2)}) collective-permute-start(bf16[64,16,128]{2,1,0:T(8,128)(2,1)S(1)} %get-tuple-element.120), channel_id=1, source_target_pairs={{0,4},{4,12},{12,8},{8,0},{1,5},{5,13},{13,9},{9,1},{2,6},{6,14},{... | collective-permute-start | bytes 786440 | tf_op jit(solution)/shard_map/ppermute | solution.py:552
  107.9 5.8 %collective-permute-done.27 = bf16[64,16,128]{2,1,0:T(8,128)(2,1)S(1)} collective-permute-done((bf16[64,16,128]{2,1,0:T(8,128)(2,1)S(1)}, bf16[64,16,128]{2,1,0:T(8,128)(2,1)S(1)}, u32[]{:S(2)}, u32[]{:S(2)}) %collective-permute-start.27) | collective-permute-done | bytes 262176 | tf_op jit(solution)/shard_map/ppermute | solution.py:552
  121.3 3.4 %collective-permute-done.18.c_ref = bf16[64,16,128]{2,1,0:T(8,128)(2,1)S(1)} collective-permute-done((bf16[64,16,128]{2,1,0:T(8,128)(2,1)S(1)}, bf16[64,16,128]{2,1,0:T(8,128)(2,1)S(1)}, u32[]{:S(2)}, u32[]{:S(2)}) %collective-permute-start.18) | collective-permute-done | bytes 262176 | tf_op jit(solution)/shard_map/ppermute | solution.py:558
  124.7 3.5 %mid_part.6 = (bf16[64,16,128]{2,1,0:T(8,128)(2,1)S(1)}, bf16[64,16,128]{2,1,0:T(8,128)(2,1)}, f32[128,128]{1,0:T(8,128)S(1)}, f32[128,128]{1,0:T(8,128)S(1)}) custom-call(bf16[64,16,128]{2,1,0:T(8,128)(2,1)S(1)} %get-tuple-element.108.a_ref, bf16[2,64,16,128]{3,2,1,0:T(8,128)(2,1)S(1)} %collective-permute-done.17.b_ref, ...), custom_call_target="tpu_custom_call" | custom-call | flops 196608 | bytes 2048 | tf_op jit(solution)/shard_map/mid_part/pallas_call | solution.py:443
  129.7 3.5 %mid_part.7 = (bf16[64,16,128]{2,1,0:T(8,128)(2,1)S(1)}, bf16[64,16,128]{2,1,0:T(8,128)(2,1)}, f32[128,128]{1,0:T(8,128)S(1)}, f32[128,128]{1,0:T(8,128)S(1)}) custom-call(bf16[64,16,128]{2,1,0:T(8,128)(2,1)S(1)} %get-tuple-element.132.a_ref, bf16[2,64,16,128]{3,2,1,0:T(8,128)(2,1)S(1)} %collective-permute-done.26.b_ref, ...), custom_call_target="tpu_custom_call" | custom-call | flops 196608 | bytes 2048 | tf_op jit(solution)/shard_map/mid_part/pallas_call | solution.py:443
  134.6 2.6 %collective-permute-start.37 = (bf16[64,16,128]{2,1,0:T(8,128)(2,1)S(1)}, bf16[64,16,128]{2,1,0:T(8,128)(2,1)S(1)}, u32[]{:S(2)}, u32[]{:S(2)}) collective-permute-start(bf16[64,16,128]{2,1,0:T(8,128)(2,1)S(1)} %add_convert_fusion.6), channel_id=1, source_target_pairs={{0,4},{4,12},{12,8},{8,0},{1,5},{5,13},{13,9},{9,1},{2,6},{6,14},{... | collective-permute-start | bytes 786440 | tf_op jit(solution)/shard_map/ppermute | solution.py:552
  140.2 2.2 %collective-permute-done.37.b_ref = bf16[64,16,128]{2,1,0:T(8,128)(2,1)S(1)} collective-permute-done((bf16[64,16,128]{2,1,0:T(8,128)(2,1)S(1)}, bf16[64,16,128]{2,1,0:T(8,128)(2,1)S(1)}, u32[]{:S(2)}, u32[]{:S(2)}) %collective-permute-start.37) | collective-permute-done | bytes 262176 | tf_op jit(solution)/shard_map/ppermute | solution.py:552
  151.5 3.8 %collective-permute-done.38 = bf16[64,16,128]{2,1,0:T(8,128)(2,1)S(1)} collective-permute-done((bf16[64,16,128]{2,1,0:T(8,128)(2,1)S(1)}, bf16[64,16,128]{2,1,0:T(8,128)(2,1)S(1)}, u32[]{:S(2)}, u32[]{:S(2)}) %collective-permute-start.38) | collective-permute-done | bytes 262176 | tf_op jit(solution)/shard_map/ppermute | solution.py:552
  157.3 3.6 %collective-permute-done.39 = bf16[64,16,128]{2,1,0:T(8,128)(2,1)S(1)} collective-permute-done((bf16[64,16,128]{2,1,0:T(8,128)(2,1)S(1)}, bf16[64,16,128]{2,1,0:T(8,128)(2,1)S(1)}, u32[]{:S(2)}, u32[]{:S(2)}) %collective-permute-start.39) | collective-permute-done | bytes 262176 | tf_op jit(solution)/shard_map/ppermute | solution.py:552
  163.0 3.6 %collective-permute-done.42 = bf16[64,16,128]{2,1,0:T(8,128)(2,1)} collective-permute-done((bf16[64,16,128]{2,1,0:T(8,128)(2,1)}, bf16[64,16,128]{2,1,0:T(8,128)(2,1)}, u32[]{:S(2)}, u32[]{:S(2)}) %collective-permute-start.42) | collective-permute-done | bytes 262176 | tf_op jit(solution)/shard_map/ppermute | solution.py:552
  169.0 3.2 %collective-permute-done.40 = bf16[64,16,128]{2,1,0:T(8,128)(2,1)} collective-permute-done((bf16[64,16,128]{2,1,0:T(8,128)(2,1)}, bf16[64,16,128]{2,1,0:T(8,128)(2,1)}, u32[]{:S(2)}, u32[]{:S(2)}) %collective-permute-start.40) | collective-permute-done | bytes 262176 | tf_op jit(solution)/shard_map/ppermute | solution.py:552
  186.4 5.9 %final_a_part.1 = (f32[128,4096]{1,0:T(8,128)S(1)}, f32[128,256]{1,0:T(8,128)S(1)}) custom-call(bf16[64,64,128]{2,1,0:T(8,128)(2,1)S(1)} %copy-done, f32[64,64,128]{2,1,0:T(8,128)S(1)} %dleft_part.3.dleft_ref, s32[1,256]{1,0:T(1,128)S(1)} %bitcast.43, f32[1,128]{1,0:T(1,128)S(1)} %bitcast.32, bf16[128,512]{1,0:T(8,128)(2,1)S(1)} %copy-done.2, ...), custom_call_target="tpu_custom_call" | custom-call | flops 917504 | bytes 8192 | tf_op jit(solution)/shard_map/final_a_part/pallas_call | solution.py:487
  206.0 4.6 %collective-permute-done.45 = bf16[64,768]{1,0:T(8,128)(2,1)S(1)} collective-permute-done((bf16[64,768]{1,0:T(8,128)(2,1)S(1)}, bf16[64,768]{1,0:T(8,128)(2,1)S(1)}, u32[]{:S(2)}, u32[]{:S(2)}) %collective-permute-start.45) | collective-permute-done | bytes 98336 | tf_op jit(solution)/shard_map/ppermute | solution.py:558
  212.2 3.1 %collective-permute-done.46 = bf16[64,768]{1,0:T(8,128)(2,1)S(1)} collective-permute-done((bf16[64,768]{1,0:T(8,128)(2,1)S(1)}, bf16[64,768]{1,0:T(8,128)(2,1)S(1)}, u32[]{:S(2)}, u32[]{:S(2)}) %collective-permute-start.46) | collective-permute-done | bytes 98336 | tf_op jit(solution)/shard_map/ppermute | solution.py:555
  217.1 3.8 %collective-permute-done.47 = bf16[64,768]{1,0:T(8,128)(2,1)S(1)} collective-permute-done((bf16[64,768]{1,0:T(8,128)(2,1)S(1)}, bf16[64,768]{1,0:T(8,128)(2,1)S(1)}, u32[]{:S(2)}, u32[]{:S(2)}) %collective-permute-start.47) | collective-permute-done | bytes 98336 | tf_op jit(solution)/shard_map/ppermute | solution.py:555
  (201 shorter events, 103.6 us)
Async XLA Ops:
  2.6 12.9 %collective-permute-start = (bf16[64,16,128]{2,1,0:T(8,128)(2,1)S(1)}, bf16[64,16,128]{2,1,0:T(8,128)(2,1)S(1)}, u32[]{:S(2)}, u32[]{:S(2)}) collective-permute-start(bf16[64,16,128]{2,1,0:T(8,128)(2,1)S(1)} %right_part.5.s0), channel_id=1, source_target_pairs={{0,4},{4,12},{12,8},{8,0},{1,5},{5,13},{13,9},{9,1},{2,6},{6,14},{... | collective-permute-start | bytes 786440 | tf_op jit(solution)/shard_map/ppermute | solution.py:552
  7.6 11.2 %collective-permute-start.3 = (bf16[64,16,128]{2,1,0:T(8,128)(2,1)S(1)}, bf16[64,16,128]{2,1,0:T(8,128)(2,1)S(1)}, u32[]{:S(2)}, u32[]{:S(2)}) collective-permute-start(bf16[64,16,128]{2,1,0:T(8,128)(2,1)S(1)} %right_part.6.s0), channel_id=1, source_target_pairs={{0,4},{4,12},{12,8},{8,0},{1,5},{5,13},{13,9},{9,1},{2,6},{6,14},{... | collective-permute-start | bytes 786440 | tf_op jit(solution)/shard_map/ppermute | solution.py:552
  15.5 10.2 %collective-permute-start.1 = (bf16[64,16,128]{2,1,0:T(8,128)(2,1)S(1)}, bf16[64,16,128]{2,1,0:T(8,128)(2,1)S(1)}, u32[]{:S(2)}, u32[]{:S(2)}) collective-permute-start(bf16[64,16,128]{2,1,0:T(8,128)(2,1)S(1)} %collective-permute-done.s1), channel_id=1, source_target_pairs={{0,4},{4,12},{12,8},{8,0},{1,5},{5,13},{13,9},{9,1},{2,6},{6,14},{... | collective-permute-start | bytes 786440 | tf_op jit(solution)/shard_map/ppermute | solution.py:552
  18.8 12.5 %collective-permute-start.4 = (bf16[64,16,128]{2,1,0:T(8,128)(2,1)S(1)}, bf16[64,16,128]{2,1,0:T(8,128)(2,1)S(1)}, u32[]{:S(2)}, u32[]{:S(2)}) collective-permute-start(bf16[64,16,128]{2,1,0:T(8,128)(2,1)S(1)} %collective-permute-done.3.s1), channel_id=1, source_target_pairs={{0,4},{4,12},{12,8},{8,0},{1,5},{5,13},{13,9},{9,1},{2,6},{6,14},{... | collective-permute-start | bytes 786440 | tf_op jit(solution)/shard_map/ppermute | solution.py:552
  25.7 11.2 %collective-permute-start.6 = (bf16[64,16,128]{2,1,0:T(8,128)(2,1)S(1)}, bf16[64,16,128]{2,1,0:T(8,128)(2,1)S(1)}, u32[]{:S(2)}, u32[]{:S(2)}) collective-permute-start(bf16[64,16,128]{2,1,0:T(8,128)(2,1)S(1)} %collective-permute-done.1.s2), channel_id=1, source_target_pairs={{0,4},{4,12},{12,8},{8,0},{1,5},{5,13},{13,9},{9,1},{2,6},{6,14},{... | collective-permute-start | bytes 786440 | tf_op jit(solution)/shard_map/ppermute | solution.py:552
  31.3 9.8 %collective-permute-start.5 = (bf16[64,16,128]{2,1,0:T(8,128)(2,1)S(1)}, bf16[64,16,128]{2,1,0:T(8,128)(2,1)S(1)}, u32[]{:S(2)}, u32[]{:S(2)}) collective-permute-start(bf16[64,16,128]{2,1,0:T(8,128)(2,1)S(1)} %collective-permute-done.4.s2), channel_id=1, source_target_pairs={{0,4},{4,12},{12,8},{8,0},{1,5},{5,13},{13,9},{9,1},{2,6},{6,14},{... | collective-permute-start | bytes 786440 | tf_op jit(solution)/shard_map/ppermute | solution.py:552
  43.2 10.1 %collective-permute-start.2 = (bf16[64,16,128]{2,1,0:T(8,128)(2,1)S(1)}, bf16[64,16,128]{2,1,0:T(8,128)(2,1)S(1)}, u32[]{:S(2)}, u32[]{:S(2)}) collective-permute-start(bf16[64,16,128]{2,1,0:T(8,128)(2,1)S(1)} %right_part.4.s0), channel_id=1, source_target_pairs={{0,4},{4,12},{12,8},{8,0},{1,5},{5,13},{13,9},{9,1},{2,6},{6,14},{... | collective-permute-start | bytes 786440 | tf_op jit(solution)/shard_map/ppermute | solution.py:552
  46.1 19.7 %collective-permute-start.15 = (bf16[2,64,16,128]{3,2,1,0:T(8,128)(2,1)S(1)}, bf16[2,64,16,128]{3,2,1,0:T(8,128)(2,1)S(1)}, u32[]{:S(2)}, u32[]{:S(2)}) collective-permute-start(bf16[2,64,16,128]{3,2,1,0:T(8,128)(2,1)S(1)} %get-tuple-element.103), channel_id=1, source_target_pairs={{0,1},{1,0},{2,3},{3,2},{4,5},{5,4},{6,7},{7,6},{8,9},{9,8},{10,11... | collective-permute-start | bytes 1572872 | tf_op jit(solution)/shard_map/ppermute | solution.py:561
  46.3 12.6 %collective-permute-start.10 = (bf16[64,16,128]{2,1,0:T(8,128)(2,1)S(1)}, bf16[64,16,128]{2,1,0:T(8,128)(2,1)S(1)}, u32[]{:S(2)}, u32[]{:S(2)}) collective-permute-start(bf16[64,16,128]{2,1,0:T(8,128)(2,1)S(1)} %right_part.7.s0), channel_id=1, source_target_pairs={{0,4},{4,12},{12,8},{8,0},{1,5},{5,13},{13,9},{9,1},{2,6},{6,14},{... | collective-permute-start | bytes 786440 | tf_op jit(solution)/shard_map/ppermute | solution.py:552
  54.8 19.2 %collective-permute-start.8 = (bf16[64,16,128]{2,1,0:T(8,128)(2,1)S(1)}, bf16[64,16,128]{2,1,0:T(8,128)(2,1)S(1)}, u32[]{:S(2)}, u32[]{:S(2)}) collective-permute-start(bf16[64,16,128]{2,1,0:T(8,128)(2,1)S(1)} %collective-permute-done.2.s1), channel_id=1, source_target_pairs={{0,4},{4,12},{12,8},{8,0},{1,5},{5,13},{13,9},{9,1},{2,6},{6,14},{... | collective-permute-start | bytes 786440 | tf_op jit(solution)/shard_map/ppermute | solution.py:552
  64.3 9.2 %collective-permute-start.12 = (bf16[64,16,128]{2,1,0:T(8,128)(2,1)S(1)}, bf16[64,16,128]{2,1,0:T(8,128)(2,1)S(1)}, u32[]{:S(2)}, u32[]{:S(2)}) collective-permute-start(bf16[64,16,128]{2,1,0:T(8,128)(2,1)S(1)} %get-tuple-element.125.refs_0_), channel_id=1, source_target_pairs={{0,2},{1,3},{2,0},{3,1},{4,6},{5,7},{6,4},{7,5},{8,10},{9,11},{10,... | collective-permute-start | bytes 786440 | tf_op jit(solution)/shard_map/ppermute | solution.py:558
  65.9 10.5 %collective-permute-start.21 = (bf16[64,16,128]{2,1,0:T(8,128)(2,1)S(1)}, bf16[64,16,128]{2,1,0:T(8,128)(2,1)S(1)}, u32[]{:S(2)}, u32[]{:S(2)}) collective-permute-start(bf16[64,16,128]{2,1,0:T(8,128)(2,1)S(1)} %fusion.2), channel_id=1, source_target_pairs={{0,2},{1,3},{2,0},{3,1},{4,6},{5,7},{6,4},{7,5},{8,10},{9,11},{10,... | collective-permute-start | bytes 786440 | tf_op jit(solution)/shard_map/ppermute | solution.py:558
  66.5 15.0 %collective-permute-start.16 = (bf16[64,16,128]{2,1,0:T(8,128)(2,1)S(1)}, bf16[64,16,128]{2,1,0:T(8,128)(2,1)S(1)}, u32[]{:S(2)}, u32[]{:S(2)}) collective-permute-start(bf16[64,16,128]{2,1,0:T(8,128)(2,1)S(1)} %collective-permute-done.10.s1), channel_id=1, source_target_pairs={{0,4},{4,12},{12,8},{8,0},{1,5},{5,13},{13,9},{9,1},{2,6},{6,14},{... | collective-permute-start | bytes 786440 | tf_op jit(solution)/shard_map/ppermute | solution.py:552
  73.5 7.9 %collective-permute-start.14 = (bf16[64,16,128]{2,1,0:T(8,128)(2,1)S(1)}, bf16[64,16,128]{2,1,0:T(8,128)(2,1)S(1)}, u32[]{:S(2)}, u32[]{:S(2)}) collective-permute-start(bf16[64,16,128]{2,1,0:T(8,128)(2,1)S(1)} %collective-permute-done.12.refs_1_), channel_id=1, source_target_pairs={{0,1},{1,0},{2,3},{3,2},{4,5},{5,4},{6,7},{7,6},{8,9},{9,8},{10,11... | collective-permute-start | bytes 786440 | tf_op jit(solution)/shard_map/ppermute | solution.py:561
  74.0 9.5 %collective-permute-start.11 = (bf16[64,16,128]{2,1,0:T(8,128)(2,1)S(1)}, bf16[64,16,128]{2,1,0:T(8,128)(2,1)S(1)}, u32[]{:S(2)}, u32[]{:S(2)}) collective-permute-start(bf16[64,16,128]{2,1,0:T(8,128)(2,1)S(1)} %collective-permute-done.8.s2), channel_id=1, source_target_pairs={{0,4},{4,12},{12,8},{8,0},{1,5},{5,13},{13,9},{9,1},{2,6},{6,14},{... | collective-permute-start | bytes 786440 | tf_op jit(solution)/shard_map/ppermute | solution.py:552
  85.6 11.4 %collective-permute-start.17 = (bf16[2,64,16,128]{3,2,1,0:T(8,128)(2,1)S(1)}, bf16[2,64,16,128]{3,2,1,0:T(8,128)(2,1)S(1)}, u32[]{:S(2)}, u32[]{:S(2)}) collective-permute-start(bf16[2,64,16,128]{3,2,1,0:T(8,128)(2,1)S(1)} %get-tuple-element.109), channel_id=1, source_target_pairs={{0,1},{1,0},{2,3},{3,2},{4,5},{5,4},{6,7},{7,6},{8,9},{9,8},{10,11... | collective-permute-start | bytes 1572872 | tf_op jit(solution)/shard_map/ppermute | solution.py:561
  86.8 10.1 %collective-permute-start.19 = (bf16[64,16,128]{2,1,0:T(8,128)(2,1)S(1)}, bf16[64,16,128]{2,1,0:T(8,128)(2,1)S(1)}, u32[]{:S(2)}, u32[]{:S(2)}) collective-permute-start(bf16[64,16,128]{2,1,0:T(8,128)(2,1)S(1)} %get-tuple-element.106), channel_id=1, source_target_pairs={{0,4},{4,12},{12,8},{8,0},{1,5},{5,13},{13,9},{9,1},{2,6},{6,14},{... | collective-permute-start | bytes 786440 | tf_op jit(solution)/shard_map/ppermute | solution.py:552
  90.2 11.4 %collective-permute-start.22 = (bf16[64,16,128]{2,1,0:T(8,128)(2,1)S(1)}, bf16[64,16,128]{2,1,0:T(8,128)(2,1)S(1)}, u32[]{:S(2)}, u32[]{:S(2)}) collective-permute-start(bf16[64,16,128]{2,1,0:T(8,128)(2,1)S(1)} %collective-permute-done.16.s2), channel_id=1, source_target_pairs={{0,4},{4,12},{12,8},{8,0},{1,5},{5,13},{13,9},{9,1},{2,6},{6,14},{... | collective-permute-start | bytes 786440 | tf_op jit(solution)/shard_map/ppermute | solution.py:552
  103.6 13.3 %collective-permute-start.26 = (bf16[2,64,16,128]{3,2,1,0:T(8,128)(2,1)S(1)}, bf16[2,64,16,128]{3,2,1,0:T(8,128)(2,1)S(1)}, u32[]{:S(2)}, u32[]{:S(2)}) collective-permute-start(bf16[2,64,16,128]{3,2,1,0:T(8,128)(2,1)S(1)} %get-tuple-element.123), channel_id=1, source_target_pairs={{0,1},{1,0},{2,3},{3,2},{4,5},{5,4},{6,7},{7,6},{8,9},{9,8},{10,11... | collective-permute-start | bytes 1572872 | tf_op jit(solution)/shard_map/ppermute | solution.py:561
  103.6 10.1 %collective-permute-start.27 = (bf16[64,16,128]{2,1,0:T(8,128)(2,1)S(1)}, bf16[64,16,128]{2,1,0:T(8,128)(2,1)S(1)}, u32[]{:S(2)}, u32[]{:S(2)}) collective-permute-start(bf16[64,16,128]{2,1,0:T(8,128)(2,1)S(1)} %get-tuple-element.120), channel_id=1, source_target_pairs={{0,4},{4,12},{12,8},{8,0},{1,5},{5,13},{13,9},{9,1},{2,6},{6,14},{... | collective-permute-start | bytes 786440 | tf_op jit(solution)/shard_map/ppermute | solution.py:552
  106.2 13.1 %collective-permute-start.20 = (bf16[64,16,128]{2,1,0:T(8,128)(2,1)S(1)}, bf16[64,16,128]{2,1,0:T(8,128)(2,1)S(1)}, u32[]{:S(2)}, u32[]{:S(2)}) collective-permute-start(bf16[64,16,128]{2,1,0:T(8,128)(2,1)S(1)} %add_convert_fusion.7), channel_id=1, source_target_pairs={{0,4},{4,12},{12,8},{8,0},{1,5},{5,13},{13,9},{9,1},{2,6},{6,14},{... | collective-permute-start | bytes 786440 | tf_op jit(solution)/shard_map/ppermute | solution.py:552
  113.8 15.9 %collective-permute-start.29 = (bf16[64,16,128]{2,1,0:T(8,128)(2,1)S(1)}, bf16[64,16,128]{2,1,0:T(8,128)(2,1)S(1)}, u32[]{:S(2)}, u32[]{:S(2)}) collective-permute-start(bf16[64,16,128]{2,1,0:T(8,128)(2,1)S(1)} %add_convert_fusion.5), channel_id=1, source_target_pairs={{0,4},{4,12},{12,8},{8,0},{1,5},{5,13},{13,9},{9,1},{2,6},{6,14},{... | collective-permute-start | bytes 786440 | tf_op jit(solution)/shard_map/ppermute | solution.py:552
  115.4 9.2 %collective-permute-start.18 = (bf16[64,16,128]{2,1,0:T(8,128)(2,1)S(1)}, bf16[64,16,128]{2,1,0:T(8,128)(2,1)S(1)}, u32[]{:S(2)}, u32[]{:S(2)}) collective-permute-start(bf16[64,16,128]{2,1,0:T(8,128)(2,1)S(1)} %fusion.1), channel_id=1, source_target_pairs={{0,2},{1,3},{2,0},{3,1},{4,6},{5,7},{6,4},{7,5},{8,10},{9,11},{10,... | collective-permute-start | bytes 786440 | tf_op jit(solution)/shard_map/ppermute | solution.py:558
  117.0 12.8 %collective-permute-start.28 = (bf16[64,16,128]{2,1,0:T(8,128)(2,1)S(1)}, bf16[64,16,128]{2,1,0:T(8,128)(2,1)S(1)}, u32[]{:S(2)}, u32[]{:S(2)}) collective-permute-start(bf16[64,16,128]{2,1,0:T(8,128)(2,1)S(1)} %fusion), channel_id=1, source_target_pairs={{0,2},{1,3},{2,0},{3,1},{4,6},{5,7},{6,4},{7,5},{8,10},{9,11},{10,... | collective-permute-start | bytes 786440 | tf_op jit(solution)/shard_map/ppermute | solution.py:558
  128.2 9.0 %collective-permute-start.34 = (bf16[64,16,128]{2,1,0:T(8,128)(2,1)S(1)}, bf16[64,16,128]{2,1,0:T(8,128)(2,1)S(1)}, u32[]{:S(2)}, u32[]{:S(2)}) collective-permute-start(bf16[64,16,128]{2,1,0:T(8,128)(2,1)S(1)} %get-tuple-element.143.refs_0_), channel_id=1, source_target_pairs={{0,2},{1,3},{2,0},{3,1},{4,6},{5,7},{6,4},{7,5},{8,10},{9,11},{10,... | collective-permute-start | bytes 786440 | tf_op jit(solution)/shard_map/ppermute | solution.py:558
  137.7 9.8 %collective-permute-start.33 = (bf16[64,16,128]{2,1,0:T(8,128)(2,1)S(1)}, bf16[64,16,128]{2,1,0:T(8,128)(2,1)S(1)}, u32[]{:S(2)}, u32[]{:S(2)}) collective-permute-start(bf16[64,16,128]{2,1,0:T(8,128)(2,1)S(1)} %add_convert_fusion.4), channel_id=1, source_target_pairs={{0,4},{4,12},{12,8},{8,0},{1,5},{5,13},{13,9},{9,1},{2,6},{6,14},{... | collective-permute-start | bytes 786440 | tf_op jit(solution)/shard_map/ppermute | solution.py:552
  145.3 10.0 %collective-permute-start.38 = (bf16[64,16,128]{2,1,0:T(8,128)(2,1)S(1)}, bf16[64,16,128]{2,1,0:T(8,128)(2,1)S(1)}, u32[]{:S(2)}, u32[]{:S(2)}) collective-permute-start(bf16[64,16,128]{2,1,0:T(8,128)(2,1)S(1)} %get-tuple-element.139), channel_id=1, source_target_pairs={{0,4},{4,12},{12,8},{8,0},{1,5},{5,13},{13,9},{9,1},{2,6},{6,14},{... | collective-permute-start | bytes 786440 | tf_op jit(solution)/shard_map/ppermute | solution.py:552
  149.7 11.2 %collective-permute-start.39 = (bf16[64,16,128]{2,1,0:T(8,128)(2,1)S(1)}, bf16[64,16,128]{2,1,0:T(8,128)(2,1)S(1)}, u32[]{:S(2)}, u32[]{:S(2)}) collective-permute-start(bf16[64,16,128]{2,1,0:T(8,128)(2,1)S(1)} %get-tuple-element.141), channel_id=1, source_target_pairs={{0,4},{4,12},{12,8},{8,0},{1,5},{5,13},{13,9},{9,1},{2,6},{6,14},{... | collective-permute-start | bytes 786440 | tf_op jit(solution)/shard_map/ppermute | solution.py:552
  156.1 10.5 %collective-permute-start.42 = (bf16[64,16,128]{2,1,0:T(8,128)(2,1)}, bf16[64,16,128]{2,1,0:T(8,128)(2,1)}, u32[]{:S(2)}, u32[]{:S(2)}) collective-permute-start(bf16[64,16,128]{2,1,0:T(8,128)(2,1)} %add_convert_fusion.3), channel_id=1, source_target_pairs={{0,4},{4,12},{12,8},{8,0},{1,5},{5,13},{13,9},{9,1},{2,6},{6,14},{... | collective-permute-start | bytes 786440 | tf_op jit(solution)/shard_map/ppermute | solution.py:552
  161.7 10.6 %collective-permute-start.40 = (bf16[64,16,128]{2,1,0:T(8,128)(2,1)}, bf16[64,16,128]{2,1,0:T(8,128)(2,1)}, u32[]{:S(2)}, u32[]{:S(2)}) collective-permute-start(bf16[64,16,128]{2,1,0:T(8,128)(2,1)} %add_convert_fusion.2), channel_id=1, source_target_pairs={{0,4},{4,12},{12,8},{8,0},{1,5},{5,13},{13,9},{9,1},{2,6},{6,14},{... | collective-permute-start | bytes 786440 | tf_op jit(solution)/shard_map/ppermute | solution.py:552
  167.7 29.6 %collective-permute-start.43 = (bf16[64,16,128]{2,1,0:T(8,128)(2,1)S(1)}, bf16[64,16,128]{2,1,0:T(8,128)(2,1)S(1)}, u32[]{:S(2)}, u32[]{:S(2)}) collective-permute-start(bf16[64,16,128]{2,1,0:T(8,128)(2,1)S(1)} %add_convert_fusion), channel_id=1, source_target_pairs={{0,4},{4,12},{12,8},{8,0},{1,5},{5,13},{13,9},{9,1},{2,6},{6,14},{... | collective-permute-start | bytes 786440 | tf_op jit(solution)/shard_map/ppermute | solution.py:552
  173.3 26.1 %collective-permute-start.41 = (bf16[64,16,128]{2,1,0:T(8,128)(2,1)S(1)}, bf16[64,16,128]{2,1,0:T(8,128)(2,1)S(1)}, u32[]{:S(2)}, u32[]{:S(2)}) collective-permute-start(bf16[64,16,128]{2,1,0:T(8,128)(2,1)S(1)} %add_convert_fusion.1), channel_id=1, source_target_pairs={{0,4},{4,12},{12,8},{8,0},{1,5},{5,13},{13,9},{9,1},{2,6},{6,14},{... | collective-permute-start | bytes 786440 | tf_op jit(solution)/shard_map/ppermute | solution.py:552
  (59 other events, 424.6 us)

commit v10 on v9

--- a/solution.py
+++ b/solution.py
@@ -597,11 +597,12 @@
         return dright_part([blocks[0], blocks[1], blocks[2], after(blocks[3], *others)], left)
 
     tri_a, tri_b = triangle([a0, a1, a2, after(a3, b3)]), triangle([b0, b1, b2, b3])
-    x_a, x_b = over_x(after(tri_a[2], c1)), over_x(tri_b[2])
+    x_a = over_x(after(tri_a[2], c1))
     c2, d2 = forward(after(c1, tri_a[2])), forward(after(d1, tri_b[2]))
-    dtri_a, gate_a, g_out, g_gate = middle(0, tri_a, after(x_a, d1))
+    x_b = over_x(tri_b[2])
+    dtri_a, gate_a, g_out, g_gate = middle(0, tri_a, after(x_a, d1, c2))
     blocks_a = spread(dtri_a)
-    dtri_b, gate_b, g_out, g_gate = middle(1, tri_b, after(x_b, c2))
+    dtri_b, gate_b, g_out, g_gate = middle(1, tri_b, after(x_b, d2))
     blocks_b = spread(dtri_b)
     c3, d3 = forward(after(c2, dtri_a)), forward(after(d2, dtri_b))
     part_a = dright(blocks_a, d2)
@@ -609,36 +610,29 @@
     r_a, r_b = forward(part_a[1]), forward(part_b[1])
 
     tri_c = triangle([c0, c1, c2, after(c3, part_a[1])])
+    x_c = over_x(tri_c[2])
+    dtri_c, gate_c, g_out, g_gate = middle(2, tri_c, after(x_c, d3, part_b[1]))
+    blocks_c = spread(dtri_c)
     r_a = plus(r_a, part_a[2])
-    tri_d = triangle([d0, d1, d2, after(d3, part_b[1], r_a, tri_c[2])])
-    x_c, x_d = over_x(tri_c[2]), over_x(tri_d[2])
-    r_a = plus(forward(r_a), part_a[3])
+    tri_d = triangle([d0, d1, d2, after(d3, dtri_c, r_a)])
+    r_a2 = forward(r_a)
+    x_d = over_x(after(tri_d[2], r_b))
     r_b = plus(r_b, part_b[2])
+    r_b2 = forward(r_b)
+    r_a2 = plus(r_a2, part_a[3])
+    dtri_d, gate_d, g_out, g_gate = middle(3, tri_d, after(x_d, r_a2))
+    blocks_d = spread(dtri_d)
+    r_a3 = forward(r_a2)
+    r_b2 = plus(r_b2, part_b[3])
     d_left = dleft_part(
-        [after(blocks_a[0], tri_d[2], r_b)] + blocks_a[1:] + blocks_b,
+        [after(blocks_a[0], dtri_d, r_b2)] + blocks_a[1:] + blocks_b,
         [tri_a[3], tri_b[3]],
         jnp.zeros((HALF, HALF, WIDTH), F32),
     )
-    r_b = plus(forward(r_b), part_b[3])
-    dtri_c, gate_c, g_out, g_gate = middle(2, tri_c, after(x_c, r_a, d_left))
-    blocks_c = spread(dtri_c)
-    dtri_d, gate_d, g_out, g_gate = middle(3, tri_d, after(x_d, r_b))
-    blocks_d = spread(dtri_d)
-    r_a3, r_b3 = forward(r_a), forward(r_b)
-    part_c = dright(blocks_c, r_a3)
+    r_b3 = forward(r_b2)
+    part_c = dright(blocks_c, r_a3, d_left)
     part_d = dright(blocks_d, r_b3, part_c[1])
 
-    r_c, r_d = forward(part_c[1]), forward(part_d[1])
-    r_c = plus(r_c, part_c[2])
-    d_left = dleft_part(
-        [after(blocks_c[0], part_d[1], r_c)] + blocks_c[1:] + blocks_d, [tri_c[3], tri_d[3]], d_left
-    )
-    r_c = forward(r_c)
-    r_d = plus(r_d, part_d[2])
-    partial, g_a = final_a_part(
-        pair_tiles, after(d_left, r_d), tokens, gain_in, w_proj, w_gate, [gate_a, gate_b, gate_c, gate_d]
-    )
-    r_d = forward(r_d)
     zero = jnp.zeros((width, 2 * width), F32)
 
     def final(s, sums, so_far, into):
@@ -646,13 +640,22 @@
             s, pair_tiles, partial, sums, tokens, exponents, gain_in, w_proj, so_far, into
         )
 
-    r_c = plus(r_c, part_c[3])
-    d_pair, g_first = final(0, (part_a[0], after(r_a3, r_c)), zero, gain_in)
+    r_c, r_d = forward(part_c[1]), forward(part_d[1])
+    d_left = dleft_part(
+        [after(blocks_c[0], part_d[1])] + blocks_c[1:] + blocks_d, [tri_c[3], tri_d[3]], d_left
+    )
+    r_c = plus(r_c, after(part_c[2], d_left))
+    partial, g_a = final_a_part(
+        pair_tiles, after(d_left, r_c), tokens, gain_in, w_proj, w_gate, [gate_a, gate_b, gate_c, gate_d]
+    )
     r_c = forward(r_c)
-    r_d = plus(r_d, part_d[3])
-    d_pair, g_first = final(1, (part_b[0], after(r_b3, r_d)), g_first, d_pair)
+    r_d = plus(r_d, after(part_d[2], g_a))
+    d_pair, g_first = final(0, (part_a[0], after(r_a3, r_d)), zero, gain_in)
     r_d = forward(r_d)
-
+    r_c = plus(r_c, after(part_c[3], g_first))
+    d_pair, g_first = final(1, (part_b[0], after(r_b3, r_c)), g_first, d_pair)
+    r_c = forward(r_c)
+    r_d = forward(plus(r_d, after(part_d[3], g_first)))
     d_pair, g_last = final(2, (part_c[0], r_c), g_first, d_pair)
     d_pair, g_last = final(3, (part_d[0], r_d), g_last, d_pair)
 

time: 224 us -> 223 us (level)
  waiting for transfers between devices: 84.1 us -> 91.3 us
  local copies, waits for them, and re-layouts: 13.5 us -> 7.26 us
    unnamed x87 -> x57, local copies, waits for them, and re-layouts: 11.6 us -> 5.39 us
    ppermute x2, waiting for transfers between devices: 6.91 us -> 10.6 us  [over_row(): return lax.ppermute(a, 'row', [(k, k ^ bit) for k in range(4)])]
    ppermute x9, starting transfers between devices: 10.4 us -> 13.9 us  [over_x(): return lax.ppermute(a, 'col', [(k, k ^ 2) for k in range(4)])]
    ppermute x2, starting transfers between devices: 3.36 us -> 0.22 us  [over_row(): return lax.ppermute(a, 'row', [(k, k ^ bit) for k in range(4)])]
    ppermute x9, waiting for transfers between devices: 18.4 us -> 21.4 us  [over_x(): return lax.ppermute(a, 'col', [(k, k ^ 2) for k in range(4)])]
  transfers between devices with their start and end apart: 49 -> 49, of which waited for: 28 -> 26; matrix products, arithmetic and copies ran while one was open for 3% -> 3% of each run, Pallas kernels for 24% -> 22%
where the time goes in v10:
time: 223 us
  waiting for transfers between devices  91.3 us (41%)
  Pallas kernels  61.1 us (27%)
  starting transfers between devices  55.4 us (25%)
  local copies, waits for them, and re-layouts  7.26 us (3%)
  other arithmetic  6.64 us (3%)
    ppermute x24, waiting for transfers between devices, forward(): return lax.ppermute(a, 'row', [(0, 1), (1, 3), (3, 2), (2, 0)])  56.4 us
    ppermute x24, starting transfers between devices, forward(): return lax.ppermute(a, 'row', [(0, 1), (1, 3), (3, 2), (2, 0)])  39.1 us
    ppermute x9, waiting for transfers between devices, over_x(): return lax.ppermute(a, 'col', [(k, k ^ 2) for k in range(4)])  21.4 us
    pallas_call x4, Pallas kernels, mid_part(): pl.pallas_call(mid_kernel, grid=(1,), out_shape=(PANEL, pltpu.HBM(PANEL.s...  14.1 us
    ppermute x9, starting transfers between devices, over_x(): return lax.ppermute(a, 'col', [(k, k ^ 2) for k in range(4)])  13.9 us
    ppermute x2, waiting for transfers between devices, over_row(): return lax.ppermute(a, 'row', [(k, k ^ bit) for k in range(4)])  10.6 us
    pallas_call x4, Pallas kernels, dright_part(): pl.pallas_call(dright_kernel, grid=(HALF // GROUP,), out_shape=(pltpu.HBM...  8.5 us
    pallas_call x4, Pallas kernels, final_b_part(): pl.pallas_call(functools.partial(final_b_kernel, s * steps), grid=(steps,...  8.42 us
  transfers between devices with their start and end apart: 49, of which 26 were waited for; matrix products, arithmetic and copies ran while one was open for 3% of the time, Pallas kernels for 22%

profile of v10, /device:TPU:0, one launch (start us, length us, event | category | flops | bytes accessed | tf_op | source)
XLA Modules:
  0.0 222.9 jit_solution(1743053823137178938)
XLA Ops:
  2.6 3.1 %collective-permute-start = (bf16[64,16,128]{2,1,0:T(8,128)(2,1)S(1)}, bf16[64,16,128]{2,1,0:T(8,128)(2,1)S(1)}, u32[]{:S(2)}, u32[]{:S(2)}) collective-permute-start(bf16[64,16,128]{2,1,0:T(8,128)(2,1)S(1)} %right_part.5.s0), channel_id=1, source_target_pairs={{0,4},{4,12},{12,8},{8,0},{1,5},{5,13},{13,9},{9,1},{2,6},{6,14},{... | collective-permute-start | bytes 786440 | tf_op jit(solution)/shard_map/ppermute | solution.py:552
  7.6 2.6 %collective-permute-start.3 = (bf16[64,16,128]{2,1,0:T(8,128)(2,1)S(1)}, bf16[64,16,128]{2,1,0:T(8,128)(2,1)S(1)}, u32[]{:S(2)}, u32[]{:S(2)}) collective-permute-start(bf16[64,16,128]{2,1,0:T(8,128)(2,1)S(1)} %right_part.6.s0), channel_id=1, source_target_pairs={{0,4},{4,12},{12,8},{8,0},{1,5},{5,13},{13,9},{9,1},{2,6},{6,14},{... | collective-permute-start | bytes 786440 | tf_op jit(solution)/shard_map/ppermute | solution.py:552
  10.2 5.2 %left_part.1.left_ref.refs_4_ = bf16[64,2,64,128]{3,2,1,0:T(8,128)(2,1)S(1)} custom-call(bf16[64,64,128]{2,1,0:T(8,128)(2,1)} %x_ref.27, f32[1,128]{1,0:T(1,128)} %bitcast.25, bf16[128,512]{1,0:T(8,128)(2,1)} %w_ref.19, s32[1,256]{1,0:T(1,128)} %bitcast.40), custom_call_target="tpu_custom_call" | custom-call | flops 262144 | bytes 3072 | tf_op jit(solution)/shard_map/left_part/pallas_call | solution.py:410
  16.0 2.9 %collective-permute-done.3.s1 = bf16[64,16,128]{2,1,0:T(8,128)(2,1)S(1)} collective-permute-done((bf16[64,16,128]{2,1,0:T(8,128)(2,1)S(1)}, bf16[64,16,128]{2,1,0:T(8,128)(2,1)S(1)}, u32[]{:S(2)}, u32[]{:S(2)}) %collective-permute-start.3) | collective-permute-done | bytes 262176 | tf_op jit(solution)/shard_map/ppermute | solution.py:552
  27.9 3.4 %collective-permute-done.4.s2 = bf16[64,16,128]{2,1,0:T(8,128)(2,1)S(1)} collective-permute-done((bf16[64,16,128]{2,1,0:T(8,128)(2,1)S(1)}, bf16[64,16,128]{2,1,0:T(8,128)(2,1)S(1)}, u32[]{:S(2)}, u32[]{:S(2)}) %collective-permute-start.4) | collective-permute-done | bytes 262176 | tf_op jit(solution)/shard_map/ppermute | solution.py:552
  31.8 5.1 %collective-permute-done.6.s3 = bf16[64,16,128]{2,1,0:T(8,128)(2,1)S(1)} collective-permute-done((bf16[64,16,128]{2,1,0:T(8,128)(2,1)S(1)}, bf16[64,16,128]{2,1,0:T(8,128)(2,1)S(1)}, u32[]{:S(2)}, u32[]{:S(2)}) %collective-permute-start.6) | collective-permute-done | bytes 262176 | tf_op jit(solution)/shard_map/ppermute | solution.py:552
  36.9 4.2 %collective-permute-done.5.s3 = bf16[64,16,128]{2,1,0:T(8,128)(2,1)S(1)} collective-permute-done((bf16[64,16,128]{2,1,0:T(8,128)(2,1)S(1)}, bf16[64,16,128]{2,1,0:T(8,128)(2,1)S(1)}, u32[]{:S(2)}, u32[]{:S(2)}) %collective-permute-start.5) | collective-permute-done | bytes 262176 | tf_op jit(solution)/shard_map/ppermute | solution.py:552
  46.3 3.4 %collective-permute-start.10 = (bf16[64,16,128]{2,1,0:T(8,128)(2,1)S(1)}, bf16[64,16,128]{2,1,0:T(8,128)(2,1)S(1)}, u32[]{:S(2)}, u32[]{:S(2)}) collective-permute-start(bf16[64,16,128]{2,1,0:T(8,128)(2,1)S(1)} %right_part.7.s0), channel_id=1, source_target_pairs={{0,4},{4,12},{12,8},{8,0},{1,5},{5,13},{13,9},{9,1},{2,6},{6,14},{... | collective-permute-start | bytes 786440 | tf_op jit(solution)/shard_map/ppermute | solution.py:552
  49.8 3.5 %collective-permute-done.2.s1 = bf16[64,16,128]{2,1,0:T(8,128)(2,1)S(1)} collective-permute-done((bf16[64,16,128]{2,1,0:T(8,128)(2,1)S(1)}, bf16[64,16,128]{2,1,0:T(8,128)(2,1)S(1)}, u32[]{:S(2)}, u32[]{:S(2)}) %collective-permute-start.2) | collective-permute-done | bytes 262176 | tf_op jit(solution)/shard_map/ppermute | solution.py:552
  55.6 3.3 %collective-permute-done.10.s1 = bf16[64,16,128]{2,1,0:T(8,128)(2,1)S(1)} collective-permute-done((bf16[64,16,128]{2,1,0:T(8,128)(2,1)S(1)}, bf16[64,16,128]{2,1,0:T(8,128)(2,1)S(1)}, u32[]{:S(2)}, u32[]{:S(2)}) %collective-permute-start.10) | collective-permute-done | bytes 262176 | tf_op jit(solution)/shard_map/ppermute | solution.py:552
  60.7 3.4 %collective-permute-done.8.s2 = bf16[64,16,128]{2,1,0:T(8,128)(2,1)S(1)} collective-permute-done((bf16[64,16,128]{2,1,0:T(8,128)(2,1)S(1)}, bf16[64,16,128]{2,1,0:T(8,128)(2,1)S(1)}, u32[]{:S(2)}, u32[]{:S(2)}) %collective-permute-start.8) | collective-permute-done | bytes 262176 | tf_op jit(solution)/shard_map/ppermute | solution.py:552
  64.1 3.5 %mid_part.4 = (bf16[64,16,128]{2,1,0:T(8,128)(2,1)S(1)}, bf16[64,16,128]{2,1,0:T(8,128)(2,1)}, f32[128,128]{1,0:T(8,128)S(1)}, f32[128,128]{1,0:T(8,128)S(1)}) custom-call(bf16[64,16,128]{2,1,0:T(8,128)(2,1)S(1)} %get-tuple-element.101.a_ref, bf16[2,64,16,128]{3,2,1,0:T(8,128)(2,1)S(1)} %collective-permute-done.7.b_ref, ...), custom_call_target="tpu_custom_call" | custom-call | flops 196608 | bytes 2048 | tf_op jit(solution)/shard_map/mid_part/pallas_call | solution.py:443
  70.1 5.2 %collective-permute-done.12.refs_1_ = bf16[64,16,128]{2,1,0:T(8,128)(2,1)S(1)} collective-permute-done((bf16[64,16,128]{2,1,0:T(8,128)(2,1)S(1)}, bf16[64,16,128]{2,1,0:T(8,128)(2,1)S(1)}, u32[]{:S(2)}, u32[]{:S(2)}) %collective-permute-start.12) | collective-permute-done | bytes 262176 | tf_op jit(solution)/shard_map/ppermute | solution.py:558
  80.5 4.4 %collective-permute-done.11.s3 = bf16[64,16,128]{2,1,0:T(8,128)(2,1)S(1)} collective-permute-done((bf16[64,16,128]{2,1,0:T(8,128)(2,1)S(1)}, bf16[64,16,128]{2,1,0:T(8,128)(2,1)S(1)}, u32[]{:S(2)}, u32[]{:S(2)}) %collective-permute-start.11) | collective-permute-done | bytes 262176 | tf_op jit(solution)/shard_map/ppermute | solution.py:552
  87.0 3.5 %mid_part.5 = (bf16[64,16,128]{2,1,0:T(8,128)(2,1)S(1)}, bf16[64,16,128]{2,1,0:T(8,128)(2,1)}, f32[128,128]{1,0:T(8,128)S(1)}, f32[128,128]{1,0:T(8,128)S(1)}) custom-call(bf16[64,16,128]{2,1,0:T(8,128)(2,1)S(1)} %get-tuple-element.116.a_ref, bf16[2,64,16,128]{3,2,1,0:T(8,128)(2,1)S(1)} %collective-permute-done.15.b_ref, ...), custom_call_target="tpu_custom_call" | custom-call | flops 196608 | bytes 2048 | tf_op jit(solution)/shard_map/mid_part/pallas_call | solution.py:443
  92.3 7.0 %collective-permute-done.21.refs_1_.refs_5_ = bf16[64,16,128]{2,1,0:T(8,128)(2,1)S(1)} collective-permute-done((bf16[64,16,128]{2,1,0:T(8,128)(2,1)S(1)}, bf16[64,16,128]{2,1,0:T(8,128)(2,1)S(1)}, u32[]{:S(2)}, u32[]{:S(2)}) %collective-permute-start.21) | collective-permute-done | bytes 262176 | tf_op jit(solution)/shard_map/ppermute | solution.py:558
  100.5 3.4 %collective-permute-start.24 = (bf16[64,16,128]{2,1,0:T(8,128)(2,1)S(1)}, bf16[64,16,128]{2,1,0:T(8,128)(2,1)S(1)}, u32[]{:S(2)}, u32[]{:S(2)}) collective-permute-start(bf16[64,16,128]{2,1,0:T(8,128)(2,1)S(1)} %get-tuple-element.111), channel_id=1, source_target_pairs={{0,4},{4,12},{12,8},{8,0},{1,5},{5,13},{13,9},{9,1},{2,6},{6,14},{... | collective-permute-start | bytes 786440 | tf_op jit(solution)/shard_map/ppermute | solution.py:552
  107.9 6.6 %collective-permute-done.24 = bf16[64,16,128]{2,1,0:T(8,128)(2,1)S(1)} collective-permute-done((bf16[64,16,128]{2,1,0:T(8,128)(2,1)S(1)}, bf16[64,16,128]{2,1,0:T(8,128)(2,1)S(1)}, u32[]{:S(2)}, u32[]{:S(2)}) %collective-permute-start.24) | collective-permute-done | bytes 262176 | tf_op jit(solution)/shard_map/ppermute | solution.py:552
  114.6 3.5 %mid_part.6 = (bf16[64,16,128]{2,1,0:T(8,128)(2,1)S(1)}, bf16[64,16,128]{2,1,0:T(8,128)(2,1)}, f32[128,128]{1,0:T(8,128)S(1)}, f32[128,128]{1,0:T(8,128)S(1)}) custom-call(bf16[64,16,128]{2,1,0:T(8,128)(2,1)S(1)} %get-tuple-element.113.a_ref, bf16[2,64,16,128]{3,2,1,0:T(8,128)(2,1)S(1)} %collective-permute-done.17.b_ref, ...), custom_call_target="tpu_custom_call" | custom-call | flops 196608 | bytes 2048 | tf_op jit(solution)/shard_map/mid_part/pallas_call | solution.py:443
  121.0 3.4 %collective-permute-start.28 = (bf16[64,16,128]{2,1,0:T(8,128)(2,1)S(1)}, bf16[64,16,128]{2,1,0:T(8,128)(2,1)S(1)}, u32[]{:S(2)}, u32[]{:S(2)}) collective-permute-start(bf16[64,16,128]{2,1,0:T(8,128)(2,1)S(1)} %add_convert_fusion.7), channel_id=1, source_target_pairs={{0,4},{4,12},{12,8},{8,0},{1,5},{5,13},{13,9},{9,1},{2,6},{6,14},{... | collective-permute-start | bytes 786440 | tf_op jit(solution)/shard_map/ppermute | solution.py:552
  126.2 4.0 %collective-permute-done.26 = bf16[64,16,128]{2,1,0:T(8,128)(2,1)S(1)} collective-permute-done((bf16[64,16,128]{2,1,0:T(8,128)(2,1)S(1)}, bf16[64,16,128]{2,1,0:T(8,128)(2,1)S(1)}, u32[]{:S(2)}, u32[]{:S(2)}) %collective-permute-start.26) | collective-permute-done | bytes 262176 | tf_op jit(solution)/shard_map/ppermute | solution.py:552
  132.9 3.0 %collective-permute-done.28 = bf16[64,16,128]{2,1,0:T(8,128)(2,1)S(1)} collective-permute-done((bf16[64,16,128]{2,1,0:T(8,128)(2,1)S(1)}, bf16[64,16,128]{2,1,0:T(8,128)(2,1)S(1)}, u32[]{:S(2)}, u32[]{:S(2)}) %collective-permute-start.28) | collective-permute-done | bytes 262176 | tf_op jit(solution)/shard_map/ppermute | solution.py:552
  138.1 3.5 %mid_part.7 = (bf16[64,16,128]{2,1,0:T(8,128)(2,1)S(1)}, bf16[64,16,128]{2,1,0:T(8,128)(2,1)}, f32[128,128]{1,0:T(8,128)S(1)}, f32[128,128]{1,0:T(8,128)S(1)}) custom-call(bf16[64,16,128]{2,1,0:T(8,128)(2,1)S(1)} %get-tuple-element.130.a_ref, bf16[2,64,16,128]{3,2,1,0:T(8,128)(2,1)S(1)} %collective-permute-done.25.b_ref, ...), custom_call_target="tpu_custom_call" | custom-call | flops 196608 | bytes 2048 | tf_op jit(solution)/shard_map/mid_part/pallas_call | solution.py:443
  144.3 3.6 %collective-permute-start.33 = (bf16[64,16,128]{2,1,0:T(8,128)(2,1)S(1)}, bf16[64,16,128]{2,1,0:T(8,128)(2,1)S(1)}, u32[]{:S(2)}, u32[]{:S(2)}) collective-permute-start(bf16[64,16,128]{2,1,0:T(8,128)(2,1)S(1)} %add_convert_fusion.4), channel_id=1, source_target_pairs={{0,4},{4,12},{12,8},{8,0},{1,5},{5,13},{13,9},{9,1},{2,6},{6,14},{... | collective-permute-start | bytes 786440 | tf_op jit(solution)/shard_map/ppermute | solution.py:552
  148.6 4.9 %collective-permute-done.37.b_ref = bf16[64,16,128]{2,1,0:T(8,128)(2,1)S(1)} collective-permute-done((bf16[64,16,128]{2,1,0:T(8,128)(2,1)S(1)}, bf16[64,16,128]{2,1,0:T(8,128)(2,1)S(1)}, u32[]{:S(2)}, u32[]{:S(2)}) %collective-permute-start.37) | collective-permute-done | bytes 262176 | tf_op jit(solution)/shard_map/ppermute | solution.py:552
  161.2 3.4 %collective-permute-start.39 = (bf16[64,16,128]{2,1,0:T(8,128)(2,1)S(1)}, bf16[64,16,128]{2,1,0:T(8,128)(2,1)S(1)}, u32[]{:S(2)}, u32[]{:S(2)}) collective-permute-start(bf16[64,16,128]{2,1,0:T(8,128)(2,1)S(1)} %get-tuple-element.147), channel_id=1, source_target_pairs={{0,4},{4,12},{12,8},{8,0},{1,5},{5,13},{13,9},{9,1},{2,6},{6,14},{... | collective-permute-start | bytes 786440 | tf_op jit(solution)/shard_map/ppermute | solution.py:552
  169.2 5.9 %final_a_part.1 = (f32[128,4096]{1,0:T(8,128)S(1)}, f32[128,256]{1,0:T(8,128)S(1)}) custom-call(bf16[64,64,128]{2,1,0:T(8,128)(2,1)S(1)} %copy-done, f32[64,64,128]{2,1,0:T(8,128)S(1)} %dleft_part.3.dleft_ref, s32[1,256]{1,0:T(1,128)S(1)} %bitcast.43, f32[1,128]{1,0:T(1,128)S(1)} %bitcast.32, bf16[128,512]{1,0:T(8,128)(2,1)S(1)} %copy-done.2, ...), custom_call_target="tpu_custom_call" | custom-call | flops 917504 | bytes 8192 | tf_op jit(solution)/shard_map/final_a_part/pallas_call | solution.py:487
  175.9 3.4 %collective-permute-start.40 = (bf16[64,16,128]{2,1,0:T(8,128)(2,1)}, bf16[64,16,128]{2,1,0:T(8,128)(2,1)}, u32[]{:S(2)}, u32[]{:S(2)}) collective-permute-start(bf16[64,16,128]{2,1,0:T(8,128)(2,1)} %add_convert_fusion.2), channel_id=1, source_target_pairs={{0,4},{4,12},{12,8},{8,0},{1,5},{5,13},{13,9},{9,1},{2,6},{6,14},{... | collective-permute-start | bytes 786440 | tf_op jit(solution)/shard_map/ppermute | solution.py:552
  191.1 3.5 %collective-permute-done.43.b_ref = bf16[64,16,128]{2,1,0:T(8,128)(2,1)S(1)} collective-permute-done((bf16[64,16,128]{2,1,0:T(8,128)(2,1)S(1)}, bf16[64,16,128]{2,1,0:T(8,128)(2,1)S(1)}, u32[]{:S(2)}, u32[]{:S(2)}) %collective-permute-start.43) | collective-permute-done | bytes 262176 | tf_op jit(solution)/shard_map/ppermute | solution.py:552
  204.4 4.6 %collective-permute-done.45 = bf16[64,768]{1,0:T(8,128)(2,1)S(1)} collective-permute-done((bf16[64,768]{1,0:T(8,128)(2,1)S(1)}, bf16[64,768]{1,0:T(8,128)(2,1)S(1)}, u32[]{:S(2)}, u32[]{:S(2)}) %collective-permute-start.45) | collective-permute-done | bytes 98336 | tf_op jit(solution)/shard_map/ppermute | solution.py:558
  209.2 4.5 %collective-permute-done.46 = bf16[64,768]{1,0:T(8,128)(2,1)S(1)} collective-permute-done((bf16[64,768]{1,0:T(8,128)(2,1)S(1)}, bf16[64,768]{1,0:T(8,128)(2,1)S(1)}, u32[]{:S(2)}, u32[]{:S(2)}) %collective-permute-start.46) | collective-permute-done | bytes 98336 | tf_op jit(solution)/shard_map/ppermute | solution.py:555
  213.8 6.1 %collective-permute-done.47 = bf16[64,768]{1,0:T(8,128)(2,1)S(1)} collective-permute-done((bf16[64,768]{1,0:T(8,128)(2,1)S(1)}, bf16[64,768]{1,0:T(8,128)(2,1)S(1)}, u32[]{:S(2)}, u32[]{:S(2)}) %collective-permute-start.47) | collective-permute-done | bytes 98336 | tf_op jit(solution)/shard_map/ppermute | solution.py:555
  (171 shorter events, 90.8 us)
Async XLA Ops:
  2.6 12.9 %collective-permute-start = (bf16[64,16,128]{2,1,0:T(8,128)(2,1)S(1)}, bf16[64,16,128]{2,1,0:T(8,128)(2,1)S(1)}, u32[]{:S(2)}, u32[]{:S(2)}) collective-permute-start(bf16[64,16,128]{2,1,0:T(8,128)(2,1)S(1)} %right_part.5.s0), channel_id=1, source_target_pairs={{0,4},{4,12},{12,8},{8,0},{1,5},{5,13},{13,9},{9,1},{2,6},{6,14},{... | collective-permute-start | bytes 786440 | tf_op jit(solution)/shard_map/ppermute | solution.py:552
  7.6 11.2 %collective-permute-start.3 = (bf16[64,16,128]{2,1,0:T(8,128)(2,1)S(1)}, bf16[64,16,128]{2,1,0:T(8,128)(2,1)S(1)}, u32[]{:S(2)}, u32[]{:S(2)}) collective-permute-start(bf16[64,16,128]{2,1,0:T(8,128)(2,1)S(1)} %right_part.6.s0), channel_id=1, source_target_pairs={{0,4},{4,12},{12,8},{8,0},{1,5},{5,13},{13,9},{9,1},{2,6},{6,14},{... | collective-permute-start | bytes 786440 | tf_op jit(solution)/shard_map/ppermute | solution.py:552
  15.5 10.2 %collective-permute-start.1 = (bf16[64,16,128]{2,1,0:T(8,128)(2,1)S(1)}, bf16[64,16,128]{2,1,0:T(8,128)(2,1)S(1)}, u32[]{:S(2)}, u32[]{:S(2)}) collective-permute-start(bf16[64,16,128]{2,1,0:T(8,128)(2,1)S(1)} %collective-permute-done.s1), channel_id=1, source_target_pairs={{0,4},{4,12},{12,8},{8,0},{1,5},{5,13},{13,9},{9,1},{2,6},{6,14},{... | collective-permute-start | bytes 786440 | tf_op jit(solution)/shard_map/ppermute | solution.py:552
  18.8 12.5 %collective-permute-start.4 = (bf16[64,16,128]{2,1,0:T(8,128)(2,1)S(1)}, bf16[64,16,128]{2,1,0:T(8,128)(2,1)S(1)}, u32[]{:S(2)}, u32[]{:S(2)}) collective-permute-start(bf16[64,16,128]{2,1,0:T(8,128)(2,1)S(1)} %collective-permute-done.3.s1), channel_id=1, source_target_pairs={{0,4},{4,12},{12,8},{8,0},{1,5},{5,13},{13,9},{9,1},{2,6},{6,14},{... | collective-permute-start | bytes 786440 | tf_op jit(solution)/shard_map/ppermute | solution.py:552
  25.7 11.2 %collective-permute-start.6 = (bf16[64,16,128]{2,1,0:T(8,128)(2,1)S(1)}, bf16[64,16,128]{2,1,0:T(8,128)(2,1)S(1)}, u32[]{:S(2)}, u32[]{:S(2)}) collective-permute-start(bf16[64,16,128]{2,1,0:T(8,128)(2,1)S(1)} %collective-permute-done.1.s2), channel_id=1, source_target_pairs={{0,4},{4,12},{12,8},{8,0},{1,5},{5,13},{13,9},{9,1},{2,6},{6,14},{... | collective-permute-start | bytes 786440 | tf_op jit(solution)/shard_map/ppermute | solution.py:552
  31.3 9.8 %collective-permute-start.5 = (bf16[64,16,128]{2,1,0:T(8,128)(2,1)S(1)}, bf16[64,16,128]{2,1,0:T(8,128)(2,1)S(1)}, u32[]{:S(2)}, u32[]{:S(2)}) collective-permute-start(bf16[64,16,128]{2,1,0:T(8,128)(2,1)S(1)} %collective-permute-done.4.s2), channel_id=1, source_target_pairs={{0,4},{4,12},{12,8},{8,0},{1,5},{5,13},{13,9},{9,1},{2,6},{6,14},{... | collective-permute-start | bytes 786440 | tf_op jit(solution)/shard_map/ppermute | solution.py:552
  43.2 10.1 %collective-permute-start.2 = (bf16[64,16,128]{2,1,0:T(8,128)(2,1)S(1)}, bf16[64,16,128]{2,1,0:T(8,128)(2,1)S(1)}, u32[]{:S(2)}, u32[]{:S(2)}) collective-permute-start(bf16[64,16,128]{2,1,0:T(8,128)(2,1)S(1)} %right_part.4.s0), channel_id=1, source_target_pairs={{0,4},{4,12},{12,8},{8,0},{1,5},{5,13},{13,9},{9,1},{2,6},{6,14},{... | collective-permute-start | bytes 786440 | tf_op jit(solution)/shard_map/ppermute | solution.py:552
  46.1 23.1 %collective-permute-start.15 = (bf16[2,64,16,128]{3,2,1,0:T(8,128)(2,1)S(1)}, bf16[2,64,16,128]{3,2,1,0:T(8,128)(2,1)S(1)}, u32[]{:S(2)}, u32[]{:S(2)}) collective-permute-start(bf16[2,64,16,128]{3,2,1,0:T(8,128)(2,1)S(1)} %get-tuple-element.108), channel_id=1, source_target_pairs={{0,1},{1,0},{2,3},{3,2},{4,5},{5,4},{6,7},{7,6},{8,9},{9,8},{10,11... | collective-permute-start | bytes 1572872 | tf_op jit(solution)/shard_map/ppermute | solution.py:561
  46.3 12.6 %collective-permute-start.10 = (bf16[64,16,128]{2,1,0:T(8,128)(2,1)S(1)}, bf16[64,16,128]{2,1,0:T(8,128)(2,1)S(1)}, u32[]{:S(2)}, u32[]{:S(2)}) collective-permute-start(bf16[64,16,128]{2,1,0:T(8,128)(2,1)S(1)} %right_part.7.s0), channel_id=1, source_target_pairs={{0,4},{4,12},{12,8},{8,0},{1,5},{5,13},{13,9},{9,1},{2,6},{6,14},{... | collective-permute-start | bytes 786440 | tf_op jit(solution)/shard_map/ppermute | solution.py:552
  54.8 9.2 %collective-permute-start.8 = (bf16[64,16,128]{2,1,0:T(8,128)(2,1)S(1)}, bf16[64,16,128]{2,1,0:T(8,128)(2,1)S(1)}, u32[]{:S(2)}, u32[]{:S(2)}) collective-permute-start(bf16[64,16,128]{2,1,0:T(8,128)(2,1)S(1)} %collective-permute-done.2.s1), channel_id=1, source_target_pairs={{0,4},{4,12},{12,8},{8,0},{1,5},{5,13},{13,9},{9,1},{2,6},{6,14},{... | collective-permute-start | bytes 786440 | tf_op jit(solution)/shard_map/ppermute | solution.py:552
  69.3 9.1 %collective-permute-start.16 = (bf16[64,16,128]{2,1,0:T(8,128)(2,1)S(1)}, bf16[64,16,128]{2,1,0:T(8,128)(2,1)S(1)}, u32[]{:S(2)}, u32[]{:S(2)}) collective-permute-start(bf16[64,16,128]{2,1,0:T(8,128)(2,1)S(1)} %collective-permute-done.10.s1), channel_id=1, source_target_pairs={{0,4},{4,12},{12,8},{8,0},{1,5},{5,13},{13,9},{9,1},{2,6},{6,14},{... | collective-permute-start | bytes 786440 | tf_op jit(solution)/shard_map/ppermute | solution.py:552
  75.8 9.1 %collective-permute-start.11 = (bf16[64,16,128]{2,1,0:T(8,128)(2,1)S(1)}, bf16[64,16,128]{2,1,0:T(8,128)(2,1)S(1)}, u32[]{:S(2)}, u32[]{:S(2)}) collective-permute-start(bf16[64,16,128]{2,1,0:T(8,128)(2,1)S(1)} %collective-permute-done.8.s2), channel_id=1, source_target_pairs={{0,4},{4,12},{12,8},{8,0},{1,5},{5,13},{13,9},{9,1},{2,6},{6,14},{... | collective-permute-start | bytes 786440 | tf_op jit(solution)/shard_map/ppermute | solution.py:552
  76.6 10.4 %collective-permute-start.19 = (bf16[64,16,128]{2,1,0:T(8,128)(2,1)S(1)}, bf16[64,16,128]{2,1,0:T(8,128)(2,1)S(1)}, u32[]{:S(2)}, u32[]{:S(2)}) collective-permute-start(bf16[64,16,128]{2,1,0:T(8,128)(2,1)S(1)} %fusion.2), channel_id=1, source_target_pairs={{0,2},{1,3},{2,0},{3,1},{4,6},{5,7},{6,4},{7,5},{8,10},{9,11},{10,... | collective-permute-start | bytes 786440 | tf_op jit(solution)/shard_map/ppermute | solution.py:558
  86.9 17.0 %collective-permute-start.17 = (bf16[2,64,16,128]{3,2,1,0:T(8,128)(2,1)S(1)}, bf16[2,64,16,128]{3,2,1,0:T(8,128)(2,1)S(1)}, u32[]{:S(2)}, u32[]{:S(2)}) collective-permute-start(bf16[2,64,16,128]{3,2,1,0:T(8,128)(2,1)S(1)} %get-tuple-element.114), channel_id=1, source_target_pairs={{0,1},{1,0},{2,3},{3,2},{4,5},{5,4},{6,7},{7,6},{8,9},{9,8},{10,11... | collective-permute-start | bytes 1572872 | tf_op jit(solution)/shard_map/ppermute | solution.py:561
  99.7 14.8 %collective-permute-start.20 = (bf16[64,16,128]{2,1,0:T(8,128)(2,1)S(1)}, bf16[64,16,128]{2,1,0:T(8,128)(2,1)S(1)}, u32[]{:S(2)}, u32[]{:S(2)}) collective-permute-start(bf16[64,16,128]{2,1,0:T(8,128)(2,1)S(1)} %collective-permute-done.16.s2), channel_id=1, source_target_pairs={{0,4},{4,12},{12,8},{8,0},{1,5},{5,13},{13,9},{9,1},{2,6},{6,14},{... | collective-permute-start | bytes 786440 | tf_op jit(solution)/shard_map/ppermute | solution.py:552
  100.5 13.9 %collective-permute-start.24 = (bf16[64,16,128]{2,1,0:T(8,128)(2,1)S(1)}, bf16[64,16,128]{2,1,0:T(8,128)(2,1)S(1)}, u32[]{:S(2)}, u32[]{:S(2)}) collective-permute-start(bf16[64,16,128]{2,1,0:T(8,128)(2,1)S(1)} %get-tuple-element.111), channel_id=1, source_target_pairs={{0,4},{4,12},{12,8},{8,0},{1,5},{5,13},{13,9},{9,1},{2,6},{6,14},{... | collective-permute-start | bytes 786440 | tf_op jit(solution)/shard_map/ppermute | solution.py:552
  104.0 10.6 %collective-permute-start.18 = (bf16[64,16,128]{2,1,0:T(8,128)(2,1)S(1)}, bf16[64,16,128]{2,1,0:T(8,128)(2,1)S(1)}, u32[]{:S(2)}, u32[]{:S(2)}) collective-permute-start(bf16[64,16,128]{2,1,0:T(8,128)(2,1)S(1)} %fusion.1), channel_id=1, source_target_pairs={{0,2},{1,3},{2,0},{3,1},{4,6},{5,7},{6,4},{7,5},{8,10},{9,11},{10,... | collective-permute-start | bytes 786440 | tf_op jit(solution)/shard_map/ppermute | solution.py:558
  120.2 10.1 %collective-permute-start.26 = (bf16[64,16,128]{2,1,0:T(8,128)(2,1)S(1)}, bf16[64,16,128]{2,1,0:T(8,128)(2,1)S(1)}, u32[]{:S(2)}, u32[]{:S(2)}) collective-permute-start(bf16[64,16,128]{2,1,0:T(8,128)(2,1)S(1)} %get-tuple-element.123), channel_id=1, source_target_pairs={{0,4},{4,12},{12,8},{8,0},{1,5},{5,13},{13,9},{9,1},{2,6},{6,14},{... | collective-permute-start | bytes 786440 | tf_op jit(solution)/shard_map/ppermute | solution.py:552
  121.0 14.8 %collective-permute-start.28 = (bf16[64,16,128]{2,1,0:T(8,128)(2,1)S(1)}, bf16[64,16,128]{2,1,0:T(8,128)(2,1)S(1)}, u32[]{:S(2)}, u32[]{:S(2)}) collective-permute-start(bf16[64,16,128]{2,1,0:T(8,128)(2,1)S(1)} %add_convert_fusion.7), channel_id=1, source_target_pairs={{0,4},{4,12},{12,8},{8,0},{1,5},{5,13},{13,9},{9,1},{2,6},{6,14},{... | collective-permute-start | bytes 786440 | tf_op jit(solution)/shard_map/ppermute | solution.py:552
  124.4 19.3 %collective-permute-start.34 = (bf16[64,16,128]{2,1,0:T(8,128)(2,1)S(1)}, bf16[64,16,128]{2,1,0:T(8,128)(2,1)S(1)}, u32[]{:S(2)}, u32[]{:S(2)}) collective-permute-start(bf16[64,16,128]{2,1,0:T(8,128)(2,1)S(1)} %get-tuple-element.148.refs_0_), channel_id=1, source_target_pairs={{0,2},{1,3},{2,0},{3,1},{4,6},{5,7},{6,4},{7,5},{8,10},{9,11},{10,... | collective-permute-start | bytes 786440 | tf_op jit(solution)/shard_map/ppermute | solution.py:558
  132.1 12.2 %collective-permute-start.32 = (bf16[64,16,128]{2,1,0:T(8,128)(2,1)S(1)}, bf16[64,16,128]{2,1,0:T(8,128)(2,1)S(1)}, u32[]{:S(2)}, u32[]{:S(2)}) collective-permute-start(bf16[64,16,128]{2,1,0:T(8,128)(2,1)S(1)} %add_convert_fusion.5), channel_id=1, source_target_pairs={{0,4},{4,12},{12,8},{8,0},{1,5},{5,13},{13,9},{9,1},{2,6},{6,14},{... | collective-permute-start | bytes 786440 | tf_op jit(solution)/shard_map/ppermute | solution.py:552
  143.4 10.1 %collective-permute-start.37 = (bf16[64,16,128]{2,1,0:T(8,128)(2,1)S(1)}, bf16[64,16,128]{2,1,0:T(8,128)(2,1)S(1)}, u32[]{:S(2)}, u32[]{:S(2)}) collective-permute-start(bf16[64,16,128]{2,1,0:T(8,128)(2,1)S(1)} %add_convert_fusion.6), channel_id=1, source_target_pairs={{0,4},{4,12},{12,8},{8,0},{1,5},{5,13},{13,9},{9,1},{2,6},{6,14},{... | collective-permute-start | bytes 786440 | tf_op jit(solution)/shard_map/ppermute | solution.py:552
  143.7 11.7 %collective-permute-start.36 = (bf16[64,16,128]{2,1,0:T(8,128)(2,1)S(1)}, bf16[64,16,128]{2,1,0:T(8,128)(2,1)S(1)}, u32[]{:S(2)}, u32[]{:S(2)}) collective-permute-start(bf16[64,16,128]{2,1,0:T(8,128)(2,1)S(1)} %collective-permute-done.34.refs_1_), channel_id=1, source_target_pairs={{0,1},{1,0},{2,3},{3,2},{4,5},{5,4},{6,7},{7,6},{8,9},{9,8},{10,11... | collective-permute-start | bytes 786440 | tf_op jit(solution)/shard_map/ppermute | solution.py:561
  143.7 11.7 %collective-permute-start.35 = (bf16[64,16,128]{2,1,0:T(8,128)(2,1)S(1)}, bf16[64,16,128]{2,1,0:T(8,128)(2,1)S(1)}, u32[]{:S(2)}, u32[]{:S(2)}) collective-permute-start(bf16[64,16,128]{2,1,0:T(8,128)(2,1)S(1)} %get-tuple-element.148.refs_0_), channel_id=1, source_target_pairs={{0,1},{1,0},{2,3},{3,2},{4,5},{5,4},{6,7},{7,6},{8,9},{9,8},{10,11... | collective-permute-start | bytes 786440 | tf_op jit(solution)/shard_map/ppermute | solution.py:561
  144.3 14.1 %collective-permute-start.33 = (bf16[64,16,128]{2,1,0:T(8,128)(2,1)S(1)}, bf16[64,16,128]{2,1,0:T(8,128)(2,1)S(1)}, u32[]{:S(2)}, u32[]{:S(2)}) collective-permute-start(bf16[64,16,128]{2,1,0:T(8,128)(2,1)S(1)} %add_convert_fusion.4), channel_id=1, source_target_pairs={{0,4},{4,12},{12,8},{8,0},{1,5},{5,13},{13,9},{9,1},{2,6},{6,14},{... | collective-permute-start | bytes 786440 | tf_op jit(solution)/shard_map/ppermute | solution.py:552
  148.6 9.8 %collective-permute-start.31 = (bf16[64,16,128]{2,1,0:T(8,128)(2,1)S(1)}, bf16[64,16,128]{2,1,0:T(8,128)(2,1)S(1)}, u32[]{:S(2)}, u32[]{:S(2)}) collective-permute-start(bf16[64,16,128]{2,1,0:T(8,128)(2,1)S(1)} %collective-permute-done.29.refs_1_.refs_5_), channel_id=1, source_target_pairs={{0,1},{1,0},{2,3},{3,2},{4,5},{5,4},{6,7},{7,6},{8,9},{9,8},{10,11... | collective-permute-start | bytes 786440 | tf_op jit(solution)/shard_map/ppermute | solution.py:561
  158.3 10.0 %collective-permute-start.38 = (bf16[64,16,128]{2,1,0:T(8,128)(2,1)S(1)}, bf16[64,16,128]{2,1,0:T(8,128)(2,1)S(1)}, u32[]{:S(2)}, u32[]{:S(2)}) collective-permute-start(bf16[64,16,128]{2,1,0:T(8,128)(2,1)S(1)} %get-tuple-element.145), channel_id=1, source_target_pairs={{0,4},{4,12},{12,8},{8,0},{1,5},{5,13},{13,9},{9,1},{2,6},{6,14},{... | collective-permute-start | bytes 786440 | tf_op jit(solution)/shard_map/ppermute | solution.py:552
  161.2 13.9 %collective-permute-start.39 = (bf16[64,16,128]{2,1,0:T(8,128)(2,1)S(1)}, bf16[64,16,128]{2,1,0:T(8,128)(2,1)S(1)}, u32[]{:S(2)}, u32[]{:S(2)}) collective-permute-start(bf16[64,16,128]{2,1,0:T(8,128)(2,1)S(1)} %get-tuple-element.147), channel_id=1, source_target_pairs={{0,4},{4,12},{12,8},{8,0},{1,5},{5,13},{13,9},{9,1},{2,6},{6,14},{... | collective-permute-start | bytes 786440 | tf_op jit(solution)/shard_map/ppermute | solution.py:552
  169.1 14.3 %collective-permute-start.41 = (bf16[64,16,128]{2,1,0:T(8,128)(2,1)}, bf16[64,16,128]{2,1,0:T(8,128)(2,1)}, u32[]{:S(2)}, u32[]{:S(2)}) collective-permute-start(bf16[64,16,128]{2,1,0:T(8,128)(2,1)} %add_convert_fusion.3), channel_id=1, source_target_pairs={{0,4},{4,12},{12,8},{8,0},{1,5},{5,13},{13,9},{9,1},{2,6},{6,14},{... | collective-permute-start | bytes 786440 | tf_op jit(solution)/shard_map/ppermute | solution.py:552
  175.9 10.7 %collective-permute-start.40 = (bf16[64,16,128]{2,1,0:T(8,128)(2,1)}, bf16[64,16,128]{2,1,0:T(8,128)(2,1)}, u32[]{:S(2)}, u32[]{:S(2)}) collective-permute-start(bf16[64,16,128]{2,1,0:T(8,128)(2,1)} %add_convert_fusion.2), channel_id=1, source_target_pairs={{0,4},{4,12},{12,8},{8,0},{1,5},{5,13},{13,9},{9,1},{2,6},{6,14},{... | collective-permute-start | bytes 786440 | tf_op jit(solution)/shard_map/ppermute | solution.py:552
  184.4 10.2 %collective-permute-start.43 = (bf16[64,16,128]{2,1,0:T(8,128)(2,1)S(1)}, bf16[64,16,128]{2,1,0:T(8,128)(2,1)S(1)}, u32[]{:S(2)}, u32[]{:S(2)}) collective-permute-start(bf16[64,16,128]{2,1,0:T(8,128)(2,1)S(1)} %add_convert_fusion.1), channel_id=1, source_target_pairs={{0,4},{4,12},{12,8},{8,0},{1,5},{5,13},{13,9},{9,1},{2,6},{6,14},{... | collective-permute-start | bytes 786440 | tf_op jit(solution)/shard_map/ppermute | solution.py:552
  187.6 10.3 %collective-permute-start.42 = (bf16[64,16,128]{2,1,0:T(8,128)(2,1)S(1)}, bf16[64,16,128]{2,1,0:T(8,128)(2,1)S(1)}, u32[]{:S(2)}, u32[]{:S(2)}) collective-permute-start(bf16[64,16,128]{2,1,0:T(8,128)(2,1)S(1)} %add_convert_fusion), channel_id=1, source_target_pairs={{0,4},{4,12},{12,8},{8,0},{1,5},{5,13},{13,9},{9,1},{2,6},{6,14},{... | collective-permute-start | bytes 786440 | tf_op jit(solution)/shard_map/ppermute | solution.py:552
  (44 other events, 313.0 us)

commit v11 on v10

--- a/solution.py
+++ b/solution.py
@@ -127,7 +127,7 @@
 
 
 def cost(flops, size, exps=0):
-    return pl.CostEstimate(flops=flops // 1024, bytes_accessed=size // 1024, transcendentals=exps // 1024)
+    return pl.CostEstimate(flops=flops, bytes_accessed=size, transcendentals=exps)
 
 
 def first_half(rows):
@@ -574,7 +574,7 @@
     a1, b1 = forward(a0), forward(b0)
     a2, b2 = forward(a1), forward(after(b1, left))
     c0, d0 = right(2), right(3)
-    a3, b3 = forward(after(a2, b1, c0)), forward(after(b2, d0))
+    a3, b3 = forward(after(a2, c0)), forward(after(b2, d0))
     c1, d1 = forward(after(c0, b2)), forward(after(d0, a3))
 
     def triangle(slots):
@@ -596,13 +596,12 @@
     def dright(blocks, *others):
         return dright_part([blocks[0], blocks[1], blocks[2], after(blocks[3], *others)], left)
 
-    tri_a, tri_b = triangle([a0, a1, a2, after(a3, b3)]), triangle([b0, b1, b2, b3])
-    x_a = over_x(after(tri_a[2], c1))
+    tri_a, tri_b = triangle([a0, a1, a2, a3]), triangle([b0, b1, b2, b3])
+    x_a, x_b = over_x(tri_a[2]), over_x(tri_b[2])
     c2, d2 = forward(after(c1, tri_a[2])), forward(after(d1, tri_b[2]))
-    x_b = over_x(tri_b[2])
-    dtri_a, gate_a, g_out, g_gate = middle(0, tri_a, after(x_a, d1, c2))
+    dtri_a, gate_a, g_out, g_gate = middle(0, tri_a, after(x_a, d1))
     blocks_a = spread(dtri_a)
-    dtri_b, gate_b, g_out, g_gate = middle(1, tri_b, after(x_b, d2))
+    dtri_b, gate_b, g_out, g_gate = middle(1, tri_b, after(x_b, c2))
     blocks_b = spread(dtri_b)
     c3, d3 = forward(after(c2, dtri_a)), forward(after(d2, dtri_b))
     part_a = dright(blocks_a, d2)
@@ -610,28 +609,27 @@
     r_a, r_b = forward(part_a[1]), forward(part_b[1])
 
     tri_c = triangle([c0, c1, c2, after(c3, part_a[1])])
-    x_c = over_x(tri_c[2])
-    dtri_c, gate_c, g_out, g_gate = middle(2, tri_c, after(x_c, d3, part_b[1]))
-    blocks_c = spread(dtri_c)
+    tri_d = triangle([d0, d1, d2, after(d3, part_b[1])])
+    x_c, x_d = over_x(tri_c[2]), over_x(tri_d[2])
     r_a = plus(r_a, part_a[2])
-    tri_d = triangle([d0, d1, d2, after(d3, dtri_c, r_a)])
-    r_a2 = forward(r_a)
-    x_d = over_x(after(tri_d[2], r_b))
+    r_a2 = forward(after(r_a, tri_c[2]))
     r_b = plus(r_b, part_b[2])
-    r_b2 = forward(r_b)
-    r_a2 = plus(r_a2, part_a[3])
-    dtri_d, gate_d, g_out, g_gate = middle(3, tri_d, after(x_d, r_a2))
-    blocks_d = spread(dtri_d)
-    r_a3 = forward(r_a2)
-    r_b2 = plus(r_b2, part_b[3])
+    r_b2 = forward(after(r_b, tri_d[2]))
     d_left = dleft_part(
-        [after(blocks_a[0], dtri_d, r_b2)] + blocks_a[1:] + blocks_b,
+        [after(blocks_a[0], tri_d[2])] + blocks_a[1:] + blocks_b,
         [tri_a[3], tri_b[3]],
         jnp.zeros((HALF, HALF, WIDTH), F32),
     )
-    r_b3 = forward(r_b2)
-    part_c = dright(blocks_c, r_a3, d_left)
-    part_d = dright(blocks_d, r_b3, part_c[1])
+    dtri_c, gate_c, g_out, g_gate = middle(2, tri_c, after(x_c, r_a, d_left))
+    blocks_c = spread(dtri_c)
+    dtri_d, gate_d, g_out, g_gate = middle(3, tri_d, after(x_d, r_b))
+    blocks_d = spread(dtri_d)
+    r_a2 = plus(r_a2, part_a[3])
+    r_a3 = forward(after(r_a2, dtri_c))
+    r_b2 = plus(r_b2, part_b[3])
+    r_b3 = forward(after(r_b2, dtri_d))
+    part_c = dright(blocks_c, r_a2)
+    part_d = dright(blocks_d, r_b2)
 
     zero = jnp.zeros((width, 2 * width), F32)
 

time: 223 us -> 196 us (0.88)
  waiting for transfers between devices: 91.3 us -> 56 us
  starting transfers between devices: 55.4 us -> 62.4 us
  Pallas kernels: 61.1 us -> 66.1 us
  local copies, waits for them, and re-layouts: 7.26 us -> 3.45 us
    ppermute x24, waiting for transfers between devices: 56.4 us -> 37.6 us  [forward(): return lax.ppermute(a, 'row', [(0, 1), (1, 3), (3, 2), (2, 0)])]
    ppermute x9, waiting for transfers between devices: 21.4 us -> 9.43 us  [over_x(): return lax.ppermute(a, 'col', [(k, k ^ 2) for k in range(4)])]
    ppermute x24, starting transfers between devices: 39.1 us -> 46.1 us  [forward(): return lax.ppermute(a, 'row', [(0, 1), (1, 3), (3, 2), (2, 0)])]
    ppermute x2, waiting for transfers between devices: 10.6 us -> 6.09 us  [over_row(): return lax.ppermute(a, 'row', [(k, k ^ bit) for k in range(4)])]
    ppermute x2, starting transfers between devices: 0.22 us -> 4.17 us  [over_row(): return lax.ppermute(a, 'row', [(k, k ^ bit) for k in range(4)])]
    ppermute x9, starting transfers between devices: 13.9 us -> 10.7 us  [over_x(): return lax.ppermute(a, 'col', [(k, k ^ 2) for k in range(4)])]
    pallas_call x4, Pallas kernels: 8.5 us -> 11.5 us  [dright_part(): pl.pallas_call(dright_kernel, grid=(HALF // GROUP,), out_shape=(pltpu.HBM...]
    unnamed x57 -> x61, local copies, waits for them, and re-layouts: 5.39 us -> 3.17 us
  transfers between devices with their start and end apart: 49 -> 49, of which waited for: 26 -> 23; matrix products, arithmetic and copies ran while one was open for 3% -> 2% of each run, Pallas kernels for 22% -> 32%
where the time goes in v11:
time: 196 us; the launch traced here: 195 us
  Pallas kernels  66.1 us (34%)
  starting transfers between devices  62.4 us (32%)
  waiting for transfers between devices  56 us (29%)
  other arithmetic  5.8 us (3%)
  local copies, waits for them, and re-layouts  3.45 us (2%)
    ppermute x24, starting transfers between devices, forward(): return lax.ppermute(a, 'row', [(0, 1), (1, 3), (3, 2), (2, 0)])  46.1 us
    ppermute x24, waiting for transfers between devices, forward(): return lax.ppermute(a, 'row', [(0, 1), (1, 3), (3, 2), (2, 0)])  37.6 us
    pallas_call x4, Pallas kernels, mid_part(): pl.pallas_call(mid_kernel, grid=(1,), out_shape=(PANEL, pltpu.HBM(PANEL.s...  14.2 us
    pallas_call x4, Pallas kernels, dright_part(): pl.pallas_call(dright_kernel, grid=(HALF // GROUP,), out_shape=(pltpu.HBM...  11.5 us
    ppermute x9, starting transfers between devices, over_x(): return lax.ppermute(a, 'col', [(k, k ^ 2) for k in range(4)])  10.7 us
    ppermute x9, waiting for transfers between devices, over_x(): return lax.ppermute(a, 'col', [(k, k ^ 2) for k in range(4)])  9.43 us
    pallas_call x4, Pallas kernels, final_b_part(): pl.pallas_call(functools.partial(final_b_kernel, s * steps), grid=(steps,...  8.57 us
    pallas_call x4, Pallas kernels, tri_part(): pl.pallas_call(tri_kernel, grid=(HALF // GROUP,), out_shape=(PANEL, PANEL...  8.01 us
  transfers between devices with their start and end apart: 49, of which 23 were waited for; matrix products, arithmetic and copies ran while one was open for 2% of the time, Pallas kernels for 32%

profile of v11, /device:TPU:0, one launch (start us, length us, event | category | flops | bytes accessed | tf_op | source)
XLA Modules:
  0.0 195.0 jit_solution(6041634788506590557)
XLA Ops:
  2.6 3.1 %collective-permute-start.3 = (bf16[64,16,128]{2,1,0:T(8,128)(2,1)S(1)}, bf16[64,16,128]{2,1,0:T(8,128)(2,1)S(1)}, u32[]{:S(2)}, u32[]{:S(2)}) collective-permute-start(bf16[64,16,128]{2,1,0:T(8,128)(2,1)S(1)} %right_part.6.s0), channel_id=1, source_target_pairs={{0,4},{4,12},{12,8},{8,0},{1,5},{5,13},{13,9},{9,1},{2,6},{6,14},{... | collective-permute-start | bytes 786440 | tf_op jit(solution)/shard_map/ppermute | solution.py:552
  7.6 2.6 %collective-permute-start = (bf16[64,16,128]{2,1,0:T(8,128)(2,1)S(1)}, bf16[64,16,128]{2,1,0:T(8,128)(2,1)S(1)}, u32[]{:S(2)}, u32[]{:S(2)}) collective-permute-start(bf16[64,16,128]{2,1,0:T(8,128)(2,1)S(1)} %right_part.5.s0), channel_id=1, source_target_pairs={{0,4},{4,12},{12,8},{8,0},{1,5},{5,13},{13,9},{9,1},{2,6},{6,14},{... | collective-permute-start | bytes 786440 | tf_op jit(solution)/shard_map/ppermute | solution.py:552
  10.2 3.6 %collective-permute-done.3.s1 = bf16[64,16,128]{2,1,0:T(8,128)(2,1)S(1)} collective-permute-done((bf16[64,16,128]{2,1,0:T(8,128)(2,1)S(1)}, bf16[64,16,128]{2,1,0:T(8,128)(2,1)S(1)}, u32[]{:S(2)}, u32[]{:S(2)}) %collective-permute-start.3) | collective-permute-done | bytes 262176 | tf_op jit(solution)/shard_map/ppermute | solution.py:552
  15.0 5.2 %left_part.1.left_ref.refs_4_ = bf16[64,2,64,128]{3,2,1,0:T(8,128)(2,1)S(1)} custom-call(bf16[64,64,128]{2,1,0:T(8,128)(2,1)} %x_ref.27, f32[1,128]{1,0:T(1,128)} %bitcast.25, bf16[128,512]{1,0:T(8,128)(2,1)} %w_ref.19, s32[1,256]{1,0:T(1,128)} %bitcast.40), custom_call_target="tpu_custom_call" | custom-call | flops 268435456 | bytes 3145728 | tf_op jit(solution)/shard_map/left_part/pallas_call | solution.py:410
  20.2 3.4 %collective-permute-start.1 = (bf16[64,16,128]{2,1,0:T(8,128)(2,1)S(1)}, bf16[64,16,128]{2,1,0:T(8,128)(2,1)S(1)}, u32[]{:S(2)}, u32[]{:S(2)}) collective-permute-start(bf16[64,16,128]{2,1,0:T(8,128)(2,1)S(1)} %collective-permute-done.s1), channel_id=1, source_target_pairs={{0,4},{4,12},{12,8},{8,0},{1,5},{5,13},{13,9},{9,1},{2,6},{6,14},{... | collective-permute-start | bytes 786440 | tf_op jit(solution)/shard_map/ppermute | solution.py:552
  28.1 2.5 %collective-permute-done.1.s2 = bf16[64,16,128]{2,1,0:T(8,128)(2,1)S(1)} collective-permute-done((bf16[64,16,128]{2,1,0:T(8,128)(2,1)S(1)}, bf16[64,16,128]{2,1,0:T(8,128)(2,1)S(1)}, u32[]{:S(2)}, u32[]{:S(2)}) %collective-permute-start.1) | collective-permute-done | bytes 262176 | tf_op jit(solution)/shard_map/ppermute | solution.py:552
  32.9 3.4 %collective-permute-done.5.s3 = bf16[64,16,128]{2,1,0:T(8,128)(2,1)S(1)} collective-permute-done((bf16[64,16,128]{2,1,0:T(8,128)(2,1)S(1)}, bf16[64,16,128]{2,1,0:T(8,128)(2,1)S(1)}, u32[]{:S(2)}, u32[]{:S(2)}) %collective-permute-start.5) | collective-permute-done | bytes 262176 | tf_op jit(solution)/shard_map/ppermute | solution.py:552
  38.4 2.6 %collective-permute-done.14.s3 = bf16[64,16,128]{2,1,0:T(8,128)(2,1)S(1)} collective-permute-done((bf16[64,16,128]{2,1,0:T(8,128)(2,1)S(1)}, bf16[64,16,128]{2,1,0:T(8,128)(2,1)S(1)}, u32[]{:S(2)}, u32[]{:S(2)}) %collective-permute-start.14) | collective-permute-done | bytes 262176 | tf_op jit(solution)/shard_map/ppermute | solution.py:552
  44.0 3.4 %collective-permute-start.9 = (bf16[64,16,128]{2,1,0:T(8,128)(2,1)S(1)}, bf16[64,16,128]{2,1,0:T(8,128)(2,1)S(1)}, u32[]{:S(2)}, u32[]{:S(2)}) collective-permute-start(bf16[64,16,128]{2,1,0:T(8,128)(2,1)S(1)} %right_part.7.s0), channel_id=1, source_target_pairs={{0,4},{4,12},{12,8},{8,0},{1,5},{5,13},{13,9},{9,1},{2,6},{6,14},{... | collective-permute-start | bytes 786440 | tf_op jit(solution)/shard_map/ppermute | solution.py:552
  49.7 3.5 %collective-permute-done.2.s1 = bf16[64,16,128]{2,1,0:T(8,128)(2,1)S(1)} collective-permute-done((bf16[64,16,128]{2,1,0:T(8,128)(2,1)S(1)}, bf16[64,16,128]{2,1,0:T(8,128)(2,1)S(1)}, u32[]{:S(2)}, u32[]{:S(2)}) %collective-permute-start.2) | collective-permute-done | bytes 262176 | tf_op jit(solution)/shard_map/ppermute | solution.py:552
  54.0 4.8 %collective-permute-done.9.s1 = bf16[64,16,128]{2,1,0:T(8,128)(2,1)S(1)} collective-permute-done((bf16[64,16,128]{2,1,0:T(8,128)(2,1)S(1)}, bf16[64,16,128]{2,1,0:T(8,128)(2,1)S(1)}, u32[]{:S(2)}, u32[]{:S(2)}) %collective-permute-start.9) | collective-permute-done | bytes 262176 | tf_op jit(solution)/shard_map/ppermute | solution.py:552
  58.9 3.5 %mid_part.4 = (bf16[64,16,128]{2,1,0:T(8,128)(2,1)S(1)}, bf16[64,16,128]{2,1,0:T(8,128)(2,1)}, f32[128,128]{1,0:T(8,128)S(1)}, f32[128,128]{1,0:T(8,128)S(1)}) custom-call(bf16[64,16,128]{2,1,0:T(8,128)(2,1)S(1)} %get-tuple-element.100.a_ref, bf16[2,64,16,128]{3,2,1,0:T(8,128)(2,1)S(1)} %collective-permute-done.6.b_ref, ...), custom_call_target="tpu_custom_call" | custom-call | flops 201326592 | bytes 2097152 | tf_op jit(solution)/shard_map/mid_part/pallas_call | solution.py:443
  64.0 3.6 %mid_part.5 = (bf16[64,16,128]{2,1,0:T(8,128)(2,1)S(1)}, bf16[64,16,128]{2,1,0:T(8,128)(2,1)}, f32[128,128]{1,0:T(8,128)S(1)}, f32[128,128]{1,0:T(8,128)S(1)}) custom-call(bf16[64,16,128]{2,1,0:T(8,128)(2,1)S(1)} %get-tuple-element.116.a_ref, bf16[2,64,16,128]{3,2,1,0:T(8,128)(2,1)S(1)} %collective-permute-done.15.b_ref, ...), custom_call_target="tpu_custom_call" | custom-call | flops 201326592 | bytes 2097152 | tf_op jit(solution)/shard_map/mid_part/pallas_call | solution.py:443
  70.4 3.4 %collective-permute-start.10 = (bf16[64,16,128]{2,1,0:T(8,128)(2,1)S(1)}, bf16[64,16,128]{2,1,0:T(8,128)(2,1)S(1)}, u32[]{:S(2)}, u32[]{:S(2)}) collective-permute-start(bf16[64,16,128]{2,1,0:T(8,128)(2,1)S(1)} %collective-permute-done.7.s2), channel_id=1, source_target_pairs={{0,4},{4,12},{12,8},{8,0},{1,5},{5,13},{13,9},{9,1},{2,6},{6,14},{... | collective-permute-start | bytes 786440 | tf_op jit(solution)/shard_map/ppermute | solution.py:552
  75.5 3.8 %collective-permute-done.16.s2 = bf16[64,16,128]{2,1,0:T(8,128)(2,1)S(1)} collective-permute-done((bf16[64,16,128]{2,1,0:T(8,128)(2,1)S(1)}, bf16[64,16,128]{2,1,0:T(8,128)(2,1)S(1)}, u32[]{:S(2)}, u32[]{:S(2)}) %collective-permute-start.16) | collective-permute-done | bytes 262176 | tf_op jit(solution)/shard_map/ppermute | solution.py:552
  86.2 3.2 %collective-permute-start.19 = (bf16[64,16,128]{2,1,0:T(8,128)(2,1)S(1)}, bf16[64,16,128]{2,1,0:T(8,128)(2,1)S(1)}, u32[]{:S(2)}, u32[]{:S(2)}) collective-permute-start(bf16[64,16,128]{2,1,0:T(8,128)(2,1)S(1)} %get-tuple-element.110), channel_id=1, source_target_pairs={{0,4},{4,12},{12,8},{8,0},{1,5},{5,13},{13,9},{9,1},{2,6},{6,14},{... | collective-permute-start | bytes 786440 | tf_op jit(solution)/shard_map/ppermute | solution.py:552
  98.9 2.3 %collective-permute-start.35 = (bf16[64,16,128]{2,1,0:T(8,128)(2,1)}, bf16[64,16,128]{2,1,0:T(8,128)(2,1)}, u32[]{:S(2)}, u32[]{:S(2)}) collective-permute-start(bf16[64,16,128]{2,1,0:T(8,128)(2,1)} %add_convert_fusion.7), channel_id=1, source_target_pairs={{0,4},{4,12},{12,8},{8,0},{1,5},{5,13},{13,9},{9,1},{2,6},{6,14},{... | collective-permute-start | bytes 786440 | tf_op jit(solution)/shard_map/ppermute | solution.py:552
  103.1 2.8 %collective-permute-done.18.c_ref = bf16[64,16,128]{2,1,0:T(8,128)(2,1)S(1)} collective-permute-done((bf16[64,16,128]{2,1,0:T(8,128)(2,1)S(1)}, bf16[64,16,128]{2,1,0:T(8,128)(2,1)S(1)}, u32[]{:S(2)}, u32[]{:S(2)}) %collective-permute-start.18) | collective-permute-done | bytes 262176 | tf_op jit(solution)/shard_map/ppermute | solution.py:558
  106.0 3.5 %mid_part.6 = (bf16[64,16,128]{2,1,0:T(8,128)(2,1)S(1)}, bf16[64,16,128]{2,1,0:T(8,128)(2,1)}, f32[128,128]{1,0:T(8,128)S(1)}, f32[128,128]{1,0:T(8,128)S(1)}) custom-call(bf16[64,16,128]{2,1,0:T(8,128)(2,1)S(1)} %get-tuple-element.112.a_ref, bf16[2,64,16,128]{3,2,1,0:T(8,128)(2,1)S(1)} %collective-permute-done.17.b_ref, ...), custom_call_target="tpu_custom_call" | custom-call | flops 201326592 | bytes 2097152 | tf_op jit(solution)/shard_map/mid_part/pallas_call | solution.py:443
  110.9 3.6 %mid_part.7 = (bf16[64,16,128]{2,1,0:T(8,128)(2,1)}, bf16[64,16,128]{2,1,0:T(8,128)(2,1)}, f32[128,128]{1,0:T(8,128)S(1)}, f32[128,128]{1,0:T(8,128)S(1)}) custom-call(bf16[64,16,128]{2,1,0:T(8,128)(2,1)S(1)} %get-tuple-element.134.a_ref, bf16[2,64,16,128]{3,2,1,0:T(8,128)(2,1)S(1)} %collective-permute-done.25.b_ref, ...), custom_call_target="tpu_custom_call" | custom-call | flops 201326592 | bytes 2097152 | tf_op jit(solution)/shard_map/mid_part/pallas_call | solution.py:443
  117.1 2.4 %collective-permute-start.31 = (bf16[64,16,128]{2,1,0:T(8,128)(2,1)}, bf16[64,16,128]{2,1,0:T(8,128)(2,1)S(1)}, u32[]{:S(2)}, u32[]{:S(2)}) collective-permute-start(bf16[64,16,128]{2,1,0:T(8,128)(2,1)} %add_convert_fusion.6), channel_id=1, source_target_pairs={{0,4},{4,12},{12,8},{8,0},{1,5},{5,13},{13,9},{9,1},{2,6},{6,14},{... | collective-permute-start | bytes 786440 | tf_op jit(solution)/shard_map/ppermute | solution.py:552
  124.2 3.7 %dright_part.7 = (bf16[64,16,128]{2,1,0:T(8,128)(2,1)}, bf16[64,16,128]{2,1,0:T(8,128)(2,1)S(1)}, bf16[64,16,128]{2,1,0:T(8,128)(2,1)S(1)}, bf16[64,16,128]{2,1,0:T(8,128)(2,1)S(1)}) custom-call(bf16[64,16,128]{2,1,0:T(8,128)(2,1)S(1)} %get-tuple-element.144.refs_0_, bf16[64,16,128]{2,1,0:T(8,128)(2,1)} %collective-permute-done.32.refs_1_, ...), custom_call_target="tpu_custom_call" | custom-call | flops 268435456 | bytes 6291456 | tf_op jit(solution)/shard_map/dright_part/pallas_call | solution.py:459
  130.4 3.6 %dright_part.6 = (bf16[64,16,128]{2,1,0:T(8,128)(2,1)}, bf16[64,16,128]{2,1,0:T(8,128)(2,1)S(1)}, bf16[64,16,128]{2,1,0:T(8,128)(2,1)S(1)}, bf16[64,16,128]{2,1,0:T(8,128)(2,1)S(1)}) custom-call(bf16[64,16,128]{2,1,0:T(8,128)(2,1)} %get-tuple-element.139.refs_0_.refs_4_, bf16[64,16,128]{2,1,0:T(8,128)(2,1)} %collective-permute-done.28.refs_1_.refs_5_, ...), custom_call_target="tpu_custom_call" | custom-call | flops 268435456 | bytes 6291456 | tf_op jit(solution)/shard_map/dright_part/pallas_call | solution.py:459
  135.8 3.2 %dleft_part.3.dleft_ref = f32[64,64,128]{2,1,0:T(8,128)S(1)} custom-call(bf16[64,16,128]{2,1,0:T(8,128)(2,1)S(1)} %get-tuple-element.144.refs_0_, bf16[64,16,128]{2,1,0:T(8,128)(2,1)} %collective-permute-done.32.refs_1_, bf16[64,16,128]{2,1,0:T(8,128)(2,1)} %collective-permute-done.33.refs_2_, bf16[64,16,128]{2,1,0:T(8,128)(2,1)} %collective-permute-done.34.refs_3_, ...), custom_call_target="tpu_custom_call" | custom-call | flops 268435456 | bytes 8388608 | tf_op jit(solution)/shard_map/dleft_part/pallas_call | solution.py:474
  140.1 6.0 %final_a_part.1 = (f32[128,4096]{1,0:T(8,128)S(1)}, f32[128,256]{1,0:T(8,128)S(1)}) custom-call(bf16[64,64,128]{2,1,0:T(8,128)(2,1)S(1)} %copy-done, f32[64,64,128]{2,1,0:T(8,128)S(1)} %dleft_part.3.dleft_ref, s32[1,256]{1,0:T(1,128)S(1)} %bitcast.43, f32[1,128]{1,0:T(1,128)S(1)} %bitcast.32, bf16[128,512]{1,0:T(8,128)(2,1)S(1)} %copy-done.2, ...), custom_call_target="tpu_custom_call" | custom-call | flops 939524096 | bytes 8388608 | tf_op jit(solution)/shard_map/final_a_part/pallas_call | solution.py:487
  146.1 3.1 %collective-permute-done.37 = bf16[64,16,128]{2,1,0:T(8,128)(2,1)S(1)} collective-permute-done((bf16[64,16,128]{2,1,0:T(8,128)(2,1)S(1)}, bf16[64,16,128]{2,1,0:T(8,128)(2,1)S(1)}, u32[]{:S(2)}, u32[]{:S(2)}) %collective-permute-start.37) | collective-permute-done | bytes 262176 | tf_op jit(solution)/shard_map/ppermute | solution.py:552
  162.8 3.3 %collective-permute-done.43.b_ref = bf16[64,16,128]{2,1,0:T(8,128)(2,1)S(1)} collective-permute-done((bf16[64,16,128]{2,1,0:T(8,128)(2,1)S(1)}, bf16[64,16,128]{2,1,0:T(8,128)(2,1)S(1)}, u32[]{:S(2)}, u32[]{:S(2)}) %collective-permute-start.43) | collective-permute-done | bytes 262176 | tf_op jit(solution)/shard_map/ppermute | solution.py:552
  168.2 3.2 %collective-permute-done.42.b_ref = bf16[64,16,128]{2,1,0:T(8,128)(2,1)S(1)} collective-permute-done((bf16[64,16,128]{2,1,0:T(8,128)(2,1)S(1)}, bf16[64,16,128]{2,1,0:T(8,128)(2,1)S(1)}, u32[]{:S(2)}, u32[]{:S(2)}) %collective-permute-start.42) | collective-permute-done | bytes 262176 | tf_op jit(solution)/shard_map/ppermute | solution.py:552
  178.2 3.5 %collective-permute-done.45 = bf16[64,768]{1,0:T(8,128)(2,1)S(1)} collective-permute-done((bf16[64,768]{1,0:T(8,128)(2,1)S(1)}, bf16[64,768]{1,0:T(8,128)(2,1)S(1)}, u32[]{:S(2)}, u32[]{:S(2)}) %collective-permute-start.45) | collective-permute-done | bytes 98336 | tf_op jit(solution)/shard_map/ppermute | solution.py:558
  183.2 3.1 %collective-permute-done.46 = bf16[64,768]{1,0:T(8,128)(2,1)S(1)} collective-permute-done((bf16[64,768]{1,0:T(8,128)(2,1)S(1)}, bf16[64,768]{1,0:T(8,128)(2,1)S(1)}, u32[]{:S(2)}, u32[]{:S(2)}) %collective-permute-start.46) | collective-permute-done | bytes 98336 | tf_op jit(solution)/shard_map/ppermute | solution.py:555
  186.4 2.6 %collective-permute-start.47 = (bf16[64,768]{1,0:T(8,128)(2,1)S(1)}, bf16[64,768]{1,0:T(8,128)(2,1)S(1)}, u32[]{:S(2)}, u32[]{:S(2)}) collective-permute-start(bf16[64,768]{1,0:T(8,128)(2,1)S(1)} %add_convert_fusion.8), channel_id=1, source_target_pairs={{0,8},{4,12},{8,0},{12,4},{1,9},{5,13},{9,1},{13,5},{2,10},{6,14},... | collective-permute-start | bytes 294920 | tf_op jit(solution)/shard_map/ppermute | solution.py:555
  189.0 2.9 %collective-permute-done.47 = bf16[64,768]{1,0:T(8,128)(2,1)S(1)} collective-permute-done((bf16[64,768]{1,0:T(8,128)(2,1)S(1)}, bf16[64,768]{1,0:T(8,128)(2,1)S(1)}, u32[]{:S(2)}, u32[]{:S(2)}) %collective-permute-start.47) | collective-permute-done | bytes 98336 | tf_op jit(solution)/shard_map/ppermute | solution.py:555
  (175 shorter events, 85.2 us)
Async XLA Ops:
  2.6 11.2 %collective-permute-start.3 = (bf16[64,16,128]{2,1,0:T(8,128)(2,1)S(1)}, bf16[64,16,128]{2,1,0:T(8,128)(2,1)S(1)}, u32[]{:S(2)}, u32[]{:S(2)}) collective-permute-start(bf16[64,16,128]{2,1,0:T(8,128)(2,1)S(1)} %right_part.6.s0), channel_id=1, source_target_pairs={{0,4},{4,12},{12,8},{8,0},{1,5},{5,13},{13,9},{9,1},{2,6},{6,14},{... | collective-permute-start | bytes 786440 | tf_op jit(solution)/shard_map/ppermute | solution.py:552
  7.6 12.6 %collective-permute-start = (bf16[64,16,128]{2,1,0:T(8,128)(2,1)S(1)}, bf16[64,16,128]{2,1,0:T(8,128)(2,1)S(1)}, u32[]{:S(2)}, u32[]{:S(2)}) collective-permute-start(bf16[64,16,128]{2,1,0:T(8,128)(2,1)S(1)} %right_part.5.s0), channel_id=1, source_target_pairs={{0,4},{4,12},{12,8},{8,0},{1,5},{5,13},{13,9},{9,1},{2,6},{6,14},{... | collective-permute-start | bytes 786440 | tf_op jit(solution)/shard_map/ppermute | solution.py:552
  13.8 11.8 %collective-permute-start.4 = (bf16[64,16,128]{2,1,0:T(8,128)(2,1)S(1)}, bf16[64,16,128]{2,1,0:T(8,128)(2,1)S(1)}, u32[]{:S(2)}, u32[]{:S(2)}) collective-permute-start(bf16[64,16,128]{2,1,0:T(8,128)(2,1)S(1)} %collective-permute-done.3.s1), channel_id=1, source_target_pairs={{0,4},{4,12},{12,8},{8,0},{1,5},{5,13},{13,9},{9,1},{2,6},{6,14},{... | collective-permute-start | bytes 786440 | tf_op jit(solution)/shard_map/ppermute | solution.py:552
  20.2 10.5 %collective-permute-start.1 = (bf16[64,16,128]{2,1,0:T(8,128)(2,1)S(1)}, bf16[64,16,128]{2,1,0:T(8,128)(2,1)S(1)}, u32[]{:S(2)}, u32[]{:S(2)}) collective-permute-start(bf16[64,16,128]{2,1,0:T(8,128)(2,1)S(1)} %collective-permute-done.s1), channel_id=1, source_target_pairs={{0,4},{4,12},{12,8},{8,0},{1,5},{5,13},{13,9},{9,1},{2,6},{6,14},{... | collective-permute-start | bytes 786440 | tf_op jit(solution)/shard_map/ppermute | solution.py:552
  25.6 10.7 %collective-permute-start.5 = (bf16[64,16,128]{2,1,0:T(8,128)(2,1)S(1)}, bf16[64,16,128]{2,1,0:T(8,128)(2,1)S(1)}, u32[]{:S(2)}, u32[]{:S(2)}) collective-permute-start(bf16[64,16,128]{2,1,0:T(8,128)(2,1)S(1)} %collective-permute-done.4.s2), channel_id=1, source_target_pairs={{0,4},{4,12},{12,8},{8,0},{1,5},{5,13},{13,9},{9,1},{2,6},{6,14},{... | collective-permute-start | bytes 786440 | tf_op jit(solution)/shard_map/ppermute | solution.py:552
  30.7 10.4 %collective-permute-start.14 = (bf16[64,16,128]{2,1,0:T(8,128)(2,1)S(1)}, bf16[64,16,128]{2,1,0:T(8,128)(2,1)S(1)}, u32[]{:S(2)}, u32[]{:S(2)}) collective-permute-start(bf16[64,16,128]{2,1,0:T(8,128)(2,1)S(1)} %collective-permute-done.1.s2), channel_id=1, source_target_pairs={{0,4},{4,12},{12,8},{8,0},{1,5},{5,13},{13,9},{9,1},{2,6},{6,14},{... | collective-permute-start | bytes 786440 | tf_op jit(solution)/shard_map/ppermute | solution.py:552
  43.2 10.1 %collective-permute-start.2 = (bf16[64,16,128]{2,1,0:T(8,128)(2,1)S(1)}, bf16[64,16,128]{2,1,0:T(8,128)(2,1)S(1)}, u32[]{:S(2)}, u32[]{:S(2)}) collective-permute-start(bf16[64,16,128]{2,1,0:T(8,128)(2,1)S(1)} %right_part.4.s0), channel_id=1, source_target_pairs={{0,4},{4,12},{12,8},{8,0},{1,5},{5,13},{13,9},{9,1},{2,6},{6,14},{... | collective-permute-start | bytes 786440 | tf_op jit(solution)/shard_map/ppermute | solution.py:552
  44.0 14.8 %collective-permute-start.9 = (bf16[64,16,128]{2,1,0:T(8,128)(2,1)S(1)}, bf16[64,16,128]{2,1,0:T(8,128)(2,1)S(1)}, u32[]{:S(2)}, u32[]{:S(2)}) collective-permute-start(bf16[64,16,128]{2,1,0:T(8,128)(2,1)S(1)} %right_part.7.s0), channel_id=1, source_target_pairs={{0,4},{4,12},{12,8},{8,0},{1,5},{5,13},{13,9},{9,1},{2,6},{6,14},{... | collective-permute-start | bytes 786440 | tf_op jit(solution)/shard_map/ppermute | solution.py:552
  47.5 11.3 %collective-permute-start.8 = (bf16[64,16,128]{2,1,0:T(8,128)(2,1)S(1)}, bf16[64,16,128]{2,1,0:T(8,128)(2,1)S(1)}, u32[]{:S(2)}, u32[]{:S(2)}) collective-permute-start(bf16[64,16,128]{2,1,0:T(8,128)(2,1)S(1)} %fusion.3), channel_id=1, source_target_pairs={{0,2},{1,3},{2,0},{3,1},{4,6},{5,7},{6,4},{7,5},{8,10},{9,11},{10,... | collective-permute-start | bytes 786440 | tf_op jit(solution)/shard_map/ppermute | solution.py:558
  49.1 14.8 %collective-permute-start.20 = (bf16[64,16,128]{2,1,0:T(8,128)(2,1)S(1)}, bf16[64,16,128]{2,1,0:T(8,128)(2,1)S(1)}, u32[]{:S(2)}, u32[]{:S(2)}) collective-permute-start(bf16[64,16,128]{2,1,0:T(8,128)(2,1)S(1)} %fusion.2), channel_id=1, source_target_pairs={{0,2},{1,3},{2,0},{3,1},{4,6},{5,7},{6,4},{7,5},{8,10},{9,11},{10,... | collective-permute-start | bytes 786440 | tf_op jit(solution)/shard_map/ppermute | solution.py:558
  53.2 10.8 %collective-permute-start.7 = (bf16[64,16,128]{2,1,0:T(8,128)(2,1)S(1)}, bf16[64,16,128]{2,1,0:T(8,128)(2,1)S(1)}, u32[]{:S(2)}, u32[]{:S(2)}) collective-permute-start(bf16[64,16,128]{2,1,0:T(8,128)(2,1)S(1)} %collective-permute-done.2.s1), channel_id=1, source_target_pairs={{0,4},{4,12},{12,8},{8,0},{1,5},{5,13},{13,9},{9,1},{2,6},{6,14},{... | collective-permute-start | bytes 786440 | tf_op jit(solution)/shard_map/ppermute | solution.py:552
  69.1 10.1 %collective-permute-start.16 = (bf16[64,16,128]{2,1,0:T(8,128)(2,1)S(1)}, bf16[64,16,128]{2,1,0:T(8,128)(2,1)S(1)}, u32[]{:S(2)}, u32[]{:S(2)}) collective-permute-start(bf16[64,16,128]{2,1,0:T(8,128)(2,1)S(1)} %collective-permute-done.9.s1), channel_id=1, source_target_pairs={{0,4},{4,12},{12,8},{8,0},{1,5},{5,13},{13,9},{9,1},{2,6},{6,14},{... | collective-permute-start | bytes 786440 | tf_op jit(solution)/shard_map/ppermute | solution.py:552
  69.9 10.1 %collective-permute-start.12 = (bf16[64,16,128]{2,1,0:T(8,128)(2,1)S(1)}, bf16[64,16,128]{2,1,0:T(8,128)(2,1)S(1)}, u32[]{:S(2)}, u32[]{:S(2)}) collective-permute-start(bf16[64,16,128]{2,1,0:T(8,128)(2,1)S(1)} %get-tuple-element.127.refs_0_), channel_id=1, source_target_pairs={{0,1},{1,0},{2,3},{3,2},{4,5},{5,4},{6,7},{7,6},{8,9},{9,8},{10,11... | collective-permute-start | bytes 786440 | tf_op jit(solution)/shard_map/ppermute | solution.py:561
  70.4 12.8 %collective-permute-start.10 = (bf16[64,16,128]{2,1,0:T(8,128)(2,1)S(1)}, bf16[64,16,128]{2,1,0:T(8,128)(2,1)S(1)}, u32[]{:S(2)}, u32[]{:S(2)}) collective-permute-start(bf16[64,16,128]{2,1,0:T(8,128)(2,1)S(1)} %collective-permute-done.7.s2), channel_id=1, source_target_pairs={{0,4},{4,12},{12,8},{8,0},{1,5},{5,13},{13,9},{9,1},{2,6},{6,14},{... | collective-permute-start | bytes 786440 | tf_op jit(solution)/shard_map/ppermute | solution.py:552
  75.5 14.0 %collective-permute-start.24 = (bf16[64,16,128]{2,1,0:T(8,128)(2,1)S(1)}, bf16[64,16,128]{2,1,0:T(8,128)(2,1)S(1)}, u32[]{:S(2)}, u32[]{:S(2)}) collective-permute-start(bf16[64,16,128]{2,1,0:T(8,128)(2,1)S(1)} %collective-permute-done.22.refs_1_.refs_5_), channel_id=1, source_target_pairs={{0,1},{1,0},{2,3},{3,2},{4,5},{5,4},{6,7},{7,6},{8,9},{9,8},{10,11... | collective-permute-start | bytes 786440 | tf_op jit(solution)/shard_map/ppermute | solution.py:561
  79.2 10.2 %collective-permute-start.23 = (bf16[64,16,128]{2,1,0:T(8,128)(2,1)S(1)}, bf16[64,16,128]{2,1,0:T(8,128)(2,1)S(1)}, u32[]{:S(2)}, u32[]{:S(2)}) collective-permute-start(bf16[64,16,128]{2,1,0:T(8,128)(2,1)S(1)} %get-tuple-element.120.refs_0_.refs_4_), channel_id=1, source_target_pairs={{0,1},{1,0},{2,3},{3,2},{4,5},{5,4},{6,7},{7,6},{8,9},{9,8},{10,11... | collective-permute-start | bytes 786440 | tf_op jit(solution)/shard_map/ppermute | solution.py:561
  79.2 12.3 %collective-permute-start.21 = (bf16[64,16,128]{2,1,0:T(8,128)(2,1)S(1)}, bf16[64,16,128]{2,1,0:T(8,128)(2,1)S(1)}, u32[]{:S(2)}, u32[]{:S(2)}) collective-permute-start(bf16[64,16,128]{2,1,0:T(8,128)(2,1)S(1)} %collective-permute-done.16.s2), channel_id=1, source_target_pairs={{0,4},{4,12},{12,8},{8,0},{1,5},{5,13},{13,9},{9,1},{2,6},{6,14},{... | collective-permute-start | bytes 786440 | tf_op jit(solution)/shard_map/ppermute | solution.py:552
  86.2 10.4 %collective-permute-start.17 = (bf16[2,64,16,128]{3,2,1,0:T(8,128)(2,1)S(1)}, bf16[2,64,16,128]{3,2,1,0:T(8,128)(2,1)S(1)}, u32[]{:S(2)}, u32[]{:S(2)}) collective-permute-start(bf16[2,64,16,128]{3,2,1,0:T(8,128)(2,1)S(1)} %get-tuple-element.113), channel_id=1, source_target_pairs={{0,1},{1,0},{2,3},{3,2},{4,5},{5,4},{6,7},{7,6},{8,9},{9,8},{10,11... | collective-permute-start | bytes 1572872 | tf_op jit(solution)/shard_map/ppermute | solution.py:561
  86.2 9.6 %collective-permute-start.19 = (bf16[64,16,128]{2,1,0:T(8,128)(2,1)S(1)}, bf16[64,16,128]{2,1,0:T(8,128)(2,1)S(1)}, u32[]{:S(2)}, u32[]{:S(2)}) collective-permute-start(bf16[64,16,128]{2,1,0:T(8,128)(2,1)S(1)} %get-tuple-element.110), channel_id=1, source_target_pairs={{0,4},{4,12},{12,8},{8,0},{1,5},{5,13},{13,9},{9,1},{2,6},{6,14},{... | collective-permute-start | bytes 786440 | tf_op jit(solution)/shard_map/ppermute | solution.py:552
  93.7 16.3 %collective-permute-start.27 = (bf16[64,16,128]{2,1,0:T(8,128)(2,1)S(1)}, bf16[64,16,128]{2,1,0:T(8,128)(2,1)S(1)}, u32[]{:S(2)}, u32[]{:S(2)}) collective-permute-start(bf16[64,16,128]{2,1,0:T(8,128)(2,1)S(1)} %get-tuple-element.123), channel_id=1, source_target_pairs={{0,4},{4,12},{12,8},{8,0},{1,5},{5,13},{13,9},{9,1},{2,6},{6,14},{... | collective-permute-start | bytes 786440 | tf_op jit(solution)/shard_map/ppermute | solution.py:552
  97.3 13.6 %collective-permute-start.26 = (bf16[64,16,128]{2,1,0:T(8,128)(2,1)S(1)}, bf16[64,16,128]{2,1,0:T(8,128)(2,1)S(1)}, u32[]{:S(2)}, u32[]{:S(2)}) collective-permute-start(bf16[64,16,128]{2,1,0:T(8,128)(2,1)S(1)} %fusion), channel_id=1, source_target_pairs={{0,2},{1,3},{2,0},{3,1},{4,6},{5,7},{6,4},{7,5},{8,10},{9,11},{10,... | collective-permute-start | bytes 786440 | tf_op jit(solution)/shard_map/ppermute | solution.py:558
  98.9 20.6 %collective-permute-start.35 = (bf16[64,16,128]{2,1,0:T(8,128)(2,1)}, bf16[64,16,128]{2,1,0:T(8,128)(2,1)}, u32[]{:S(2)}, u32[]{:S(2)}) collective-permute-start(bf16[64,16,128]{2,1,0:T(8,128)(2,1)} %add_convert_fusion.7), channel_id=1, source_target_pairs={{0,4},{4,12},{12,8},{8,0},{1,5},{5,13},{13,9},{9,1},{2,6},{6,14},{... | collective-permute-start | bytes 786440 | tf_op jit(solution)/shard_map/ppermute | solution.py:552
  117.1 13.1 %collective-permute-start.31 = (bf16[64,16,128]{2,1,0:T(8,128)(2,1)}, bf16[64,16,128]{2,1,0:T(8,128)(2,1)S(1)}, u32[]{:S(2)}, u32[]{:S(2)}) collective-permute-start(bf16[64,16,128]{2,1,0:T(8,128)(2,1)} %add_convert_fusion.6), channel_id=1, source_target_pairs={{0,4},{4,12},{12,8},{8,0},{1,5},{5,13},{13,9},{9,1},{2,6},{6,14},{... | collective-permute-start | bytes 786440 | tf_op jit(solution)/shard_map/ppermute | solution.py:552
  119.5 10.9 %collective-permute-start.29 = (bf16[64,16,128]{2,1,0:T(8,128)(2,1)}, bf16[64,16,128]{2,1,0:T(8,128)(2,1)S(1)}, u32[]{:S(2)}, u32[]{:S(2)}) collective-permute-start(bf16[64,16,128]{2,1,0:T(8,128)(2,1)} %get-tuple-element.139.refs_0_.refs_4_), channel_id=1, source_target_pairs={{0,1},{1,0},{2,3},{3,2},{4,5},{5,4},{6,7},{7,6},{8,9},{9,8},{10,11... | collective-permute-start | bytes 786440 | tf_op jit(solution)/shard_map/ppermute | solution.py:561
  121.9 29.3 %collective-permute-start.41 = (bf16[64,16,128]{2,1,0:T(8,128)(2,1)S(1)}, bf16[64,16,128]{2,1,0:T(8,128)(2,1)S(1)}, u32[]{:S(2)}, u32[]{:S(2)}) collective-permute-start(bf16[64,16,128]{2,1,0:T(8,128)(2,1)S(1)} %add_convert_fusion.4), channel_id=1, source_target_pairs={{0,4},{4,12},{12,8},{8,0},{1,5},{5,13},{13,9},{9,1},{2,6},{6,14},{... | collective-permute-start | bytes 786440 | tf_op jit(solution)/shard_map/ppermute | solution.py:552
  127.9 11.1 %collective-permute-start.36 = (bf16[64,16,128]{2,1,0:T(8,128)(2,1)S(1)}, bf16[64,16,128]{2,1,0:T(8,128)(2,1)S(1)}, u32[]{:S(2)}, u32[]{:S(2)}) collective-permute-start(bf16[64,16,128]{2,1,0:T(8,128)(2,1)S(1)} %get-tuple-element.150), channel_id=1, source_target_pairs={{0,4},{4,12},{12,8},{8,0},{1,5},{5,13},{13,9},{9,1},{2,6},{6,14},{... | collective-permute-start | bytes 786440 | tf_op jit(solution)/shard_map/ppermute | solution.py:552
  130.2 26.9 %collective-permute-start.39 = (bf16[64,16,128]{2,1,0:T(8,128)(2,1)S(1)}, bf16[64,16,128]{2,1,0:T(8,128)(2,1)S(1)}, u32[]{:S(2)}, u32[]{:S(2)}) collective-permute-start(bf16[64,16,128]{2,1,0:T(8,128)(2,1)S(1)} %add_convert_fusion.5), channel_id=1, source_target_pairs={{0,4},{4,12},{12,8},{8,0},{1,5},{5,13},{13,9},{9,1},{2,6},{6,14},{... | collective-permute-start | bytes 786440 | tf_op jit(solution)/shard_map/ppermute | solution.py:552
  134.0 15.2 %collective-permute-start.37 = (bf16[64,16,128]{2,1,0:T(8,128)(2,1)S(1)}, bf16[64,16,128]{2,1,0:T(8,128)(2,1)S(1)}, u32[]{:S(2)}, u32[]{:S(2)}) collective-permute-start(bf16[64,16,128]{2,1,0:T(8,128)(2,1)S(1)} %get-tuple-element.143), channel_id=1, source_target_pairs={{0,4},{4,12},{12,8},{8,0},{1,5},{5,13},{13,9},{9,1},{2,6},{6,14},{... | collective-permute-start | bytes 786440 | tf_op jit(solution)/shard_map/ppermute | solution.py:552
  139.1 15.7 %collective-permute-start.40 = (bf16[64,16,128]{2,1,0:T(8,128)(2,1)S(1)}, bf16[64,16,128]{2,1,0:T(8,128)(2,1)S(1)}, u32[]{:S(2)}, u32[]{:S(2)}) collective-permute-start(bf16[64,16,128]{2,1,0:T(8,128)(2,1)S(1)} %add_convert_fusion.3), channel_id=1, source_target_pairs={{0,4},{4,12},{12,8},{8,0},{1,5},{5,13},{13,9},{9,1},{2,6},{6,14},{... | collective-permute-start | bytes 786440 | tf_op jit(solution)/shard_map/ppermute | solution.py:552
  149.3 11.2 %collective-permute-start.38 = (bf16[64,16,128]{2,1,0:T(8,128)(2,1)S(1)}, bf16[64,16,128]{2,1,0:T(8,128)(2,1)S(1)}, u32[]{:S(2)}, u32[]{:S(2)}) collective-permute-start(bf16[64,16,128]{2,1,0:T(8,128)(2,1)S(1)} %add_convert_fusion.2), channel_id=1, source_target_pairs={{0,4},{4,12},{12,8},{8,0},{1,5},{5,13},{13,9},{9,1},{2,6},{6,14},{... | collective-permute-start | bytes 786440 | tf_op jit(solution)/shard_map/ppermute | solution.py:552
  154.9 11.2 %collective-permute-start.43 = (bf16[64,16,128]{2,1,0:T(8,128)(2,1)S(1)}, bf16[64,16,128]{2,1,0:T(8,128)(2,1)S(1)}, u32[]{:S(2)}, u32[]{:S(2)}) collective-permute-start(bf16[64,16,128]{2,1,0:T(8,128)(2,1)S(1)} %add_convert_fusion.1), channel_id=1, source_target_pairs={{0,4},{4,12},{12,8},{8,0},{1,5},{5,13},{13,9},{9,1},{2,6},{6,14},{... | collective-permute-start | bytes 786440 | tf_op jit(solution)/shard_map/ppermute | solution.py:552
  160.5 10.9 %collective-permute-start.42 = (bf16[64,16,128]{2,1,0:T(8,128)(2,1)S(1)}, bf16[64,16,128]{2,1,0:T(8,128)(2,1)S(1)}, u32[]{:S(2)}, u32[]{:S(2)}) collective-permute-start(bf16[64,16,128]{2,1,0:T(8,128)(2,1)S(1)} %add_convert_fusion), channel_id=1, source_target_pairs={{0,4},{4,12},{12,8},{8,0},{1,5},{5,13},{13,9},{9,1},{2,6},{6,14},{... | collective-permute-start | bytes 786440 | tf_op jit(solution)/shard_map/ppermute | solution.py:552
  (46 other events, 374.9 us)

commit v12 on v11

--- a/solution.py
+++ b/solution.py
@@ -629,7 +629,7 @@
     r_b2 = plus(r_b2, part_b[3])
     r_b3 = forward(after(r_b2, dtri_d))
     part_c = dright(blocks_c, r_a2)
-    part_d = dright(blocks_d, r_b2)
+    part_d = dright(blocks_d, r_b2, r_a3)
 
     zero = jnp.zeros((width, 2 * width), F32)
 
@@ -642,18 +642,18 @@
     d_left = dleft_part(
         [after(blocks_c[0], part_d[1])] + blocks_c[1:] + blocks_d, [tri_c[3], tri_d[3]], d_left
     )
-    r_c = plus(r_c, after(part_c[2], d_left))
+    r_c = forward(plus(r_c, after(part_c[2], d_left)))
+    r_d = plus(r_d, after(part_d[2], d_left))
     partial, g_a = final_a_part(
-        pair_tiles, after(d_left, r_c), tokens, gain_in, w_proj, w_gate, [gate_a, gate_b, gate_c, gate_d]
-    )
+        pair_tiles, after(d_left, r_d), tokens, gain_in, w_proj, w_gate, [gate_a, gate_b, gate_c, gate_d]
+    )
+    r_d = forward(r_d)
+    r_c = plus(r_c, after(part_c[3], g_a))
+    d_pair, g_first = final(0, (part_a[0], after(r_a3, r_c)), zero, gain_in)
     r_c = forward(r_c)
-    r_d = plus(r_d, after(part_d[2], g_a))
-    d_pair, g_first = final(0, (part_a[0], after(r_a3, r_d)), zero, gain_in)
+    r_d = plus(r_d, after(part_d[3], g_first))
+    d_pair, g_first = final(1, (part_b[0], after(r_b3, r_d)), g_first, d_pair)
     r_d = forward(r_d)
-    r_c = plus(r_c, after(part_c[3], g_first))
-    d_pair, g_first = final(1, (part_b[0], after(r_b3, r_c)), g_first, d_pair)
-    r_c = forward(r_c)
-    r_d = forward(plus(r_d, after(part_d[3], g_first)))
     d_pair, g_last = final(2, (part_c[0], r_c), g_first, d_pair)
     d_pair, g_last = final(3, (part_d[0], r_d), g_last, d_pair)
 

time: 196 us -> 196 us (level)
  starting transfers between devices: 62.4 us -> 64.5 us
  waiting for transfers between devices: 56 us -> 53.9 us
    ppermute x24, starting transfers between devices: 46.1 us -> 48.2 us  [forward(): return lax.ppermute(a, 'row', [(0, 1), (1, 3), (3, 2), (2, 0)])]
    ppermute x24, waiting for transfers between devices: 37.6 us -> 35.5 us  [forward(): return lax.ppermute(a, 'row', [(0, 1), (1, 3), (3, 2), (2, 0)])]
  transfers between devices with their start and end apart: 49 -> 49, of which waited for: 23 -> 22; matrix products, arithmetic and copies ran while one was open for 2% -> 2% of each run, Pallas kernels for 32% -> 32%
where the time goes in v12:
time: 196 us; the launch traced here: 195 us
  Pallas kernels  66.1 us (34%)
  starting transfers between devices  64.5 us (33%)
  waiting for transfers between devices  53.9 us (28%)
  other arithmetic  5.8 us (3%)
  local copies, waits for them, and re-layouts  3.45 us (2%)
    ppermute x24, starting transfers between devices, forward(): return lax.ppermute(a, 'row', [(0, 1), (1, 3), (3, 2), (2, 0)])  48.2 us
    ppermute x24, waiting for transfers between devices, forward(): return lax.ppermute(a, 'row', [(0, 1), (1, 3), (3, 2), (2, 0)])  35.5 us
    pallas_call x4, Pallas kernels, mid_part(): pl.pallas_call(mid_kernel, grid=(1,), out_shape=(PANEL, pltpu.HBM(PANEL.s...  14.2 us
    pallas_call x4, Pallas kernels, dright_part(): pl.pallas_call(dright_kernel, grid=(HALF // GROUP,), out_shape=(pltpu.HBM...  11.5 us
    ppermute x9, starting transfers between devices, over_x(): return lax.ppermute(a, 'col', [(k, k ^ 2) for k in range(4)])  10.7 us
    ppermute x9, waiting for transfers between devices, over_x(): return lax.ppermute(a, 'col', [(k, k ^ 2) for k in range(4)])  9.43 us
    pallas_call x4, Pallas kernels, final_b_part(): pl.pallas_call(functools.partial(final_b_kernel, s * steps), grid=(steps,...  8.56 us
    pallas_call x4, Pallas kernels, tri_part(): pl.pallas_call(tri_kernel, grid=(HALF // GROUP,), out_shape=(PANEL, PANEL...  8.01 us
  transfers between devices with their start and end apart: 49, of which 22 were waited for; matrix products, arithmetic and copies ran while one was open for 2% of the time, Pallas kernels for 32%

profile of v12, /device:TPU:0, one launch (start us, length us, event | category | flops | bytes accessed | tf_op | source)
XLA Modules:
  0.0 195.0 jit_solution(288419115226687793)
XLA Ops:
  2.6 3.1 %collective-permute-start.3 = (bf16[64,16,128]{2,1,0:T(8,128)(2,1)S(1)}, bf16[64,16,128]{2,1,0:T(8,128)(2,1)S(1)}, u32[]{:S(2)}, u32[]{:S(2)}) collective-permute-start(bf16[64,16,128]{2,1,0:T(8,128)(2,1)S(1)} %right_part.6.s0), channel_id=1, source_target_pairs={{0,4},{4,12},{12,8},{8,0},{1,5},{5,13},{13,9},{9,1},{2,6},{6,14},{... | collective-permute-start | bytes 786440 | tf_op jit(solution)/shard_map/ppermute | solution.py:552
  7.6 2.6 %collective-permute-start = (bf16[64,16,128]{2,1,0:T(8,128)(2,1)S(1)}, bf16[64,16,128]{2,1,0:T(8,128)(2,1)S(1)}, u32[]{:S(2)}, u32[]{:S(2)}) collective-permute-start(bf16[64,16,128]{2,1,0:T(8,128)(2,1)S(1)} %right_part.5.s0), channel_id=1, source_target_pairs={{0,4},{4,12},{12,8},{8,0},{1,5},{5,13},{13,9},{9,1},{2,6},{6,14},{... | collective-permute-start | bytes 786440 | tf_op jit(solution)/shard_map/ppermute | solution.py:552
  10.2 3.6 %collective-permute-done.3.s1 = bf16[64,16,128]{2,1,0:T(8,128)(2,1)S(1)} collective-permute-done((bf16[64,16,128]{2,1,0:T(8,128)(2,1)S(1)}, bf16[64,16,128]{2,1,0:T(8,128)(2,1)S(1)}, u32[]{:S(2)}, u32[]{:S(2)}) %collective-permute-start.3) | collective-permute-done | bytes 262176 | tf_op jit(solution)/shard_map/ppermute | solution.py:552
  15.0 5.2 %left_part.1.left_ref.refs_4_ = bf16[64,2,64,128]{3,2,1,0:T(8,128)(2,1)S(1)} custom-call(bf16[64,64,128]{2,1,0:T(8,128)(2,1)} %x_ref.27, f32[1,128]{1,0:T(1,128)} %bitcast.25, bf16[128,512]{1,0:T(8,128)(2,1)} %w_ref.19, s32[1,256]{1,0:T(1,128)} %bitcast.40), custom_call_target="tpu_custom_call" | custom-call | flops 268435456 | bytes 3145728 | tf_op jit(solution)/shard_map/left_part/pallas_call | solution.py:410
  20.2 3.4 %collective-permute-start.1 = (bf16[64,16,128]{2,1,0:T(8,128)(2,1)S(1)}, bf16[64,16,128]{2,1,0:T(8,128)(2,1)S(1)}, u32[]{:S(2)}, u32[]{:S(2)}) collective-permute-start(bf16[64,16,128]{2,1,0:T(8,128)(2,1)S(1)} %collective-permute-done.s1), channel_id=1, source_target_pairs={{0,4},{4,12},{12,8},{8,0},{1,5},{5,13},{13,9},{9,1},{2,6},{6,14},{... | collective-permute-start | bytes 786440 | tf_op jit(solution)/shard_map/ppermute | solution.py:552
  28.1 2.5 %collective-permute-done.1.s2 = bf16[64,16,128]{2,1,0:T(8,128)(2,1)S(1)} collective-permute-done((bf16[64,16,128]{2,1,0:T(8,128)(2,1)S(1)}, bf16[64,16,128]{2,1,0:T(8,128)(2,1)S(1)}, u32[]{:S(2)}, u32[]{:S(2)}) %collective-permute-start.1) | collective-permute-done | bytes 262176 | tf_op jit(solution)/shard_map/ppermute | solution.py:552
  32.9 3.4 %collective-permute-done.5.s3 = bf16[64,16,128]{2,1,0:T(8,128)(2,1)S(1)} collective-permute-done((bf16[64,16,128]{2,1,0:T(8,128)(2,1)S(1)}, bf16[64,16,128]{2,1,0:T(8,128)(2,1)S(1)}, u32[]{:S(2)}, u32[]{:S(2)}) %collective-permute-start.5) | collective-permute-done | bytes 262176 | tf_op jit(solution)/shard_map/ppermute | solution.py:552
  38.4 2.6 %collective-permute-done.14.s3 = bf16[64,16,128]{2,1,0:T(8,128)(2,1)S(1)} collective-permute-done((bf16[64,16,128]{2,1,0:T(8,128)(2,1)S(1)}, bf16[64,16,128]{2,1,0:T(8,128)(2,1)S(1)}, u32[]{:S(2)}, u32[]{:S(2)}) %collective-permute-start.14) | collective-permute-done | bytes 262176 | tf_op jit(solution)/shard_map/ppermute | solution.py:552
  44.0 3.4 %collective-permute-start.9 = (bf16[64,16,128]{2,1,0:T(8,128)(2,1)S(1)}, bf16[64,16,128]{2,1,0:T(8,128)(2,1)S(1)}, u32[]{:S(2)}, u32[]{:S(2)}) collective-permute-start(bf16[64,16,128]{2,1,0:T(8,128)(2,1)S(1)} %right_part.7.s0), channel_id=1, source_target_pairs={{0,4},{4,12},{12,8},{8,0},{1,5},{5,13},{13,9},{9,1},{2,6},{6,14},{... | collective-permute-start | bytes 786440 | tf_op jit(solution)/shard_map/ppermute | solution.py:552
  49.7 3.5 %collective-permute-done.2.s1 = bf16[64,16,128]{2,1,0:T(8,128)(2,1)S(1)} collective-permute-done((bf16[64,16,128]{2,1,0:T(8,128)(2,1)S(1)}, bf16[64,16,128]{2,1,0:T(8,128)(2,1)S(1)}, u32[]{:S(2)}, u32[]{:S(2)}) %collective-permute-start.2) | collective-permute-done | bytes 262176 | tf_op jit(solution)/shard_map/ppermute | solution.py:552
  54.0 4.8 %collective-permute-done.9.s1 = bf16[64,16,128]{2,1,0:T(8,128)(2,1)S(1)} collective-permute-done((bf16[64,16,128]{2,1,0:T(8,128)(2,1)S(1)}, bf16[64,16,128]{2,1,0:T(8,128)(2,1)S(1)}, u32[]{:S(2)}, u32[]{:S(2)}) %collective-permute-start.9) | collective-permute-done | bytes 262176 | tf_op jit(solution)/shard_map/ppermute | solution.py:552
  58.9 3.5 %mid_part.4 = (bf16[64,16,128]{2,1,0:T(8,128)(2,1)S(1)}, bf16[64,16,128]{2,1,0:T(8,128)(2,1)}, f32[128,128]{1,0:T(8,128)S(1)}, f32[128,128]{1,0:T(8,128)S(1)}) custom-call(bf16[64,16,128]{2,1,0:T(8,128)(2,1)S(1)} %get-tuple-element.100.a_ref, bf16[2,64,16,128]{3,2,1,0:T(8,128)(2,1)S(1)} %collective-permute-done.6.b_ref, ...), custom_call_target="tpu_custom_call" | custom-call | flops 201326592 | bytes 2097152 | tf_op jit(solution)/shard_map/mid_part/pallas_call | solution.py:443
  64.0 3.6 %mid_part.5 = (bf16[64,16,128]{2,1,0:T(8,128)(2,1)S(1)}, bf16[64,16,128]{2,1,0:T(8,128)(2,1)}, f32[128,128]{1,0:T(8,128)S(1)}, f32[128,128]{1,0:T(8,128)S(1)}) custom-call(bf16[64,16,128]{2,1,0:T(8,128)(2,1)S(1)} %get-tuple-element.116.a_ref, bf16[2,64,16,128]{3,2,1,0:T(8,128)(2,1)S(1)} %collective-permute-done.15.b_ref, ...), custom_call_target="tpu_custom_call" | custom-call | flops 201326592 | bytes 2097152 | tf_op jit(solution)/shard_map/mid_part/pallas_call | solution.py:443
  70.4 3.4 %collective-permute-start.10 = (bf16[64,16,128]{2,1,0:T(8,128)(2,1)S(1)}, bf16[64,16,128]{2,1,0:T(8,128)(2,1)S(1)}, u32[]{:S(2)}, u32[]{:S(2)}) collective-permute-start(bf16[64,16,128]{2,1,0:T(8,128)(2,1)S(1)} %collective-permute-done.7.s2), channel_id=1, source_target_pairs={{0,4},{4,12},{12,8},{8,0},{1,5},{5,13},{13,9},{9,1},{2,6},{6,14},{... | collective-permute-start | bytes 786440 | tf_op jit(solution)/shard_map/ppermute | solution.py:552
  75.5 3.8 %collective-permute-done.16.s2 = bf16[64,16,128]{2,1,0:T(8,128)(2,1)S(1)} collective-permute-done((bf16[64,16,128]{2,1,0:T(8,128)(2,1)S(1)}, bf16[64,16,128]{2,1,0:T(8,128)(2,1)S(1)}, u32[]{:S(2)}, u32[]{:S(2)}) %collective-permute-start.16) | collective-permute-done | bytes 262176 | tf_op jit(solution)/shard_map/ppermute | solution.py:552
  86.2 3.2 %collective-permute-start.19 = (bf16[64,16,128]{2,1,0:T(8,128)(2,1)S(1)}, bf16[64,16,128]{2,1,0:T(8,128)(2,1)S(1)}, u32[]{:S(2)}, u32[]{:S(2)}) collective-permute-start(bf16[64,16,128]{2,1,0:T(8,128)(2,1)S(1)} %get-tuple-element.110), channel_id=1, source_target_pairs={{0,4},{4,12},{12,8},{8,0},{1,5},{5,13},{13,9},{9,1},{2,6},{6,14},{... | collective-permute-start | bytes 786440 | tf_op jit(solution)/shard_map/ppermute | solution.py:552
  98.9 2.3 %collective-permute-start.32 = (bf16[64,16,128]{2,1,0:T(8,128)(2,1)}, bf16[64,16,128]{2,1,0:T(8,128)(2,1)}, u32[]{:S(2)}, u32[]{:S(2)}) collective-permute-start(bf16[64,16,128]{2,1,0:T(8,128)(2,1)} %add_convert_fusion.7), channel_id=1, source_target_pairs={{0,4},{4,12},{12,8},{8,0},{1,5},{5,13},{13,9},{9,1},{2,6},{6,14},{... | collective-permute-start | bytes 786440 | tf_op jit(solution)/shard_map/ppermute | solution.py:552
  103.1 2.8 %collective-permute-done.18.c_ref = bf16[64,16,128]{2,1,0:T(8,128)(2,1)S(1)} collective-permute-done((bf16[64,16,128]{2,1,0:T(8,128)(2,1)S(1)}, bf16[64,16,128]{2,1,0:T(8,128)(2,1)S(1)}, u32[]{:S(2)}, u32[]{:S(2)}) %collective-permute-start.18) | collective-permute-done | bytes 262176 | tf_op jit(solution)/shard_map/ppermute | solution.py:558
  106.0 3.5 %mid_part.6 = (bf16[64,16,128]{2,1,0:T(8,128)(2,1)S(1)}, bf16[64,16,128]{2,1,0:T(8,128)(2,1)}, f32[128,128]{1,0:T(8,128)S(1)}, f32[128,128]{1,0:T(8,128)S(1)}) custom-call(bf16[64,16,128]{2,1,0:T(8,128)(2,1)S(1)} %get-tuple-element.112.a_ref, bf16[2,64,16,128]{3,2,1,0:T(8,128)(2,1)S(1)} %collective-permute-done.17.b_ref, ...), custom_call_target="tpu_custom_call" | custom-call | flops 201326592 | bytes 2097152 | tf_op jit(solution)/shard_map/mid_part/pallas_call | solution.py:443
  110.9 3.6 %mid_part.7 = (bf16[64,16,128]{2,1,0:T(8,128)(2,1)}, bf16[64,16,128]{2,1,0:T(8,128)(2,1)}, f32[128,128]{1,0:T(8,128)S(1)}, f32[128,128]{1,0:T(8,128)S(1)}) custom-call(bf16[64,16,128]{2,1,0:T(8,128)(2,1)S(1)} %get-tuple-element.134.a_ref, bf16[2,64,16,128]{3,2,1,0:T(8,128)(2,1)S(1)} %collective-permute-done.25.b_ref, ...), custom_call_target="tpu_custom_call" | custom-call | flops 201326592 | bytes 2097152 | tf_op jit(solution)/shard_map/mid_part/pallas_call | solution.py:443
  117.1 2.4 %collective-permute-start.31 = (bf16[64,16,128]{2,1,0:T(8,128)(2,1)}, bf16[64,16,128]{2,1,0:T(8,128)(2,1)S(1)}, u32[]{:S(2)}, u32[]{:S(2)}) collective-permute-start(bf16[64,16,128]{2,1,0:T(8,128)(2,1)} %add_convert_fusion.6), channel_id=1, source_target_pairs={{0,4},{4,12},{12,8},{8,0},{1,5},{5,13},{13,9},{9,1},{2,6},{6,14},{... | collective-permute-start | bytes 786440 | tf_op jit(solution)/shard_map/ppermute | solution.py:552
  124.2 3.7 %dright_part.7 = (bf16[64,16,128]{2,1,0:T(8,128)(2,1)}, bf16[64,16,128]{2,1,0:T(8,128)(2,1)S(1)}, bf16[64,16,128]{2,1,0:T(8,128)(2,1)S(1)}, bf16[64,16,128]{2,1,0:T(8,128)(2,1)S(1)}) custom-call(bf16[64,16,128]{2,1,0:T(8,128)(2,1)S(1)} %get-tuple-element.147.refs_0_, bf16[64,16,128]{2,1,0:T(8,128)(2,1)} %collective-permute-done.34.refs_1_, ...), custom_call_target="tpu_custom_call" | custom-call | flops 268435456 | bytes 6291456 | tf_op jit(solution)/shard_map/dright_part/pallas_call | solution.py:459
  132.1 3.6 %dright_part.6 = (bf16[64,16,128]{2,1,0:T(8,128)(2,1)}, bf16[64,16,128]{2,1,0:T(8,128)(2,1)S(1)}, bf16[64,16,128]{2,1,0:T(8,128)(2,1)S(1)}, bf16[64,16,128]{2,1,0:T(8,128)(2,1)S(1)}) custom-call(bf16[64,16,128]{2,1,0:T(8,128)(2,1)} %get-tuple-element.139.refs_0_.refs_4_, bf16[64,16,128]{2,1,0:T(8,128)(2,1)} %collective-permute-done.28.refs_1_.refs_5_, ...), custom_call_target="tpu_custom_call" | custom-call | flops 268435456 | bytes 6291456 | tf_op jit(solution)/shard_map/dright_part/pallas_call | solution.py:459
  137.9 3.2 %dleft_part.3.dleft_ref = f32[64,64,128]{2,1,0:T(8,128)S(1)} custom-call(bf16[64,16,128]{2,1,0:T(8,128)(2,1)S(1)} %get-tuple-element.147.refs_0_, bf16[64,16,128]{2,1,0:T(8,128)(2,1)} %collective-permute-done.34.refs_1_, bf16[64,16,128]{2,1,0:T(8,128)(2,1)} %collective-permute-done.35.refs_2_, bf16[64,16,128]{2,1,0:T(8,128)(2,1)} %collective-permute-done.36.refs_3_, ...), custom_call_target="tpu_custom_call" | custom-call | flops 268435456 | bytes 8388608 | tf_op jit(solution)/shard_map/dleft_part/pallas_call | solution.py:474
  141.2 3.4 %collective-permute-start.40 = (bf16[64,16,128]{2,1,0:T(8,128)(2,1)S(1)}, bf16[64,16,128]{2,1,0:T(8,128)(2,1)S(1)}, u32[]{:S(2)}, u32[]{:S(2)}) collective-permute-start(bf16[64,16,128]{2,1,0:T(8,128)(2,1)S(1)} %add_convert_fusion.2), channel_id=1, source_target_pairs={{0,4},{4,12},{12,8},{8,0},{1,5},{5,13},{13,9},{9,1},{2,6},{6,14},{... | collective-permute-start | bytes 786440 | tf_op jit(solution)/shard_map/ppermute | solution.py:552
  144.6 4.5 %collective-permute-done.37 = bf16[64,16,128]{2,1,0:T(8,128)(2,1)S(1)} collective-permute-done((bf16[64,16,128]{2,1,0:T(8,128)(2,1)S(1)}, bf16[64,16,128]{2,1,0:T(8,128)(2,1)S(1)}, u32[]{:S(2)}, u32[]{:S(2)}) %collective-permute-start.37) | collective-permute-done | bytes 262176 | tf_op jit(solution)/shard_map/ppermute | solution.py:552
  151.3 6.0 %final_a_part.1 = (f32[128,4096]{1,0:T(8,128)S(1)}, f32[128,256]{1,0:T(8,128)S(1)}) custom-call(bf16[64,64,128]{2,1,0:T(8,128)(2,1)S(1)} %copy-done, f32[64,64,128]{2,1,0:T(8,128)S(1)} %dleft_part.3.dleft_ref, s32[1,256]{1,0:T(1,128)S(1)} %bitcast.43, f32[1,128]{1,0:T(1,128)S(1)} %bitcast.32, bf16[128,512]{1,0:T(8,128)(2,1)S(1)} %copy-done.2, ...), custom_call_target="tpu_custom_call" | custom-call | flops 939524096 | bytes 8388608 | tf_op jit(solution)/shard_map/final_a_part/pallas_call | solution.py:487
  157.3 3.4 %collective-permute-start.42 = (bf16[64,16,128]{2,1,0:T(8,128)(2,1)S(1)}, bf16[64,16,128]{2,1,0:T(8,128)(2,1)S(1)}, u32[]{:S(2)}, u32[]{:S(2)}) collective-permute-start(bf16[64,16,128]{2,1,0:T(8,128)(2,1)S(1)} %add_convert_fusion.1), channel_id=1, source_target_pairs={{0,4},{4,12},{12,8},{8,0},{1,5},{5,13},{13,9},{9,1},{2,6},{6,14},{... | collective-permute-start | bytes 786440 | tf_op jit(solution)/shard_map/ppermute | solution.py:552
  178.2 3.5 %collective-permute-done.45 = bf16[64,768]{1,0:T(8,128)(2,1)S(1)} collective-permute-done((bf16[64,768]{1,0:T(8,128)(2,1)S(1)}, bf16[64,768]{1,0:T(8,128)(2,1)S(1)}, u32[]{:S(2)}, u32[]{:S(2)}) %collective-permute-start.45) | collective-permute-done | bytes 98336 | tf_op jit(solution)/shard_map/ppermute | solution.py:558
  183.2 3.1 %collective-permute-done.46 = bf16[64,768]{1,0:T(8,128)(2,1)S(1)} collective-permute-done((bf16[64,768]{1,0:T(8,128)(2,1)S(1)}, bf16[64,768]{1,0:T(8,128)(2,1)S(1)}, u32[]{:S(2)}, u32[]{:S(2)}) %collective-permute-start.46) | collective-permute-done | bytes 98336 | tf_op jit(solution)/shard_map/ppermute | solution.py:555
  186.4 2.6 %collective-permute-start.47 = (bf16[64,768]{1,0:T(8,128)(2,1)S(1)}, bf16[64,768]{1,0:T(8,128)(2,1)S(1)}, u32[]{:S(2)}, u32[]{:S(2)}) collective-permute-start(bf16[64,768]{1,0:T(8,128)(2,1)S(1)} %add_convert_fusion.8), channel_id=1, source_target_pairs={{0,8},{4,12},{8,0},{12,4},{1,9},{5,13},{9,1},{13,5},{2,10},{6,14},... | collective-permute-start | bytes 294920 | tf_op jit(solution)/shard_map/ppermute | solution.py:555
  189.0 2.9 %collective-permute-done.47 = bf16[64,768]{1,0:T(8,128)(2,1)S(1)} collective-permute-done((bf16[64,768]{1,0:T(8,128)(2,1)S(1)}, bf16[64,768]{1,0:T(8,128)(2,1)S(1)}, u32[]{:S(2)}, u32[]{:S(2)}) %collective-permute-start.47) | collective-permute-done | bytes 98336 | tf_op jit(solution)/shard_map/ppermute | solution.py:555
  (175 shorter events, 83.3 us)
Async XLA Ops:
  2.6 11.2 %collective-permute-start.3 = (bf16[64,16,128]{2,1,0:T(8,128)(2,1)S(1)}, bf16[64,16,128]{2,1,0:T(8,128)(2,1)S(1)}, u32[]{:S(2)}, u32[]{:S(2)}) collective-permute-start(bf16[64,16,128]{2,1,0:T(8,128)(2,1)S(1)} %right_part.6.s0), channel_id=1, source_target_pairs={{0,4},{4,12},{12,8},{8,0},{1,5},{5,13},{13,9},{9,1},{2,6},{6,14},{... | collective-permute-start | bytes 786440 | tf_op jit(solution)/shard_map/ppermute | solution.py:552
  7.6 12.6 %collective-permute-start = (bf16[64,16,128]{2,1,0:T(8,128)(2,1)S(1)}, bf16[64,16,128]{2,1,0:T(8,128)(2,1)S(1)}, u32[]{:S(2)}, u32[]{:S(2)}) collective-permute-start(bf16[64,16,128]{2,1,0:T(8,128)(2,1)S(1)} %right_part.5.s0), channel_id=1, source_target_pairs={{0,4},{4,12},{12,8},{8,0},{1,5},{5,13},{13,9},{9,1},{2,6},{6,14},{... | collective-permute-start | bytes 786440 | tf_op jit(solution)/shard_map/ppermute | solution.py:552
  13.8 11.8 %collective-permute-start.4 = (bf16[64,16,128]{2,1,0:T(8,128)(2,1)S(1)}, bf16[64,16,128]{2,1,0:T(8,128)(2,1)S(1)}, u32[]{:S(2)}, u32[]{:S(2)}) collective-permute-start(bf16[64,16,128]{2,1,0:T(8,128)(2,1)S(1)} %collective-permute-done.3.s1), channel_id=1, source_target_pairs={{0,4},{4,12},{12,8},{8,0},{1,5},{5,13},{13,9},{9,1},{2,6},{6,14},{... | collective-permute-start | bytes 786440 | tf_op jit(solution)/shard_map/ppermute | solution.py:552
  20.2 10.5 %collective-permute-start.1 = (bf16[64,16,128]{2,1,0:T(8,128)(2,1)S(1)}, bf16[64,16,128]{2,1,0:T(8,128)(2,1)S(1)}, u32[]{:S(2)}, u32[]{:S(2)}) collective-permute-start(bf16[64,16,128]{2,1,0:T(8,128)(2,1)S(1)} %collective-permute-done.s1), channel_id=1, source_target_pairs={{0,4},{4,12},{12,8},{8,0},{1,5},{5,13},{13,9},{9,1},{2,6},{6,14},{... | collective-permute-start | bytes 786440 | tf_op jit(solution)/shard_map/ppermute | solution.py:552
  25.6 10.7 %collective-permute-start.5 = (bf16[64,16,128]{2,1,0:T(8,128)(2,1)S(1)}, bf16[64,16,128]{2,1,0:T(8,128)(2,1)S(1)}, u32[]{:S(2)}, u32[]{:S(2)}) collective-permute-start(bf16[64,16,128]{2,1,0:T(8,128)(2,1)S(1)} %collective-permute-done.4.s2), channel_id=1, source_target_pairs={{0,4},{4,12},{12,8},{8,0},{1,5},{5,13},{13,9},{9,1},{2,6},{6,14},{... | collective-permute-start | bytes 786440 | tf_op jit(solution)/shard_map/ppermute | solution.py:552
  30.7 10.4 %collective-permute-start.14 = (bf16[64,16,128]{2,1,0:T(8,128)(2,1)S(1)}, bf16[64,16,128]{2,1,0:T(8,128)(2,1)S(1)}, u32[]{:S(2)}, u32[]{:S(2)}) collective-permute-start(bf16[64,16,128]{2,1,0:T(8,128)(2,1)S(1)} %collective-permute-done.1.s2), channel_id=1, source_target_pairs={{0,4},{4,12},{12,8},{8,0},{1,5},{5,13},{13,9},{9,1},{2,6},{6,14},{... | collective-permute-start | bytes 786440 | tf_op jit(solution)/shard_map/ppermute | solution.py:552
  43.2 10.1 %collective-permute-start.2 = (bf16[64,16,128]{2,1,0:T(8,128)(2,1)S(1)}, bf16[64,16,128]{2,1,0:T(8,128)(2,1)S(1)}, u32[]{:S(2)}, u32[]{:S(2)}) collective-permute-start(bf16[64,16,128]{2,1,0:T(8,128)(2,1)S(1)} %right_part.4.s0), channel_id=1, source_target_pairs={{0,4},{4,12},{12,8},{8,0},{1,5},{5,13},{13,9},{9,1},{2,6},{6,14},{... | collective-permute-start | bytes 786440 | tf_op jit(solution)/shard_map/ppermute | solution.py:552
  44.0 14.8 %collective-permute-start.9 = (bf16[64,16,128]{2,1,0:T(8,128)(2,1)S(1)}, bf16[64,16,128]{2,1,0:T(8,128)(2,1)S(1)}, u32[]{:S(2)}, u32[]{:S(2)}) collective-permute-start(bf16[64,16,128]{2,1,0:T(8,128)(2,1)S(1)} %right_part.7.s0), channel_id=1, source_target_pairs={{0,4},{4,12},{12,8},{8,0},{1,5},{5,13},{13,9},{9,1},{2,6},{6,14},{... | collective-permute-start | bytes 786440 | tf_op jit(solution)/shard_map/ppermute | solution.py:552
  47.5 11.3 %collective-permute-start.8 = (bf16[64,16,128]{2,1,0:T(8,128)(2,1)S(1)}, bf16[64,16,128]{2,1,0:T(8,128)(2,1)S(1)}, u32[]{:S(2)}, u32[]{:S(2)}) collective-permute-start(bf16[64,16,128]{2,1,0:T(8,128)(2,1)S(1)} %fusion.3), channel_id=1, source_target_pairs={{0,2},{1,3},{2,0},{3,1},{4,6},{5,7},{6,4},{7,5},{8,10},{9,11},{10,... | collective-permute-start | bytes 786440 | tf_op jit(solution)/shard_map/ppermute | solution.py:558
  49.1 14.8 %collective-permute-start.20 = (bf16[64,16,128]{2,1,0:T(8,128)(2,1)S(1)}, bf16[64,16,128]{2,1,0:T(8,128)(2,1)S(1)}, u32[]{:S(2)}, u32[]{:S(2)}) collective-permute-start(bf16[64,16,128]{2,1,0:T(8,128)(2,1)S(1)} %fusion.2), channel_id=1, source_target_pairs={{0,2},{1,3},{2,0},{3,1},{4,6},{5,7},{6,4},{7,5},{8,10},{9,11},{10,... | collective-permute-start | bytes 786440 | tf_op jit(solution)/shard_map/ppermute | solution.py:558
  53.2 10.8 %collective-permute-start.7 = (bf16[64,16,128]{2,1,0:T(8,128)(2,1)S(1)}, bf16[64,16,128]{2,1,0:T(8,128)(2,1)S(1)}, u32[]{:S(2)}, u32[]{:S(2)}) collective-permute-start(bf16[64,16,128]{2,1,0:T(8,128)(2,1)S(1)} %collective-permute-done.2.s1), channel_id=1, source_target_pairs={{0,4},{4,12},{12,8},{8,0},{1,5},{5,13},{13,9},{9,1},{2,6},{6,14},{... | collective-permute-start | bytes 786440 | tf_op jit(solution)/shard_map/ppermute | solution.py:552
  69.1 10.1 %collective-permute-start.16 = (bf16[64,16,128]{2,1,0:T(8,128)(2,1)S(1)}, bf16[64,16,128]{2,1,0:T(8,128)(2,1)S(1)}, u32[]{:S(2)}, u32[]{:S(2)}) collective-permute-start(bf16[64,16,128]{2,1,0:T(8,128)(2,1)S(1)} %collective-permute-done.9.s1), channel_id=1, source_target_pairs={{0,4},{4,12},{12,8},{8,0},{1,5},{5,13},{13,9},{9,1},{2,6},{6,14},{... | collective-permute-start | bytes 786440 | tf_op jit(solution)/shard_map/ppermute | solution.py:552
  69.9 9.4 %collective-permute-start.13 = (bf16[64,16,128]{2,1,0:T(8,128)(2,1)S(1)}, bf16[64,16,128]{2,1,0:T(8,128)(2,1)S(1)}, u32[]{:S(2)}, u32[]{:S(2)}) collective-permute-start(bf16[64,16,128]{2,1,0:T(8,128)(2,1)S(1)} %collective-permute-done.11.refs_1_), channel_id=1, source_target_pairs={{0,1},{1,0},{2,3},{3,2},{4,5},{5,4},{6,7},{7,6},{8,9},{9,8},{10,11... | collective-permute-start | bytes 786440 | tf_op jit(solution)/shard_map/ppermute | solution.py:561
  69.9 10.1 %collective-permute-start.12 = (bf16[64,16,128]{2,1,0:T(8,128)(2,1)S(1)}, bf16[64,16,128]{2,1,0:T(8,128)(2,1)S(1)}, u32[]{:S(2)}, u32[]{:S(2)}) collective-permute-start(bf16[64,16,128]{2,1,0:T(8,128)(2,1)S(1)} %get-tuple-element.127.refs_0_), channel_id=1, source_target_pairs={{0,1},{1,0},{2,3},{3,2},{4,5},{5,4},{6,7},{7,6},{8,9},{9,8},{10,11... | collective-permute-start | bytes 786440 | tf_op jit(solution)/shard_map/ppermute | solution.py:561
  70.4 12.8 %collective-permute-start.10 = (bf16[64,16,128]{2,1,0:T(8,128)(2,1)S(1)}, bf16[64,16,128]{2,1,0:T(8,128)(2,1)S(1)}, u32[]{:S(2)}, u32[]{:S(2)}) collective-permute-start(bf16[64,16,128]{2,1,0:T(8,128)(2,1)S(1)} %collective-permute-done.7.s2), channel_id=1, source_target_pairs={{0,4},{4,12},{12,8},{8,0},{1,5},{5,13},{13,9},{9,1},{2,6},{6,14},{... | collective-permute-start | bytes 786440 | tf_op jit(solution)/shard_map/ppermute | solution.py:552
  75.5 14.0 %collective-permute-start.24 = (bf16[64,16,128]{2,1,0:T(8,128)(2,1)S(1)}, bf16[64,16,128]{2,1,0:T(8,128)(2,1)S(1)}, u32[]{:S(2)}, u32[]{:S(2)}) collective-permute-start(bf16[64,16,128]{2,1,0:T(8,128)(2,1)S(1)} %collective-permute-done.22.refs_1_.refs_5_), channel_id=1, source_target_pairs={{0,1},{1,0},{2,3},{3,2},{4,5},{5,4},{6,7},{7,6},{8,9},{9,8},{10,11... | collective-permute-start | bytes 786440 | tf_op jit(solution)/shard_map/ppermute | solution.py:561
  79.2 10.2 %collective-permute-start.23 = (bf16[64,16,128]{2,1,0:T(8,128)(2,1)S(1)}, bf16[64,16,128]{2,1,0:T(8,128)(2,1)S(1)}, u32[]{:S(2)}, u32[]{:S(2)}) collective-permute-start(bf16[64,16,128]{2,1,0:T(8,128)(2,1)S(1)} %get-tuple-element.120.refs_0_.refs_4_), channel_id=1, source_target_pairs={{0,1},{1,0},{2,3},{3,2},{4,5},{5,4},{6,7},{7,6},{8,9},{9,8},{10,11... | collective-permute-start | bytes 786440 | tf_op jit(solution)/shard_map/ppermute | solution.py:561
  79.2 12.3 %collective-permute-start.21 = (bf16[64,16,128]{2,1,0:T(8,128)(2,1)S(1)}, bf16[64,16,128]{2,1,0:T(8,128)(2,1)S(1)}, u32[]{:S(2)}, u32[]{:S(2)}) collective-permute-start(bf16[64,16,128]{2,1,0:T(8,128)(2,1)S(1)} %collective-permute-done.16.s2), channel_id=1, source_target_pairs={{0,4},{4,12},{12,8},{8,0},{1,5},{5,13},{13,9},{9,1},{2,6},{6,14},{... | collective-permute-start | bytes 786440 | tf_op jit(solution)/shard_map/ppermute | solution.py:552
  86.2 10.4 %collective-permute-start.17 = (bf16[2,64,16,128]{3,2,1,0:T(8,128)(2,1)S(1)}, bf16[2,64,16,128]{3,2,1,0:T(8,128)(2,1)S(1)}, u32[]{:S(2)}, u32[]{:S(2)}) collective-permute-start(bf16[2,64,16,128]{3,2,1,0:T(8,128)(2,1)S(1)} %get-tuple-element.113), channel_id=1, source_target_pairs={{0,1},{1,0},{2,3},{3,2},{4,5},{5,4},{6,7},{7,6},{8,9},{9,8},{10,11... | collective-permute-start | bytes 1572872 | tf_op jit(solution)/shard_map/ppermute | solution.py:561
  86.2 9.6 %collective-permute-start.19 = (bf16[64,16,128]{2,1,0:T(8,128)(2,1)S(1)}, bf16[64,16,128]{2,1,0:T(8,128)(2,1)S(1)}, u32[]{:S(2)}, u32[]{:S(2)}) collective-permute-start(bf16[64,16,128]{2,1,0:T(8,128)(2,1)S(1)} %get-tuple-element.110), channel_id=1, source_target_pairs={{0,4},{4,12},{12,8},{8,0},{1,5},{5,13},{13,9},{9,1},{2,6},{6,14},{... | collective-permute-start | bytes 786440 | tf_op jit(solution)/shard_map/ppermute | solution.py:552
  93.7 16.3 %collective-permute-start.27 = (bf16[64,16,128]{2,1,0:T(8,128)(2,1)S(1)}, bf16[64,16,128]{2,1,0:T(8,128)(2,1)S(1)}, u32[]{:S(2)}, u32[]{:S(2)}) collective-permute-start(bf16[64,16,128]{2,1,0:T(8,128)(2,1)S(1)} %get-tuple-element.123), channel_id=1, source_target_pairs={{0,4},{4,12},{12,8},{8,0},{1,5},{5,13},{13,9},{9,1},{2,6},{6,14},{... | collective-permute-start | bytes 786440 | tf_op jit(solution)/shard_map/ppermute | solution.py:552
  97.3 13.6 %collective-permute-start.26 = (bf16[64,16,128]{2,1,0:T(8,128)(2,1)S(1)}, bf16[64,16,128]{2,1,0:T(8,128)(2,1)S(1)}, u32[]{:S(2)}, u32[]{:S(2)}) collective-permute-start(bf16[64,16,128]{2,1,0:T(8,128)(2,1)S(1)} %fusion), channel_id=1, source_target_pairs={{0,2},{1,3},{2,0},{3,1},{4,6},{5,7},{6,4},{7,5},{8,10},{9,11},{10,... | collective-permute-start | bytes 786440 | tf_op jit(solution)/shard_map/ppermute | solution.py:558
  98.9 20.6 %collective-permute-start.32 = (bf16[64,16,128]{2,1,0:T(8,128)(2,1)}, bf16[64,16,128]{2,1,0:T(8,128)(2,1)}, u32[]{:S(2)}, u32[]{:S(2)}) collective-permute-start(bf16[64,16,128]{2,1,0:T(8,128)(2,1)} %add_convert_fusion.7), channel_id=1, source_target_pairs={{0,4},{4,12},{12,8},{8,0},{1,5},{5,13},{13,9},{9,1},{2,6},{6,14},{... | collective-permute-start | bytes 786440 | tf_op jit(solution)/shard_map/ppermute | solution.py:552
  117.1 13.1 %collective-permute-start.31 = (bf16[64,16,128]{2,1,0:T(8,128)(2,1)}, bf16[64,16,128]{2,1,0:T(8,128)(2,1)S(1)}, u32[]{:S(2)}, u32[]{:S(2)}) collective-permute-start(bf16[64,16,128]{2,1,0:T(8,128)(2,1)} %add_convert_fusion.6), channel_id=1, source_target_pairs={{0,4},{4,12},{12,8},{8,0},{1,5},{5,13},{13,9},{9,1},{2,6},{6,14},{... | collective-permute-start | bytes 786440 | tf_op jit(solution)/shard_map/ppermute | solution.py:552
  119.5 12.6 %collective-permute-start.29 = (bf16[64,16,128]{2,1,0:T(8,128)(2,1)}, bf16[64,16,128]{2,1,0:T(8,128)(2,1)S(1)}, u32[]{:S(2)}, u32[]{:S(2)}) collective-permute-start(bf16[64,16,128]{2,1,0:T(8,128)(2,1)} %get-tuple-element.139.refs_0_.refs_4_), channel_id=1, source_target_pairs={{0,1},{1,0},{2,3},{3,2},{4,5},{5,4},{6,7},{7,6},{8,9},{9,8},{10,11... | collective-permute-start | bytes 786440 | tf_op jit(solution)/shard_map/ppermute | solution.py:561
  121.9 10.2 %collective-permute-start.33 = (bf16[64,16,128]{2,1,0:T(8,128)(2,1)S(1)}, bf16[64,16,128]{2,1,0:T(8,128)(2,1)S(1)}, u32[]{:S(2)}, u32[]{:S(2)}) collective-permute-start(bf16[64,16,128]{2,1,0:T(8,128)(2,1)S(1)} %add_convert_fusion.4), channel_id=1, source_target_pairs={{0,4},{4,12},{12,8},{8,0},{1,5},{5,13},{13,9},{9,1},{2,6},{6,14},{... | collective-permute-start | bytes 786440 | tf_op jit(solution)/shard_map/ppermute | solution.py:552
  127.9 13.2 %collective-permute-start.39 = (bf16[64,16,128]{2,1,0:T(8,128)(2,1)S(1)}, bf16[64,16,128]{2,1,0:T(8,128)(2,1)S(1)}, u32[]{:S(2)}, u32[]{:S(2)}) collective-permute-start(bf16[64,16,128]{2,1,0:T(8,128)(2,1)S(1)} %get-tuple-element.162), channel_id=1, source_target_pairs={{0,4},{4,12},{12,8},{8,0},{1,5},{5,13},{13,9},{9,1},{2,6},{6,14},{... | collective-permute-start | bytes 786440 | tf_op jit(solution)/shard_map/ppermute | solution.py:552
  130.2 33.1 %collective-permute-start.43 = (bf16[64,16,128]{2,1,0:T(8,128)(2,1)S(1)}, bf16[64,16,128]{2,1,0:T(8,128)(2,1)S(1)}, u32[]{:S(2)}, u32[]{:S(2)}) collective-permute-start(bf16[64,16,128]{2,1,0:T(8,128)(2,1)S(1)} %add_convert_fusion.5), channel_id=1, source_target_pairs={{0,4},{4,12},{12,8},{8,0},{1,5},{5,13},{13,9},{9,1},{2,6},{6,14},{... | collective-permute-start | bytes 786440 | tf_op jit(solution)/shard_map/ppermute | solution.py:552
  135.7 13.5 %collective-permute-start.37 = (bf16[64,16,128]{2,1,0:T(8,128)(2,1)S(1)}, bf16[64,16,128]{2,1,0:T(8,128)(2,1)S(1)}, u32[]{:S(2)}, u32[]{:S(2)}) collective-permute-start(bf16[64,16,128]{2,1,0:T(8,128)(2,1)S(1)} %get-tuple-element.146), channel_id=1, source_target_pairs={{0,4},{4,12},{12,8},{8,0},{1,5},{5,13},{13,9},{9,1},{2,6},{6,14},{... | collective-permute-start | bytes 786440 | tf_op jit(solution)/shard_map/ppermute | solution.py:552
  141.2 16.0 %collective-permute-start.40 = (bf16[64,16,128]{2,1,0:T(8,128)(2,1)S(1)}, bf16[64,16,128]{2,1,0:T(8,128)(2,1)S(1)}, u32[]{:S(2)}, u32[]{:S(2)}) collective-permute-start(bf16[64,16,128]{2,1,0:T(8,128)(2,1)S(1)} %add_convert_fusion.2), channel_id=1, source_target_pairs={{0,4},{4,12},{12,8},{8,0},{1,5},{5,13},{13,9},{9,1},{2,6},{6,14},{... | collective-permute-start | bytes 786440 | tf_op jit(solution)/shard_map/ppermute | solution.py:552
  149.3 13.7 %collective-permute-start.38 = (bf16[64,16,128]{2,1,0:T(8,128)(2,1)S(1)}, bf16[64,16,128]{2,1,0:T(8,128)(2,1)S(1)}, u32[]{:S(2)}, u32[]{:S(2)}) collective-permute-start(bf16[64,16,128]{2,1,0:T(8,128)(2,1)S(1)} %add_convert_fusion.3), channel_id=1, source_target_pairs={{0,4},{4,12},{12,8},{8,0},{1,5},{5,13},{13,9},{9,1},{2,6},{6,14},{... | collective-permute-start | bytes 786440 | tf_op jit(solution)/shard_map/ppermute | solution.py:552
  157.3 10.2 %collective-permute-start.42 = (bf16[64,16,128]{2,1,0:T(8,128)(2,1)S(1)}, bf16[64,16,128]{2,1,0:T(8,128)(2,1)S(1)}, u32[]{:S(2)}, u32[]{:S(2)}) collective-permute-start(bf16[64,16,128]{2,1,0:T(8,128)(2,1)S(1)} %add_convert_fusion.1), channel_id=1, source_target_pairs={{0,4},{4,12},{12,8},{8,0},{1,5},{5,13},{13,9},{9,1},{2,6},{6,14},{... | collective-permute-start | bytes 786440 | tf_op jit(solution)/shard_map/ppermute | solution.py:552
  (46 other events, 423.5 us)

commit v13 on v11

--- a/solution.py
+++ b/solution.py
@@ -574,7 +574,7 @@
     a1, b1 = forward(a0), forward(b0)
     a2, b2 = forward(a1), forward(after(b1, left))
     c0, d0 = right(2), right(3)
-    a3, b3 = forward(after(a2, c0)), forward(after(b2, d0))
+    a3, b3 = forward(after(a2, b1, c0)), forward(after(b2, d0))
     c1, d1 = forward(after(c0, b2)), forward(after(d0, a3))
 
     def triangle(slots):
@@ -596,7 +596,7 @@
     def dright(blocks, *others):
         return dright_part([blocks[0], blocks[1], blocks[2], after(blocks[3], *others)], left)
 
-    tri_a, tri_b = triangle([a0, a1, a2, a3]), triangle([b0, b1, b2, b3])
+    tri_a, tri_b = triangle([a0, a1, a2, after(a3, b2)]), triangle([b0, b1, b2, after(b3, c1)])
     x_a, x_b = over_x(tri_a[2]), over_x(tri_b[2])
     c2, d2 = forward(after(c1, tri_a[2])), forward(after(d1, tri_b[2]))
     dtri_a, gate_a, g_out, g_gate = middle(0, tri_a, after(x_a, d1))
@@ -604,7 +604,7 @@
     dtri_b, gate_b, g_out, g_gate = middle(1, tri_b, after(x_b, c2))
     blocks_b = spread(dtri_b)
     c3, d3 = forward(after(c2, dtri_a)), forward(after(d2, dtri_b))
-    part_a = dright(blocks_a, d2)
+    part_a = dright(blocks_a, d2, c3)
     part_b = dright(blocks_b, c3)
     r_a, r_b = forward(part_a[1]), forward(part_b[1])
 

time: 196 us -> 201 us (1.026)
  waiting for transfers between devices: 56 us -> 68.5 us
  starting transfers between devices: 62.4 us -> 55.7 us
    ppermute x24, waiting for transfers between devices: 37.6 us -> 44.8 us  [forward(): return lax.ppermute(a, 'row', [(0, 1), (1, 3), (3, 2), (2, 0)])]
    ppermute x24, starting transfers between devices: 46.1 us -> 41.8 us  [forward(): return lax.ppermute(a, 'row', [(0, 1), (1, 3), (3, 2), (2, 0)])]
    ppermute x2, waiting for transfers between devices: 6.09 us -> 9.55 us  [over_row(): return lax.ppermute(a, 'row', [(k, k ^ bit) for k in range(4)])]
    ppermute x2, starting transfers between devices: 4.17 us -> 1.77 us  [over_row(): return lax.ppermute(a, 'row', [(k, k ^ bit) for k in range(4)])]
  transfers between devices with their start and end apart: 49 -> 49, of which waited for: 23 -> 24; matrix products, arithmetic and copies ran while one was open for 2% -> 2% of each run, Pallas kernels for 32% -> 31%
where the time goes in v13:
time: 201 us
  waiting for transfers between devices  68.5 us (34%)
  Pallas kernels  66.1 us (33%)
  starting transfers between devices  55.7 us (28%)
  other arithmetic  5.8 us (3%)
  local copies, waits for them, and re-layouts  3.45 us (2%)
    ppermute x24, waiting for transfers between devices, forward(): return lax.ppermute(a, 'row', [(0, 1), (1, 3), (3, 2), (2, 0)])  44.8 us
    ppermute x24, starting transfers between devices, forward(): return lax.ppermute(a, 'row', [(0, 1), (1, 3), (3, 2), (2, 0)])  41.8 us
    pallas_call x4, Pallas kernels, mid_part(): pl.pallas_call(mid_kernel, grid=(1,), out_shape=(PANEL, pltpu.HBM(PANEL.s...  14.2 us
    pallas_call x4, Pallas kernels, dright_part(): pl.pallas_call(dright_kernel, grid=(HALF // GROUP,), out_shape=(pltpu.HBM...  11.5 us
    ppermute x9, waiting for transfers between devices, over_x(): return lax.ppermute(a, 'col', [(k, k ^ 2) for k in range(4)])  11.3 us
    ppermute x9, starting transfers between devices, over_x(): return lax.ppermute(a, 'col', [(k, k ^ 2) for k in range(4)])  10.5 us
    ppermute x2, waiting for transfers between devices, over_row(): return lax.ppermute(a, 'row', [(k, k ^ bit) for k in range(4)])  9.55 us
    pallas_call x4, Pallas kernels, final_b_part(): pl.pallas_call(functools.partial(final_b_kernel, s * steps), grid=(steps,...  8.56 us
  transfers between devices with their start and end apart: 49, of which 24 were waited for; matrix products, arithmetic and copies ran while one was open for 2% of the time, Pallas kernels for 31%

profile of v13, /device:TPU:0, one launch (start us, length us, event | category | flops | bytes accessed | tf_op | source)
XLA Modules:
  0.0 200.7 jit_solution(12983770982552553489)
XLA Ops:
  2.6 3.1 %collective-permute-start.3 = (bf16[64,16,128]{2,1,0:T(8,128)(2,1)S(1)}, bf16[64,16,128]{2,1,0:T(8,128)(2,1)S(1)}, u32[]{:S(2)}, u32[]{:S(2)}) collective-permute-start(bf16[64,16,128]{2,1,0:T(8,128)(2,1)S(1)} %right_part.6.s0), channel_id=1, source_target_pairs={{0,4},{4,12},{12,8},{8,0},{1,5},{5,13},{13,9},{9,1},{2,6},{6,14},{... | collective-permute-start | bytes 786440 | tf_op jit(solution)/shard_map/ppermute | solution.py:552
  7.6 2.6 %collective-permute-start = (bf16[64,16,128]{2,1,0:T(8,128)(2,1)S(1)}, bf16[64,16,128]{2,1,0:T(8,128)(2,1)S(1)}, u32[]{:S(2)}, u32[]{:S(2)}) collective-permute-start(bf16[64,16,128]{2,1,0:T(8,128)(2,1)S(1)} %right_part.5.s0), channel_id=1, source_target_pairs={{0,4},{4,12},{12,8},{8,0},{1,5},{5,13},{13,9},{9,1},{2,6},{6,14},{... | collective-permute-start | bytes 786440 | tf_op jit(solution)/shard_map/ppermute | solution.py:552
  10.2 3.6 %collective-permute-done.3.s1 = bf16[64,16,128]{2,1,0:T(8,128)(2,1)S(1)} collective-permute-done((bf16[64,16,128]{2,1,0:T(8,128)(2,1)S(1)}, bf16[64,16,128]{2,1,0:T(8,128)(2,1)S(1)}, u32[]{:S(2)}, u32[]{:S(2)}) %collective-permute-start.3) | collective-permute-done | bytes 262176 | tf_op jit(solution)/shard_map/ppermute | solution.py:552
  15.0 5.2 %left_part.1.left_ref.refs_4_ = bf16[64,2,64,128]{3,2,1,0:T(8,128)(2,1)S(1)} custom-call(bf16[64,64,128]{2,1,0:T(8,128)(2,1)} %x_ref.27, f32[1,128]{1,0:T(1,128)} %bitcast.25, bf16[128,512]{1,0:T(8,128)(2,1)} %w_ref.19, s32[1,256]{1,0:T(1,128)} %bitcast.40), custom_call_target="tpu_custom_call" | custom-call | flops 268435456 | bytes 3145728 | tf_op jit(solution)/shard_map/left_part/pallas_call | solution.py:410
  20.2 3.4 %collective-permute-start.1 = (bf16[64,16,128]{2,1,0:T(8,128)(2,1)S(1)}, bf16[64,16,128]{2,1,0:T(8,128)(2,1)S(1)}, u32[]{:S(2)}, u32[]{:S(2)}) collective-permute-start(bf16[64,16,128]{2,1,0:T(8,128)(2,1)S(1)} %collective-permute-done.s1), channel_id=1, source_target_pairs={{0,4},{4,12},{12,8},{8,0},{1,5},{5,13},{13,9},{9,1},{2,6},{6,14},{... | collective-permute-start | bytes 786440 | tf_op jit(solution)/shard_map/ppermute | solution.py:552
  28.1 2.5 %collective-permute-done.1.s2 = bf16[64,16,128]{2,1,0:T(8,128)(2,1)S(1)} collective-permute-done((bf16[64,16,128]{2,1,0:T(8,128)(2,1)S(1)}, bf16[64,16,128]{2,1,0:T(8,128)(2,1)S(1)}, u32[]{:S(2)}, u32[]{:S(2)}) %collective-permute-start.1) | collective-permute-done | bytes 262176 | tf_op jit(solution)/shard_map/ppermute | solution.py:552
  32.9 2.3 %collective-permute-start.14 = (bf16[64,16,128]{2,1,0:T(8,128)(2,1)S(1)}, bf16[64,16,128]{2,1,0:T(8,128)(2,1)S(1)}, u32[]{:S(2)}, u32[]{:S(2)}) collective-permute-start(bf16[64,16,128]{2,1,0:T(8,128)(2,1)S(1)} %collective-permute-done.1.s2), channel_id=1, source_target_pairs={{0,4},{4,12},{12,8},{8,0},{1,5},{5,13},{13,9},{9,1},{2,6},{6,14},{... | collective-permute-start | bytes 786440 | tf_op jit(solution)/shard_map/ppermute | solution.py:552
  38.4 3.5 %collective-permute-done.2.s1 = bf16[64,16,128]{2,1,0:T(8,128)(2,1)S(1)} collective-permute-done((bf16[64,16,128]{2,1,0:T(8,128)(2,1)S(1)}, bf16[64,16,128]{2,1,0:T(8,128)(2,1)S(1)}, u32[]{:S(2)}, u32[]{:S(2)}) %collective-permute-start.2) | collective-permute-done | bytes 262176 | tf_op jit(solution)/shard_map/ppermute | solution.py:552
  41.9 4.8 %collective-permute-done.14.s3 = bf16[64,16,128]{2,1,0:T(8,128)(2,1)S(1)} collective-permute-done((bf16[64,16,128]{2,1,0:T(8,128)(2,1)S(1)}, bf16[64,16,128]{2,1,0:T(8,128)(2,1)S(1)}, u32[]{:S(2)}, u32[]{:S(2)}) %collective-permute-start.14) | collective-permute-done | bytes 262176 | tf_op jit(solution)/shard_map/ppermute | solution.py:552
  52.4 3.0 %collective-permute-start.7 = (bf16[64,16,128]{2,1,0:T(8,128)(2,1)S(1)}, bf16[64,16,128]{2,1,0:T(8,128)(2,1)S(1)}, u32[]{:S(2)}, u32[]{:S(2)}) collective-permute-start(bf16[64,16,128]{2,1,0:T(8,128)(2,1)S(1)} %collective-permute-done.2.s1), channel_id=1, source_target_pairs={{0,4},{4,12},{12,8},{8,0},{1,5},{5,13},{13,9},{9,1},{2,6},{6,14},{... | collective-permute-start | bytes 786440 | tf_op jit(solution)/shard_map/ppermute | solution.py:552
  55.4 3.5 %collective-permute-done.9.s1 = bf16[64,16,128]{2,1,0:T(8,128)(2,1)S(1)} collective-permute-done((bf16[64,16,128]{2,1,0:T(8,128)(2,1)S(1)}, bf16[64,16,128]{2,1,0:T(8,128)(2,1)S(1)}, u32[]{:S(2)}, u32[]{:S(2)}) %collective-permute-start.9) | collective-permute-done | bytes 262176 | tf_op jit(solution)/shard_map/ppermute | solution.py:552
  59.0 3.5 %mid_part.4 = (bf16[64,16,128]{2,1,0:T(8,128)(2,1)S(1)}, bf16[64,16,128]{2,1,0:T(8,128)(2,1)}, f32[128,128]{1,0:T(8,128)S(1)}, f32[128,128]{1,0:T(8,128)S(1)}) custom-call(bf16[64,16,128]{2,1,0:T(8,128)(2,1)S(1)} %get-tuple-element.103.a_ref, bf16[2,64,16,128]{3,2,1,0:T(8,128)(2,1)S(1)} %collective-permute-done.6.b_ref, ...), custom_call_target="tpu_custom_call" | custom-call | flops 201326592 | bytes 2097152 | tf_op jit(solution)/shard_map/mid_part/pallas_call | solution.py:443
  64.0 3.5 %mid_part.5 = (bf16[64,16,128]{2,1,0:T(8,128)(2,1)S(1)}, bf16[64,16,128]{2,1,0:T(8,128)(2,1)}, f32[128,128]{1,0:T(8,128)S(1)}, f32[128,128]{1,0:T(8,128)S(1)}) custom-call(bf16[64,16,128]{2,1,0:T(8,128)(2,1)S(1)} %get-tuple-element.120.a_ref, bf16[2,64,16,128]{3,2,1,0:T(8,128)(2,1)S(1)} %collective-permute-done.15.b_ref, ...), custom_call_target="tpu_custom_call" | custom-call | flops 201326592 | bytes 2097152 | tf_op jit(solution)/shard_map/mid_part/pallas_call | solution.py:443
  69.1 3.2 %collective-permute-start.16 = (bf16[64,16,128]{2,1,0:T(8,128)(2,1)S(1)}, bf16[64,16,128]{2,1,0:T(8,128)(2,1)S(1)}, u32[]{:S(2)}, u32[]{:S(2)}) collective-permute-start(bf16[64,16,128]{2,1,0:T(8,128)(2,1)S(1)} %collective-permute-done.9.s1), channel_id=1, source_target_pairs={{0,4},{4,12},{12,8},{8,0},{1,5},{5,13},{13,9},{9,1},{2,6},{6,14},{... | collective-permute-start | bytes 786440 | tf_op jit(solution)/shard_map/ppermute | solution.py:552
  75.5 3.8 %collective-permute-done.16.s2 = bf16[64,16,128]{2,1,0:T(8,128)(2,1)S(1)} collective-permute-done((bf16[64,16,128]{2,1,0:T(8,128)(2,1)S(1)}, bf16[64,16,128]{2,1,0:T(8,128)(2,1)S(1)}, u32[]{:S(2)}, u32[]{:S(2)}) %collective-permute-start.16) | collective-permute-done | bytes 262176 | tf_op jit(solution)/shard_map/ppermute | solution.py:552
  79.2 4.0 %collective-permute-done.10.s3 = bf16[64,16,128]{2,1,0:T(8,128)(2,1)S(1)} collective-permute-done((bf16[64,16,128]{2,1,0:T(8,128)(2,1)S(1)}, bf16[64,16,128]{2,1,0:T(8,128)(2,1)S(1)}, u32[]{:S(2)}, u32[]{:S(2)}) %collective-permute-start.10) | collective-permute-done | bytes 262176 | tf_op jit(solution)/shard_map/ppermute | solution.py:552
  90.9 2.3 %collective-permute-start.19 = (bf16[64,16,128]{2,1,0:T(8,128)(2,1)S(1)}, bf16[64,16,128]{2,1,0:T(8,128)(2,1)S(1)}, u32[]{:S(2)}, u32[]{:S(2)}) collective-permute-start(bf16[64,16,128]{2,1,0:T(8,128)(2,1)S(1)} %get-tuple-element.114), channel_id=1, source_target_pairs={{0,4},{4,12},{12,8},{8,0},{1,5},{5,13},{13,9},{9,1},{2,6},{6,14},{... | collective-permute-start | bytes 786440 | tf_op jit(solution)/shard_map/ppermute | solution.py:552
  97.9 2.6 %collective-permute-done.19 = bf16[64,16,128]{2,1,0:T(8,128)(2,1)S(1)} collective-permute-done((bf16[64,16,128]{2,1,0:T(8,128)(2,1)S(1)}, bf16[64,16,128]{2,1,0:T(8,128)(2,1)S(1)}, u32[]{:S(2)}, u32[]{:S(2)}) %collective-permute-start.19) | collective-permute-done | bytes 262176 | tf_op jit(solution)/shard_map/ppermute | solution.py:552
  107.3 3.4 %collective-permute-done.18.c_ref = bf16[64,16,128]{2,1,0:T(8,128)(2,1)S(1)} collective-permute-done((bf16[64,16,128]{2,1,0:T(8,128)(2,1)S(1)}, bf16[64,16,128]{2,1,0:T(8,128)(2,1)S(1)}, u32[]{:S(2)}, u32[]{:S(2)}) %collective-permute-start.18) | collective-permute-done | bytes 262176 | tf_op jit(solution)/shard_map/ppermute | solution.py:558
  110.7 3.5 %mid_part.6 = (bf16[64,16,128]{2,1,0:T(8,128)(2,1)S(1)}, bf16[64,16,128]{2,1,0:T(8,128)(2,1)}, f32[128,128]{1,0:T(8,128)S(1)}, f32[128,128]{1,0:T(8,128)S(1)}) custom-call(bf16[64,16,128]{2,1,0:T(8,128)(2,1)S(1)} %get-tuple-element.116.a_ref, bf16[2,64,16,128]{3,2,1,0:T(8,128)(2,1)S(1)} %collective-permute-done.17.b_ref, ...), custom_call_target="tpu_custom_call" | custom-call | flops 201326592 | bytes 2097152 | tf_op jit(solution)/shard_map/mid_part/pallas_call | solution.py:443
  115.6 3.6 %mid_part.7 = (bf16[64,16,128]{2,1,0:T(8,128)(2,1)}, bf16[64,16,128]{2,1,0:T(8,128)(2,1)}, f32[128,128]{1,0:T(8,128)S(1)}, f32[128,128]{1,0:T(8,128)S(1)}) custom-call(bf16[64,16,128]{2,1,0:T(8,128)(2,1)S(1)} %get-tuple-element.138.a_ref, bf16[2,64,16,128]{3,2,1,0:T(8,128)(2,1)S(1)} %collective-permute-done.25.b_ref, ...), custom_call_target="tpu_custom_call" | custom-call | flops 201326592 | bytes 2097152 | tf_op jit(solution)/shard_map/mid_part/pallas_call | solution.py:443
  128.3 3.7 %dright_part.7 = (bf16[64,16,128]{2,1,0:T(8,128)(2,1)}, bf16[64,16,128]{2,1,0:T(8,128)(2,1)S(1)}, bf16[64,16,128]{2,1,0:T(8,128)(2,1)S(1)}, bf16[64,16,128]{2,1,0:T(8,128)(2,1)S(1)}) custom-call(bf16[64,16,128]{2,1,0:T(8,128)(2,1)S(1)} %get-tuple-element.148.refs_0_, bf16[64,16,128]{2,1,0:T(8,128)(2,1)} %collective-permute-done.32.refs_1_, ...), custom_call_target="tpu_custom_call" | custom-call | flops 268435456 | bytes 6291456 | tf_op jit(solution)/shard_map/dright_part/pallas_call | solution.py:459
  133.3 3.6 %dright_part.6 = (bf16[64,16,128]{2,1,0:T(8,128)(2,1)}, bf16[64,16,128]{2,1,0:T(8,128)(2,1)S(1)}, bf16[64,16,128]{2,1,0:T(8,128)(2,1)S(1)}, bf16[64,16,128]{2,1,0:T(8,128)(2,1)S(1)}) custom-call(bf16[64,16,128]{2,1,0:T(8,128)(2,1)} %get-tuple-element.143.refs_0_.refs_4_, bf16[64,16,128]{2,1,0:T(8,128)(2,1)} %collective-permute-done.28.refs_1_.refs_5_, ...), custom_call_target="tpu_custom_call" | custom-call | flops 268435456 | bytes 6291456 | tf_op jit(solution)/shard_map/dright_part/pallas_call | solution.py:459
  136.9 2.3 %collective-permute-start.37 = (bf16[64,16,128]{2,1,0:T(8,128)(2,1)S(1)}, bf16[64,16,128]{2,1,0:T(8,128)(2,1)S(1)}, u32[]{:S(2)}, u32[]{:S(2)}) collective-permute-start(bf16[64,16,128]{2,1,0:T(8,128)(2,1)S(1)} %get-tuple-element.147), channel_id=1, source_target_pairs={{0,4},{4,12},{12,8},{8,0},{1,5},{5,13},{13,9},{9,1},{2,6},{6,14},{... | collective-permute-start | bytes 786440 | tf_op jit(solution)/shard_map/ppermute | solution.py:552
  139.2 3.2 %dleft_part.3.dleft_ref = f32[64,64,128]{2,1,0:T(8,128)S(1)} custom-call(bf16[64,16,128]{2,1,0:T(8,128)(2,1)S(1)} %get-tuple-element.148.refs_0_, bf16[64,16,128]{2,1,0:T(8,128)(2,1)} %collective-permute-done.32.refs_1_, bf16[64,16,128]{2,1,0:T(8,128)(2,1)} %collective-permute-done.33.refs_2_, bf16[64,16,128]{2,1,0:T(8,128)(2,1)} %collective-permute-done.34.refs_3_, ...), custom_call_target="tpu_custom_call" | custom-call | flops 268435456 | bytes 8388608 | tf_op jit(solution)/shard_map/dleft_part/pallas_call | solution.py:474
  144.4 6.0 %final_a_part.1 = (f32[128,4096]{1,0:T(8,128)S(1)}, f32[128,256]{1,0:T(8,128)S(1)}) custom-call(bf16[64,64,128]{2,1,0:T(8,128)(2,1)S(1)} %copy-done, f32[64,64,128]{2,1,0:T(8,128)S(1)} %dleft_part.3.dleft_ref, s32[1,256]{1,0:T(1,128)S(1)} %bitcast.43, f32[1,128]{1,0:T(1,128)S(1)} %bitcast.32, bf16[128,512]{1,0:T(8,128)(2,1)S(1)} %copy-done.2, ...), custom_call_target="tpu_custom_call" | custom-call | flops 939524096 | bytes 8388608 | tf_op jit(solution)/shard_map/final_a_part/pallas_call | solution.py:487
  150.4 3.9 %collective-permute-done.37 = bf16[64,16,128]{2,1,0:T(8,128)(2,1)S(1)} collective-permute-done((bf16[64,16,128]{2,1,0:T(8,128)(2,1)S(1)}, bf16[64,16,128]{2,1,0:T(8,128)(2,1)S(1)}, u32[]{:S(2)}, u32[]{:S(2)}) %collective-permute-start.37) | collective-permute-done | bytes 262176 | tf_op jit(solution)/shard_map/ppermute | solution.py:552
  166.9 4.3 %collective-permute-done.43.b_ref = bf16[64,16,128]{2,1,0:T(8,128)(2,1)S(1)} collective-permute-done((bf16[64,16,128]{2,1,0:T(8,128)(2,1)S(1)}, bf16[64,16,128]{2,1,0:T(8,128)(2,1)S(1)}, u32[]{:S(2)}, u32[]{:S(2)}) %collective-permute-start.43) | collective-permute-done | bytes 262176 | tf_op jit(solution)/shard_map/ppermute | solution.py:552
  173.3 2.8 %collective-permute-done.42.b_ref = bf16[64,16,128]{2,1,0:T(8,128)(2,1)S(1)} collective-permute-done((bf16[64,16,128]{2,1,0:T(8,128)(2,1)S(1)}, bf16[64,16,128]{2,1,0:T(8,128)(2,1)S(1)}, u32[]{:S(2)}, u32[]{:S(2)}) %collective-permute-start.42) | collective-permute-done | bytes 262176 | tf_op jit(solution)/shard_map/ppermute | solution.py:552
  182.3 4.1 %collective-permute-done.45 = bf16[64,768]{1,0:T(8,128)(2,1)S(1)} collective-permute-done((bf16[64,768]{1,0:T(8,128)(2,1)S(1)}, bf16[64,768]{1,0:T(8,128)(2,1)S(1)}, u32[]{:S(2)}, u32[]{:S(2)}) %collective-permute-start.45) | collective-permute-done | bytes 98336 | tf_op jit(solution)/shard_map/ppermute | solution.py:558
  187.4 3.7 %collective-permute-done.46 = bf16[64,768]{1,0:T(8,128)(2,1)S(1)} collective-permute-done((bf16[64,768]{1,0:T(8,128)(2,1)S(1)}, bf16[64,768]{1,0:T(8,128)(2,1)S(1)}, u32[]{:S(2)}, u32[]{:S(2)}) %collective-permute-start.46) | collective-permute-done | bytes 98336 | tf_op jit(solution)/shard_map/ppermute | solution.py:555
  192.0 5.8 %collective-permute-done.47 = bf16[64,768]{1,0:T(8,128)(2,1)S(1)} collective-permute-done((bf16[64,768]{1,0:T(8,128)(2,1)S(1)}, bf16[64,768]{1,0:T(8,128)(2,1)S(1)}, u32[]{:S(2)}, u32[]{:S(2)}) %collective-permute-start.47) | collective-permute-done | bytes 98336 | tf_op jit(solution)/shard_map/ppermute | solution.py:555
  (175 shorter events, 85.3 us)
Async XLA Ops:
  2.6 11.2 %collective-permute-start.3 = (bf16[64,16,128]{2,1,0:T(8,128)(2,1)S(1)}, bf16[64,16,128]{2,1,0:T(8,128)(2,1)S(1)}, u32[]{:S(2)}, u32[]{:S(2)}) collective-permute-start(bf16[64,16,128]{2,1,0:T(8,128)(2,1)S(1)} %right_part.6.s0), channel_id=1, source_target_pairs={{0,4},{4,12},{12,8},{8,0},{1,5},{5,13},{13,9},{9,1},{2,6},{6,14},{... | collective-permute-start | bytes 786440 | tf_op jit(solution)/shard_map/ppermute | solution.py:552
  7.6 12.6 %collective-permute-start = (bf16[64,16,128]{2,1,0:T(8,128)(2,1)S(1)}, bf16[64,16,128]{2,1,0:T(8,128)(2,1)S(1)}, u32[]{:S(2)}, u32[]{:S(2)}) collective-permute-start(bf16[64,16,128]{2,1,0:T(8,128)(2,1)S(1)} %right_part.5.s0), channel_id=1, source_target_pairs={{0,4},{4,12},{12,8},{8,0},{1,5},{5,13},{13,9},{9,1},{2,6},{6,14},{... | collective-permute-start | bytes 786440 | tf_op jit(solution)/shard_map/ppermute | solution.py:552
  13.8 11.8 %collective-permute-start.4 = (bf16[64,16,128]{2,1,0:T(8,128)(2,1)S(1)}, bf16[64,16,128]{2,1,0:T(8,128)(2,1)S(1)}, u32[]{:S(2)}, u32[]{:S(2)}) collective-permute-start(bf16[64,16,128]{2,1,0:T(8,128)(2,1)S(1)} %collective-permute-done.3.s1), channel_id=1, source_target_pairs={{0,4},{4,12},{12,8},{8,0},{1,5},{5,13},{13,9},{9,1},{2,6},{6,14},{... | collective-permute-start | bytes 786440 | tf_op jit(solution)/shard_map/ppermute | solution.py:552
  20.2 10.5 %collective-permute-start.1 = (bf16[64,16,128]{2,1,0:T(8,128)(2,1)S(1)}, bf16[64,16,128]{2,1,0:T(8,128)(2,1)S(1)}, u32[]{:S(2)}, u32[]{:S(2)}) collective-permute-start(bf16[64,16,128]{2,1,0:T(8,128)(2,1)S(1)} %collective-permute-done.s1), channel_id=1, source_target_pairs={{0,4},{4,12},{12,8},{8,0},{1,5},{5,13},{13,9},{9,1},{2,6},{6,14},{... | collective-permute-start | bytes 786440 | tf_op jit(solution)/shard_map/ppermute | solution.py:552
  25.6 10.7 %collective-permute-start.5 = (bf16[64,16,128]{2,1,0:T(8,128)(2,1)S(1)}, bf16[64,16,128]{2,1,0:T(8,128)(2,1)S(1)}, u32[]{:S(2)}, u32[]{:S(2)}) collective-permute-start(bf16[64,16,128]{2,1,0:T(8,128)(2,1)S(1)} %collective-permute-done.4.s2), channel_id=1, source_target_pairs={{0,4},{4,12},{12,8},{8,0},{1,5},{5,13},{13,9},{9,1},{2,6},{6,14},{... | collective-permute-start | bytes 786440 | tf_op jit(solution)/shard_map/ppermute | solution.py:552
  30.7 11.2 %collective-permute-start.2 = (bf16[64,16,128]{2,1,0:T(8,128)(2,1)S(1)}, bf16[64,16,128]{2,1,0:T(8,128)(2,1)S(1)}, u32[]{:S(2)}, u32[]{:S(2)}) collective-permute-start(bf16[64,16,128]{2,1,0:T(8,128)(2,1)S(1)} %right_part.4.s0), channel_id=1, source_target_pairs={{0,4},{4,12},{12,8},{8,0},{1,5},{5,13},{13,9},{9,1},{2,6},{6,14},{... | collective-permute-start | bytes 786440 | tf_op jit(solution)/shard_map/ppermute | solution.py:552
  32.9 13.8 %collective-permute-start.14 = (bf16[64,16,128]{2,1,0:T(8,128)(2,1)S(1)}, bf16[64,16,128]{2,1,0:T(8,128)(2,1)S(1)}, u32[]{:S(2)}, u32[]{:S(2)}) collective-permute-start(bf16[64,16,128]{2,1,0:T(8,128)(2,1)S(1)} %collective-permute-done.1.s2), channel_id=1, source_target_pairs={{0,4},{4,12},{12,8},{8,0},{1,5},{5,13},{13,9},{9,1},{2,6},{6,14},{... | collective-permute-start | bytes 786440 | tf_op jit(solution)/shard_map/ppermute | solution.py:552
  38.4 11.3 %collective-permute-start.6 = (bf16[2,64,16,128]{3,2,1,0:T(8,128)(2,1)S(1)}, bf16[2,64,16,128]{3,2,1,0:T(8,128)(2,1)S(1)}, u32[]{:S(2)}, u32[]{:S(2)}) collective-permute-start(bf16[2,64,16,128]{3,2,1,0:T(8,128)(2,1)S(1)} %get-tuple-element.101), channel_id=1, source_target_pairs={{0,1},{1,0},{2,3},{3,2},{4,5},{5,4},{6,7},{7,6},{8,9},{9,8},{10,11... | collective-permute-start | bytes 1572872 | tf_op jit(solution)/shard_map/ppermute | solution.py:561
  48.8 10.1 %collective-permute-start.9 = (bf16[64,16,128]{2,1,0:T(8,128)(2,1)S(1)}, bf16[64,16,128]{2,1,0:T(8,128)(2,1)S(1)}, u32[]{:S(2)}, u32[]{:S(2)}) collective-permute-start(bf16[64,16,128]{2,1,0:T(8,128)(2,1)S(1)} %right_part.7.s0), channel_id=1, source_target_pairs={{0,4},{4,12},{12,8},{8,0},{1,5},{5,13},{13,9},{9,1},{2,6},{6,14},{... | collective-permute-start | bytes 786440 | tf_op jit(solution)/shard_map/ppermute | solution.py:552
  51.4 12.7 %collective-permute-start.20 = (bf16[64,16,128]{2,1,0:T(8,128)(2,1)S(1)}, bf16[64,16,128]{2,1,0:T(8,128)(2,1)S(1)}, u32[]{:S(2)}, u32[]{:S(2)}) collective-permute-start(bf16[64,16,128]{2,1,0:T(8,128)(2,1)S(1)} %fusion.2), channel_id=1, source_target_pairs={{0,2},{1,3},{2,0},{3,1},{4,6},{5,7},{6,4},{7,5},{8,10},{9,11},{10,... | collective-permute-start | bytes 786440 | tf_op jit(solution)/shard_map/ppermute | solution.py:558
  52.4 11.7 %collective-permute-start.7 = (bf16[64,16,128]{2,1,0:T(8,128)(2,1)S(1)}, bf16[64,16,128]{2,1,0:T(8,128)(2,1)S(1)}, u32[]{:S(2)}, u32[]{:S(2)}) collective-permute-start(bf16[64,16,128]{2,1,0:T(8,128)(2,1)S(1)} %collective-permute-done.2.s1), channel_id=1, source_target_pairs={{0,4},{4,12},{12,8},{8,0},{1,5},{5,13},{13,9},{9,1},{2,6},{6,14},{... | collective-permute-start | bytes 786440 | tf_op jit(solution)/shard_map/ppermute | solution.py:552
  62.5 10.7 %collective-permute-start.11 = (bf16[64,16,128]{2,1,0:T(8,128)(2,1)S(1)}, bf16[64,16,128]{2,1,0:T(8,128)(2,1)S(1)}, u32[]{:S(2)}, u32[]{:S(2)}) collective-permute-start(bf16[64,16,128]{2,1,0:T(8,128)(2,1)S(1)} %get-tuple-element.131.refs_0_), channel_id=1, source_target_pairs={{0,2},{1,3},{2,0},{3,1},{4,6},{5,7},{6,4},{7,5},{8,10},{9,11},{10,... | collective-permute-start | bytes 786440 | tf_op jit(solution)/shard_map/ppermute | solution.py:558
  69.1 10.1 %collective-permute-start.16 = (bf16[64,16,128]{2,1,0:T(8,128)(2,1)S(1)}, bf16[64,16,128]{2,1,0:T(8,128)(2,1)S(1)}, u32[]{:S(2)}, u32[]{:S(2)}) collective-permute-start(bf16[64,16,128]{2,1,0:T(8,128)(2,1)S(1)} %collective-permute-done.9.s1), channel_id=1, source_target_pairs={{0,4},{4,12},{12,8},{8,0},{1,5},{5,13},{13,9},{9,1},{2,6},{6,14},{... | collective-permute-start | bytes 786440 | tf_op jit(solution)/shard_map/ppermute | solution.py:552
  72.3 10.9 %collective-permute-start.10 = (bf16[64,16,128]{2,1,0:T(8,128)(2,1)S(1)}, bf16[64,16,128]{2,1,0:T(8,128)(2,1)S(1)}, u32[]{:S(2)}, u32[]{:S(2)}) collective-permute-start(bf16[64,16,128]{2,1,0:T(8,128)(2,1)S(1)} %collective-permute-done.7.s2), channel_id=1, source_target_pairs={{0,4},{4,12},{12,8},{8,0},{1,5},{5,13},{13,9},{9,1},{2,6},{6,14},{... | collective-permute-start | bytes 786440 | tf_op jit(solution)/shard_map/ppermute | solution.py:552
  73.3 11.9 %collective-permute-start.13 = (bf16[64,16,128]{2,1,0:T(8,128)(2,1)S(1)}, bf16[64,16,128]{2,1,0:T(8,128)(2,1)S(1)}, u32[]{:S(2)}, u32[]{:S(2)}) collective-permute-start(bf16[64,16,128]{2,1,0:T(8,128)(2,1)S(1)} %collective-permute-done.11.refs_1_), channel_id=1, source_target_pairs={{0,1},{1,0},{2,3},{3,2},{4,5},{5,4},{6,7},{7,6},{8,9},{9,8},{10,11... | collective-permute-start | bytes 786440 | tf_op jit(solution)/shard_map/ppermute | solution.py:561
  73.3 11.9 %collective-permute-start.12 = (bf16[64,16,128]{2,1,0:T(8,128)(2,1)S(1)}, bf16[64,16,128]{2,1,0:T(8,128)(2,1)S(1)}, u32[]{:S(2)}, u32[]{:S(2)}) collective-permute-start(bf16[64,16,128]{2,1,0:T(8,128)(2,1)S(1)} %get-tuple-element.131.refs_0_), channel_id=1, source_target_pairs={{0,1},{1,0},{2,3},{3,2},{4,5},{5,4},{6,7},{7,6},{8,9},{9,8},{10,11... | collective-permute-start | bytes 786440 | tf_op jit(solution)/shard_map/ppermute | solution.py:561
  75.5 17.7 %collective-permute-start.24 = (bf16[64,16,128]{2,1,0:T(8,128)(2,1)S(1)}, bf16[64,16,128]{2,1,0:T(8,128)(2,1)S(1)}, u32[]{:S(2)}, u32[]{:S(2)}) collective-permute-start(bf16[64,16,128]{2,1,0:T(8,128)(2,1)S(1)} %collective-permute-done.22.refs_1_.refs_5_), channel_id=1, source_target_pairs={{0,1},{1,0},{2,3},{3,2},{4,5},{5,4},{6,7},{7,6},{8,9},{9,8},{10,11... | collective-permute-start | bytes 786440 | tf_op jit(solution)/shard_map/ppermute | solution.py:561
  79.2 13.9 %collective-permute-start.23 = (bf16[64,16,128]{2,1,0:T(8,128)(2,1)S(1)}, bf16[64,16,128]{2,1,0:T(8,128)(2,1)S(1)}, u32[]{:S(2)}, u32[]{:S(2)}) collective-permute-start(bf16[64,16,128]{2,1,0:T(8,128)(2,1)S(1)} %get-tuple-element.124.refs_0_.refs_4_), channel_id=1, source_target_pairs={{0,1},{1,0},{2,3},{3,2},{4,5},{5,4},{6,7},{7,6},{8,9},{9,8},{10,11... | collective-permute-start | bytes 786440 | tf_op jit(solution)/shard_map/ppermute | solution.py:561
  83.2 12.1 %collective-permute-start.21 = (bf16[64,16,128]{2,1,0:T(8,128)(2,1)S(1)}, bf16[64,16,128]{2,1,0:T(8,128)(2,1)S(1)}, u32[]{:S(2)}, u32[]{:S(2)}) collective-permute-start(bf16[64,16,128]{2,1,0:T(8,128)(2,1)S(1)} %collective-permute-done.16.s2), channel_id=1, source_target_pairs={{0,4},{4,12},{12,8},{8,0},{1,5},{5,13},{13,9},{9,1},{2,6},{6,14},{... | collective-permute-start | bytes 786440 | tf_op jit(solution)/shard_map/ppermute | solution.py:552
  90.9 10.4 %collective-permute-start.17 = (bf16[2,64,16,128]{3,2,1,0:T(8,128)(2,1)S(1)}, bf16[2,64,16,128]{3,2,1,0:T(8,128)(2,1)S(1)}, u32[]{:S(2)}, u32[]{:S(2)}) collective-permute-start(bf16[2,64,16,128]{3,2,1,0:T(8,128)(2,1)S(1)} %get-tuple-element.117), channel_id=1, source_target_pairs={{0,1},{1,0},{2,3},{3,2},{4,5},{5,4},{6,7},{7,6},{8,9},{9,8},{10,11... | collective-permute-start | bytes 1572872 | tf_op jit(solution)/shard_map/ppermute | solution.py:561
  97.6 17.2 %collective-permute-start.27 = (bf16[64,16,128]{2,1,0:T(8,128)(2,1)S(1)}, bf16[64,16,128]{2,1,0:T(8,128)(2,1)S(1)}, u32[]{:S(2)}, u32[]{:S(2)}) collective-permute-start(bf16[64,16,128]{2,1,0:T(8,128)(2,1)S(1)} %get-tuple-element.127), channel_id=1, source_target_pairs={{0,4},{4,12},{12,8},{8,0},{1,5},{5,13},{13,9},{9,1},{2,6},{6,14},{... | collective-permute-start | bytes 786440 | tf_op jit(solution)/shard_map/ppermute | solution.py:552
  102.1 13.5 %collective-permute-start.26 = (bf16[64,16,128]{2,1,0:T(8,128)(2,1)S(1)}, bf16[64,16,128]{2,1,0:T(8,128)(2,1)S(1)}, u32[]{:S(2)}, u32[]{:S(2)}) collective-permute-start(bf16[64,16,128]{2,1,0:T(8,128)(2,1)S(1)} %fusion), channel_id=1, source_target_pairs={{0,2},{1,3},{2,0},{3,1},{4,6},{5,7},{6,4},{7,5},{8,10},{9,11},{10,... | collective-permute-start | bytes 786440 | tf_op jit(solution)/shard_map/ppermute | solution.py:558
  103.7 20.0 %collective-permute-start.35 = (bf16[64,16,128]{2,1,0:T(8,128)(2,1)}, bf16[64,16,128]{2,1,0:T(8,128)(2,1)}, u32[]{:S(2)}, u32[]{:S(2)}) collective-permute-start(bf16[64,16,128]{2,1,0:T(8,128)(2,1)} %add_convert_fusion.7), channel_id=1, source_target_pairs={{0,4},{4,12},{12,8},{8,0},{1,5},{5,13},{13,9},{9,1},{2,6},{6,14},{... | collective-permute-start | bytes 786440 | tf_op jit(solution)/shard_map/ppermute | solution.py:552
  121.8 11.3 %collective-permute-start.31 = (bf16[64,16,128]{2,1,0:T(8,128)(2,1)}, bf16[64,16,128]{2,1,0:T(8,128)(2,1)S(1)}, u32[]{:S(2)}, u32[]{:S(2)}) collective-permute-start(bf16[64,16,128]{2,1,0:T(8,128)(2,1)} %add_convert_fusion.6), channel_id=1, source_target_pairs={{0,4},{4,12},{12,8},{8,0},{1,5},{5,13},{13,9},{9,1},{2,6},{6,14},{... | collective-permute-start | bytes 786440 | tf_op jit(solution)/shard_map/ppermute | solution.py:552
  126.7 29.0 %collective-permute-start.41 = (bf16[64,16,128]{2,1,0:T(8,128)(2,1)S(1)}, bf16[64,16,128]{2,1,0:T(8,128)(2,1)S(1)}, u32[]{:S(2)}, u32[]{:S(2)}) collective-permute-start(bf16[64,16,128]{2,1,0:T(8,128)(2,1)S(1)} %add_convert_fusion.4), channel_id=1, source_target_pairs={{0,4},{4,12},{12,8},{8,0},{1,5},{5,13},{13,9},{9,1},{2,6},{6,14},{... | collective-permute-start | bytes 786440 | tf_op jit(solution)/shard_map/ppermute | solution.py:552
  132.1 11.0 %collective-permute-start.36 = (bf16[64,16,128]{2,1,0:T(8,128)(2,1)S(1)}, bf16[64,16,128]{2,1,0:T(8,128)(2,1)S(1)}, u32[]{:S(2)}, u32[]{:S(2)}) collective-permute-start(bf16[64,16,128]{2,1,0:T(8,128)(2,1)S(1)} %get-tuple-element.154), channel_id=1, source_target_pairs={{0,4},{4,12},{12,8},{8,0},{1,5},{5,13},{13,9},{9,1},{2,6},{6,14},{... | collective-permute-start | bytes 786440 | tf_op jit(solution)/shard_map/ppermute | solution.py:552
  133.2 28.3 %collective-permute-start.39 = (bf16[64,16,128]{2,1,0:T(8,128)(2,1)S(1)}, bf16[64,16,128]{2,1,0:T(8,128)(2,1)S(1)}, u32[]{:S(2)}, u32[]{:S(2)}) collective-permute-start(bf16[64,16,128]{2,1,0:T(8,128)(2,1)S(1)} %add_convert_fusion.5), channel_id=1, source_target_pairs={{0,4},{4,12},{12,8},{8,0},{1,5},{5,13},{13,9},{9,1},{2,6},{6,14},{... | collective-permute-start | bytes 786440 | tf_op jit(solution)/shard_map/ppermute | solution.py:552
  136.9 17.4 %collective-permute-start.37 = (bf16[64,16,128]{2,1,0:T(8,128)(2,1)S(1)}, bf16[64,16,128]{2,1,0:T(8,128)(2,1)S(1)}, u32[]{:S(2)}, u32[]{:S(2)}) collective-permute-start(bf16[64,16,128]{2,1,0:T(8,128)(2,1)S(1)} %get-tuple-element.147), channel_id=1, source_target_pairs={{0,4},{4,12},{12,8},{8,0},{1,5},{5,13},{13,9},{9,1},{2,6},{6,14},{... | collective-permute-start | bytes 786440 | tf_op jit(solution)/shard_map/ppermute | solution.py:552
  143.1 16.8 %collective-permute-start.40 = (bf16[64,16,128]{2,1,0:T(8,128)(2,1)S(1)}, bf16[64,16,128]{2,1,0:T(8,128)(2,1)S(1)}, u32[]{:S(2)}, u32[]{:S(2)}) collective-permute-start(bf16[64,16,128]{2,1,0:T(8,128)(2,1)S(1)} %add_convert_fusion.3), channel_id=1, source_target_pairs={{0,4},{4,12},{12,8},{8,0},{1,5},{5,13},{13,9},{9,1},{2,6},{6,14},{... | collective-permute-start | bytes 786440 | tf_op jit(solution)/shard_map/ppermute | solution.py:552
  154.4 11.2 %collective-permute-start.38 = (bf16[64,16,128]{2,1,0:T(8,128)(2,1)S(1)}, bf16[64,16,128]{2,1,0:T(8,128)(2,1)S(1)}, u32[]{:S(2)}, u32[]{:S(2)}) collective-permute-start(bf16[64,16,128]{2,1,0:T(8,128)(2,1)S(1)} %add_convert_fusion.2), channel_id=1, source_target_pairs={{0,4},{4,12},{12,8},{8,0},{1,5},{5,13},{13,9},{9,1},{2,6},{6,14},{... | collective-permute-start | bytes 786440 | tf_op jit(solution)/shard_map/ppermute | solution.py:552
  160.0 11.2 %collective-permute-start.43 = (bf16[64,16,128]{2,1,0:T(8,128)(2,1)S(1)}, bf16[64,16,128]{2,1,0:T(8,128)(2,1)S(1)}, u32[]{:S(2)}, u32[]{:S(2)}) collective-permute-start(bf16[64,16,128]{2,1,0:T(8,128)(2,1)S(1)} %add_convert_fusion.1), channel_id=1, source_target_pairs={{0,4},{4,12},{12,8},{8,0},{1,5},{5,13},{13,9},{9,1},{2,6},{6,14},{... | collective-permute-start | bytes 786440 | tf_op jit(solution)/shard_map/ppermute | solution.py:552
  165.6 10.5 %collective-permute-start.42 = (bf16[64,16,128]{2,1,0:T(8,128)(2,1)S(1)}, bf16[64,16,128]{2,1,0:T(8,128)(2,1)S(1)}, u32[]{:S(2)}, u32[]{:S(2)}) collective-permute-start(bf16[64,16,128]{2,1,0:T(8,128)(2,1)S(1)} %add_convert_fusion), channel_id=1, source_target_pairs={{0,4},{4,12},{12,8},{8,0},{1,5},{5,13},{13,9},{9,1},{2,6},{6,14},{... | collective-permute-start | bytes 786440 | tf_op jit(solution)/shard_map/ppermute | solution.py:552
  (46 other events, 377.1 us)

commit v14 on v11

--- a/solution.py
+++ b/solution.py
@@ -622,13 +622,13 @@
     )
     dtri_c, gate_c, g_out, g_gate = middle(2, tri_c, after(x_c, r_a, d_left))
     blocks_c = spread(dtri_c)
-    dtri_d, gate_d, g_out, g_gate = middle(3, tri_d, after(x_d, r_b))
+    r_a2 = plus(r_a2, part_a[3])
+    dtri_d, gate_d, g_out, g_gate = middle(3, tri_d, after(x_d, r_b, r_a2))
     blocks_d = spread(dtri_d)
-    r_a2 = plus(r_a2, part_a[3])
     r_a3 = forward(after(r_a2, dtri_c))
     r_b2 = plus(r_b2, part_b[3])
     r_b3 = forward(after(r_b2, dtri_d))
-    part_c = dright(blocks_c, r_a2)
+    part_c = dright(blocks_c, r_a3)
     part_d = dright(blocks_d, r_b2)
 
     zero = jnp.zeros((width, 2 * width), F32)

time: 196 us -> 199 us (1.015)
  waiting for transfers between devices: 56 us -> 60.4 us
    ppermute x24, waiting for transfers between devices: 37.6 us -> 39.7 us  [forward(): return lax.ppermute(a, 'row', [(0, 1), (1, 3), (3, 2), (2, 0)])]
  transfers between devices with their start and end apart: 49 -> 49, of which waited for: 23 -> 21; matrix products, arithmetic and copies ran while one was open for 2% -> 2% of each run, Pallas kernels for 32% -> 32%
where the time goes in v14:
time: 199 us; the launch traced here: 198 us
  Pallas kernels  67 us (34%)
  starting transfers between devices  60.9 us (31%)
  waiting for transfers between devices  60.4 us (30%)
  other arithmetic  5.69 us (3%)
  local copies, waits for them, and re-layouts  2.74 us (1%)
    ppermute x24, starting transfers between devices, forward(): return lax.ppermute(a, 'row', [(0, 1), (1, 3), (3, 2), (2, 0)])  44.6 us
    ppermute x24, waiting for transfers between devices, forward(): return lax.ppermute(a, 'row', [(0, 1), (1, 3), (3, 2), (2, 0)])  39.7 us
    pallas_call x4, Pallas kernels, mid_part(): pl.pallas_call(mid_kernel, grid=(1,), out_shape=(PANEL, pltpu.HBM(PANEL.s...  14.3 us
    pallas_call x4, Pallas kernels, dright_part(): pl.pallas_call(dright_kernel, grid=(HALF // GROUP,), out_shape=(pltpu.HBM...  11.4 us
    ppermute x9, waiting for transfers between devices, over_x(): return lax.ppermute(a, 'col', [(k, k ^ 2) for k in range(4)])  11 us
    ppermute x9, starting transfers between devices, over_x(): return lax.ppermute(a, 'col', [(k, k ^ 2) for k in range(4)])  10.9 us
    pallas_call x4, Pallas kernels, final_b_part(): pl.pallas_call(functools.partial(final_b_kernel, s * steps), grid=(steps,...  9.55 us
    pallas_call x4, Pallas kernels, tri_part(): pl.pallas_call(tri_kernel, grid=(HALF // GROUP,), out_shape=(PANEL, PANEL...  8.01 us
  transfers between devices with their start and end apart: 49, of which 21 were waited for; matrix products, arithmetic and copies ran while one was open for 2% of the time, Pallas kernels for 32%

profile of v14, /device:TPU:0, one launch (start us, length us, event | category | flops | bytes accessed | tf_op | source)
XLA Modules:
  0.0 198.0 jit_solution(6157107670756354633)
XLA Ops:
  2.6 3.1 %collective-permute-start.3 = (bf16[64,16,128]{2,1,0:T(8,128)(2,1)S(1)}, bf16[64,16,128]{2,1,0:T(8,128)(2,1)S(1)}, u32[]{:S(2)}, u32[]{:S(2)}) collective-permute-start(bf16[64,16,128]{2,1,0:T(8,128)(2,1)S(1)} %right_part.6.s0), channel_id=1, source_target_pairs={{0,4},{4,12},{12,8},{8,0},{1,5},{5,13},{13,9},{9,1},{2,6},{6,14},{... | collective-permute-start | bytes 786440 | tf_op jit(solution)/shard_map/ppermute | solution.py:552
  7.6 2.6 %collective-permute-start = (bf16[64,16,128]{2,1,0:T(8,128)(2,1)S(1)}, bf16[64,16,128]{2,1,0:T(8,128)(2,1)S(1)}, u32[]{:S(2)}, u32[]{:S(2)}) collective-permute-start(bf16[64,16,128]{2,1,0:T(8,128)(2,1)S(1)} %right_part.5.s0), channel_id=1, source_target_pairs={{0,4},{4,12},{12,8},{8,0},{1,5},{5,13},{13,9},{9,1},{2,6},{6,14},{... | collective-permute-start | bytes 786440 | tf_op jit(solution)/shard_map/ppermute | solution.py:552
  10.2 3.6 %collective-permute-done.3.s1 = bf16[64,16,128]{2,1,0:T(8,128)(2,1)S(1)} collective-permute-done((bf16[64,16,128]{2,1,0:T(8,128)(2,1)S(1)}, bf16[64,16,128]{2,1,0:T(8,128)(2,1)S(1)}, u32[]{:S(2)}, u32[]{:S(2)}) %collective-permute-start.3) | collective-permute-done | bytes 262176 | tf_op jit(solution)/shard_map/ppermute | solution.py:552
  15.0 5.2 %left_part.1.left_ref.refs_4_ = bf16[64,2,64,128]{3,2,1,0:T(8,128)(2,1)S(1)} custom-call(bf16[64,64,128]{2,1,0:T(8,128)(2,1)} %x_ref.27, f32[1,128]{1,0:T(1,128)} %bitcast.25, bf16[128,512]{1,0:T(8,128)(2,1)} %w_ref.19, s32[1,256]{1,0:T(1,128)} %bitcast.40), custom_call_target="tpu_custom_call" | custom-call | flops 268435456 | bytes 3145728 | tf_op jit(solution)/shard_map/left_part/pallas_call | solution.py:410
  20.2 3.4 %collective-permute-start.1 = (bf16[64,16,128]{2,1,0:T(8,128)(2,1)S(1)}, bf16[64,16,128]{2,1,0:T(8,128)(2,1)S(1)}, u32[]{:S(2)}, u32[]{:S(2)}) collective-permute-start(bf16[64,16,128]{2,1,0:T(8,128)(2,1)S(1)} %collective-permute-done.s1), channel_id=1, source_target_pairs={{0,4},{4,12},{12,8},{8,0},{1,5},{5,13},{13,9},{9,1},{2,6},{6,14},{... | collective-permute-start | bytes 786440 | tf_op jit(solution)/shard_map/ppermute | solution.py:552
  32.9 3.4 %collective-permute-done.5.s3 = bf16[64,16,128]{2,1,0:T(8,128)(2,1)S(1)} collective-permute-done((bf16[64,16,128]{2,1,0:T(8,128)(2,1)S(1)}, bf16[64,16,128]{2,1,0:T(8,128)(2,1)S(1)}, u32[]{:S(2)}, u32[]{:S(2)}) %collective-permute-start.5) | collective-permute-done | bytes 262176 | tf_op jit(solution)/shard_map/ppermute | solution.py:552
  38.4 2.6 %collective-permute-done.14.s3 = bf16[64,16,128]{2,1,0:T(8,128)(2,1)S(1)} collective-permute-done((bf16[64,16,128]{2,1,0:T(8,128)(2,1)S(1)}, bf16[64,16,128]{2,1,0:T(8,128)(2,1)S(1)}, u32[]{:S(2)}, u32[]{:S(2)}) %collective-permute-start.14) | collective-permute-done | bytes 262176 | tf_op jit(solution)/shard_map/ppermute | solution.py:552
  44.0 3.4 %collective-permute-start.9 = (bf16[64,16,128]{2,1,0:T(8,128)(2,1)S(1)}, bf16[64,16,128]{2,1,0:T(8,128)(2,1)S(1)}, u32[]{:S(2)}, u32[]{:S(2)}) collective-permute-start(bf16[64,16,128]{2,1,0:T(8,128)(2,1)S(1)} %right_part.7.s0), channel_id=1, source_target_pairs={{0,4},{4,12},{12,8},{8,0},{1,5},{5,13},{13,9},{9,1},{2,6},{6,14},{... | collective-permute-start | bytes 786440 | tf_op jit(solution)/shard_map/ppermute | solution.py:552
  49.7 3.5 %collective-permute-done.2.s1 = bf16[64,16,128]{2,1,0:T(8,128)(2,1)S(1)} collective-permute-done((bf16[64,16,128]{2,1,0:T(8,128)(2,1)S(1)}, bf16[64,16,128]{2,1,0:T(8,128)(2,1)S(1)}, u32[]{:S(2)}, u32[]{:S(2)}) %collective-permute-start.2) | collective-permute-done | bytes 262176 | tf_op jit(solution)/shard_map/ppermute | solution.py:552
  54.0 4.8 %collective-permute-done.9.s1 = bf16[64,16,128]{2,1,0:T(8,128)(2,1)S(1)} collective-permute-done((bf16[64,16,128]{2,1,0:T(8,128)(2,1)S(1)}, bf16[64,16,128]{2,1,0:T(8,128)(2,1)S(1)}, u32[]{:S(2)}, u32[]{:S(2)}) %collective-permute-start.9) | collective-permute-done | bytes 262176 | tf_op jit(solution)/shard_map/ppermute | solution.py:552
  58.9 3.5 %mid_part.4 = (bf16[64,16,128]{2,1,0:T(8,128)(2,1)S(1)}, bf16[64,16,128]{2,1,0:T(8,128)(2,1)}, f32[128,128]{1,0:T(8,128)S(1)}, f32[128,128]{1,0:T(8,128)S(1)}) custom-call(bf16[64,16,128]{2,1,0:T(8,128)(2,1)S(1)} %get-tuple-element.100.a_ref, bf16[2,64,16,128]{3,2,1,0:T(8,128)(2,1)S(1)} %collective-permute-done.6.b_ref, ...), custom_call_target="tpu_custom_call" | custom-call | flops 201326592 | bytes 2097152 | tf_op jit(solution)/shard_map/mid_part/pallas_call | solution.py:443
  64.0 3.5 %mid_part.5 = (bf16[64,16,128]{2,1,0:T(8,128)(2,1)S(1)}, bf16[64,16,128]{2,1,0:T(8,128)(2,1)}, f32[128,128]{1,0:T(8,128)S(1)}, f32[128,128]{1,0:T(8,128)S(1)}) custom-call(bf16[64,16,128]{2,1,0:T(8,128)(2,1)S(1)} %get-tuple-element.116.a_ref, bf16[2,64,16,128]{3,2,1,0:T(8,128)(2,1)S(1)} %collective-permute-done.15.b_ref, ...), custom_call_target="tpu_custom_call" | custom-call | flops 201326592 | bytes 2097152 | tf_op jit(solution)/shard_map/mid_part/pallas_call | solution.py:443
  70.4 3.4 %collective-permute-start.10 = (bf16[64,16,128]{2,1,0:T(8,128)(2,1)S(1)}, bf16[64,16,128]{2,1,0:T(8,128)(2,1)S(1)}, u32[]{:S(2)}, u32[]{:S(2)}) collective-permute-start(bf16[64,16,128]{2,1,0:T(8,128)(2,1)S(1)} %collective-permute-done.7.s2), channel_id=1, source_target_pairs={{0,4},{4,12},{12,8},{8,0},{1,5},{5,13},{13,9},{9,1},{2,6},{6,14},{... | collective-permute-start | bytes 786440 | tf_op jit(solution)/shard_map/ppermute | solution.py:552
  75.5 3.7 %collective-permute-done.16.s2 = bf16[64,16,128]{2,1,0:T(8,128)(2,1)S(1)} collective-permute-done((bf16[64,16,128]{2,1,0:T(8,128)(2,1)S(1)}, bf16[64,16,128]{2,1,0:T(8,128)(2,1)S(1)}, u32[]{:S(2)}, u32[]{:S(2)}) %collective-permute-start.16) | collective-permute-done | bytes 262176 | tf_op jit(solution)/shard_map/ppermute | solution.py:552
  82.1 3.4 %collective-permute-start.19 = (bf16[64,16,128]{2,1,0:T(8,128)(2,1)S(1)}, bf16[64,16,128]{2,1,0:T(8,128)(2,1)S(1)}, u32[]{:S(2)}, u32[]{:S(2)}) collective-permute-start(bf16[64,16,128]{2,1,0:T(8,128)(2,1)S(1)} %get-tuple-element.110), channel_id=1, source_target_pairs={{0,4},{4,12},{12,8},{8,0},{1,5},{5,13},{13,9},{9,1},{2,6},{6,14},{... | collective-permute-start | bytes 786440 | tf_op jit(solution)/shard_map/ppermute | solution.py:552
  94.5 5.7 %collective-permute-done.27 = bf16[64,16,128]{2,1,0:T(8,128)(2,1)S(1)} collective-permute-done((bf16[64,16,128]{2,1,0:T(8,128)(2,1)S(1)}, bf16[64,16,128]{2,1,0:T(8,128)(2,1)S(1)}, u32[]{:S(2)}, u32[]{:S(2)}) %collective-permute-start.27) | collective-permute-done | bytes 262176 | tf_op jit(solution)/shard_map/ppermute | solution.py:552
  105.8 4.5 %collective-permute-done.18.c_ref = bf16[64,16,128]{2,1,0:T(8,128)(2,1)S(1)} collective-permute-done((bf16[64,16,128]{2,1,0:T(8,128)(2,1)S(1)}, bf16[64,16,128]{2,1,0:T(8,128)(2,1)S(1)}, u32[]{:S(2)}, u32[]{:S(2)}) %collective-permute-start.18) | collective-permute-done | bytes 262176 | tf_op jit(solution)/shard_map/ppermute | solution.py:558
  110.3 3.5 %mid_part.6 = (bf16[64,16,128]{2,1,0:T(8,128)(2,1)S(1)}, bf16[64,16,128]{2,1,0:T(8,128)(2,1)}, f32[128,128]{1,0:T(8,128)S(1)}, f32[128,128]{1,0:T(8,128)S(1)}) custom-call(bf16[64,16,128]{2,1,0:T(8,128)(2,1)S(1)} %get-tuple-element.112.a_ref, bf16[2,64,16,128]{3,2,1,0:T(8,128)(2,1)S(1)} %collective-permute-done.17.b_ref, ...), custom_call_target="tpu_custom_call" | custom-call | flops 201326592 | bytes 2097152 | tf_op jit(solution)/shard_map/mid_part/pallas_call | solution.py:443
  115.9 3.6 %mid_part.7 = (bf16[64,16,128]{2,1,0:T(8,128)(2,1)}, bf16[64,16,128]{2,1,0:T(8,128)(2,1)}, f32[128,128]{1,0:T(8,128)S(1)}, f32[128,128]{1,0:T(8,128)S(1)}) custom-call(bf16[64,16,128]{2,1,0:T(8,128)(2,1)S(1)} %get-tuple-element.134.a_ref, bf16[2,64,16,128]{3,2,1,0:T(8,128)(2,1)S(1)} %collective-permute-done.25.b_ref, ...), custom_call_target="tpu_custom_call" | custom-call | flops 201326592 | bytes 2097152 | tf_op jit(solution)/shard_map/mid_part/pallas_call | solution.py:443
  122.1 3.4 %collective-permute-start.32 = (bf16[64,16,128]{2,1,0:T(8,128)(2,1)}, bf16[64,16,128]{2,1,0:T(8,128)(2,1)}, u32[]{:S(2)}, u32[]{:S(2)}) collective-permute-start(bf16[64,16,128]{2,1,0:T(8,128)(2,1)} %add_convert_fusion.6), channel_id=1, source_target_pairs={{0,4},{4,12},{12,8},{8,0},{1,5},{5,13},{13,9},{9,1},{2,6},{6,14},{... | collective-permute-start | bytes 786440 | tf_op jit(solution)/shard_map/ppermute | solution.py:552
  126.9 3.7 %dright_part.7 = (bf16[64,16,128]{2,1,0:T(8,128)(2,1)}, bf16[64,16,128]{2,1,0:T(8,128)(2,1)S(1)}, bf16[64,16,128]{2,1,0:T(8,128)(2,1)S(1)}, bf16[64,16,128]{2,1,0:T(8,128)(2,1)S(1)}) custom-call(bf16[64,16,128]{2,1,0:T(8,128)(2,1)S(1)} %get-tuple-element.146.refs_0_, bf16[64,16,128]{2,1,0:T(8,128)(2,1)} %collective-permute-done.33.refs_1_, ...), custom_call_target="tpu_custom_call" | custom-call | flops 268435456 | bytes 6291456 | tf_op jit(solution)/shard_map/dright_part/pallas_call | solution.py:459
  130.6 3.4 %collective-permute-start.37 = (bf16[64,16,128]{2,1,0:T(8,128)(2,1)S(1)}, bf16[64,16,128]{2,1,0:T(8,128)(2,1)S(1)}, u32[]{:S(2)}, u32[]{:S(2)}) collective-permute-start(bf16[64,16,128]{2,1,0:T(8,128)(2,1)S(1)} %get-tuple-element.151), channel_id=1, source_target_pairs={{0,4},{4,12},{12,8},{8,0},{1,5},{5,13},{13,9},{9,1},{2,6},{6,14},{... | collective-permute-start | bytes 786440 | tf_op jit(solution)/shard_map/ppermute | solution.py:552
  135.4 3.6 %dright_part.6 = (bf16[64,16,128]{2,1,0:T(8,128)(2,1)}, bf16[64,16,128]{2,1,0:T(8,128)(2,1)S(1)}, bf16[64,16,128]{2,1,0:T(8,128)(2,1)S(1)}, bf16[64,16,128]{2,1,0:T(8,128)(2,1)S(1)}) custom-call(bf16[64,16,128]{2,1,0:T(8,128)(2,1)} %get-tuple-element.141.refs_0_.refs_4_, bf16[64,16,128]{2,1,0:T(8,128)(2,1)} %collective-permute-done.29.refs_1_.refs_5_, ...), custom_call_target="tpu_custom_call" | custom-call | flops 268435456 | bytes 6291456 | tf_op jit(solution)/shard_map/dright_part/pallas_call | solution.py:459
  140.0 3.2 %dleft_part.3.dleft_ref = f32[64,64,128]{2,1,0:T(8,128)S(1)} custom-call(bf16[64,16,128]{2,1,0:T(8,128)(2,1)S(1)} %get-tuple-element.146.refs_0_, bf16[64,16,128]{2,1,0:T(8,128)(2,1)} %collective-permute-done.33.refs_1_, bf16[64,16,128]{2,1,0:T(8,128)(2,1)} %collective-permute-done.34.refs_2_, bf16[64,16,128]{2,1,0:T(8,128)(2,1)} %collective-permute-done.35.refs_3_, ...), custom_call_target="tpu_custom_call" | custom-call | flops 268435456 | bytes 8388608 | tf_op jit(solution)/shard_map/dleft_part/pallas_call | solution.py:474
  144.0 5.9 %final_a_part.1 = (f32[128,4096]{1,0:T(8,128)S(1)}, f32[128,256]{1,0:T(8,128)S(1)}) custom-call(bf16[64,64,128]{2,1,0:T(8,128)(2,1)S(1)} %copy-done, f32[64,64,128]{2,1,0:T(8,128)S(1)} %dleft_part.3.dleft_ref, s32[1,256]{1,0:T(1,128)S(1)} %bitcast.43, f32[1,128]{1,0:T(1,128)S(1)} %bitcast.32, bf16[128,512]{1,0:T(8,128)(2,1)S(1)} %copy-done.2, ...), custom_call_target="tpu_custom_call" | custom-call | flops 939524096 | bytes 8388608 | tf_op jit(solution)/shard_map/final_a_part/pallas_call | solution.py:487
  154.5 3.1 %final_b_part.4 = (bf16[64,64,128]{2,1,0:T(8,128)(2,1)}, f32[128,256]{1,0:T(8,128)S(1)}) custom-call(bf16[64,64,128]{2,1,0:T(8,128)(2,1)S(1)} %copy-done, f32[128,4096]{1,0:T(8,128)S(1)} %get-tuple-element.159.part_ref, bf16[64,16,128]{2,1,0:T(8,128)(2,1)S(1)} %copy-done.14, bf16[64,16,128]{2,1,0:T(8,128)(2,1)} %collective-permute-done.36.b_ref, ...), custom_call_target="tpu_custom_call" | custom-call | flops 469762048 | bytes 4194304 | tf_op jit(solution)/shard_map/final_b_part/pallas_call | solution.py:515
  163.2 2.8 %collective-permute-start.42 = (bf16[64,16,128]{2,1,0:T(8,128)(2,1)S(1)}, bf16[64,16,128]{2,1,0:T(8,128)(2,1)S(1)}, u32[]{:S(2)}, u32[]{:S(2)}) collective-permute-start(bf16[64,16,128]{2,1,0:T(8,128)(2,1)S(1)} %add_convert_fusion), channel_id=1, source_target_pairs={{0,4},{4,12},{12,8},{8,0},{1,5},{5,13},{13,9},{9,1},{2,6},{6,14},{... | collective-permute-start | bytes 786440 | tf_op jit(solution)/shard_map/ppermute | solution.py:552
  166.0 2.7 %collective-permute-done.43.b_ref = bf16[64,16,128]{2,1,0:T(8,128)(2,1)S(1)} collective-permute-done((bf16[64,16,128]{2,1,0:T(8,128)(2,1)S(1)}, bf16[64,16,128]{2,1,0:T(8,128)(2,1)S(1)}, u32[]{:S(2)}, u32[]{:S(2)}) %collective-permute-start.43) | collective-permute-done | bytes 262176 | tf_op jit(solution)/shard_map/ppermute | solution.py:552
  170.9 3.1 %collective-permute-done.42.b_ref = bf16[64,16,128]{2,1,0:T(8,128)(2,1)S(1)} collective-permute-done((bf16[64,16,128]{2,1,0:T(8,128)(2,1)S(1)}, bf16[64,16,128]{2,1,0:T(8,128)(2,1)S(1)}, u32[]{:S(2)}, u32[]{:S(2)}) %collective-permute-start.42) | collective-permute-done | bytes 262176 | tf_op jit(solution)/shard_map/ppermute | solution.py:552
  180.8 3.4 %collective-permute-done.45 = bf16[64,768]{1,0:T(8,128)(2,1)S(1)} collective-permute-done((bf16[64,768]{1,0:T(8,128)(2,1)S(1)}, bf16[64,768]{1,0:T(8,128)(2,1)S(1)}, u32[]{:S(2)}, u32[]{:S(2)}) %collective-permute-start.45) | collective-permute-done | bytes 98336 | tf_op jit(solution)/shard_map/ppermute | solution.py:558
  186.8 2.6 %collective-permute-done.46 = bf16[64,768]{1,0:T(8,128)(2,1)S(1)} collective-permute-done((bf16[64,768]{1,0:T(8,128)(2,1)S(1)}, bf16[64,768]{1,0:T(8,128)(2,1)S(1)}, u32[]{:S(2)}, u32[]{:S(2)}) %collective-permute-start.46) | collective-permute-done | bytes 98336 | tf_op jit(solution)/shard_map/ppermute | solution.py:555
  190.7 4.3 %collective-permute-done.47 = bf16[64,768]{1,0:T(8,128)(2,1)S(1)} collective-permute-done((bf16[64,768]{1,0:T(8,128)(2,1)S(1)}, bf16[64,768]{1,0:T(8,128)(2,1)S(1)}, u32[]{:S(2)}, u32[]{:S(2)}) %collective-permute-start.47) | collective-permute-done | bytes 98336 | tf_op jit(solution)/shard_map/ppermute | solution.py:555
  (173 shorter events, 81.0 us)
Async XLA Ops:
  2.6 11.2 %collective-permute-start.3 = (bf16[64,16,128]{2,1,0:T(8,128)(2,1)S(1)}, bf16[64,16,128]{2,1,0:T(8,128)(2,1)S(1)}, u32[]{:S(2)}, u32[]{:S(2)}) collective-permute-start(bf16[64,16,128]{2,1,0:T(8,128)(2,1)S(1)} %right_part.6.s0), channel_id=1, source_target_pairs={{0,4},{4,12},{12,8},{8,0},{1,5},{5,13},{13,9},{9,1},{2,6},{6,14},{... | collective-permute-start | bytes 786440 | tf_op jit(solution)/shard_map/ppermute | solution.py:552
  7.6 12.6 %collective-permute-start = (bf16[64,16,128]{2,1,0:T(8,128)(2,1)S(1)}, bf16[64,16,128]{2,1,0:T(8,128)(2,1)S(1)}, u32[]{:S(2)}, u32[]{:S(2)}) collective-permute-start(bf16[64,16,128]{2,1,0:T(8,128)(2,1)S(1)} %right_part.5.s0), channel_id=1, source_target_pairs={{0,4},{4,12},{12,8},{8,0},{1,5},{5,13},{13,9},{9,1},{2,6},{6,14},{... | collective-permute-start | bytes 786440 | tf_op jit(solution)/shard_map/ppermute | solution.py:552
  13.8 11.8 %collective-permute-start.4 = (bf16[64,16,128]{2,1,0:T(8,128)(2,1)S(1)}, bf16[64,16,128]{2,1,0:T(8,128)(2,1)S(1)}, u32[]{:S(2)}, u32[]{:S(2)}) collective-permute-start(bf16[64,16,128]{2,1,0:T(8,128)(2,1)S(1)} %collective-permute-done.3.s1), channel_id=1, source_target_pairs={{0,4},{4,12},{12,8},{8,0},{1,5},{5,13},{13,9},{9,1},{2,6},{6,14},{... | collective-permute-start | bytes 786440 | tf_op jit(solution)/shard_map/ppermute | solution.py:552
  20.2 10.5 %collective-permute-start.1 = (bf16[64,16,128]{2,1,0:T(8,128)(2,1)S(1)}, bf16[64,16,128]{2,1,0:T(8,128)(2,1)S(1)}, u32[]{:S(2)}, u32[]{:S(2)}) collective-permute-start(bf16[64,16,128]{2,1,0:T(8,128)(2,1)S(1)} %collective-permute-done.s1), channel_id=1, source_target_pairs={{0,4},{4,12},{12,8},{8,0},{1,5},{5,13},{13,9},{9,1},{2,6},{6,14},{... | collective-permute-start | bytes 786440 | tf_op jit(solution)/shard_map/ppermute | solution.py:552
  25.6 10.7 %collective-permute-start.5 = (bf16[64,16,128]{2,1,0:T(8,128)(2,1)S(1)}, bf16[64,16,128]{2,1,0:T(8,128)(2,1)S(1)}, u32[]{:S(2)}, u32[]{:S(2)}) collective-permute-start(bf16[64,16,128]{2,1,0:T(8,128)(2,1)S(1)} %collective-permute-done.4.s2), channel_id=1, source_target_pairs={{0,4},{4,12},{12,8},{8,0},{1,5},{5,13},{13,9},{9,1},{2,6},{6,14},{... | collective-permute-start | bytes 786440 | tf_op jit(solution)/shard_map/ppermute | solution.py:552
  30.7 10.4 %collective-permute-start.14 = (bf16[64,16,128]{2,1,0:T(8,128)(2,1)S(1)}, bf16[64,16,128]{2,1,0:T(8,128)(2,1)S(1)}, u32[]{:S(2)}, u32[]{:S(2)}) collective-permute-start(bf16[64,16,128]{2,1,0:T(8,128)(2,1)S(1)} %collective-permute-done.1.s2), channel_id=1, source_target_pairs={{0,4},{4,12},{12,8},{8,0},{1,5},{5,13},{13,9},{9,1},{2,6},{6,14},{... | collective-permute-start | bytes 786440 | tf_op jit(solution)/shard_map/ppermute | solution.py:552
  43.2 10.1 %collective-permute-start.2 = (bf16[64,16,128]{2,1,0:T(8,128)(2,1)S(1)}, bf16[64,16,128]{2,1,0:T(8,128)(2,1)S(1)}, u32[]{:S(2)}, u32[]{:S(2)}) collective-permute-start(bf16[64,16,128]{2,1,0:T(8,128)(2,1)S(1)} %right_part.4.s0), channel_id=1, source_target_pairs={{0,4},{4,12},{12,8},{8,0},{1,5},{5,13},{13,9},{9,1},{2,6},{6,14},{... | collective-permute-start | bytes 786440 | tf_op jit(solution)/shard_map/ppermute | solution.py:552
  44.0 14.8 %collective-permute-start.9 = (bf16[64,16,128]{2,1,0:T(8,128)(2,1)S(1)}, bf16[64,16,128]{2,1,0:T(8,128)(2,1)S(1)}, u32[]{:S(2)}, u32[]{:S(2)}) collective-permute-start(bf16[64,16,128]{2,1,0:T(8,128)(2,1)S(1)} %right_part.7.s0), channel_id=1, source_target_pairs={{0,4},{4,12},{12,8},{8,0},{1,5},{5,13},{13,9},{9,1},{2,6},{6,14},{... | collective-permute-start | bytes 786440 | tf_op jit(solution)/shard_map/ppermute | solution.py:552
  47.5 11.3 %collective-permute-start.8 = (bf16[64,16,128]{2,1,0:T(8,128)(2,1)S(1)}, bf16[64,16,128]{2,1,0:T(8,128)(2,1)S(1)}, u32[]{:S(2)}, u32[]{:S(2)}) collective-permute-start(bf16[64,16,128]{2,1,0:T(8,128)(2,1)S(1)} %fusion.3), channel_id=1, source_target_pairs={{0,2},{1,3},{2,0},{3,1},{4,6},{5,7},{6,4},{7,5},{8,10},{9,11},{10,... | collective-permute-start | bytes 786440 | tf_op jit(solution)/shard_map/ppermute | solution.py:558
  49.1 14.8 %collective-permute-start.20 = (bf16[64,16,128]{2,1,0:T(8,128)(2,1)S(1)}, bf16[64,16,128]{2,1,0:T(8,128)(2,1)S(1)}, u32[]{:S(2)}, u32[]{:S(2)}) collective-permute-start(bf16[64,16,128]{2,1,0:T(8,128)(2,1)S(1)} %fusion.2), channel_id=1, source_target_pairs={{0,2},{1,3},{2,0},{3,1},{4,6},{5,7},{6,4},{7,5},{8,10},{9,11},{10,... | collective-permute-start | bytes 786440 | tf_op jit(solution)/shard_map/ppermute | solution.py:558
  53.2 10.8 %collective-permute-start.7 = (bf16[64,16,128]{2,1,0:T(8,128)(2,1)S(1)}, bf16[64,16,128]{2,1,0:T(8,128)(2,1)S(1)}, u32[]{:S(2)}, u32[]{:S(2)}) collective-permute-start(bf16[64,16,128]{2,1,0:T(8,128)(2,1)S(1)} %collective-permute-done.2.s1), channel_id=1, source_target_pairs={{0,4},{4,12},{12,8},{8,0},{1,5},{5,13},{13,9},{9,1},{2,6},{6,14},{... | collective-permute-start | bytes 786440 | tf_op jit(solution)/shard_map/ppermute | solution.py:552
  69.1 10.1 %collective-permute-start.16 = (bf16[64,16,128]{2,1,0:T(8,128)(2,1)S(1)}, bf16[64,16,128]{2,1,0:T(8,128)(2,1)S(1)}, u32[]{:S(2)}, u32[]{:S(2)}) collective-permute-start(bf16[64,16,128]{2,1,0:T(8,128)(2,1)S(1)} %collective-permute-done.9.s1), channel_id=1, source_target_pairs={{0,4},{4,12},{12,8},{8,0},{1,5},{5,13},{13,9},{9,1},{2,6},{6,14},{... | collective-permute-start | bytes 786440 | tf_op jit(solution)/shard_map/ppermute | solution.py:552
  69.9 10.1 %collective-permute-start.12 = (bf16[64,16,128]{2,1,0:T(8,128)(2,1)S(1)}, bf16[64,16,128]{2,1,0:T(8,128)(2,1)S(1)}, u32[]{:S(2)}, u32[]{:S(2)}) collective-permute-start(bf16[64,16,128]{2,1,0:T(8,128)(2,1)S(1)} %get-tuple-element.127.refs_0_), channel_id=1, source_target_pairs={{0,1},{1,0},{2,3},{3,2},{4,5},{5,4},{6,7},{7,6},{8,9},{9,8},{10,11... | collective-permute-start | bytes 786440 | tf_op jit(solution)/shard_map/ppermute | solution.py:561
  70.4 15.1 %collective-permute-start.10 = (bf16[64,16,128]{2,1,0:T(8,128)(2,1)S(1)}, bf16[64,16,128]{2,1,0:T(8,128)(2,1)S(1)}, u32[]{:S(2)}, u32[]{:S(2)}) collective-permute-start(bf16[64,16,128]{2,1,0:T(8,128)(2,1)S(1)} %collective-permute-done.7.s2), channel_id=1, source_target_pairs={{0,4},{4,12},{12,8},{8,0},{1,5},{5,13},{13,9},{9,1},{2,6},{6,14},{... | collective-permute-start | bytes 786440 | tf_op jit(solution)/shard_map/ppermute | solution.py:552
  75.5 10.0 %collective-permute-start.24 = (bf16[64,16,128]{2,1,0:T(8,128)(2,1)S(1)}, bf16[64,16,128]{2,1,0:T(8,128)(2,1)S(1)}, u32[]{:S(2)}, u32[]{:S(2)}) collective-permute-start(bf16[64,16,128]{2,1,0:T(8,128)(2,1)S(1)} %collective-permute-done.22.refs_1_.refs_5_), channel_id=1, source_target_pairs={{0,1},{1,0},{2,3},{3,2},{4,5},{5,4},{6,7},{7,6},{8,9},{9,8},{10,11... | collective-permute-start | bytes 786440 | tf_op jit(solution)/shard_map/ppermute | solution.py:561
  79.2 11.6 %collective-permute-start.21 = (bf16[64,16,128]{2,1,0:T(8,128)(2,1)S(1)}, bf16[64,16,128]{2,1,0:T(8,128)(2,1)S(1)}, u32[]{:S(2)}, u32[]{:S(2)}) collective-permute-start(bf16[64,16,128]{2,1,0:T(8,128)(2,1)S(1)} %collective-permute-done.16.s2), channel_id=1, source_target_pairs={{0,4},{4,12},{12,8},{8,0},{1,5},{5,13},{13,9},{9,1},{2,6},{6,14},{... | collective-permute-start | bytes 786440 | tf_op jit(solution)/shard_map/ppermute | solution.py:552
  82.1 12.4 %collective-permute-start.19 = (bf16[64,16,128]{2,1,0:T(8,128)(2,1)S(1)}, bf16[64,16,128]{2,1,0:T(8,128)(2,1)S(1)}, u32[]{:S(2)}, u32[]{:S(2)}) collective-permute-start(bf16[64,16,128]{2,1,0:T(8,128)(2,1)S(1)} %get-tuple-element.110), channel_id=1, source_target_pairs={{0,4},{4,12},{12,8},{8,0},{1,5},{5,13},{13,9},{9,1},{2,6},{6,14},{... | collective-permute-start | bytes 786440 | tf_op jit(solution)/shard_map/ppermute | solution.py:552
  88.5 12.5 %collective-permute-start.17 = (bf16[2,64,16,128]{3,2,1,0:T(8,128)(2,1)S(1)}, bf16[2,64,16,128]{3,2,1,0:T(8,128)(2,1)S(1)}, u32[]{:S(2)}, u32[]{:S(2)}) collective-permute-start(bf16[2,64,16,128]{3,2,1,0:T(8,128)(2,1)S(1)} %get-tuple-element.113), channel_id=1, source_target_pairs={{0,1},{1,0},{2,3},{3,2},{4,5},{5,4},{6,7},{7,6},{8,9},{9,8},{10,11... | collective-permute-start | bytes 1572872 | tf_op jit(solution)/shard_map/ppermute | solution.py:561
  90.6 9.6 %collective-permute-start.27 = (bf16[64,16,128]{2,1,0:T(8,128)(2,1)S(1)}, bf16[64,16,128]{2,1,0:T(8,128)(2,1)S(1)}, u32[]{:S(2)}, u32[]{:S(2)}) collective-permute-start(bf16[64,16,128]{2,1,0:T(8,128)(2,1)S(1)} %get-tuple-element.123), channel_id=1, source_target_pairs={{0,4},{4,12},{12,8},{8,0},{1,5},{5,13},{13,9},{9,1},{2,6},{6,14},{... | collective-permute-start | bytes 786440 | tf_op jit(solution)/shard_map/ppermute | solution.py:552
  92.8 9.5 %collective-permute-start.25 = (bf16[2,64,16,128]{3,2,1,0:T(8,128)(2,1)S(1)}, bf16[2,64,16,128]{3,2,1,0:T(8,128)(2,1)S(1)}, u32[]{:S(2)}, u32[]{:S(2)}) collective-permute-start(bf16[2,64,16,128]{3,2,1,0:T(8,128)(2,1)S(1)} %get-tuple-element.126), channel_id=1, source_target_pairs={{0,1},{1,0},{2,3},{3,2},{4,5},{5,4},{6,7},{7,6},{8,9},{9,8},{10,11... | collective-permute-start | bytes 1572872 | tf_op jit(solution)/shard_map/ppermute | solution.py:561
  101.7 12.8 %collective-permute-start.28 = (bf16[64,16,128]{2,1,0:T(8,128)(2,1)S(1)}, bf16[64,16,128]{2,1,0:T(8,128)(2,1)S(1)}, u32[]{:S(2)}, u32[]{:S(2)}) collective-permute-start(bf16[64,16,128]{2,1,0:T(8,128)(2,1)S(1)} %add_convert_fusion.7), channel_id=1, source_target_pairs={{0,4},{4,12},{12,8},{8,0},{1,5},{5,13},{13,9},{9,1},{2,6},{6,14},{... | collective-permute-start | bytes 786440 | tf_op jit(solution)/shard_map/ppermute | solution.py:552
  102.4 12.8 %collective-permute-start.26 = (bf16[64,16,128]{2,1,0:T(8,128)(2,1)S(1)}, bf16[64,16,128]{2,1,0:T(8,128)(2,1)S(1)}, u32[]{:S(2)}, u32[]{:S(2)}) collective-permute-start(bf16[64,16,128]{2,1,0:T(8,128)(2,1)S(1)} %fusion), channel_id=1, source_target_pairs={{0,2},{1,3},{2,0},{3,1},{4,6},{5,7},{6,4},{7,5},{8,10},{9,11},{10,... | collective-permute-start | bytes 786440 | tf_op jit(solution)/shard_map/ppermute | solution.py:558
  115.2 10.3 %collective-permute-start.36 = (bf16[64,16,128]{2,1,0:T(8,128)(2,1)}, bf16[64,16,128]{2,1,0:T(8,128)(2,1)}, u32[]{:S(2)}, u32[]{:S(2)}) collective-permute-start(bf16[64,16,128]{2,1,0:T(8,128)(2,1)} %add_convert_fusion.5), channel_id=1, source_target_pairs={{0,4},{4,12},{12,8},{8,0},{1,5},{5,13},{13,9},{9,1},{2,6},{6,14},{... | collective-permute-start | bytes 786440 | tf_op jit(solution)/shard_map/ppermute | solution.py:552
  122.1 11.9 %collective-permute-start.32 = (bf16[64,16,128]{2,1,0:T(8,128)(2,1)}, bf16[64,16,128]{2,1,0:T(8,128)(2,1)}, u32[]{:S(2)}, u32[]{:S(2)}) collective-permute-start(bf16[64,16,128]{2,1,0:T(8,128)(2,1)} %add_convert_fusion.6), channel_id=1, source_target_pairs={{0,4},{4,12},{12,8},{8,0},{1,5},{5,13},{13,9},{9,1},{2,6},{6,14},{... | collective-permute-start | bytes 786440 | tf_op jit(solution)/shard_map/ppermute | solution.py:552
  125.5 9.9 %collective-permute-start.30 = (bf16[64,16,128]{2,1,0:T(8,128)(2,1)}, bf16[64,16,128]{2,1,0:T(8,128)(2,1)S(1)}, u32[]{:S(2)}, u32[]{:S(2)}) collective-permute-start(bf16[64,16,128]{2,1,0:T(8,128)(2,1)} %get-tuple-element.141.refs_0_.refs_4_), channel_id=1, source_target_pairs={{0,1},{1,0},{2,3},{3,2},{4,5},{5,4},{6,7},{7,6},{8,9},{9,8},{10,11... | collective-permute-start | bytes 786440 | tf_op jit(solution)/shard_map/ppermute | solution.py:561
  130.6 12.6 %collective-permute-start.37 = (bf16[64,16,128]{2,1,0:T(8,128)(2,1)S(1)}, bf16[64,16,128]{2,1,0:T(8,128)(2,1)S(1)}, u32[]{:S(2)}, u32[]{:S(2)}) collective-permute-start(bf16[64,16,128]{2,1,0:T(8,128)(2,1)S(1)} %get-tuple-element.151), channel_id=1, source_target_pairs={{0,4},{4,12},{12,8},{8,0},{1,5},{5,13},{13,9},{9,1},{2,6},{6,14},{... | collective-permute-start | bytes 786440 | tf_op jit(solution)/shard_map/ppermute | solution.py:552
  135.0 25.1 %collective-permute-start.40 = (bf16[64,16,128]{2,1,0:T(8,128)(2,1)S(1)}, bf16[64,16,128]{2,1,0:T(8,128)(2,1)S(1)}, u32[]{:S(2)}, u32[]{:S(2)}) collective-permute-start(bf16[64,16,128]{2,1,0:T(8,128)(2,1)S(1)} %add_convert_fusion.4), channel_id=1, source_target_pairs={{0,4},{4,12},{12,8},{8,0},{1,5},{5,13},{13,9},{9,1},{2,6},{6,14},{... | collective-permute-start | bytes 786440 | tf_op jit(solution)/shard_map/ppermute | solution.py:552
  139.0 12.9 %collective-permute-start.38 = (bf16[64,16,128]{2,1,0:T(8,128)(2,1)S(1)}, bf16[64,16,128]{2,1,0:T(8,128)(2,1)S(1)}, u32[]{:S(2)}, u32[]{:S(2)}) collective-permute-start(bf16[64,16,128]{2,1,0:T(8,128)(2,1)S(1)} %get-tuple-element.145), channel_id=1, source_target_pairs={{0,4},{4,12},{12,8},{8,0},{1,5},{5,13},{13,9},{9,1},{2,6},{6,14},{... | collective-permute-start | bytes 786440 | tf_op jit(solution)/shard_map/ppermute | solution.py:552
  143.3 14.4 %collective-permute-start.41 = (bf16[64,16,128]{2,1,0:T(8,128)(2,1)S(1)}, bf16[64,16,128]{2,1,0:T(8,128)(2,1)S(1)}, u32[]{:S(2)}, u32[]{:S(2)}) collective-permute-start(bf16[64,16,128]{2,1,0:T(8,128)(2,1)S(1)} %add_convert_fusion.3), channel_id=1, source_target_pairs={{0,4},{4,12},{12,8},{8,0},{1,5},{5,13},{13,9},{9,1},{2,6},{6,14},{... | collective-permute-start | bytes 786440 | tf_op jit(solution)/shard_map/ppermute | solution.py:552
  151.9 11.2 %collective-permute-start.39 = (bf16[64,16,128]{2,1,0:T(8,128)(2,1)S(1)}, bf16[64,16,128]{2,1,0:T(8,128)(2,1)S(1)}, u32[]{:S(2)}, u32[]{:S(2)}) collective-permute-start(bf16[64,16,128]{2,1,0:T(8,128)(2,1)S(1)} %add_convert_fusion.2), channel_id=1, source_target_pairs={{0,4},{4,12},{12,8},{8,0},{1,5},{5,13},{13,9},{9,1},{2,6},{6,14},{... | collective-permute-start | bytes 786440 | tf_op jit(solution)/shard_map/ppermute | solution.py:552
  157.7 11.0 %collective-permute-start.43 = (bf16[64,16,128]{2,1,0:T(8,128)(2,1)S(1)}, bf16[64,16,128]{2,1,0:T(8,128)(2,1)S(1)}, u32[]{:S(2)}, u32[]{:S(2)}) collective-permute-start(bf16[64,16,128]{2,1,0:T(8,128)(2,1)S(1)} %add_convert_fusion.1), channel_id=1, source_target_pairs={{0,4},{4,12},{12,8},{8,0},{1,5},{5,13},{13,9},{9,1},{2,6},{6,14},{... | collective-permute-start | bytes 786440 | tf_op jit(solution)/shard_map/ppermute | solution.py:552
  163.2 10.8 %collective-permute-start.42 = (bf16[64,16,128]{2,1,0:T(8,128)(2,1)S(1)}, bf16[64,16,128]{2,1,0:T(8,128)(2,1)S(1)}, u32[]{:S(2)}, u32[]{:S(2)}) collective-permute-start(bf16[64,16,128]{2,1,0:T(8,128)(2,1)S(1)} %add_convert_fusion), channel_id=1, source_target_pairs={{0,4},{4,12},{12,8},{8,0},{1,5},{5,13},{13,9},{9,1},{2,6},{6,14},{... | collective-permute-start | bytes 786440 | tf_op jit(solution)/shard_map/ppermute | solution.py:552
  (45 other events, 386.0 us)
